TPU v7x, 32 devices: a whole 2x2x4 slice. The times are simulated.
32 devices in a mesh: grp: 2 (over x), aux: 16 (over z, y, core).
Axes of the slice: x: 2, y: 2, z: 4, core: 2. Of those that a mesh axis runs over, the one named last changes fastest.
Arguments:
- tiles: bfloat16 [2048, 5, 128, 128], P(('grp', 'aux')), parts along dimension 0, may hold values from -6 to 6
- c_orbitals: bfloat16 [8192, 128], P(('grp', 'aux')), parts along dimension 0, may hold values from -0.0078125 to 0.0078125
- basis_order: int32 [64], P('grp'), parts along dimension 0, may hold values from 0 to 31, as said below
- tile_block: int32 [2048], P(('grp', 'aux')), parts along dimension 0, may hold values from 0 to 31, as said below
- tile_aux: int32 [2048], P(('grp', 'aux')), parts along dimension 0, may hold values from 0 to 7
- live: int32 [32], P(('grp', 'aux')), parts along dimension 0, may hold values from 1 to 64, as said below
Outputs:
- exchange_c: bfloat16 [8192, 128], P(('grp', 'aux')), parts along dimension 0
There are 2 independent parts, one for each index of `grp`. A program takes and returns all parts, laid end to end along the dimension named above; each array names one. Nothing has to cross between parts.
Inputs may be any that keep to these rules, and one draw needn't show every extreme that they name: `basis_order`: a permutation of the 32 basis blocks; device d owns positions d * 2 to (d + 1) * 2 - 1. `tile_block`: the tiles of one device name at most one of the blocks owned by any one device. `live`: some device uses all 64 slots.
All inputs are finite; a program needn't handle non-finite values.
Results may differ from a plain program's by a relative error of at most 0.0034.
Values may be sent and summed in bfloat16 or wider, within the bound.
No kernel may reach another device: no remote copies, remote signals or barrier semaphores. Data moves between devices by JAX's collectives and lax.ppermute only.
A program may use at most 128 MiB of HBM per device.

v0:
```python
import jax
import jax.numpy as jnp
from jax import lax
from jax.sharding import PartitionSpec as P

AB_DEV = 8


def on_device(tiles, c_orbitals, basis_order, tile_block, tile_aux, live):
    slots, auxb, blk, nocc = tiles.shape
    nbb = basis_order.shape[0]
    n_aux = lax.axis_size("aux")
    bb_dev = nbb // n_aux
    alive = (lax.iota(jnp.int32, slots) < live[0]).astype(jnp.float32)
    position = jnp.sum(
        jnp.where(
            basis_order[None, :] == tile_block[:, None], lax.iota(jnp.int32, nbb)[None, :], 0
        ),
        axis=1,
    )
    whole = lax.all_gather(c_orbitals, "aux", axis=0, tiled=True)
    picked = whole.reshape(nbb, blk, nocc)[position]
    half = jnp.einsum("tpmi,tmj->tpij", tiles, picked, preferred_element_type=jnp.float32)
    member = (tile_aux[None, :] == lax.iota(jnp.int32, AB_DEV)[:, None]).astype(
        jnp.float32
    ) * alive[None, :]
    fitted = jnp.dot(
        member, half.reshape(slots, auxb * nocc * nocc), precision=lax.Precision.HIGHEST
    )
    fitted = fitted.reshape(AB_DEV, auxb, nocc, nocc).astype(jnp.bfloat16)
    per_tile = fitted[tile_aux]
    partial_value = (
        jnp.einsum("tpmi,tpij->tmj", tiles, per_tile, preferred_element_type=jnp.float32)
        * alive[:, None, None]
    )
    flat = partial_value.reshape(slots, blk * nocc)
    count = lax.axis_size("aux") * (bb_dev * blk)
    nblk = count // blk
    onehot = (position[None, :] == lax.iota(jnp.int32, nblk)[:, None]).astype(jnp.float32) * alive[
        None, :
    ]
    summed = lax.psum_scatter(
        jnp.dot(onehot, flat, precision=lax.Precision.HIGHEST).reshape(count, nocc),
        "aux",
        scatter_dimension=0,
        tiled=True,
    )
    return summed.astype(jnp.bfloat16)


def solution(mesh):
    return jax.shard_map(
        on_device,
        mesh=mesh,
        in_specs=(
            P(("grp", "aux"), None, None, None),
            P(("grp", "aux"), None),
            P("grp"),
            P(("grp", "aux")),
            P(("grp", "aux")),
            P(("grp", "aux")),
        ),
        out_specs=P(("grp", "aux"), None),
        check_vma=False,
    )
```

profile of v0, /device:TPU:0, one launch (start us, length us, event | category | flops | bytes accessed | tf_op | source)
XLA Modules:
  0.0 246.5 jit_solution(14934277549401055096)
XLA Ops:
  6.5 0.0 all-gather.2.cloned.1.call-start
  6.5 0.7 all-gather.2.cloned.1.call-update
  7.3 0.0 reduce-scatter.2.cloned.1.call-start
  8.0 0.8 select_reduce_fusion
  8.7 0.7 compare_select_fusion
  9.4 40.8 %all-gather.2.cloned.1.call-done = bf16[4096,128]{1,0:T(8,128)(2,1)} async-done(((bf16[256,128]{1,0:T(8,128)(2,1)}), bf16[4096,128]{1,0:T(8,128)(2,1)}) %all-gather.2.cloned.1.call-update) | async-done | bytes 1048592 | tf_op jit(solution)/shard_map/all_gather | solution.py:21
  50.2 2.2 gather_fusion
  52.4 13.9 %convolution_bitcast_fusion = f32[64,5,128,128]{2,3,1,0:T(8,128)} fusion(bf16[64,5,128,128]{3,2,1,0:T(8,128)(2,1)} %param.6, bf16[64,128,128]{2,1,0:T(8,128)(2,1)S(1)} %gather_fusion), kind=kOutput, calls=%fused_computation.5 | convolution fusion | flops 1342177280 | bytes 33554432 | tf_op jit(solution)/shard_map/tpmi,tmj->tpij/dot_general | solution.py:23
  66.2 22.6 %copy.12 = f32[64,5,128,128]{3,2,1,0:T(8,128)} copy(f32[64,5,128,128]{2,3,1,0:T(8,128)} %convolution_bitcast_fusion) | data formatting | bytes 41943040 | tf_op jit(solution)/shard_map/tpmi,tmj->tpij/dot_general | solution.py:23
  88.8 21.2 %copy.35 = f32[8,8,640,128]{3,1,2,0:T(8,128)S(1)} copy(f32[8,8,640,128]{3,2,1,0:T(8,128)} %bitcast.46) | data formatting | bytes 41943040
  110.0 0.0 copy-start
  110.0 8.3 %copy.24 = f32[8,8,640,128]{3,2,1,0:T(8,128)} copy(f32[8,8,640,128]{3,1,2,0:T(8,128)S(1)} %copy.35) | data formatting | bytes 41943040
  118.3 0.0 copy-done
  118.4 27.6 %fusion.7 = bf16[8,5,128,128]{3,0,2,1:T(8,128)(2,1)S(1)} fusion(f32[5,128,128,64]{2,1,0,3:T(8,128)} %bitcast.47, f32[64]{0:T(128)S(1)} %compare_convert_fusion, s32[64]{0:T(128)S(1)} %copy-done), kind=kOutput, calls=%fused_computation.12 | convolution fusion | flops 503972864 | bytes 22282752 | tf_op jit(solution)/shard_map/dot_general | solution.py:27
  146.0 0.3 copy.14
  146.3 6.7 %gather_fusion.1 = bf16[64,5,128,128]{3,2,1,0:T(8,128)(2,1)} fusion(bf16[8,5,128,128]{3,2,1,0:T(8,128)(2,1)S(1)} %copy.14, s32[1024]{0:T(1024)S(1)} %pad_clamp_fusion), kind=kCustom, calls=%fused_computation.1 | custom fusion | bytes 20971776 | tf_op jit(solution)/shard_map/gather | solution.py:31
  153.0 10.4 %fusion.5 = f32[64,128,128]{1,2,0:T(8,128)} fusion(bf16[64,5,128,128]{3,2,1,0:T(8,128)(2,1)} %gather_fusion.1, bf16[64,5,128,128]{3,2,1,0:T(8,128)(2,1)} %param.6, f32[64]{0:T(128)S(1)} %compare_convert_fusion), kind=kOutput, calls=%fused_computation.10 | convolution fusion | flops 1343225856 | bytes 25166080 | tf_op jit(solution)/shard_map/tpmi,tpij->tmj/dot_general | solution.py:33
  163.4 5.6 %copy.16 = f32[64,128,128]{2,1,0:T(8,128)} copy(f32[64,128,128]{1,2,0:T(8,128)} %fusion.5) | data formatting | bytes 8388608 | tf_op jit(solution)/shard_map/mul | solution.py:33
  169.0 6.9 %fusion.2 = f32[32,16384]{1,0:T(8,128)S(1)} fusion(f32[8,8,128,128]{3,2,1,0:T(8,128)} %bitcast.48, f32[64]{0:T(128)S(1)} %compare_convert_fusion, s32[64]{0:T(128)S(1)} %select_reduce_fusion), kind=kOutput, calls=%fused_computation.6 | convolution fusion | flops 402657280 | bytes 6291968 | tf_op jit(solution)/shard_map/dot_general | solution.py:43
  176.0 1.5 reshape.44
  177.5 0.0 reduce-scatter.2.cloned.1.call-update
  177.5 60.6 %reduce-scatter.2.cloned.1.call-done = f32[256,128]{1,0:T(8,128)} async-done(((f32[4096,128]{1,0:T(8,128)}), f32[256,128]{1,0:T(8,128)}) %reduce-scatter.2.cloned.1.call-update) | async-done | bytes 131088 | tf_op jit(solution)/shard_map/reduce_scatter | solution.py:42
  238.1 1.5 convert_element_type.21
  (4 shorter events, 0.0 us)
Async XLA Ops:
  6.5 43.7 %all-gather.2.cloned.1.call-start = ((), (), s32[]{:S(2)}) async-start(), calls=%async_computation.1 | async-start | bytes 1114112 | tf_op jit(solution)/shard_map/all_gather | solution.py:21
  7.3 230.9 %reduce-scatter.2.cloned.1.call-start = ((), (), s32[]{:S(2)}) async-start(), calls=%async_computation.2 | async-start | bytes 2228224 | tf_op jit(solution)/shard_map/reduce_scatter | solution.py:42
  110.0 8.3 %copy-start = (s32[64]{0:T(128)S(1)}, s32[64]{0:T(128)}, u32[]{:S(2)}) copy-start(s32[64]{0:T(128)} %param.10) | copy-start | bytes 772
Sparse Core Ops, SparseCore 0:
  9.5 40.6 all-gather.1
  177.6 60.4 reduce-scatter.1
where the time goes:
time: 247 us; the launch traced here: 246 us
  waiting for transfers between devices  102 us (41%)
  local copies, waits for them, and re-layouts  68.4 us (28%)
  matrix products  58.8 us (24%)
  between operations  14.1 us (6%)
  other arithmetic  2.99 us (1%)
    reduce_scatter x1, waiting for transfers between devices, on_device(): lax.psum_scatter(jnp.dot(onehot, flat, precision=lax.Precision.HIGHEST).r...  60.6 us
    all_gather x1, waiting for transfers between devices, on_device(): whole = lax.all_gather(c_orbitals, 'aux', axis=0, tiled=True)  40.8 us
    unnamed x4, local copies, waits for them, and re-layouts  29.5 us
    dot_general x1, matrix products, on_device(): jnp.dot(member, half.reshape(slots, auxb * nocc * nocc), precision=lax.Pr...  27.6 us
    dot_general x1, local copies, waits for them, and re-layouts, on_device(): jnp.einsum('tpmi,tmj->tpij', tiles, picked, preferred_element_type=jnp.fl...  22.6 us
    dot_general x1, matrix products, on_device(): jnp.einsum('tpmi,tmj->tpij', tiles, picked, preferred_element_type=jnp.fl...  13.9 us
    dot_general x1, matrix products, on_device(): jnp.einsum('tpmi,tpij->tmj', tiles, per_tile, preferred_element_type=jnp....  10.4 us
    dot_general x1, matrix products, on_device(): jnp.dot(onehot, flat, precision=lax.Precision.HIGHEST).reshape(count, nocc)  6.94 us
  transfers between devices with their start and end apart: 2, of which 2 were waited for; matrix products, arithmetic and copies ran while one was open for 1% of the time, Pallas kernels for 0%

commit v1 on v0

v1 whole, which is shorter than its diff:
```python
import functools

import jax
import jax.numpy as jnp
from jax import lax
from jax.experimental import pallas as pl
from jax.experimental.pallas import tpu as pltpu
from jax.sharding import PartitionSpec as P

AB_DEV = 8
CHUNK = 4
AHEAD = 8
TAIL = 16
DIRECT_LIMIT = 32


def plan(tile_block, tile_aux, live, basis_order, own, n_aux, bb_dev):
    slots = tile_block.shape[0]
    nbb = basis_order.shape[0]
    chunks = slots // CHUNK + AB_DEV
    t = lax.iota(jnp.int32, slots)
    alive = t < live[0]
    position = jnp.sum(
        jnp.where(
            basis_order[None, :] == tile_block[:, None], lax.iota(jnp.int32, nbb)[None, :], 0
        ),
        axis=1,
    )
    where_to = position // bb_dev
    where_to = jnp.bitwise_xor(where_to, own)
    which = position % bb_dev
    group = jnp.where(alive, tile_aux, AB_DEV)
    ids = lax.iota(jnp.int32, AB_DEV)
    counts = jnp.sum((group[None, :] == ids[:, None]).astype(jnp.int32), axis=1)
    need = (counts + CHUNK - 1) // CHUNK
    ends = jnp.sum(jnp.where(ids[None, :] <= ids[:, None], need[None, :], 0), axis=1)
    rank = jnp.sum(
        ((group[None, :] == group[:, None]) & (t[None, :] < t[:, None])).astype(jnp.int32), axis=1
    )
    start = jnp.sum(jnp.where(group[:, None] > ids[None, :], need[None, :], 0), axis=1)
    place = jnp.where(alive, start * CHUNK + rank, -1)
    q = lax.iota(jnp.int32, chunks * CHUNK)
    hit = place[None, :] == q[:, None]
    lead = place[None, :] == (q // CHUNK * CHUNK)[:, None]
    valid = jnp.any(hit, axis=1)
    slot = jnp.sum(jnp.where(hit, t[None, :], 0), axis=1)
    slot = jnp.where(valid, slot, jnp.sum(jnp.where(lead, t[None, :], 0), axis=1))
    block = jnp.where(valid, jnp.sum(jnp.where(hit, where_to[None, :], 0), axis=1), n_aux)
    gid = jnp.sum(
        (lax.iota(jnp.int32, chunks)[:, None] >= ends[None, :]).astype(jnp.int32), axis=1
    )
    bit = jnp.max(
        jnp.where(
            (where_to[None, :] == lax.iota(jnp.int32, n_aux)[:, None]) & alive[None, :],
            which[None, :],
            0,
        ),
        axis=1,
    )
    return slot, block, jnp.concatenate([gid, ends]), bit


def build_kernel(
    direct, n_aux, chunks, slot_ref, block_ref, gid_ref, bit_ref, tiles_hbm, *refs
):
    n_refs = n_aux if direct else 1
    c_refs, out_refs = refs[:n_refs], refs[n_refs : 2 * n_refs]
    tiles, ct, zacc, zb, acc, sems = refs[2 * n_refs :]
    blk, nocc = ct.shape[2], ct.shape[1]
    auxb = tiles.shape[1]
    total = gid_ref[chunks + AB_DEV - 1]

    def copies(chunk):
        for i in range(CHUNK):
            pos = chunk * CHUNK + i
            slot = slot_ref[pos]
            yield block_ref[pos] < n_aux, pltpu.make_async_copy(
                tiles_hbm.at[slot], tiles.at[slot], sems.at[chunk]
            )

    def start(chunk):
        for used, copy in copies(chunk):
            @pl.when(used)
            def _():
                copy.start()

    def wait(chunk):
        for used, copy in copies(chunk):
            @pl.when(used)
            def _():
                copy.wait()

    @pl.loop(0, jnp.minimum(total, AHEAD))
    def _(chunk):
        start(chunk)

    def turn(m, source):
        ct[m] = source[pl.ds(pl.multiple_of(bit_ref[m] * blk, blk), blk), :].T

    if direct:
        for m in range(n_aux):
            turn(m, c_refs[m])
    else:
        @pl.loop(0, n_aux)
        def _(m):
            turn(m, c_refs[0].at[m])

    ct[n_aux] = jnp.zeros((nocc, blk), ct.dtype)
    acc[...] = jnp.zeros(acc.shape, acc.dtype)
    zacc[...] = jnp.zeros(zacc.shape, zacc.dtype)

    @pl.loop(0, total)
    def _(chunk):
        @pl.when(chunk + AHEAD < total)
        def _():
            start(chunk + AHEAD)

        wait(chunk)
        g = gid_ref[chunk]
        spots = [chunk * CHUNK + i for i in range(CHUNK)]
        left = jnp.concatenate([ct[block_ref[pos]] for pos in spots], axis=1)
        for p in range(auxb):
            right = jnp.concatenate([tiles[slot_ref[pos], p] for pos in spots], axis=0)
            zacc[g, p] += jnp.dot(left, right, preferred_element_type=jnp.float32)

    for g in range(AB_DEV):
        for p in range(auxb):
            zb[g, :, p * nocc : (p + 1) * nocc] = zacc[g, p].astype(zb.dtype)

    @pl.loop(0, total)
    def _(chunk):
        g = gid_ref[chunk]
        spots = [chunk * CHUNK + i for i in range(CHUNK)]
        left = jnp.concatenate(
            [
                jnp.concatenate([tiles[slot_ref[pos], p] for p in range(auxb)], axis=1)
                for pos in spots
            ],
            axis=0,
        )
        value = lax.dot_general(
            left, zb[g], (((1,), (1,)), ((), ())), preferred_element_type=jnp.float32
        )
        for i, pos in enumerate(spots):
            acc[block_ref[pos]] += value[i * blk : (i + 1) * blk]

    def put(m, target):
        target[:blk, :] = acc[m].astype(target.dtype)
        target[blk:, :] = jnp.full((TAIL, nocc), bit_ref[m], jnp.int32).astype(
            jnp.float32
        ).astype(target.dtype)

    if direct:
        for m in range(n_aux):
            put(m, out_refs[m])
    else:
        @pl.loop(0, n_aux)
        def _(m):
            put(m, out_refs[0].at[m])


def contributions(direct, n_aux, meta, tiles, shards):
    slots, auxb, blk, nocc = tiles.shape
    chunks = slots // CHUNK + AB_DEV
    rows = blk + TAIL
    smem = pl.BlockSpec(memory_space=pltpu.SMEM)
    vmem = pl.BlockSpec(memory_space=pltpu.VMEM)
    if direct:
        out_shape = [jax.ShapeDtypeStruct((rows, nocc), jnp.bfloat16)] * n_aux
    else:
        out_shape = [jax.ShapeDtypeStruct((n_aux, rows, nocc), jnp.bfloat16)]
    return pl.pallas_call(
        functools.partial(build_kernel, direct, n_aux, chunks),
        out_shape=out_shape,
        in_specs=[smem] * 4 + [pl.BlockSpec(memory_space=pl.ANY)] + [vmem] * len(shards),
        out_specs=[vmem] * len(out_shape),
        scratch_shapes=[
            pltpu.VMEM(tiles.shape, jnp.bfloat16),
            pltpu.VMEM((n_aux + 1, nocc, blk), jnp.bfloat16),
            pltpu.VMEM((AB_DEV, auxb, nocc, nocc), jnp.float32),
            pltpu.VMEM((AB_DEV, nocc, auxb * nocc), jnp.bfloat16),
            pltpu.VMEM((n_aux + 1, blk, nocc), jnp.float32),
            pltpu.SemaphoreType.DMA((chunks,)),
        ],
        compiler_params=pltpu.CompilerParams(vmem_limit_bytes=44 * 1024 * 1024),
        cost_estimate=pl.CostEstimate(
            flops=4 * tiles.size * nocc, bytes_accessed=2 * tiles.size, transcendentals=0
        ),
        name="exchange",
    )(*meta, tiles, *shards)


def on_device(tiles, c_orbitals, basis_order, tile_block, tile_aux, live):
    blk, nocc = tiles.shape[2:]
    n_aux = lax.axis_size("aux")
    bb_dev = basis_order.shape[0] // n_aux
    me = lax.axis_index("aux")
    direct = n_aux <= DIRECT_LIMIT

    def swap(array, m):
        return lax.ppermute(array, "aux", [(i, i ^ m) for i in range(n_aux)])

    if direct:
        shards = [c_orbitals] + [None] * (n_aux - 1)
        for m in range(2, n_aux, 2):
            shards[m] = swap(c_orbitals, m)
        for m in range(0, n_aux, 2):
            shards[m + 1] = swap(shards[m], 1)
    else:
        whole = lax.all_gather(c_orbitals, "aux", axis=0, tiled=True)
        shards = [whole.reshape(n_aux, bb_dev * blk, nocc)]
    meta = plan(
        tile_block, tile_aux, live, basis_order, me if direct else jnp.int32(0), n_aux, bb_dev
    )
    parts = contributions(direct, n_aux, meta, tiles, shards)
    if direct:
        parts = [parts[0]] + [swap(parts[m], m) for m in range(1, n_aux)]
    else:
        moved = lax.all_to_all(parts[0], "aux", 0, 0, tiled=True)
        parts = [moved[m] for m in range(n_aux)]
    sums = [jnp.zeros((blk, nocc), jnp.float32) for _ in range(bb_dev)]
    for part in parts:
        value = part[:blk].astype(jnp.float32)
        which = part[blk, 0].astype(jnp.float32)
        for b in range(bb_dev):
            sums[b] = sums[b] + jnp.where(which == b, value, 0.0)
    return jnp.concatenate(sums, axis=0).astype(jnp.bfloat16)


def solution(mesh):
    return jax.shard_map(
        on_device,
        mesh=mesh,
        in_specs=(
            P(("grp", "aux"), None, None, None),
            P(("grp", "aux"), None),
            P("grp"),
            P(("grp", "aux")),
            P(("grp", "aux")),
            P(("grp", "aux")),
        ),
        out_specs=P(("grp", "aux"), None),
        check_vma=False,
    )
```

time: 247 us -> 91.2 us (0.37)
  waiting for transfers between devices: 102 us -> 6.24 us
  local copies, waits for them, and re-layouts: 68.4 us -> 9.04 us
  matrix products: 58.8 us -> 0 us
  starting transfers between devices: 0.04 us -> 35.8 us
  Pallas kernels: 0 us -> 14 us
  between operations: 14.1 us -> 21.7 us
    reduce_scatter x1 -> x0, waiting for transfers between devices: 60.6 us -> none  [on_device(): lax.psum_scatter(jnp.dot(onehot, flat, precision=lax.Precision.HIGHEST).r...]
    dot_general x4 -> x0, matrix products: 58.8 us -> none  [the longest x1 27.6 us: on_device(): jnp.dot(member, half.reshape(slots, auxb * nocc * nocc), precision=lax.Pr...]
    all_gather x1 -> x0, waiting for transfers between devices: 40.8 us -> none  [on_device(): whole = lax.all_gather(c_orbitals, 'aux', axis=0, tiled=True)]
    ppermute x0 -> x30, starting transfers between devices: none -> 35.8 us  [swap(): return lax.ppermute(array, 'aux', [(i, i ^ m) for i in range(n_aux)])]
    unnamed x4 -> x2, local copies, waits for them, and re-layouts: 29.5 us -> 0.84 us
    dot_general x1 -> x0, local copies, waits for them, and re-layouts: 22.6 us -> none  [on_device(): jnp.einsum('tpmi,tmj->tpij', tiles, picked, preferred_element_type=jnp.fl...]
    pallas_call x0 -> x1, Pallas kernels: none -> 14 us  [contributions(): pl.pallas_call(functools.partial(build_kernel, direct, n_aux, chunks), ou...]
    gather x2 -> x0, local copies, waits for them, and re-layouts: 8.92 us -> none  [the longest x1 6.75 us: on_device(): per_tile = fitted[tile_aux]]
  transfers between devices with their start and end apart: 2 -> 30, of which waited for: 2 -> 6; matrix products, arithmetic and copies ran while one was open for 1% -> 11% of each run, Pallas kernels for 0% -> 0%
where the time goes in v1:
time: 91.2 us; the launch traced here: 90.1 us
  starting transfers between devices  35.8 us (39%)
  between operations  21.7 us (24%)
  Pallas kernels  14 us (15%)
  local copies, waits for them, and re-layouts  9.04 us (10%)
  waiting for transfers between devices  6.24 us (7%)
  other arithmetic  3.38 us (4%)
    ppermute x30, starting transfers between devices, swap(): return lax.ppermute(array, 'aux', [(i, i ^ m) for i in range(n_aux)])  35.8 us
    pallas_call x1, Pallas kernels, contributions(): pl.pallas_call(functools.partial(build_kernel, direct, n_aux, chunks), ou...  14 us
    slice x16, local copies, waits for them, and re-layouts, on_device(): which = part[blk, 0].astype(jnp.float32)  8.2 us
    ppermute x30, waiting for transfers between devices, swap(): return lax.ppermute(array, 'aux', [(i, i ^ m) for i in range(n_aux)])  6.24 us
  transfers between devices with their start and end apart: 30, of which 6 were waited for; matrix products, arithmetic and copies ran while one was open for 11% of the time, Pallas kernels for 0%

profile of v1, /device:TPU:0, one launch (start us, length us, event | category | flops | bytes accessed | tf_op | source)
XLA Modules:
  0.0 90.1 jit_solution(687846369437473040)
XLA Ops:
  0.0 5.0 %collective-permute-start.11 = (bf16[256,128]{1,0:T(8,128)(2,1)}, bf16[256,128]{1,0:T(8,128)(2,1)S(1)}, u32[]{:S(2)}, u32[]{:S(2)}) collective-permute-start(bf16[256,128]{1,0:T(8,128)(2,1)} %refs_0_.1), channel_id=1, source_target_pairs={{0,12},{1,13},{2,14},{3,15},{4,8},{5,9},{6,10},{7,11},{8,4},{9,5},... | collective-permute-start | bytes 196616 | tf_op jit(solution)/shard_map/ppermute | solution.py:201
  5.4 3.5 %collective-permute-start.7 = (bf16[256,128]{1,0:T(8,128)(2,1)}, bf16[256,128]{1,0:T(8,128)(2,1)S(1)}, u32[]{:S(2)}, u32[]{:S(2)}) collective-permute-start(bf16[256,128]{1,0:T(8,128)(2,1)} %refs_0_.1), channel_id=1, source_target_pairs={{0,8},{1,9},{2,10},{3,11},{4,12},{5,13},{6,14},{7,15},{8,0},{9,1},... | collective-permute-start | bytes 196616 | tf_op jit(solution)/shard_map/ppermute | solution.py:201
  8.9 2.0 %collective-permute-start.3 = (bf16[256,128]{1,0:T(8,128)(2,1)}, bf16[256,128]{1,0:T(8,128)(2,1)S(1)}, u32[]{:S(2)}, u32[]{:S(2)}) collective-permute-start(bf16[256,128]{1,0:T(8,128)(2,1)} %refs_0_.1), channel_id=1, source_target_pairs={{0,4},{1,5},{2,6},{3,7},{4,0},{5,1},{6,2},{7,3},{8,12},{9,13},{10,... | collective-permute-start | bytes 196616 | tf_op jit(solution)/shard_map/ppermute | solution.py:201
  11.6 0.7 broadcast_select_fusion.1
  12.8 0.8 select_reduce_fusion.3
  13.8 1.6 %collective-permute-start.1 = (bf16[256,128]{1,0:T(8,128)(2,1)}, bf16[256,128]{1,0:T(8,128)(2,1)S(1)}, u32[]{:S(2)}, u32[]{:S(2)}) collective-permute-start(bf16[256,128]{1,0:T(8,128)(2,1)} %refs_0_.1), channel_id=1, source_target_pairs={{0,2},{1,3},{2,0},{3,1},{4,6},{5,7},{6,4},{7,5},{8,10},{9,11},{10,... | collective-permute-start | bytes 196616 | tf_op jit(solution)/shard_map/ppermute | solution.py:201
  15.4 1.8 %collective-permute-start.13 = (bf16[256,128]{1,0:T(8,128)(2,1)}, bf16[256,128]{1,0:T(8,128)(2,1)S(1)}, u32[]{:S(2)}, u32[]{:S(2)}) collective-permute-start(bf16[256,128]{1,0:T(8,128)(2,1)} %refs_0_.1), channel_id=1, source_target_pairs={{0,14},{1,15},{2,12},{3,13},{4,10},{5,11},{6,8},{7,9},{8,6},{9,7},... | collective-permute-start | bytes 196616 | tf_op jit(solution)/shard_map/ppermute | solution.py:201
  18.9 4.0 %collective-permute-done.13.refs_14_ = bf16[256,128]{1,0:T(8,128)(2,1)S(1)} collective-permute-done((bf16[256,128]{1,0:T(8,128)(2,1)}, bf16[256,128]{1,0:T(8,128)(2,1)S(1)}, u32[]{:S(2)}, u32[]{:S(2)}) %collective-permute-start.13) | collective-permute-done | bytes 65568 | tf_op jit(solution)/shard_map/ppermute | solution.py:201
  23.5 0.6 collective-permute-done.4.refs_5_
  24.6 0.8 copy-done
  25.5 14.0 %exchange.1 = (bf16[144,128]{1,0:T(8,128)(2,1)S(1)}, bf16[144,128]{1,0:T(8,128)(2,1)S(1)}, bf16[144,128]{1,0:T(8,128)(2,1)S(1)}, bf16[144,128]{1,0:T(8,128)(2,1)...) custom-call(s32[96]{0:T(128)S(1)} %get-tuple-element.43.slot_ref, ...), custom_call_target="tpu_custom_call" | custom-call | flops 2684354560 | bytes 10485760 | tf_op jit(solution)/shard_map/exchange/pallas_call | solution.py:172
  39.6 1.8 %collective-permute-start.17 = (bf16[144,128]{1,0:T(8,128)(2,1)S(1)}, bf16[144,128]{1,0:T(8,128)(2,1)S(1)}, u32[]{:S(2)}, u32[]{:S(2)}) collective-permute-start(bf16[144,128]{1,0:T(8,128)(2,1)S(1)} %get-tuple-element.24), channel_id=1, source_target_pairs={{0,3},{1,2},{2,1},{3,0},{4,7},{5,6},{6,5},{7,4},{8,11},{9,10},{10,... | collective-permute-start | bytes 110600 | tf_op jit(solution)/shard_map/ppermute | solution.py:201
  41.4 1.7 %collective-permute-start.19 = (bf16[144,128]{1,0:T(8,128)(2,1)S(1)}, bf16[144,128]{1,0:T(8,128)(2,1)S(1)}, u32[]{:S(2)}, u32[]{:S(2)}) collective-permute-start(bf16[144,128]{1,0:T(8,128)(2,1)S(1)} %get-tuple-element.26), channel_id=1, source_target_pairs={{0,5},{1,4},{2,7},{3,6},{4,1},{5,0},{6,3},{7,2},{8,13},{9,12},{10,... | collective-permute-start | bytes 110600 | tf_op jit(solution)/shard_map/ppermute | solution.py:201
  43.2 0.7 collective-permute-done.16
  43.8 2.0 %collective-permute-start.21 = (bf16[144,128]{1,0:T(8,128)(2,1)S(1)}, bf16[144,128]{1,0:T(8,128)(2,1)S(1)}, u32[]{:S(2)}, u32[]{:S(2)}) collective-permute-start(bf16[144,128]{1,0:T(8,128)(2,1)S(1)} %get-tuple-element.28), channel_id=1, source_target_pairs={{0,7},{1,6},{2,5},{3,4},{4,3},{5,2},{6,1},{7,0},{8,15},{9,14},{10,... | collective-permute-start | bytes 110600 | tf_op jit(solution)/shard_map/ppermute | solution.py:201
  46.1 2.3 %collective-permute-start.23 = (bf16[144,128]{1,0:T(8,128)(2,1)S(1)}, bf16[144,128]{1,0:T(8,128)(2,1)S(1)}, u32[]{:S(2)}, u32[]{:S(2)}) collective-permute-start(bf16[144,128]{1,0:T(8,128)(2,1)S(1)} %get-tuple-element.30), channel_id=1, source_target_pairs={{0,9},{1,8},{2,11},{3,10},{4,13},{5,12},{6,15},{7,14},{8,1},{9,0},... | collective-permute-start | bytes 110600 | tf_op jit(solution)/shard_map/ppermute | solution.py:201
  48.4 1.2 %collective-permute-start.24 = (bf16[144,128]{1,0:T(8,128)(2,1)S(1)}, bf16[144,128]{1,0:T(8,128)(2,1)S(1)}, u32[]{:S(2)}, u32[]{:S(2)}) collective-permute-start(bf16[144,128]{1,0:T(8,128)(2,1)S(1)} %get-tuple-element.31), channel_id=1, source_target_pairs={{0,10},{1,11},{2,8},{3,9},{4,14},{5,15},{6,12},{7,13},{8,2},{9,3},... | collective-permute-start | bytes 110600 | tf_op jit(solution)/shard_map/ppermute | solution.py:201
  49.6 2.4 %collective-permute-start.25 = (bf16[144,128]{1,0:T(8,128)(2,1)S(1)}, bf16[144,128]{1,0:T(8,128)(2,1)S(1)}, u32[]{:S(2)}, u32[]{:S(2)}) collective-permute-start(bf16[144,128]{1,0:T(8,128)(2,1)S(1)} %get-tuple-element.32), channel_id=1, source_target_pairs={{0,11},{1,10},{2,9},{3,8},{4,15},{5,14},{6,13},{7,12},{8,3},{9,2},... | collective-permute-start | bytes 110600 | tf_op jit(solution)/shard_map/ppermute | solution.py:201
  52.0 1.1 %collective-permute-start.26 = (bf16[144,128]{1,0:T(8,128)(2,1)S(1)}, bf16[144,128]{1,0:T(8,128)(2,1)S(1)}, u32[]{:S(2)}, u32[]{:S(2)}) collective-permute-start(bf16[144,128]{1,0:T(8,128)(2,1)S(1)} %get-tuple-element.33), channel_id=1, source_target_pairs={{0,12},{1,13},{2,14},{3,15},{4,8},{5,9},{6,10},{7,11},{8,4},{9,5},... | collective-permute-start | bytes 110600 | tf_op jit(solution)/shard_map/ppermute | solution.py:201
  53.1 2.3 %collective-permute-start.27 = (bf16[144,128]{1,0:T(8,128)(2,1)S(1)}, bf16[144,128]{1,0:T(8,128)(2,1)S(1)}, u32[]{:S(2)}, u32[]{:S(2)}) collective-permute-start(bf16[144,128]{1,0:T(8,128)(2,1)S(1)} %get-tuple-element.34), channel_id=1, source_target_pairs={{0,13},{1,12},{2,15},{3,14},{4,9},{5,8},{6,11},{7,10},{8,5},{9,4},... | collective-permute-start | bytes 110600 | tf_op jit(solution)/shard_map/ppermute | solution.py:201
  55.5 2.4 %collective-permute-start.28 = (bf16[144,128]{1,0:T(8,128)(2,1)S(1)}, bf16[144,128]{1,0:T(8,128)(2,1)S(1)}, u32[]{:S(2)}, u32[]{:S(2)}) collective-permute-start(bf16[144,128]{1,0:T(8,128)(2,1)S(1)} %get-tuple-element.35), channel_id=1, source_target_pairs={{0,14},{1,15},{2,12},{3,13},{4,10},{5,11},{6,8},{7,9},{8,6},{9,7},... | collective-permute-start | bytes 110600 | tf_op jit(solution)/shard_map/ppermute | solution.py:201
  57.9 2.1 %collective-permute-start.29 = (bf16[144,128]{1,0:T(8,128)(2,1)S(1)}, bf16[144,128]{1,0:T(8,128)(2,1)S(1)}, u32[]{:S(2)}, u32[]{:S(2)}) collective-permute-start(bf16[144,128]{1,0:T(8,128)(2,1)S(1)} %get-tuple-element.36), channel_id=1, source_target_pairs={{0,15},{1,14},{2,13},{3,12},{4,11},{5,10},{6,9},{7,8},{8,7},{9,6},... | collective-permute-start | bytes 110600 | tf_op jit(solution)/shard_map/ppermute | solution.py:201
  61.8 0.5 slice.128
  89.5 0.6 pad_maximum_fusion
  (74 shorter events, 12.6 us)
Async XLA Ops:
  0.0 13.8 %collective-permute-start.11 = (bf16[256,128]{1,0:T(8,128)(2,1)}, bf16[256,128]{1,0:T(8,128)(2,1)S(1)}, u32[]{:S(2)}, u32[]{:S(2)}) collective-permute-start(bf16[256,128]{1,0:T(8,128)(2,1)} %refs_0_.1), channel_id=1, source_target_pairs={{0,12},{1,13},{2,14},{3,15},{4,8},{5,9},{6,10},{7,11},{8,4},{9,5},... | collective-permute-start | bytes 196616 | tf_op jit(solution)/shard_map/ppermute | solution.py:201
  5.0 10.4 %collective-permute-start.9 = (bf16[256,128]{1,0:T(8,128)(2,1)}, bf16[256,128]{1,0:T(8,128)(2,1)S(1)}, u32[]{:S(2)}, u32[]{:S(2)}) collective-permute-start(bf16[256,128]{1,0:T(8,128)(2,1)} %refs_0_.1), channel_id=1, source_target_pairs={{0,10},{1,11},{2,8},{3,9},{4,14},{5,15},{6,12},{7,13},{8,2},{9,3},... | collective-permute-start | bytes 196616 | tf_op jit(solution)/shard_map/ppermute | solution.py:201
  5.4 10.0 %collective-permute-start.7 = (bf16[256,128]{1,0:T(8,128)(2,1)}, bf16[256,128]{1,0:T(8,128)(2,1)S(1)}, u32[]{:S(2)}, u32[]{:S(2)}) collective-permute-start(bf16[256,128]{1,0:T(8,128)(2,1)} %refs_0_.1), channel_id=1, source_target_pairs={{0,8},{1,9},{2,10},{3,11},{4,12},{5,13},{6,14},{7,15},{8,0},{9,1},... | collective-permute-start | bytes 196616 | tf_op jit(solution)/shard_map/ppermute | solution.py:201
  8.9 8.3 %collective-permute-start.5 = (bf16[256,128]{1,0:T(8,128)(2,1)}, bf16[256,128]{1,0:T(8,128)(2,1)S(1)}, u32[]{:S(2)}, u32[]{:S(2)}) collective-permute-start(bf16[256,128]{1,0:T(8,128)(2,1)} %refs_0_.1), channel_id=1, source_target_pairs={{0,6},{1,7},{2,4},{3,5},{4,2},{5,3},{6,0},{7,1},{8,14},{9,15},{10,... | collective-permute-start | bytes 196616 | tf_op jit(solution)/shard_map/ppermute | solution.py:201
  8.9 8.3 %collective-permute-start.3 = (bf16[256,128]{1,0:T(8,128)(2,1)}, bf16[256,128]{1,0:T(8,128)(2,1)S(1)}, u32[]{:S(2)}, u32[]{:S(2)}) collective-permute-start(bf16[256,128]{1,0:T(8,128)(2,1)} %refs_0_.1), channel_id=1, source_target_pairs={{0,4},{1,5},{2,6},{3,7},{4,0},{5,1},{6,2},{7,3},{8,12},{9,13},{10,... | collective-permute-start | bytes 196616 | tf_op jit(solution)/shard_map/ppermute | solution.py:201
  13.8 4.5 %collective-permute-start.1 = (bf16[256,128]{1,0:T(8,128)(2,1)}, bf16[256,128]{1,0:T(8,128)(2,1)S(1)}, u32[]{:S(2)}, u32[]{:S(2)}) collective-permute-start(bf16[256,128]{1,0:T(8,128)(2,1)} %refs_0_.1), channel_id=1, source_target_pairs={{0,2},{1,3},{2,0},{3,1},{4,6},{5,7},{6,4},{7,5},{8,10},{9,11},{10,... | collective-permute-start | bytes 196616 | tf_op jit(solution)/shard_map/ppermute | solution.py:201
  15.4 7.4 %collective-permute-start.13 = (bf16[256,128]{1,0:T(8,128)(2,1)}, bf16[256,128]{1,0:T(8,128)(2,1)S(1)}, u32[]{:S(2)}, u32[]{:S(2)}) collective-permute-start(bf16[256,128]{1,0:T(8,128)(2,1)} %refs_0_.1), channel_id=1, source_target_pairs={{0,14},{1,15},{2,12},{3,13},{4,10},{5,11},{6,8},{7,9},{8,6},{9,7},... | collective-permute-start | bytes 196616 | tf_op jit(solution)/shard_map/ppermute | solution.py:201
  17.3 5.6 %collective-permute-start.12 = (bf16[256,128]{1,0:T(8,128)(2,1)S(1)}, bf16[256,128]{1,0:T(8,128)(2,1)S(1)}, u32[]{:S(2)}, u32[]{:S(2)}) collective-permute-start(bf16[256,128]{1,0:T(8,128)(2,1)S(1)} %collective-permute-done.11.refs_12_), channel_id=1, source_target_pairs={{0,1},{1,0},{2,3},{3,2},{4,5},{5,4},{6,7},{7,6},{8,9},{9,8},{10,11... | collective-permute-start | bytes 196616 | tf_op jit(solution)/shard_map/ppermute | solution.py:201
  17.3 6.1 %collective-permute-start.10 = (bf16[256,128]{1,0:T(8,128)(2,1)S(1)}, bf16[256,128]{1,0:T(8,128)(2,1)S(1)}, u32[]{:S(2)}, u32[]{:S(2)}) collective-permute-start(bf16[256,128]{1,0:T(8,128)(2,1)S(1)} %collective-permute-done.9.refs_10_), channel_id=1, source_target_pairs={{0,1},{1,0},{2,3},{3,2},{4,5},{5,4},{6,7},{7,6},{8,9},{9,8},{10,11... | collective-permute-start | bytes 196616 | tf_op jit(solution)/shard_map/ppermute | solution.py:201
  18.4 5.1 %collective-permute-start.8 = (bf16[256,128]{1,0:T(8,128)(2,1)S(1)}, bf16[256,128]{1,0:T(8,128)(2,1)S(1)}, u32[]{:S(2)}, u32[]{:S(2)}) collective-permute-start(bf16[256,128]{1,0:T(8,128)(2,1)S(1)} %collective-permute-done.7.refs_8_), channel_id=1, source_target_pairs={{0,1},{1,0},{2,3},{3,2},{4,5},{5,4},{6,7},{7,6},{8,9},{9,8},{10,11... | collective-permute-start | bytes 196616 | tf_op jit(solution)/shard_map/ppermute | solution.py:201
  18.4 5.1 %collective-permute-start.6 = (bf16[256,128]{1,0:T(8,128)(2,1)S(1)}, bf16[256,128]{1,0:T(8,128)(2,1)S(1)}, u32[]{:S(2)}, u32[]{:S(2)}) collective-permute-start(bf16[256,128]{1,0:T(8,128)(2,1)S(1)} %collective-permute-done.5.refs_6_), channel_id=1, source_target_pairs={{0,1},{1,0},{2,3},{3,2},{4,5},{5,4},{6,7},{7,6},{8,9},{9,8},{10,11... | collective-permute-start | bytes 196616 | tf_op jit(solution)/shard_map/ppermute | solution.py:201
  39.6 6.2 %collective-permute-start.17 = (bf16[144,128]{1,0:T(8,128)(2,1)S(1)}, bf16[144,128]{1,0:T(8,128)(2,1)S(1)}, u32[]{:S(2)}, u32[]{:S(2)}) collective-permute-start(bf16[144,128]{1,0:T(8,128)(2,1)S(1)} %get-tuple-element.24), channel_id=1, source_target_pairs={{0,3},{1,2},{2,1},{3,0},{4,7},{5,6},{6,5},{7,4},{8,11},{9,10},{10,... | collective-permute-start | bytes 110600 | tf_op jit(solution)/shard_map/ppermute | solution.py:201
  41.4 4.7 %collective-permute-start.18 = (bf16[144,128]{1,0:T(8,128)(2,1)S(1)}, bf16[144,128]{1,0:T(8,128)(2,1)S(1)}, u32[]{:S(2)}, u32[]{:S(2)}) collective-permute-start(bf16[144,128]{1,0:T(8,128)(2,1)S(1)} %get-tuple-element.25), channel_id=1, source_target_pairs={{0,4},{1,5},{2,6},{3,7},{4,0},{5,1},{6,2},{7,3},{8,12},{9,13},{10,... | collective-permute-start | bytes 110600 | tf_op jit(solution)/shard_map/ppermute | solution.py:201
  41.4 7.0 %collective-permute-start.19 = (bf16[144,128]{1,0:T(8,128)(2,1)S(1)}, bf16[144,128]{1,0:T(8,128)(2,1)S(1)}, u32[]{:S(2)}, u32[]{:S(2)}) collective-permute-start(bf16[144,128]{1,0:T(8,128)(2,1)S(1)} %get-tuple-element.26), channel_id=1, source_target_pairs={{0,5},{1,4},{2,7},{3,6},{4,1},{5,0},{6,3},{7,2},{8,13},{9,12},{10,... | collective-permute-start | bytes 110600 | tf_op jit(solution)/shard_map/ppermute | solution.py:201
  43.1 6.6 %collective-permute-start.20 = (bf16[144,128]{1,0:T(8,128)(2,1)S(1)}, bf16[144,128]{1,0:T(8,128)(2,1)S(1)}, u32[]{:S(2)}, u32[]{:S(2)}) collective-permute-start(bf16[144,128]{1,0:T(8,128)(2,1)S(1)} %get-tuple-element.27), channel_id=1, source_target_pairs={{0,6},{1,7},{2,4},{3,5},{4,2},{5,3},{6,0},{7,1},{8,14},{9,15},{10,... | collective-permute-start | bytes 110600 | tf_op jit(solution)/shard_map/ppermute | solution.py:201
  43.8 8.2 %collective-permute-start.21 = (bf16[144,128]{1,0:T(8,128)(2,1)S(1)}, bf16[144,128]{1,0:T(8,128)(2,1)S(1)}, u32[]{:S(2)}, u32[]{:S(2)}) collective-permute-start(bf16[144,128]{1,0:T(8,128)(2,1)S(1)} %get-tuple-element.28), channel_id=1, source_target_pairs={{0,7},{1,6},{2,5},{3,4},{4,3},{5,2},{6,1},{7,0},{8,15},{9,14},{10,... | collective-permute-start | bytes 110600 | tf_op jit(solution)/shard_map/ppermute | solution.py:201
  45.8 7.3 %collective-permute-start.22 = (bf16[144,128]{1,0:T(8,128)(2,1)S(1)}, bf16[144,128]{1,0:T(8,128)(2,1)S(1)}, u32[]{:S(2)}, u32[]{:S(2)}) collective-permute-start(bf16[144,128]{1,0:T(8,128)(2,1)S(1)} %get-tuple-element.29), channel_id=1, source_target_pairs={{0,8},{1,9},{2,10},{3,11},{4,12},{5,13},{6,14},{7,15},{8,0},{9,1},... | collective-permute-start | bytes 110600 | tf_op jit(solution)/shard_map/ppermute | solution.py:201
  46.1 9.4 %collective-permute-start.23 = (bf16[144,128]{1,0:T(8,128)(2,1)S(1)}, bf16[144,128]{1,0:T(8,128)(2,1)S(1)}, u32[]{:S(2)}, u32[]{:S(2)}) collective-permute-start(bf16[144,128]{1,0:T(8,128)(2,1)S(1)} %get-tuple-element.30), channel_id=1, source_target_pairs={{0,9},{1,8},{2,11},{3,10},{4,13},{5,12},{6,15},{7,14},{8,1},{9,0},... | collective-permute-start | bytes 110600 | tf_op jit(solution)/shard_map/ppermute | solution.py:201
  48.4 9.5 %collective-permute-start.24 = (bf16[144,128]{1,0:T(8,128)(2,1)S(1)}, bf16[144,128]{1,0:T(8,128)(2,1)S(1)}, u32[]{:S(2)}, u32[]{:S(2)}) collective-permute-start(bf16[144,128]{1,0:T(8,128)(2,1)S(1)} %get-tuple-element.31), channel_id=1, source_target_pairs={{0,10},{1,11},{2,8},{3,9},{4,14},{5,15},{6,12},{7,13},{8,2},{9,3},... | collective-permute-start | bytes 110600 | tf_op jit(solution)/shard_map/ppermute | solution.py:201
  49.6 30.4 %collective-permute-start.25 = (bf16[144,128]{1,0:T(8,128)(2,1)S(1)}, bf16[144,128]{1,0:T(8,128)(2,1)S(1)}, u32[]{:S(2)}, u32[]{:S(2)}) collective-permute-start(bf16[144,128]{1,0:T(8,128)(2,1)S(1)} %get-tuple-element.32), channel_id=1, source_target_pairs={{0,11},{1,10},{2,9},{3,8},{4,15},{5,14},{6,13},{7,12},{8,3},{9,2},... | collective-permute-start | bytes 110600 | tf_op jit(solution)/shard_map/ppermute | solution.py:201
  52.0 29.9 %collective-permute-start.26 = (bf16[144,128]{1,0:T(8,128)(2,1)S(1)}, bf16[144,128]{1,0:T(8,128)(2,1)S(1)}, u32[]{:S(2)}, u32[]{:S(2)}) collective-permute-start(bf16[144,128]{1,0:T(8,128)(2,1)S(1)} %get-tuple-element.33), channel_id=1, source_target_pairs={{0,12},{1,13},{2,14},{3,15},{4,8},{5,9},{6,10},{7,11},{8,4},{9,5},... | collective-permute-start | bytes 110600 | tf_op jit(solution)/shard_map/ppermute | solution.py:201
  53.1 30.6 %collective-permute-start.27 = (bf16[144,128]{1,0:T(8,128)(2,1)S(1)}, bf16[144,128]{1,0:T(8,128)(2,1)S(1)}, u32[]{:S(2)}, u32[]{:S(2)}) collective-permute-start(bf16[144,128]{1,0:T(8,128)(2,1)S(1)} %get-tuple-element.34), channel_id=1, source_target_pairs={{0,13},{1,12},{2,15},{3,14},{4,9},{5,8},{6,11},{7,10},{8,5},{9,4},... | collective-permute-start | bytes 110600 | tf_op jit(solution)/shard_map/ppermute | solution.py:201
  55.5 30.0 %collective-permute-start.28 = (bf16[144,128]{1,0:T(8,128)(2,1)S(1)}, bf16[144,128]{1,0:T(8,128)(2,1)S(1)}, u32[]{:S(2)}, u32[]{:S(2)}) collective-permute-start(bf16[144,128]{1,0:T(8,128)(2,1)S(1)} %get-tuple-element.35), channel_id=1, source_target_pairs={{0,14},{1,15},{2,12},{3,13},{4,10},{5,11},{6,8},{7,9},{8,6},{9,7},... | collective-permute-start | bytes 110600 | tf_op jit(solution)/shard_map/ppermute | solution.py:201
  57.9 29.5 %collective-permute-start.29 = (bf16[144,128]{1,0:T(8,128)(2,1)S(1)}, bf16[144,128]{1,0:T(8,128)(2,1)S(1)}, u32[]{:S(2)}, u32[]{:S(2)}) collective-permute-start(bf16[144,128]{1,0:T(8,128)(2,1)S(1)} %get-tuple-element.36), channel_id=1, source_target_pairs={{0,15},{1,14},{2,13},{3,12},{4,11},{5,10},{6,9},{7,8},{8,7},{9,6},... | collective-permute-start | bytes 110600 | tf_op jit(solution)/shard_map/ppermute | solution.py:201
  (7 other events, 15.6 us)

commit v2 on v1

--- a/solution.py
+++ b/solution.py
@@ -14,7 +14,7 @@
 DIRECT_LIMIT = 32
 
 
-def plan(tile_block, tile_aux, live, basis_order, own, n_aux, bb_dev):
+def plan(tile_block, tile_aux, live, basis_order, me, n_aux, bb_dev):
     slots = tile_block.shape[0]
     nbb = basis_order.shape[0]
     chunks = slots // CHUNK + AB_DEV
@@ -27,7 +27,6 @@
         axis=1,
     )
     where_to = position // bb_dev
-    where_to = jnp.bitwise_xor(where_to, own)
     which = position % bb_dev
     group = jnp.where(alive, tile_aux, AB_DEV)
     ids = lax.iota(jnp.int32, AB_DEV)
@@ -57,15 +56,13 @@
         ),
         axis=1,
     )
-    return slot, block, jnp.concatenate([gid, ends]), bit
+    return slot, block, jnp.concatenate([gid, ends]), jnp.concatenate([bit, me[None]])
 
 
 def build_kernel(
     direct, n_aux, chunks, slot_ref, block_ref, gid_ref, bit_ref, tiles_hbm, *refs
 ):
-    n_refs = n_aux if direct else 1
-    c_refs, out_refs = refs[:n_refs], refs[n_refs : 2 * n_refs]
-    tiles, ct, zacc, zb, acc, sems = refs[2 * n_refs :]
+    c_refs, (out_ref, tiles, ct, zacc, zb, acc, sems) = refs[:-7], refs[-7:]
     blk, nocc = ct.shape[2], ct.shape[1]
     auxb = tiles.shape[1]
     total = gid_ref[chunks + AB_DEV - 1]
@@ -98,8 +95,10 @@
         ct[m] = source[pl.ds(pl.multiple_of(bit_ref[m] * blk, blk), blk), :].T
 
     if direct:
-        for m in range(n_aux):
-            turn(m, c_refs[m])
+        core = lax.rem(bit_ref[n_aux], 2)
+        for chip in range(n_aux // 2):
+            turn(2 * chip + core, c_refs[0].at[chip])
+            turn(2 * chip + 1 - core, c_refs[1].at[chip])
     else:
         @pl.loop(0, n_aux)
         def _(m):
@@ -144,36 +143,25 @@
         for i, pos in enumerate(spots):
             acc[block_ref[pos]] += value[i * blk : (i + 1) * blk]
 
-    def put(m, target):
-        target[:blk, :] = acc[m].astype(target.dtype)
-        target[blk:, :] = jnp.full((TAIL, nocc), bit_ref[m], jnp.int32).astype(
+    @pl.loop(0, n_aux, unroll=8)
+    def _(m):
+        out_ref[m, :blk, :] = acc[m].astype(out_ref.dtype)
+        out_ref[m, blk:, :] = jnp.full((TAIL, nocc), bit_ref[m], jnp.int32).astype(
             jnp.float32
-        ).astype(target.dtype)
-
-    if direct:
-        for m in range(n_aux):
-            put(m, out_refs[m])
-    else:
-        @pl.loop(0, n_aux)
-        def _(m):
-            put(m, out_refs[0].at[m])
+        ).astype(out_ref.dtype)
 
 
 def contributions(direct, n_aux, meta, tiles, shards):
     slots, auxb, blk, nocc = tiles.shape
     chunks = slots // CHUNK + AB_DEV
-    rows = blk + TAIL
     smem = pl.BlockSpec(memory_space=pltpu.SMEM)
     vmem = pl.BlockSpec(memory_space=pltpu.VMEM)
-    if direct:
-        out_shape = [jax.ShapeDtypeStruct((rows, nocc), jnp.bfloat16)] * n_aux
-    else:
-        out_shape = [jax.ShapeDtypeStruct((n_aux, rows, nocc), jnp.bfloat16)]
+    out_shape = jax.ShapeDtypeStruct((n_aux, blk + TAIL, nocc), jnp.bfloat16)
     return pl.pallas_call(
         functools.partial(build_kernel, direct, n_aux, chunks),
         out_shape=out_shape,
         in_specs=[smem] * 4 + [pl.BlockSpec(memory_space=pl.ANY)] + [vmem] * len(shards),
-        out_specs=[vmem] * len(out_shape),
+        out_specs=vmem,
         scratch_shapes=[
             pltpu.VMEM(tiles.shape, jnp.bfloat16),
             pltpu.VMEM((n_aux + 1, nocc, blk), jnp.bfloat16),
@@ -190,41 +178,49 @@
     )(*meta, tiles, *shards)
 
 
+def owner_sum(parts, blk, bb_dev):
+    n_aux, rows, nocc = parts.shape
+
+    def kernel(parts_ref, out_ref):
+        sums = [jnp.zeros((blk, nocc), jnp.float32) for _ in range(bb_dev)]
+        for s in range(n_aux):
+            value = parts_ref[s, :blk, :].astype(jnp.float32)
+            which = parts_ref[s, blk:, :][:1].astype(jnp.float32)
+            for b in range(bb_dev):
+                sums[b] = sums[b] + jnp.where(which == b, value, 0.0)
+        for b in range(bb_dev):
+            out_ref[b * blk : (b + 1) * blk, :] = sums[b].astype(out_ref.dtype)
+
+    vmem = pl.BlockSpec(memory_space=pltpu.VMEM)
+    return pl.pallas_call(
+        kernel,
+        out_shape=jax.ShapeDtypeStruct((bb_dev * blk, nocc), jnp.bfloat16),
+        in_specs=[vmem],
+        out_specs=vmem,
+        name="owner_sum",
+    )(parts)
+
+
 def on_device(tiles, c_orbitals, basis_order, tile_block, tile_aux, live):
     blk, nocc = tiles.shape[2:]
     n_aux = lax.axis_size("aux")
     bb_dev = basis_order.shape[0] // n_aux
     me = lax.axis_index("aux")
     direct = n_aux <= DIRECT_LIMIT
-
-    def swap(array, m):
-        return lax.ppermute(array, "aux", [(i, i ^ m) for i in range(n_aux)])
-
     if direct:
-        shards = [c_orbitals] + [None] * (n_aux - 1)
-        for m in range(2, n_aux, 2):
-            shards[m] = swap(c_orbitals, m)
-        for m in range(0, n_aux, 2):
-            shards[m + 1] = swap(shards[m], 1)
+        chips = n_aux // 2
+        same = [[2 * chip + core for chip in range(chips)] for core in range(2)]
+        wide = jnp.broadcast_to(c_orbitals[None], (chips,) + c_orbitals.shape)
+        mine = lax.all_to_all(wide, "aux", 0, 0, axis_index_groups=same, tiled=True)
+        other = lax.ppermute(mine, "aux", [(i, i ^ 1) for i in range(n_aux)])
+        shards = [mine, other]
     else:
         whole = lax.all_gather(c_orbitals, "aux", axis=0, tiled=True)
         shards = [whole.reshape(n_aux, bb_dev * blk, nocc)]
-    meta = plan(
-        tile_block, tile_aux, live, basis_order, me if direct else jnp.int32(0), n_aux, bb_dev
-    )
+    meta = plan(tile_block, tile_aux, live, basis_order, me, n_aux, bb_dev)
     parts = contributions(direct, n_aux, meta, tiles, shards)
-    if direct:
-        parts = [parts[0]] + [swap(parts[m], m) for m in range(1, n_aux)]
-    else:
-        moved = lax.all_to_all(parts[0], "aux", 0, 0, tiled=True)
-        parts = [moved[m] for m in range(n_aux)]
-    sums = [jnp.zeros((blk, nocc), jnp.float32) for _ in range(bb_dev)]
-    for part in parts:
-        value = part[:blk].astype(jnp.float32)
-        which = part[blk, 0].astype(jnp.float32)
-        for b in range(bb_dev):
-            sums[b] = sums[b] + jnp.where(which == b, value, 0.0)
-    return jnp.concatenate(sums, axis=0).astype(jnp.bfloat16)
+    moved = lax.all_to_all(parts, "aux", 0, 0, tiled=True)
+    return owner_sum(moved, blk, bb_dev)
 
 
 def solution(mesh):

time: 91.2 us -> 63.8 us (0.70)
  starting transfers between devices: 35.8 us -> 7.28 us
  blocking collectives: 0 us -> 24.1 us
  between operations: 21.7 us -> 0.68 us
  local copies, waits for them, and re-layouts: 9.04 us -> 1.7 us
  waiting for transfers between devices: 6.24 us -> 13.2 us
    ppermute x30 -> x1, starting transfers between devices: 35.8 us -> 0.01 us  [on_device(): other = lax.ppermute(mine, 'aux', [(i, i ^ 1) for i in range(n_aux)])]
    all_to_all x0 -> x1, blocking collectives: none -> 24.1 us  [on_device(): moved = lax.all_to_all(parts, 'aux', 0, 0, tiled=True)]
    all_to_all x0 -> x1, waiting for transfers between devices: none -> 11.6 us  [on_device(): mine = lax.all_to_all(wide, 'aux', 0, 0, axis_index_groups=same, tiled=True)]
    slice x16 -> x0, local copies, waits for them, and re-layouts: 8.2 us -> none  [on_device(): which = part[blk, 0].astype(jnp.float32)]
    all_to_all x0 -> x1, starting transfers between devices: none -> 7.28 us  [on_device(): mine = lax.all_to_all(wide, 'aux', 0, 0, axis_index_groups=same, tiled=True)]
    ppermute x30 -> x1, waiting for transfers between devices: 6.24 us -> 1.62 us  [on_device(): other = lax.ppermute(mine, 'aux', [(i, i ^ 1) for i in range(n_aux)])]
    pallas_call x1, Pallas kernels: 14 us -> 11.2 us  [contributions(): pl.pallas_call(functools.partial(build_kernel, direct, n_aux, chunks), ou...]
    pallas_call x0 -> x1, Pallas kernels: none -> 1.92 us  [owner_sum(): pl.pallas_call(kernel, out_shape=jax.ShapeDtypeStruct((bb_dev * blk, nocc...]
  transfers between devices with their start and end apart: 30 -> 2, of which waited for: 6 -> 2; matrix products, arithmetic and copies ran while one was open for 11% -> 4% of each run, Pallas kernels for 0% -> 0%
where the time goes in v2:
time: 63.8 us; the launch traced here: 62.6 us
  blocking collectives  24.1 us (38%)
  waiting for transfers between devices  13.2 us (21%)
  Pallas kernels  13.1 us (21%)
  starting transfers between devices  7.28 us (11%)
  other arithmetic  2.52 us (4%)
  local copies, waits for them, and re-layouts  1.7 us (3%)
  between operations  0.68 us (1%)
    all_to_all x1, blocking collectives, on_device(): moved = lax.all_to_all(parts, 'aux', 0, 0, tiled=True)  24.1 us
    all_to_all x1, waiting for transfers between devices, on_device(): mine = lax.all_to_all(wide, 'aux', 0, 0, axis_index_groups=same, tiled=True)  11.6 us
    pallas_call x1, Pallas kernels, contributions(): pl.pallas_call(functools.partial(build_kernel, direct, n_aux, chunks), ou...  11.2 us
    all_to_all x1, starting transfers between devices, on_device(): mine = lax.all_to_all(wide, 'aux', 0, 0, axis_index_groups=same, tiled=True)  7.28 us
    pallas_call x1, Pallas kernels, owner_sum(): pl.pallas_call(kernel, out_shape=jax.ShapeDtypeStruct((bb_dev * blk, nocc...  1.92 us
    broadcast_in_dim x1, local copies, waits for them, and re-layouts, on_device(): wide = jnp.broadcast_to(c_orbitals[None], (chips,) + c_orbitals.shape)  1.7 us
    ppermute x1, waiting for transfers between devices, on_device(): other = lax.ppermute(mine, 'aux', [(i, i ^ 1) for i in range(n_aux)])  1.62 us
  transfers between devices with their start and end apart: 2, of which 2 were waited for; matrix products, arithmetic and copies ran while one was open for 4% of the time, Pallas kernels for 0%

profile of v2, /device:TPU:0, one launch (start us, length us, event | category | flops | bytes accessed | tf_op | source)
XLA Modules:
  0.0 62.6 jit_solution(12375121368080713028)
XLA Ops:
  0.0 1.7 %broadcast_in_dim.136 = bf16[8,256,128]{2,1,0:T(8,128)(2,1)} broadcast(bf16[256,128]{1,0:T(8,128)(2,1)} %param.7), dimensions={1,2} | broadcast | bytes 589824 | tf_op jit(solution)/shard_map/broadcast_in_dim | solution.py:213
  1.7 7.3 %all-to-all-start = ((bf16[8,256,128]{2,1,0:T(8,128)(2,1)}), bf16[8,256,128]{2,1,0:T(8,128)(2,1)S(1)}, u32[]{:S(2)}, u32[]{:S(2)}) async-start(bf16[8,256,128]{2,1,0:T(8,128)(2,1)} %broadcast_in_dim.136), calls=%async_computation | async-start | bytes 1048576 | tf_op jit(solution)/shard_map/all_to_all | solution.py:214
  9.6 0.7 %broadcast_select_fusion.1 = s32[64]{0:T(128)S(1)} fusion(s32[64]{0:T(128)} %param.10, s32[]{:T(128)} %bitcast.4), kind=kLoop, calls=%fused_computation.39 | loop fusion | flops 128 | bytes 516 | tf_op jit(solution)/shard_map/jit(_where)/select_n | solution.py:31
  10.3 0.1 convert_reduce_fusion.2
  10.4 0.1 select_reduce_fusion.5
  10.5 0.1 convert_reduce_fusion.1
  10.6 0.1 pad_add_fusion.gid_ref
  10.7 0.2 convert_reduce_fusion
  10.9 0.1 select_reduce_fusion.6
  11.0 0.8 %select_reduce_fusion.3 = s32[64]{0:T(128)S(1)} fusion(s32[64]{0:T(128)} %param.9, s32[32]{0:T(128)} %param.8), kind=kLoop, calls=%fused_computation.8 | loop fusion | flops 6080 | bytes 640 | tf_op jit(solution)/shard_map/reduce_sum | solution.py:23
  11.8 0.1 select_reduce_fusion.4
  11.9 11.6 %all-to-all-done.refs_0_ = bf16[8,256,128]{2,1,0:T(8,128)(2,1)S(1)} async-done(((bf16[8,256,128]{2,1,0:T(8,128)(2,1)}), bf16[8,256,128]{2,1,0:T(8,128)(2,1)S(1)}, u32[]{:S(2)}, u32[]{:S(2)}) %all-to-all-start) | async-done | bytes 524320 | tf_op jit(solution)/shard_map/all_to_all | solution.py:214
  23.5 0.0 collective-permute-start
  23.5 0.1 pad_add_fusion.1.bit_ref
  23.5 0.1 fusion
  23.6 0.1 select_reduce_fusion
  23.8 1.6 %collective-permute-done.refs_1_ = bf16[8,256,128]{2,1,0:T(8,128)(2,1)S(1)} collective-permute-done((bf16[8,256,128]{2,1,0:T(8,128)(2,1)S(1)}, bf16[8,256,128]{2,1,0:T(8,128)(2,1)S(1)}, u32[]{:S(2)}, u32[]{:S(2)}) %collective-permute-start) | collective-permute-done | bytes 524320 | tf_op jit(solution)/shard_map/ppermute | solution.py:215
  25.4 11.2 %exchange.1 = bf16[16,144,128]{2,1,0:T(8,128)(2,1)S(1)} custom-call(s32[96]{0:T(128)S(1)} %get-tuple-element.11.slot_ref, s32[96]{0:T(128)S(1)} %get-tuple-element.10.block_ref, s32[32]{0:T(128)S(1)} %pad_add_fusion.gid_ref, s32[17]{0:T(128)S(1)} %pad_add_fusion.1.bit_ref, bf16[64,5,128,128]{3,2,1,0:T(8,128)(2,1)} %tiles_hbm.1, ...), custom_call_target="tpu_custom_call" | custom-call | flops 2684354560 | bytes 10485760 | tf_op jit(solution)/shard_map/exchange/pallas_call | solution.py:160
  36.6 24.1 %all_to_all.10.parts_ref = bf16[16,144,128]{2,1,0:T(8,128)(2,1)} all-to-all(bf16[16,144,128]{2,1,0:T(8,128)(2,1)S(1)} %exchange.1), channel_id=1, replica_groups=mesh['grp'=2,'aux'=16] {'aux'}, dimensions={0} | all-to-all | bytes 1179648 | tf_op jit(solution)/shard_map/all_to_all | solution.py:222
  60.7 1.9 %owner_sum.1 = bf16[256,128]{1,0:T(8,128)(2,1)} custom-call(bf16[16,144,128]{2,1,0:T(8,128)(2,1)} %all_to_all.10.parts_ref), custom_call_target="tpu_custom_call" | custom-call | tf_op jit(solution)/shard_map/owner_sum/pallas_call | solution.py:195
  (5 shorter events, 0.0 us)
Async XLA Ops:
  1.7 21.8 %all-to-all-start = ((bf16[8,256,128]{2,1,0:T(8,128)(2,1)}), bf16[8,256,128]{2,1,0:T(8,128)(2,1)S(1)}, u32[]{:S(2)}, u32[]{:S(2)}) async-start(bf16[8,256,128]{2,1,0:T(8,128)(2,1)} %broadcast_in_dim.136), calls=%async_computation | async-start | bytes 1048576 | tf_op jit(solution)/shard_map/all_to_all | solution.py:214
  23.5 1.9 %collective-permute-start = (bf16[8,256,128]{2,1,0:T(8,128)(2,1)S(1)}, bf16[8,256,128]{2,1,0:T(8,128)(2,1)S(1)}, u32[]{:S(2)}, u32[]{:S(2)}) collective-permute-start(bf16[8,256,128]{2,1,0:T(8,128)(2,1)S(1)} %all-to-all-done.refs_0_), channel_id=1, source_target_pairs={{0,1},{1,0},{2,3},{3,2},{4,5},{5,4},{6,7},{7,6},{8,9},{9,8},{10,11... | collective-permute-start | bytes 1572872 | tf_op jit(solution)/shard_map/ppermute | solution.py:215

commit v3 on v2

v3 whole, which is shorter than its diff:
```python
import functools

import jax
import jax.numpy as jnp
from jax import lax
from jax.experimental import pallas as pl
from jax.experimental.pallas import tpu as pltpu
from jax.sharding import PartitionSpec as P

AB_DEV = 8
CHUNK = 4
UNROLL = 2
TAIL = 16
PLANE = 4
DIRECT = 16


def plan(tile_block, tile_aux, live, basis_order, me, n_aux, bb_dev):
    slots = tile_block.shape[0]
    nbb = basis_order.shape[0]
    chunks = slots // CHUNK + AB_DEV
    t = lax.iota(jnp.int32, slots)
    alive = t < live[0]
    position = jnp.sum(
        jnp.where(
            basis_order[None, :] == tile_block[:, None], lax.iota(jnp.int32, nbb)[None, :], 0
        ),
        axis=1,
    )
    where_to = position // bb_dev
    which = position % bb_dev
    group = jnp.where(alive, tile_aux, AB_DEV)
    ids = lax.iota(jnp.int32, AB_DEV)
    counts = jnp.sum((group[None, :] == ids[:, None]).astype(jnp.int32), axis=1)
    need = (counts + CHUNK - 1) // CHUNK
    ends = jnp.sum(jnp.where(ids[None, :] <= ids[:, None], need[None, :], 0), axis=1)
    rank = jnp.sum(
        ((group[None, :] == group[:, None]) & (t[None, :] < t[:, None])).astype(jnp.int32), axis=1
    )
    start = jnp.sum(jnp.where(group[:, None] > ids[None, :], need[None, :], 0), axis=1)
    place = jnp.where(alive, start * CHUNK + rank, -1)
    q = lax.iota(jnp.int32, chunks * CHUNK)
    hit = place[None, :] == q[:, None]
    lead = place[None, :] == (q // CHUNK * CHUNK)[:, None]
    valid = jnp.any(hit, axis=1)
    slot = jnp.sum(jnp.where(hit, t[None, :], 0), axis=1)
    slot = jnp.where(valid, slot, jnp.sum(jnp.where(lead, t[None, :], 0), axis=1))
    block = jnp.where(valid, jnp.sum(jnp.where(hit, where_to[None, :], 0), axis=1), n_aux)
    gid = jnp.sum(
        (lax.iota(jnp.int32, chunks)[:, None] >= ends[None, :]).astype(jnp.int32), axis=1
    )
    bit = jnp.max(
        jnp.where(
            (where_to[None, :] == lax.iota(jnp.int32, n_aux)[:, None]) & alive[None, :],
            which[None, :],
            0,
        ),
        axis=1,
    )
    gid = jnp.minimum(gid, AB_DEV - 1)
    return slot, block, jnp.concatenate([gid, ends]), jnp.concatenate([bit, me[None]])


def build_kernel(
    direct, n_aux, chunks, n_in, slot_ref, block_ref, gid_ref, bit_ref, tiles, *refs
):
    c_refs, out_refs, (ct, zacc, zb, acc) = refs[:n_in], refs[n_in:-4], refs[-4:]
    blk, nocc = ct.shape[2], ct.shape[1]
    auxb = tiles.shape[1]
    total = gid_ref[chunks + AB_DEV - 1]
    turns = (total + UNROLL - 1) // UNROLL

    def turn(o, source):
        ct[o] = source[pl.ds(pl.multiple_of(bit_ref[o] * blk, blk), blk), :].T

    me = bit_ref[n_aux]
    if direct:
        for m in range(n_aux):
            turn(me ^ m, c_refs[m])
    else:
        @pl.loop(0, n_aux)
        def _(o):
            turn(o, c_refs[0].at[o])

    ct[n_aux] = jnp.zeros((nocc, blk), ct.dtype)
    acc[...] = jnp.zeros(acc.shape, acc.dtype)
    zacc[...] = jnp.zeros(zacc.shape, zacc.dtype)

    def slab(slot):
        return jnp.concatenate([tiles[slot, p] for p in range(auxb)], axis=1)

    @pl.loop(0, turns)
    def _(step):
        for chunk in [step * UNROLL + u for u in range(UNROLL)]:
            g = gid_ref[chunk]
            spots = [chunk * CHUNK + i for i in range(CHUNK)]
            left = jnp.concatenate([ct[block_ref[pos]] for pos in spots], axis=1)
            right = jnp.concatenate([slab(slot_ref[pos]) for pos in spots], axis=0)
            zacc[g] += jnp.dot(left, right, preferred_element_type=jnp.float32)

    for g in range(AB_DEV):
        zb[g] = zacc[g].astype(zb.dtype)

    @pl.loop(0, turns)
    def _(step):
        for chunk in [step * UNROLL + u for u in range(UNROLL)]:
            g = gid_ref[chunk]
            spots = [chunk * CHUNK + i for i in range(CHUNK)]
            left = jnp.concatenate([slab(slot_ref[pos]) for pos in spots], axis=0)
            value = lax.dot_general(
                left, zb[g], (((1,), (1,)), ((), ())), preferred_element_type=jnp.float32
            )
            for i, pos in enumerate(spots):
                acc[block_ref[pos]] += value[i * blk : (i + 1) * blk]

    def put(o, out_ref, at):
        out_ref[at, :blk, :] = acc[o].astype(out_ref.dtype)
        out_ref[at, blk:, :] = jnp.full((TAIL, nocc), bit_ref[o], jnp.int32).astype(
            jnp.float32
        ).astype(out_ref.dtype)

    if direct:
        half = n_aux // PLANE // 2
        for m in range(n_aux):
            dz, r = divmod(m, PLANE)
            put(me ^ m, out_refs[dz // half * PLANE + r], dz % half)
    else:
        @pl.loop(0, n_aux)
        def _(o):
            put(o, out_refs[0], o)


def contributions(direct, n_aux, meta, tiles, shards):
    slots, auxb, blk, nocc = tiles.shape
    chunks = slots // CHUNK + AB_DEV
    smem = pl.BlockSpec(memory_space=pltpu.SMEM)
    vmem = pl.BlockSpec(memory_space=pltpu.VMEM)
    if direct:
        shape = (n_aux // PLANE // 2, blk + TAIL, nocc)
        out_shape = [jax.ShapeDtypeStruct(shape, jnp.bfloat16)] * (2 * PLANE)
    else:
        out_shape = [jax.ShapeDtypeStruct((n_aux, blk + TAIL, nocc), jnp.bfloat16)]
    return pl.pallas_call(
        functools.partial(build_kernel, direct, n_aux, chunks, len(shards)),
        out_shape=out_shape,
        in_specs=[smem] * 4 + [vmem] * (1 + len(shards)),
        out_specs=[vmem] * len(out_shape),
        scratch_shapes=[
            pltpu.VMEM((n_aux + 1, nocc, blk), jnp.bfloat16),
            pltpu.VMEM((AB_DEV, nocc, auxb * nocc), jnp.float32),
            pltpu.VMEM((AB_DEV, nocc, auxb * nocc), jnp.bfloat16),
            pltpu.VMEM((n_aux + 1, blk, nocc), jnp.float32),
        ],
        compiler_params=pltpu.CompilerParams(
            vmem_limit_bytes=(32 if direct else 46) * 1024 * 1024
        ),
        cost_estimate=pl.CostEstimate(
            flops=4 * tiles.size * nocc, bytes_accessed=2 * tiles.size, transcendentals=0
        ),
        name="exchange",
    )(*meta, tiles, *shards)


def spread(parts, dtypes, blk, bb_dev):
    count, rows, nocc = parts[0].shape

    def kernel(*refs):
        sources, targets = refs[: len(parts)], refs[len(parts) :]
        for i in range(count):
            sums = [jnp.zeros((blk, nocc), jnp.float32) for _ in range(bb_dev)]
            for source in sources:
                value = source[i, :blk, :].astype(jnp.float32)
                which = source[i, blk:, :][:1].astype(jnp.float32)
                for b in range(bb_dev):
                    sums[b] = sums[b] + jnp.where(which == b, value, 0.0)
            for b in range(bb_dev):
                targets[i][b * blk : (b + 1) * blk, :] = sums[b].astype(targets[i].dtype)

    vmem = pl.BlockSpec(memory_space=pltpu.VMEM)
    return pl.pallas_call(
        kernel,
        out_shape=[jax.ShapeDtypeStruct((bb_dev * blk, nocc), dtype) for dtype in dtypes],
        in_specs=[vmem] * len(parts),
        out_specs=[vmem] * count,
        name="spread",
    )(*parts)


def total_of(arrays):
    def kernel(*refs):
        value = refs[0][...].astype(jnp.float32)
        for ref in refs[1:-1]:
            value = value + ref[...].astype(jnp.float32)
        refs[-1][...] = value.astype(refs[-1].dtype)

    vmem = pl.BlockSpec(memory_space=pltpu.VMEM)
    return pl.pallas_call(
        kernel,
        out_shape=jax.ShapeDtypeStruct(arrays[0].shape, jnp.bfloat16),
        in_specs=[vmem] * len(arrays),
        out_specs=vmem,
        name="total_of",
    )(*arrays)


def owner_sum(parts, blk, bb_dev):
    n_aux, rows, nocc = parts.shape

    def kernel(parts_ref, out_ref):
        sums = [jnp.zeros((blk, nocc), jnp.float32) for _ in range(bb_dev)]
        for s in range(n_aux):
            value = parts_ref[s, :blk, :].astype(jnp.float32)
            which = parts_ref[s, blk:, :][:1].astype(jnp.float32)
            for b in range(bb_dev):
                sums[b] = sums[b] + jnp.where(which == b, value, 0.0)
        for b in range(bb_dev):
            out_ref[b * blk : (b + 1) * blk, :] = sums[b].astype(out_ref.dtype)

    vmem = pl.BlockSpec(memory_space=pltpu.VMEM)
    return pl.pallas_call(
        kernel,
        out_shape=jax.ShapeDtypeStruct((bb_dev * blk, nocc), jnp.bfloat16),
        in_specs=[vmem],
        out_specs=vmem,
        name="owner_sum",
    )(parts)


def on_device(tiles, c_orbitals, basis_order, tile_block, tile_aux, live):
    blk, nocc = tiles.shape[2:]
    n_aux = lax.axis_size("aux")
    bb_dev = basis_order.shape[0] // n_aux
    me = lax.axis_index("aux")
    direct = n_aux == DIRECT
    meta = plan(tile_block, tile_aux, live, basis_order, me, n_aux, bb_dev)

    def swap(array, m):
        return lax.ppermute(array, "aux", [(i, i ^ m) for i in range(n_aux)])

    if not direct:
        whole = lax.all_gather(c_orbitals, "aux", axis=0, tiled=True)
        shards = [whole.reshape(n_aux, bb_dev * blk, nocc)]
        (parts,) = contributions(direct, n_aux, meta, tiles, shards)
        moved = lax.all_to_all(parts, "aux", 0, 0, tiled=True)
        return owner_sum(moved, blk, bb_dev)

    depth = n_aux // PLANE
    shards = [c_orbitals] + [None] * (n_aux - 1)
    for dz in range(depth - 1, 0, -1):
        shards[dz * PLANE] = swap(c_orbitals, dz * PLANE)
    for dz in range(depth):
        shards[dz * PLANE + 2] = swap(shards[dz * PLANE], 2)
    for m in range(0, n_aux, 2):
        shards[m + 1] = swap(shards[m], 1)
    parts = contributions(direct, n_aux, meta, tiles, shards)
    half = depth // 2
    near, far = parts[:PLANE], parts[PLANE:]
    far = [far[0]] + [swap(far[r], r) for r in range(1, PLANE)]
    near = [near[0]] + [swap(near[r], r) for r in range(1, PLANE)]
    far = spread(far, [jnp.bfloat16] * half, blk, bb_dev)
    near = spread(near, [jnp.float32] + [jnp.bfloat16] * (half - 1), blk, bb_dev)
    sums = list(near) + list(far)
    return total_of([sums[0]] + [swap(sums[dz], dz * PLANE) for dz in range(1, depth)])


def solution(mesh):
    return jax.shard_map(
        on_device,
        mesh=mesh,
        in_specs=(
            P(("grp", "aux"), None, None, None),
            P(("grp", "aux"), None),
            P("grp"),
            P(("grp", "aux")),
            P(("grp", "aux")),
            P(("grp", "aux")),
        ),
        out_specs=P(("grp", "aux"), None),
        check_vma=False,
    )
```

time: 63.8 us -> 58.2 us (0.912); the launches traced: 62.6 us -> 58.2 us
  blocking collectives: 24.1 us -> 0 us
  starting transfers between devices: 7.28 us -> 21.7 us
  local copies, waits for them, and re-layouts: 1.7 us -> 7.99 us
  Pallas kernels: 13.1 us -> 11.5 us
    all_to_all x1 -> x0, blocking collectives: 24.1 us -> none  [on_device(): moved = lax.all_to_all(parts, 'aux', 0, 0, tiled=True)]
    ppermute x1 -> x24, starting transfers between devices: 0.01 us -> 21.7 us  [swap(): return lax.ppermute(array, 'aux', [(i, i ^ m) for i in range(n_aux)])]
    ppermute x1 -> x24, waiting for transfers between devices: 1.62 us -> 13.7 us  [swap(): return lax.ppermute(array, 'aux', [(i, i ^ m) for i in range(n_aux)])]
    all_to_all x1 -> x0, waiting for transfers between devices: 11.6 us -> none  [on_device(): mine = lax.all_to_all(wide, 'aux', 0, 0, axis_index_groups=same, tiled=True)]
    unnamed x0 -> x26, local copies, waits for them, and re-layouts: none -> 7.99 us
    all_to_all x1 -> x0, starting transfers between devices: 7.28 us -> none  [on_device(): mine = lax.all_to_all(wide, 'aux', 0, 0, axis_index_groups=same, tiled=True)]
    broadcast_in_dim x1 -> x0, local copies, waits for them, and re-layouts: 1.7 us -> none  [on_device(): wide = jnp.broadcast_to(c_orbitals[None], (chips,) + c_orbitals.shape)]
    pallas_call x2 -> x4, Pallas kernels: 13.1 us -> 11.5 us  [the longest x1 6.46 us: contributions(): pl.pallas_call(functools.partial(build_kernel, direct, n_aux, chunks, len...]
  transfers between devices with their start and end apart: 2 -> 24, of which waited for: 2 -> 9; matrix products, arithmetic and copies ran while one was open for 4% -> 4% of each run, Pallas kernels for 0% -> 6%
where the time goes in v3:
time: 58.2 us
  starting transfers between devices  21.7 us (37%)
  waiting for transfers between devices  13.7 us (24%)
  Pallas kernels  11.5 us (20%)
  local copies, waits for them, and re-layouts  7.99 us (14%)
  other arithmetic  2.51 us (4%)
  between operations  0.78 us (1%)
    ppermute x24, starting transfers between devices, swap(): return lax.ppermute(array, 'aux', [(i, i ^ m) for i in range(n_aux)])  21.7 us
    ppermute x24, waiting for transfers between devices, swap(): return lax.ppermute(array, 'aux', [(i, i ^ m) for i in range(n_aux)])  13.7 us
    unnamed x26, local copies, waits for them, and re-layouts  7.99 us
    pallas_call x1, Pallas kernels, contributions(): pl.pallas_call(functools.partial(build_kernel, direct, n_aux, chunks, len...  6.46 us
    pallas_call x2, Pallas kernels, spread(): pl.pallas_call(kernel, out_shape=[jax.ShapeDtypeStruct((bb_dev * blk, noc...  3.45 us
    pallas_call x1, Pallas kernels, total_of(): pl.pallas_call(kernel, out_shape=jax.ShapeDtypeStruct(arrays[0].shape, jn...  1.63 us
  transfers between devices with their start and end apart: 24, of which 9 were waited for; matrix products, arithmetic and copies ran while one was open for 4% of the time, Pallas kernels for 6%

profile of v3, /device:TPU:0, one launch (start us, length us, event | category | flops | bytes accessed | tf_op | source)
XLA Modules:
  0.0 58.2 jit_solution(10301897736690009693)
XLA Ops:
  0.0 4.0 %collective-permute-start.7 = (bf16[256,128]{1,0:T(8,128)(2,1)}, bf16[256,128]{1,0:T(8,128)(2,1)S(1)}, u32[]{:S(2)}, u32[]{:S(2)}) collective-permute-start(bf16[256,128]{1,0:T(8,128)(2,1)} %refs_0_.1), channel_id=1, source_target_pairs={{0,8},{1,9},{2,10},{3,11},{4,12},{5,13},{6,14},{7,15},{8,0},{9,1},... | collective-permute-start | bytes 196616 | tf_op jit(solution)/shard_map/ppermute | solution.py:238
  4.0 1.6 %collective-permute-start.3 = (bf16[256,128]{1,0:T(8,128)(2,1)}, bf16[256,128]{1,0:T(8,128)(2,1)S(1)}, u32[]{:S(2)}, u32[]{:S(2)}) collective-permute-start(bf16[256,128]{1,0:T(8,128)(2,1)} %refs_0_.1), channel_id=1, source_target_pairs={{0,4},{1,5},{2,6},{3,7},{4,0},{5,1},{6,2},{7,3},{8,12},{9,13},{10,... | collective-permute-start | bytes 196616 | tf_op jit(solution)/shard_map/ppermute | solution.py:238
  5.6 1.5 %collective-permute-start.1 = (bf16[256,128]{1,0:T(8,128)(2,1)}, bf16[256,128]{1,0:T(8,128)(2,1)S(1)}, u32[]{:S(2)}, u32[]{:S(2)}) collective-permute-start(bf16[256,128]{1,0:T(8,128)(2,1)} %refs_0_.1), channel_id=1, source_target_pairs={{0,2},{1,3},{2,0},{3,1},{4,6},{5,7},{6,4},{7,5},{8,10},{9,11},{10,... | collective-permute-start | bytes 196616 | tf_op jit(solution)/shard_map/ppermute | solution.py:238
  8.0 0.7 %broadcast_select_fusion.1 = s32[64]{0:T(128)S(1)} fusion(s32[64]{0:T(128)} %param.10, s32[]{:T(128)} %bitcast.4), kind=kLoop, calls=%fused_computation.40 | loop fusion | flops 128 | bytes 516 | tf_op jit(solution)/shard_map/jit(_where)/select_n | solution.py:32
  9.3 0.8 %select_reduce_fusion.3 = s32[64]{0:T(128)S(1)} fusion(s32[64]{0:T(128)} %param.9, s32[32]{0:T(128)} %param.8), kind=kLoop, calls=%fused_computation.8 | loop fusion | flops 6080 | bytes 640 | tf_op jit(solution)/shard_map/reduce_sum | solution.py:24
  11.0 1.6 %collective-permute-start.5 = (bf16[256,128]{1,0:T(8,128)(2,1)S(1)}, bf16[256,128]{1,0:T(8,128)(2,1)S(1)}, u32[]{:S(2)}, u32[]{:S(2)}) collective-permute-start(bf16[256,128]{1,0:T(8,128)(2,1)S(1)} %collective-permute-done.3.refs_4_), channel_id=1, source_target_pairs={{0,2},{1,3},{2,0},{3,1},{4,6},{5,7},{6,4},{7,5},{8,10},{9,11},{10,... | collective-permute-start | bytes 196616 | tf_op jit(solution)/shard_map/ppermute | solution.py:238
  12.7 0.9 %collective-permute-done.11.refs_12_ = bf16[256,128]{1,0:T(8,128)(2,1)S(1)} collective-permute-done((bf16[256,128]{1,0:T(8,128)(2,1)}, bf16[256,128]{1,0:T(8,128)(2,1)S(1)}, u32[]{:S(2)}, u32[]{:S(2)}) %collective-permute-start.11) | collective-permute-done | bytes 65568 | tf_op jit(solution)/shard_map/ppermute | solution.py:238
  14.2 1.2 %collective-permute-done.9.refs_10_ = bf16[256,128]{1,0:T(8,128)(2,1)S(1)} collective-permute-done((bf16[256,128]{1,0:T(8,128)(2,1)S(1)}, bf16[256,128]{1,0:T(8,128)(2,1)S(1)}, u32[]{:S(2)}, u32[]{:S(2)}) %collective-permute-start.9) | collective-permute-done | bytes 65568 | tf_op jit(solution)/shard_map/ppermute | solution.py:238
  16.8 1.1 %collective-permute-done.13.refs_14_ = bf16[256,128]{1,0:T(8,128)(2,1)S(1)} collective-permute-done((bf16[256,128]{1,0:T(8,128)(2,1)S(1)}, bf16[256,128]{1,0:T(8,128)(2,1)S(1)}, u32[]{:S(2)}, u32[]{:S(2)}) %collective-permute-start.13) | collective-permute-done | bytes 65568 | tf_op jit(solution)/shard_map/ppermute | solution.py:238
  18.0 1.2 %collective-permute-done.14.refs_15_ = bf16[256,128]{1,0:T(8,128)(2,1)S(1)} collective-permute-done((bf16[256,128]{1,0:T(8,128)(2,1)S(1)}, bf16[256,128]{1,0:T(8,128)(2,1)S(1)}, u32[]{:S(2)}, u32[]{:S(2)}) %collective-permute-start.14) | collective-permute-done | bytes 65568 | tf_op jit(solution)/shard_map/ppermute | solution.py:238
  19.2 4.0 %copy-done = bf16[64,5,128,128]{3,2,1,0:T(8,128)(2,1)S(1)} copy-done((bf16[64,5,128,128]{3,2,1,0:T(8,128)(2,1)S(1)}, bf16[64,5,128,128]{3,2,1,0:T(8,128)(2,1)}, u32[]{:S(2)}) %copy-start) | copy-done | bytes 10485784
  23.2 0.8 %copy-done.3 = bf16[256,128]{1,0:T(8,128)(2,1)S(1)} copy-done((bf16[256,128]{1,0:T(8,128)(2,1)S(1)}, bf16[256,128]{1,0:T(8,128)(2,1)}, u32[]{:S(2)}) %copy-start.3) | copy-done | bytes 65560
  24.0 6.5 %exchange.1 = (bf16[2,144,128]{2,1,0:T(8,128)(2,1)S(1)}, bf16[2,144,128]{2,1,0:T(8,128)(2,1)S(1)}, bf16[2,144,128]{2,1,0:T(8,128)(2,1)S(1)}, bf16[2,144,128]{2,1...) custom-call(s32[96]{0:T(128)S(1)} %get-tuple-element.35.slot_ref, ...), custom_call_target="tpu_custom_call" | custom-call | flops 2684354560 | bytes 10485760 | tf_op jit(solution)/shard_map/exchange/pallas_call | solution.py:143
  30.5 0.6 %copy-done.1 = bf16[2,144,128]{2,1,0:T(8,128)(2,1)} copy-done((bf16[2,144,128]{2,1,0:T(8,128)(2,1)}, bf16[2,144,128]{2,1,0:T(8,128)(2,1)S(1)}, u32[]{:S(2)}) %copy-start.1) | copy-done | bytes 73752
  31.9 3.1 %collective-permute-start.16 = (bf16[2,144,128]{2,1,0:T(8,128)(2,1)S(1)}, bf16[2,144,128]{2,1,0:T(8,128)(2,1)S(1)}, u32[]{:S(2)}, u32[]{:S(2)}) collective-permute-start(bf16[2,144,128]{2,1,0:T(8,128)(2,1)S(1)} %get-tuple-element.19), channel_id=1, source_target_pairs={{0,2},{1,3},{2,0},{3,1},{4,6},{5,7},{6,4},{7,5},{8,10},{9,11},{10,... | collective-permute-start | bytes 221192 | tf_op jit(solution)/shard_map/ppermute | solution.py:238
  35.2 2.0 %collective-permute-start.20 = (bf16[2,144,128]{2,1,0:T(8,128)(2,1)S(1)}, bf16[2,144,128]{2,1,0:T(8,128)(2,1)S(1)}, u32[]{:S(2)}, u32[]{:S(2)}) collective-permute-start(bf16[2,144,128]{2,1,0:T(8,128)(2,1)S(1)} %get-tuple-element.25), channel_id=1, source_target_pairs={{0,2},{1,3},{2,0},{3,1},{4,6},{5,7},{6,4},{7,5},{8,10},{9,11},{10,... | collective-permute-start | bytes 221192 | tf_op jit(solution)/shard_map/ppermute | solution.py:238
  37.7 1.9 %collective-permute-done.17.refs_3_ = bf16[2,144,128]{2,1,0:T(8,128)(2,1)S(1)} collective-permute-done((bf16[2,144,128]{2,1,0:T(8,128)(2,1)S(1)}, bf16[2,144,128]{2,1,0:T(8,128)(2,1)S(1)}, u32[]{:S(2)}, u32[]{:S(2)}) %collective-permute-start.17) | collective-permute-done | bytes 73760 | tf_op jit(solution)/shard_map/ppermute | solution.py:238
  40.2 1.7 %spread.2 = (f32[256,128]{1,0:T(8,128)}, bf16[256,128]{1,0:T(8,128)(2,1)}) custom-call(bf16[2,144,128]{2,1,0:T(8,128)(2,1)} %copy-done.2, bf16[2,144,128]{2,1,0:T(8,128)(2,1)} %copy-done.7, bf16[2,144,128]{2,1,0:T(8,128)(2,1)} %copy-done.8, bf16[2,144,128]{2,1,0:T(8,128)(2,1)} %copy-done.9), custom_call_target="tpu_custom_call" | custom-call | tf_op jit(solution)/shard_map/spread/pallas_call | solution.py:180
  42.0 1.8 %collective-permute-start.18 = (bf16[256,128]{1,0:T(8,128)(2,1)}, bf16[256,128]{1,0:T(8,128)(2,1)S(1)}, u32[]{:S(2)}, u32[]{:S(2)}) collective-permute-start(bf16[256,128]{1,0:T(8,128)(2,1)} %get-tuple-element.22), channel_id=1, source_target_pairs={{0,4},{1,5},{2,6},{3,7},{4,0},{5,1},{6,2},{7,3},{8,12},{9,13},{10,... | collective-permute-start | bytes 196616 | tf_op jit(solution)/shard_map/ppermute | solution.py:238
  44.5 1.7 %spread.3 = (bf16[256,128]{1,0:T(8,128)(2,1)}, bf16[256,128]{1,0:T(8,128)(2,1)}) custom-call(bf16[2,144,128]{2,1,0:T(8,128)(2,1)} %copy-done.1, bf16[2,144,128]{2,1,0:T(8,128)(2,1)} %copy-done.4, bf16[2,144,128]{2,1,0:T(8,128)(2,1)} %copy-done.5, bf16[2,144,128]{2,1,0:T(8,128)(2,1)} %copy-done.6), custom_call_target="tpu_custom_call" | custom-call | tf_op jit(solution)/shard_map/spread/pallas_call | solution.py:180
  46.2 3.1 %collective-permute-start.22 = (bf16[256,128]{1,0:T(8,128)(2,1)}, bf16[256,128]{1,0:T(8,128)(2,1)S(1)}, u32[]{:S(2)}, u32[]{:S(2)}) collective-permute-start(bf16[256,128]{1,0:T(8,128)(2,1)} %get-tuple-element.27), channel_id=1, source_target_pairs={{0,8},{1,9},{2,10},{3,11},{4,12},{5,13},{6,14},{7,15},{8,0},{9,1},... | collective-permute-start | bytes 196616 | tf_op jit(solution)/shard_map/ppermute | solution.py:238
  49.4 4.3 %collective-permute-done.22.refs_2_ = bf16[256,128]{1,0:T(8,128)(2,1)S(1)} collective-permute-done((bf16[256,128]{1,0:T(8,128)(2,1)}, bf16[256,128]{1,0:T(8,128)(2,1)S(1)}, u32[]{:S(2)}, u32[]{:S(2)}) %collective-permute-start.22) | collective-permute-done | bytes 65568 | tf_op jit(solution)/shard_map/ppermute | solution.py:238
  53.8 2.2 %collective-permute-done.23.refs_3_ = bf16[256,128]{1,0:T(8,128)(2,1)S(1)} collective-permute-done((bf16[256,128]{1,0:T(8,128)(2,1)}, bf16[256,128]{1,0:T(8,128)(2,1)S(1)}, u32[]{:S(2)}, u32[]{:S(2)}) %collective-permute-start.23) | collective-permute-done | bytes 65568 | tf_op jit(solution)/shard_map/ppermute | solution.py:238
  56.6 1.6 %total_of.1 = bf16[256,128]{1,0:T(8,128)(2,1)} custom-call(f32[256,128]{1,0:T(8,128)} %get-tuple-element.21.refs_0_, bf16[256,128]{1,0:T(8,128)(2,1)} %copy-done.10, bf16[256,128]{1,0:T(8,128)(2,1)} %copy-done.11, bf16[256,128]{1,0:T(8,128)(2,1)} %copy-done.12), custom_call_target="tpu_custom_call" | custom-call | tf_op jit(solution)/shard_map/total_of/pallas_call | solution.py:197
  (72 shorter events, 7.5 us)
Async XLA Ops:
  0.0 10.4 %collective-permute-start.7 = (bf16[256,128]{1,0:T(8,128)(2,1)}, bf16[256,128]{1,0:T(8,128)(2,1)S(1)}, u32[]{:S(2)}, u32[]{:S(2)}) collective-permute-start(bf16[256,128]{1,0:T(8,128)(2,1)} %refs_0_.1), channel_id=1, source_target_pairs={{0,8},{1,9},{2,10},{3,11},{4,12},{5,13},{6,14},{7,15},{8,0},{9,1},... | collective-permute-start | bytes 196616 | tf_op jit(solution)/shard_map/ppermute | solution.py:238
  4.0 6.7 %collective-permute-start.3 = (bf16[256,128]{1,0:T(8,128)(2,1)}, bf16[256,128]{1,0:T(8,128)(2,1)S(1)}, u32[]{:S(2)}, u32[]{:S(2)}) collective-permute-start(bf16[256,128]{1,0:T(8,128)(2,1)} %refs_0_.1), channel_id=1, source_target_pairs={{0,4},{1,5},{2,6},{3,7},{4,0},{5,1},{6,2},{7,3},{8,12},{9,13},{10,... | collective-permute-start | bytes 196616 | tf_op jit(solution)/shard_map/ppermute | solution.py:238
  5.6 5.4 %collective-permute-start.1 = (bf16[256,128]{1,0:T(8,128)(2,1)}, bf16[256,128]{1,0:T(8,128)(2,1)S(1)}, u32[]{:S(2)}, u32[]{:S(2)}) collective-permute-start(bf16[256,128]{1,0:T(8,128)(2,1)} %refs_0_.1), channel_id=1, source_target_pairs={{0,2},{1,3},{2,0},{3,1},{4,6},{5,7},{6,4},{7,5},{8,10},{9,11},{10,... | collective-permute-start | bytes 196616 | tf_op jit(solution)/shard_map/ppermute | solution.py:238
  7.1 5.4 %collective-permute-start = (bf16[256,128]{1,0:T(8,128)(2,1)}, bf16[256,128]{1,0:T(8,128)(2,1)S(1)}, u32[]{:S(2)}, u32[]{:S(2)}) collective-permute-start(bf16[256,128]{1,0:T(8,128)(2,1)} %refs_0_.1), channel_id=1, source_target_pairs={{0,1},{1,0},{2,3},{3,2},{4,5},{5,4},{6,7},{7,6},{8,9},{9,8},{10,11... | collective-permute-start | bytes 196616 | tf_op jit(solution)/shard_map/ppermute | solution.py:238
  7.1 6.5 %collective-permute-start.11 = (bf16[256,128]{1,0:T(8,128)(2,1)}, bf16[256,128]{1,0:T(8,128)(2,1)S(1)}, u32[]{:S(2)}, u32[]{:S(2)}) collective-permute-start(bf16[256,128]{1,0:T(8,128)(2,1)} %refs_0_.1), channel_id=1, source_target_pairs={{0,12},{1,13},{2,14},{3,15},{4,8},{5,9},{6,10},{7,11},{8,4},{9,5},... | collective-permute-start | bytes 196616 | tf_op jit(solution)/shard_map/ppermute | solution.py:238
  10.4 5.0 %collective-permute-start.9 = (bf16[256,128]{1,0:T(8,128)(2,1)S(1)}, bf16[256,128]{1,0:T(8,128)(2,1)S(1)}, u32[]{:S(2)}, u32[]{:S(2)}) collective-permute-start(bf16[256,128]{1,0:T(8,128)(2,1)S(1)} %collective-permute-done.7.refs_8_), channel_id=1, source_target_pairs={{0,2},{1,3},{2,0},{3,1},{4,6},{5,7},{6,4},{7,5},{8,10},{9,11},{10,... | collective-permute-start | bytes 196616 | tf_op jit(solution)/shard_map/ppermute | solution.py:238
  10.8 4.6 %collective-permute-start.8 = (bf16[256,128]{1,0:T(8,128)(2,1)S(1)}, bf16[256,128]{1,0:T(8,128)(2,1)S(1)}, u32[]{:S(2)}, u32[]{:S(2)}) collective-permute-start(bf16[256,128]{1,0:T(8,128)(2,1)S(1)} %collective-permute-done.7.refs_8_), channel_id=1, source_target_pairs={{0,1},{1,0},{2,3},{3,2},{4,5},{5,4},{6,7},{7,6},{8,9},{9,8},{10,11... | collective-permute-start | bytes 196616 | tf_op jit(solution)/shard_map/ppermute | solution.py:238
  11.0 5.3 %collective-permute-start.5 = (bf16[256,128]{1,0:T(8,128)(2,1)S(1)}, bf16[256,128]{1,0:T(8,128)(2,1)S(1)}, u32[]{:S(2)}, u32[]{:S(2)}) collective-permute-start(bf16[256,128]{1,0:T(8,128)(2,1)S(1)} %collective-permute-done.3.refs_4_), channel_id=1, source_target_pairs={{0,2},{1,3},{2,0},{3,1},{4,6},{5,7},{6,4},{7,5},{8,10},{9,11},{10,... | collective-permute-start | bytes 196616 | tf_op jit(solution)/shard_map/ppermute | solution.py:238
  12.6 3.7 %collective-permute-start.4 = (bf16[256,128]{1,0:T(8,128)(2,1)S(1)}, bf16[256,128]{1,0:T(8,128)(2,1)S(1)}, u32[]{:S(2)}, u32[]{:S(2)}) collective-permute-start(bf16[256,128]{1,0:T(8,128)(2,1)S(1)} %collective-permute-done.3.refs_4_), channel_id=1, source_target_pairs={{0,1},{1,0},{2,3},{3,2},{4,5},{5,4},{6,7},{7,6},{8,9},{9,8},{10,11... | collective-permute-start | bytes 196616 | tf_op jit(solution)/shard_map/ppermute | solution.py:238
  13.7 4.3 %collective-permute-start.13 = (bf16[256,128]{1,0:T(8,128)(2,1)S(1)}, bf16[256,128]{1,0:T(8,128)(2,1)S(1)}, u32[]{:S(2)}, u32[]{:S(2)}) collective-permute-start(bf16[256,128]{1,0:T(8,128)(2,1)S(1)} %collective-permute-done.11.refs_12_), channel_id=1, source_target_pairs={{0,2},{1,3},{2,0},{3,1},{4,6},{5,7},{6,4},{7,5},{8,10},{9,11},{10,... | collective-permute-start | bytes 196616 | tf_op jit(solution)/shard_map/ppermute | solution.py:238
  15.4 2.6 %collective-permute-start.12 = (bf16[256,128]{1,0:T(8,128)(2,1)S(1)}, bf16[256,128]{1,0:T(8,128)(2,1)S(1)}, u32[]{:S(2)}, u32[]{:S(2)}) collective-permute-start(bf16[256,128]{1,0:T(8,128)(2,1)S(1)} %collective-permute-done.11.refs_12_), channel_id=1, source_target_pairs={{0,1},{1,0},{2,3},{3,2},{4,5},{5,4},{6,7},{7,6},{8,9},{9,8},{10,11... | collective-permute-start | bytes 196616 | tf_op jit(solution)/shard_map/ppermute | solution.py:238
  15.4 2.6 %collective-permute-start.2 = (bf16[256,128]{1,0:T(8,128)(2,1)S(1)}, bf16[256,128]{1,0:T(8,128)(2,1)S(1)}, u32[]{:S(2)}, u32[]{:S(2)}) collective-permute-start(bf16[256,128]{1,0:T(8,128)(2,1)S(1)} %collective-permute-done.1.refs_2_), channel_id=1, source_target_pairs={{0,1},{1,0},{2,3},{3,2},{4,5},{5,4},{6,7},{7,6},{8,9},{9,8},{10,11... | collective-permute-start | bytes 196616 | tf_op jit(solution)/shard_map/ppermute | solution.py:238
  16.3 1.7 %collective-permute-start.10 = (bf16[256,128]{1,0:T(8,128)(2,1)S(1)}, bf16[256,128]{1,0:T(8,128)(2,1)S(1)}, u32[]{:S(2)}, u32[]{:S(2)}) collective-permute-start(bf16[256,128]{1,0:T(8,128)(2,1)S(1)} %collective-permute-done.9.refs_10_), channel_id=1, source_target_pairs={{0,1},{1,0},{2,3},{3,2},{4,5},{5,4},{6,7},{7,6},{8,9},{9,8},{10,11... | collective-permute-start | bytes 196616 | tf_op jit(solution)/shard_map/ppermute | solution.py:238
  16.3 1.7 %collective-permute-start.6 = (bf16[256,128]{1,0:T(8,128)(2,1)S(1)}, bf16[256,128]{1,0:T(8,128)(2,1)S(1)}, u32[]{:S(2)}, u32[]{:S(2)}) collective-permute-start(bf16[256,128]{1,0:T(8,128)(2,1)S(1)} %collective-permute-done.5.refs_6_), channel_id=1, source_target_pairs={{0,1},{1,0},{2,3},{3,2},{4,5},{5,4},{6,7},{7,6},{8,9},{9,8},{10,11... | collective-permute-start | bytes 196616 | tf_op jit(solution)/shard_map/ppermute | solution.py:238
  17.9 1.3 %collective-permute-start.14 = (bf16[256,128]{1,0:T(8,128)(2,1)S(1)}, bf16[256,128]{1,0:T(8,128)(2,1)S(1)}, u32[]{:S(2)}, u32[]{:S(2)}) collective-permute-start(bf16[256,128]{1,0:T(8,128)(2,1)S(1)} %collective-permute-done.13.refs_14_), channel_id=1, source_target_pairs={{0,1},{1,0},{2,3},{3,2},{4,5},{5,4},{6,7},{7,6},{8,9},{9,8},{10,11... | collective-permute-start | bytes 196616 | tf_op jit(solution)/shard_map/ppermute | solution.py:238
  31.7 5.4 %collective-permute-start.15 = (bf16[2,144,128]{2,1,0:T(8,128)(2,1)S(1)}, bf16[2,144,128]{2,1,0:T(8,128)(2,1)S(1)}, u32[]{:S(2)}, u32[]{:S(2)}) collective-permute-start(bf16[2,144,128]{2,1,0:T(8,128)(2,1)S(1)} %get-tuple-element.18), channel_id=1, source_target_pairs={{0,1},{1,0},{2,3},{3,2},{4,5},{5,4},{6,7},{7,6},{8,9},{9,8},{10,11... | collective-permute-start | bytes 221192 | tf_op jit(solution)/shard_map/ppermute | solution.py:238
  31.9 5.8 %collective-permute-start.16 = (bf16[2,144,128]{2,1,0:T(8,128)(2,1)S(1)}, bf16[2,144,128]{2,1,0:T(8,128)(2,1)S(1)}, u32[]{:S(2)}, u32[]{:S(2)}) collective-permute-start(bf16[2,144,128]{2,1,0:T(8,128)(2,1)S(1)} %get-tuple-element.19), channel_id=1, source_target_pairs={{0,2},{1,3},{2,0},{3,1},{4,6},{5,7},{6,4},{7,5},{8,10},{9,11},{10,... | collective-permute-start | bytes 221192 | tf_op jit(solution)/shard_map/ppermute | solution.py:238
  35.0 4.6 %collective-permute-start.17 = (bf16[2,144,128]{2,1,0:T(8,128)(2,1)S(1)}, bf16[2,144,128]{2,1,0:T(8,128)(2,1)S(1)}, u32[]{:S(2)}, u32[]{:S(2)}) collective-permute-start(bf16[2,144,128]{2,1,0:T(8,128)(2,1)S(1)} %get-tuple-element.20), channel_id=1, source_target_pairs={{0,3},{1,2},{2,1},{3,0},{4,7},{5,6},{6,5},{7,4},{8,11},{9,10},{10,... | collective-permute-start | bytes 221192 | tf_op jit(solution)/shard_map/ppermute | solution.py:238
  35.0 8.8 %collective-permute-start.19 = (bf16[2,144,128]{2,1,0:T(8,128)(2,1)S(1)}, bf16[2,144,128]{2,1,0:T(8,128)(2,1)S(1)}, u32[]{:S(2)}, u32[]{:S(2)}) collective-permute-start(bf16[2,144,128]{2,1,0:T(8,128)(2,1)S(1)} %get-tuple-element.24), channel_id=1, source_target_pairs={{0,1},{1,0},{2,3},{3,2},{4,5},{5,4},{6,7},{7,6},{8,9},{9,8},{10,11... | collective-permute-start | bytes 221192 | tf_op jit(solution)/shard_map/ppermute | solution.py:238
  35.2 8.6 %collective-permute-start.20 = (bf16[2,144,128]{2,1,0:T(8,128)(2,1)S(1)}, bf16[2,144,128]{2,1,0:T(8,128)(2,1)S(1)}, u32[]{:S(2)}, u32[]{:S(2)}) collective-permute-start(bf16[2,144,128]{2,1,0:T(8,128)(2,1)S(1)} %get-tuple-element.25), channel_id=1, source_target_pairs={{0,2},{1,3},{2,0},{3,1},{4,6},{5,7},{6,4},{7,5},{8,10},{9,11},{10,... | collective-permute-start | bytes 221192 | tf_op jit(solution)/shard_map/ppermute | solution.py:238
  37.2 6.6 %collective-permute-start.21 = (bf16[2,144,128]{2,1,0:T(8,128)(2,1)S(1)}, bf16[2,144,128]{2,1,0:T(8,128)(2,1)S(1)}, u32[]{:S(2)}, u32[]{:S(2)}) collective-permute-start(bf16[2,144,128]{2,1,0:T(8,128)(2,1)S(1)} %get-tuple-element.26), channel_id=1, source_target_pairs={{0,3},{1,2},{2,1},{3,0},{4,7},{5,6},{6,5},{7,4},{8,11},{9,10},{10,... | collective-permute-start | bytes 221192 | tf_op jit(solution)/shard_map/ppermute | solution.py:238
  42.0 7.5 %collective-permute-start.18 = (bf16[256,128]{1,0:T(8,128)(2,1)}, bf16[256,128]{1,0:T(8,128)(2,1)S(1)}, u32[]{:S(2)}, u32[]{:S(2)}) collective-permute-start(bf16[256,128]{1,0:T(8,128)(2,1)} %get-tuple-element.22), channel_id=1, source_target_pairs={{0,4},{1,5},{2,6},{3,7},{4,0},{5,1},{6,2},{7,3},{8,12},{9,13},{10,... | collective-permute-start | bytes 196616 | tf_op jit(solution)/shard_map/ppermute | solution.py:238
  46.2 7.6 %collective-permute-start.22 = (bf16[256,128]{1,0:T(8,128)(2,1)}, bf16[256,128]{1,0:T(8,128)(2,1)S(1)}, u32[]{:S(2)}, u32[]{:S(2)}) collective-permute-start(bf16[256,128]{1,0:T(8,128)(2,1)} %get-tuple-element.27), channel_id=1, source_target_pairs={{0,8},{1,9},{2,10},{3,11},{4,12},{5,13},{6,14},{7,15},{8,0},{9,1},... | collective-permute-start | bytes 196616 | tf_op jit(solution)/shard_map/ppermute | solution.py:238
  49.3 6.7 %collective-permute-start.23 = (bf16[256,128]{1,0:T(8,128)(2,1)}, bf16[256,128]{1,0:T(8,128)(2,1)S(1)}, u32[]{:S(2)}, u32[]{:S(2)}) collective-permute-start(bf16[256,128]{1,0:T(8,128)(2,1)} %get-tuple-element.28), channel_id=1, source_target_pairs={{0,12},{1,13},{2,14},{3,15},{4,8},{5,9},{6,10},{7,11},{8,4},{9,5},... | collective-permute-start | bytes 196616 | tf_op jit(solution)/shard_map/ppermute | solution.py:238
  (13 other events, 22.3 us)

commit v4 on v0

v4 whole, which is shorter than its diff:
```python
import functools

import jax
import jax.numpy as jnp
from jax import lax
from jax.experimental import pallas as pl
from jax.experimental.pallas import tpu as pltpu
from jax.sharding import PartitionSpec as P

AB_DEV = 8
CHUNK = 4
UNROLL = 2
LOADS = 8
TAIL = 16
PLANE = 4
SPREAD_COST = 10**10
DIRECT = 16


def layout_of(slots, n_aux):
    chunks = slots // CHUNK + 2 * AB_DEV
    places = chunks * CHUNK
    return chunks, places, {
        "slot": 0,
        "block": places,
        "gid": 2 * places,
        "far": 2 * places + chunks,
        "all": 2 * places + chunks + 1,
        "bit": 2 * places + chunks + 2,
        "size": 2 * places + chunks + 2 + n_aux,
    }


def prepare(tiles, tile_block, tile_aux, live, basis_order, base, n_aux, split, gates):
    slots = tiles.shape[0]
    nbb = basis_order.shape[0]
    bb_dev = nbb // n_aux
    chunks, places, at = layout_of(slots, n_aux)
    step = slots // LOADS

    def kernel(block_ref, aux_ref, live_ref, order_ref, base_ref, source, *refs):
        target, meta, merged, inverse, owner, key_of, spot, sems = refs[len(gates) :]
        for i, gate in enumerate(refs[: len(gates)]):
            merged[i] = gate[...]
        copies = [
            pltpu.make_async_copy(
                source.at[pl.ds(i * step, step)], target.at[pl.ds(i * step, step)], sems.at[i]
            )
            for i in range(LOADS)
        ]
        for copy in copies:
            copy.start()

        @pl.loop(0, nbb)
        def _(k):
            inverse[order_ref[k]] = k

        @pl.loop(0, places)
        def _(i):
            meta[at["slot"] + i] = 0
            meta[at["block"] + i] = n_aux

        @pl.loop(0, chunks)
        def _(i):
            meta[at["gid"] + i] = 0

        @pl.loop(0, n_aux)
        def _(m):
            meta[at["bit"] + m] = 0

        for key in range(2 * AB_DEV):
            spot[key] = 0

        @pl.loop(0, live_ref[0])
        def _(t):
            k = inverse[block_ref[t]]
            m = (k // bb_dev) ^ base_ref[0]
            key = aux_ref[t] + jnp.where(m < split, AB_DEV, 0)
            owner[t] = m
            key_of[t] = key
            spot[key] = spot[key] + 1
            meta[at["bit"] + m] = k % bb_dev

        used = jnp.int32(0)
        for key in range(2 * AB_DEV):
            need = (spot[key] + CHUNK - 1) // CHUNK
            spot[key] = used * CHUNK
            used = used + need
            if key == AB_DEV - 1:
                meta[at["far"]] = used
        meta[at["all"]] = used

        @pl.loop(0, live_ref[0])
        def _(t):
            key = key_of[t]
            pos = spot[key]
            spot[key] = pos + 1
            meta[at["block"] + pos] = owner[t]
            meta[at["slot"] + pos] = t

            @pl.when(pos % CHUNK == 0)
            def _():
                for i in range(1, CHUNK):
                    meta[at["slot"] + pos + i] = t
                meta[at["gid"] + pos // CHUNK] = aux_ref[t]

        for copy in copies:
            copy.wait()

    smem = pl.BlockSpec(memory_space=pltpu.SMEM)
    hbm = pl.BlockSpec(memory_space=pl.ANY)
    vmem = pl.BlockSpec(memory_space=pltpu.VMEM)
    return pl.pallas_call(
        kernel,
        out_shape=[
            jax.ShapeDtypeStruct(tiles.shape, tiles.dtype),
            jax.ShapeDtypeStruct((at["size"],), jnp.int32),
            jax.ShapeDtypeStruct((len(gates),) + gates[0].shape, gates[0].dtype),
        ],
        in_specs=[smem] * 5 + [hbm] + [vmem] * len(gates),
        out_specs=[vmem, smem, vmem],
        scratch_shapes=[
            pltpu.SMEM((nbb,), jnp.int32),
            pltpu.SMEM((slots,), jnp.int32),
            pltpu.SMEM((slots,), jnp.int32),
            pltpu.SMEM((2 * AB_DEV,), jnp.int32),
            pltpu.SemaphoreType.DMA((LOADS,)),
        ],
        cost_estimate=pl.CostEstimate(flops=0, bytes_accessed=4 * tiles.size, transcendentals=0),
        compiler_params=pltpu.CompilerParams(vmem_limit_bytes=16 * 1024 * 1024),
        name="prepare",
    )(tile_block, tile_aux, live, basis_order, base, tiles, *gates)


def slab(tiles, slot):
    return jnp.concatenate([tiles[slot, p] for p in range(tiles.shape[1])], axis=1)


def apply_fitted(meta, at, tiles, zb, acc, low, high):
    blk = acc.shape[2]
    turns = (high - low + UNROLL - 1) // UNROLL

    @pl.loop(0, turns)
    def _(step):
        for chunk in [low + step * UNROLL + u for u in range(UNROLL)]:
            spots = [chunk * CHUNK + i for i in range(CHUNK)]
            right = jnp.concatenate(
                [slab(tiles, meta[at["slot"] + pos]) for pos in spots], axis=0
            )
            value = lax.dot_general(
                zb[meta[at["gid"] + chunk]],
                right,
                (((1,), (1,)), ((), ())),
                preferred_element_type=jnp.float32,
            )
            for i, pos in enumerate(spots):
                acc[meta[at["block"] + pos]] += value[:, i * blk : (i + 1) * blk]


def put(meta, at, acc, m, out_ref, place):
    nocc, blk = acc.shape[1:]
    out_ref[place, :nocc, :] = acc[m].astype(out_ref.dtype)
    out_ref[place, nocc:, :] = jnp.full((TAIL, blk), meta[at["bit"] + m], jnp.int32).astype(
        jnp.float32
    ).astype(out_ref.dtype)


def first_part(direct, n_aux, meta_array, tiles_array, shards, sources):
    slots, auxb, blk, nocc = tiles_array.shape
    chunks, places, at = layout_of(slots, n_aux)
    n_in = len(shards)

    def kernel(meta, tiles, *refs):
        c_refs, out_refs = refs[:n_in], refs[n_in:-4]
        zb, ct, zacc, acc = refs[-4:]
        far, total = meta[at["far"]], meta[at["all"]]

        def turn(m, source):
            row = pl.multiple_of(meta[at["bit"] + m] * blk, blk)
            ct[m] = source[pl.ds(row, blk), :].T

        if direct:
            for m in range(n_aux):
                ref, i = sources[m]
                turn(m, c_refs[ref] if i is None else c_refs[ref].at[i])
        else:
            @pl.loop(0, n_aux)
            def _(m):
                turn(m, c_refs[0].at[m])

        ct[n_aux] = jnp.zeros((nocc, blk), ct.dtype)
        acc[...] = jnp.zeros(acc.shape, acc.dtype)
        zacc[...] = jnp.zeros(zacc.shape, zacc.dtype)

        @pl.loop(0, (total + UNROLL - 1) // UNROLL)
        def _(step):
            for chunk in [step * UNROLL + u for u in range(UNROLL)]:
                spots = [chunk * CHUNK + i for i in range(CHUNK)]
                left = jnp.concatenate([ct[meta[at["block"] + pos]] for pos in spots], axis=1)
                right = jnp.concatenate(
                    [slab(tiles, meta[at["slot"] + pos]) for pos in spots], axis=0
                )
                zacc[meta[at["gid"] + chunk]] += jnp.dot(
                    left, right, preferred_element_type=jnp.float32
                )

        for g in range(AB_DEV):
            zb[g] = zacc[g].astype(zb.dtype)
        apply_fitted(meta, at, tiles, zb, acc, 0, far)
        if direct:
            for m in range(n_aux // 2, n_aux):
                put(meta, at, acc, m, out_refs[m % PLANE], (m - n_aux // 2) // PLANE)
        else:
            @pl.loop(0, n_aux)
            def _(m):
                put(meta, at, acc, m, out_refs[0], m)

    smem = pl.BlockSpec(memory_space=pltpu.SMEM)
    vmem = pl.BlockSpec(memory_space=pltpu.VMEM)
    if direct:
        shape = (n_aux // PLANE // 2, nocc + TAIL, blk)
        out_shape = [jax.ShapeDtypeStruct(shape, jnp.bfloat16)] * PLANE
    else:
        out_shape = [jax.ShapeDtypeStruct((n_aux, nocc + TAIL, blk), jnp.bfloat16)]
    out_shape = out_shape + [jax.ShapeDtypeStruct((AB_DEV, nocc, auxb * nocc), jnp.bfloat16)]
    return pl.pallas_call(
        kernel,
        out_shape=out_shape,
        in_specs=[smem] + [vmem] * (1 + n_in),
        out_specs=[vmem] * len(out_shape),
        scratch_shapes=[
            pltpu.VMEM((n_aux + 1, nocc, blk), jnp.bfloat16),
            pltpu.VMEM((AB_DEV, nocc, auxb * nocc), jnp.float32),
            pltpu.VMEM((n_aux + 1, nocc, blk), jnp.float32),
        ],
        compiler_params=pltpu.CompilerParams(
            vmem_limit_bytes=(20 if direct else 46) * 1024 * 1024
        ),
        cost_estimate=pl.CostEstimate(
            flops=3 * tiles_array.size * nocc, bytes_accessed=tiles_array.size, transcendentals=0
        ),
        name="first_part",
    )(meta_array, tiles_array, *shards)


def second_part(n_aux, meta_array, tiles_array, fitted):
    slots, auxb, blk, nocc = tiles_array.shape
    chunks, places, at = layout_of(slots, n_aux)

    def kernel(meta, tiles, zb, *refs):
        out_refs, acc = refs[:-1], refs[-1]
        acc[...] = jnp.zeros(acc.shape, acc.dtype)
        apply_fitted(meta, at, tiles, zb, acc, meta[at["far"]], meta[at["all"]])
        for m in range(n_aux // 2):
            put(meta, at, acc, m, out_refs[m % PLANE], m // PLANE)

    smem = pl.BlockSpec(memory_space=pltpu.SMEM)
    vmem = pl.BlockSpec(memory_space=pltpu.VMEM)
    shape = (n_aux // PLANE // 2, nocc + TAIL, blk)
    return pl.pallas_call(
        kernel,
        out_shape=[jax.ShapeDtypeStruct(shape, jnp.bfloat16)] * PLANE,
        in_specs=[smem, vmem, vmem],
        out_specs=[vmem] * PLANE,
        scratch_shapes=[pltpu.VMEM((n_aux + 1, nocc, blk), jnp.float32)],
        compiler_params=pltpu.CompilerParams(vmem_limit_bytes=20 * 1024 * 1024),
        cost_estimate=pl.CostEstimate(
            flops=10**10, bytes_accessed=tiles_array.size, transcendentals=0
        ),
        name="second_part",
    )(meta_array, tiles_array, fitted)


def spread(parts, after, dtypes, blk, bb_dev):
    count, rows, nocc = parts[0].shape

    def kernel(*refs):
        sources, targets = refs[: len(parts)], refs[len(parts) + len(after) :]
        for i in range(count):
            sums = [jnp.zeros((blk, nocc), jnp.float32) for _ in range(bb_dev)]
            for source in sources:
                value = source[i, :blk, :].astype(jnp.float32)
                which = source[i, blk:, :][:1].astype(jnp.float32)
                for b in range(bb_dev):
                    sums[b] = sums[b] + jnp.where(which == b, value, 0.0)
            for b in range(bb_dev):
                targets[i][b * blk : (b + 1) * blk, :] = sums[b].astype(targets[i].dtype)

    vmem = pl.BlockSpec(memory_space=pltpu.VMEM)
    return pl.pallas_call(
        kernel,
        out_shape=[jax.ShapeDtypeStruct((bb_dev * blk, nocc), dtype) for dtype in dtypes],
        in_specs=[vmem] * len(parts) + [pl.BlockSpec(memory_space=pl.ANY)] * len(after),
        out_specs=[vmem] * count,
        compiler_params=pltpu.CompilerParams(vmem_limit_bytes=4 * 1024 * 1024),
        cost_estimate=pl.CostEstimate(
            flops=SPREAD_COST, bytes_accessed=SPREAD_COST // 1000, transcendentals=0
        ),
        name="spread",
    )(*parts, *after)


def total_of(arrays, blk):
    rows, nocc = arrays[0].shape

    def kernel(*refs):
        value = refs[0][...].astype(jnp.float32)
        for ref in refs[1:-1]:
            value = value + ref[...].astype(jnp.float32)
        for row in range(0, rows, blk):
            refs[-1][row : row + blk, :] = value[row : row + blk].T.astype(refs[-1].dtype)

    vmem = pl.BlockSpec(memory_space=pltpu.VMEM)
    return pl.pallas_call(
        kernel,
        out_shape=jax.ShapeDtypeStruct((rows, nocc), jnp.bfloat16),
        in_specs=[vmem] * len(arrays),
        out_specs=vmem,
        compiler_params=pltpu.CompilerParams(vmem_limit_bytes=4 * 1024 * 1024),
        name="total_of",
    )(*arrays)


def owner_sum(parts, blk, bb_dev):
    n_aux, rows, nocc = parts.shape

    def kernel(parts_ref, out_ref):
        sums = [jnp.zeros((blk, nocc), jnp.float32) for _ in range(bb_dev)]
        for s in range(n_aux):
            value = parts_ref[s, :blk, :].astype(jnp.float32)
            which = parts_ref[s, blk:, :][:1].astype(jnp.float32)
            for b in range(bb_dev):
                sums[b] = sums[b] + jnp.where(which == b, value, 0.0)
        for b in range(bb_dev):
            out_ref[b * blk : (b + 1) * blk, :] = sums[b].T.astype(out_ref.dtype)

    vmem = pl.BlockSpec(memory_space=pltpu.VMEM)
    return pl.pallas_call(
        kernel,
        out_shape=jax.ShapeDtypeStruct((bb_dev * blk, nocc), jnp.bfloat16),
        in_specs=[vmem],
        out_specs=vmem,
        name="owner_sum",
    )(parts)


def on_device(tiles, c_orbitals, basis_order, tile_block, tile_aux, live):
    blk, nocc = tiles.shape[2:]
    n_aux = lax.axis_size("aux")
    bb_dev = basis_order.shape[0] // n_aux
    direct = n_aux == DIRECT

    def swap(array, m):
        return lax.ppermute(array, "aux", [(i, i ^ m) for i in range(n_aux)])

    def ready(base, split, gates):
        return prepare(
            tiles, tile_block, tile_aux, live, basis_order, base, n_aux, split, gates
        )

    if not direct:
        held, meta, _ = ready(jnp.zeros((1,), jnp.int32), 0, [c_orbitals])
        whole = lax.all_gather(c_orbitals, "aux", axis=0, tiled=True)
        shards = [whole.reshape(n_aux, bb_dev * blk, nocc)]
        parts, _ = first_part(direct, n_aux, meta, held, shards, None)
        moved = lax.all_to_all(parts, "aux", 0, 0, tiled=True)
        return owner_sum(moved, blk, bb_dev)

    depth = n_aux // PLANE
    half = depth // 2
    column = [c_orbitals] + [None] * (depth - 1)
    for dz in range(depth - 1, 0, -1):
        column[dz] = swap(c_orbitals, dz * PLANE)
    base = lax.axis_index("aux").astype(jnp.int32)[None]
    beside = swap(c_orbitals, 2)
    held, meta, early = ready(base, n_aux // 2, column + [beside])
    late = [swap(array, 2) for array in column[1:]]
    shards = [early, swap(early, 1)] + late + [swap(array, 1) for array in late]
    sources = [None] * n_aux
    for dz in range(depth):
        for core in range(2):
            sources[dz * PLANE + core] = (core, dz)
            sources[dz * PLANE + 2 + core] = (
                (core, depth) if dz == 0 else (1 + dz + core * (depth - 1), None)
            )
    *far, fitted = first_part(direct, n_aux, meta, held, shards, sources)
    far = [far[0]] + [swap(far[r], r) for r in range(1, PLANE)]
    near = second_part(n_aux, meta, held, fitted)
    near = [near[0]] + [swap(near[r], r) for r in range(1, PLANE)]
    far = spread(far, [], [jnp.bfloat16] * half, blk, bb_dev)
    near = spread(
        near, [far[0]], [jnp.float32] + [jnp.bfloat16] * (half - 1), blk, bb_dev
    )
    sums = list(near) + list(far)
    return total_of([sums[0]] + [swap(sums[dz], dz * PLANE) for dz in range(1, depth)], blk)


def solution(mesh):
    return jax.shard_map(
        on_device,
        mesh=mesh,
        in_specs=(
            P(("grp", "aux"), None, None, None),
            P(("grp", "aux"), None),
            P("grp"),
            P(("grp", "aux")),
            P(("grp", "aux")),
            P(("grp", "aux")),
        ),
        out_specs=P(("grp", "aux"), None),
        check_vma=False,
    )
```

time: 247 us -> 64.6 us (0.26)
  waiting for transfers between devices: 102 us -> 19.4 us
  local copies, waits for them, and re-layouts: 68.4 us -> 6.78 us
  matrix products: 58.8 us -> 0 us
  Pallas kernels: 0 us -> 18.5 us
  starting transfers between devices: 0.04 us -> 18.2 us
  between operations: 14.1 us -> 0.74 us
  other arithmetic: 2.99 us -> 0 us
    reduce_scatter x1 -> x0, waiting for transfers between devices: 60.6 us -> none  [on_device(): lax.psum_scatter(jnp.dot(onehot, flat, precision=lax.Precision.HIGHEST).r...]
    dot_general x4 -> x0, matrix products: 58.8 us -> none  [the longest x1 27.6 us: on_device(): jnp.dot(member, half.reshape(slots, auxb * nocc * nocc), precision=lax.Pr...]
    all_gather x1 -> x0, waiting for transfers between devices: 40.8 us -> none  [on_device(): whole = lax.all_gather(c_orbitals, 'aux', axis=0, tiled=True)]
    unnamed x4 -> x10, local copies, waits for them, and re-layouts: 29.5 us -> 6.78 us
    dot_general x1 -> x0, local copies, waits for them, and re-layouts: 22.6 us -> none  [on_device(): jnp.einsum('tpmi,tmj->tpij', tiles, picked, preferred_element_type=jnp.fl...]
    ppermute x0 -> x20, waiting for transfers between devices: none -> 19.4 us  [swap(): return lax.ppermute(array, 'aux', [(i, i ^ m) for i in range(n_aux)])]
    pallas_call x0 -> x6, Pallas kernels: none -> 18.5 us  [the longest x1 7.93 us: first_part(): pl.pallas_call(kernel, out_shape=out_shape, in_specs=[smem] + [vmem] * (1...]
    ppermute x0 -> x20, starting transfers between devices: none -> 18.2 us  [swap(): return lax.ppermute(array, 'aux', [(i, i ^ m) for i in range(n_aux)])]
  transfers between devices with their start and end apart: 2 -> 20, of which waited for: 2 -> 11; matrix products, arithmetic and copies ran while one was open for 1% -> 0% of each run, Pallas kernels for 0% -> 6%
where the time goes in v4:
time: 64.6 us; the launch traced here: 63.5 us
  waiting for transfers between devices  19.4 us (30%)
  Pallas kernels  18.5 us (29%)
  starting transfers between devices  18.2 us (28%)
  local copies, waits for them, and re-layouts  6.78 us (10%)
  between operations  0.74 us (1%)
    ppermute x20, waiting for transfers between devices, swap(): return lax.ppermute(array, 'aux', [(i, i ^ m) for i in range(n_aux)])  19.4 us
    ppermute x20, starting transfers between devices, swap(): return lax.ppermute(array, 'aux', [(i, i ^ m) for i in range(n_aux)])  18.2 us
    pallas_call x1, Pallas kernels, first_part(): pl.pallas_call(kernel, out_shape=out_shape, in_specs=[smem] + [vmem] * (1...  7.93 us
    unnamed x10, local copies, waits for them, and re-layouts  6.78 us
    pallas_call x1, Pallas kernels, prepare(): pl.pallas_call(kernel, out_shape=[jax.ShapeDtypeStruct(tiles.shape, tiles...  6.02 us
    pallas_call x1, Pallas kernels, second_part(): pl.pallas_call(kernel, out_shape=[jax.ShapeDtypeStruct(shape, jnp.bfloat1...  3.57 us
  transfers between devices with their start and end apart: 20, of which 11 were waited for; matrix products, arithmetic and copies ran while one was open for 0% of the time, Pallas kernels for 6%

profile of v4, /device:TPU:0, one launch (start us, length us, event | category | flops | bytes accessed | tf_op | source)
XLA Modules:
  0.0 63.5 jit_solution(11104873447916324093)
XLA Ops:
  0.0 5.0 %collective-permute-start.2 = (bf16[256,128]{1,0:T(8,128)(2,1)}, bf16[256,128]{1,0:T(8,128)(2,1)S(1)}, u32[]{:S(2)}, u32[]{:S(2)}) collective-permute-start(bf16[256,128]{1,0:T(8,128)(2,1)} %refs_0_.1), channel_id=1, source_target_pairs={{0,12},{1,13},{2,14},{3,15},{4,8},{5,9},{6,10},{7,11},{8,4},{9,5},... | collective-permute-start | bytes 196616 | tf_op jit(solution)/shard_map/ppermute | solution.py:354
  5.6 1.7 %collective-permute-start.3 = (bf16[256,128]{1,0:T(8,128)(2,1)}, bf16[256,128]{1,0:T(8,128)(2,1)S(1)}, u32[]{:S(2)}, u32[]{:S(2)}) collective-permute-start(bf16[256,128]{1,0:T(8,128)(2,1)} %refs_0_.1), channel_id=1, source_target_pairs={{0,2},{1,3},{2,0},{3,1},{4,6},{5,7},{6,4},{7,5},{8,10},{9,11},{10,... | collective-permute-start | bytes 196616 | tf_op jit(solution)/shard_map/ppermute | solution.py:354
  8.0 2.8 %collective-permute-done.1.refs_2_ = bf16[256,128]{1,0:T(8,128)(2,1)S(1)} collective-permute-done((bf16[256,128]{1,0:T(8,128)(2,1)}, bf16[256,128]{1,0:T(8,128)(2,1)S(1)}, u32[]{:S(2)}, u32[]{:S(2)}) %collective-permute-start.1) | collective-permute-done | bytes 65568 | tf_op jit(solution)/shard_map/ppermute | solution.py:354
  10.9 4.0 %copy-done = bf16[64,5,128,128]{3,2,1,0:T(8,128)(2,1)S(1)} copy-done((bf16[64,5,128,128]{3,2,1,0:T(8,128)(2,1)S(1)}, bf16[64,5,128,128]{3,2,1,0:T(8,128)(2,1)}, u32[]{:S(2)}) %copy-start) | copy-done | bytes 10485784
  14.9 0.8 %copy-done.1 = bf16[256,128]{1,0:T(8,128)(2,1)S(1)} copy-done((bf16[256,128]{1,0:T(8,128)(2,1)S(1)}, bf16[256,128]{1,0:T(8,128)(2,1)}, u32[]{:S(2)}) %copy-start.1) | copy-done | bytes 65560
  15.7 0.7 %copy-done.2 = s32[64]{0:T(128)S(1)} copy-done((s32[64]{0:T(128)S(1)}, s32[64]{0:T(128)}, u32[]{:S(2)}) %copy-start.2) | copy-done | bytes 280
  17.7 6.0 %prepare.1 = (bf16[64,5,128,128]{3,2,1,0:T(8,128)(2,1)S(1)}, s32[306]{0:T(512)S(1)}, bf16[5,256,128]{2,1,0:T(8,128)(2,1)S(1)}) custom-call(s32[64]{0:T(128)S(1)} %copy-done.2, s32[64]{0:T(128)S(1)} %copy-done.3, s32[1]{0:T(128)S(6)} %copy.7.live_ref, s32[32]{0:T(128)S(1)} %copy-done.4, s32[1]{0:T(128)} %bitcast.base_ref, ...), custom_call_target="tpu_custom_call" | custom-call | bytes 20971520 | tf_op jit(solution)/shard_map/prepare/pallas_call | solution.py:113
  23.8 0.8 %collective-permute-start.7 = (bf16[256,128]{1,0:T(8,128)(2,1)S(1)}, bf16[256,128]{1,0:T(8,128)(2,1)S(1)}, u32[]{:S(2)}, u32[]{:S(2)}) collective-permute-start(bf16[256,128]{1,0:T(8,128)(2,1)S(1)} %collective-permute-done.2.refs_3_), channel_id=1, source_target_pairs={{0,2},{1,3},{2,0},{3,1},{4,6},{5,7},{6,4},{7,5},{8,10},{9,11},{10,... | collective-permute-start | bytes 196616 | tf_op jit(solution)/shard_map/ppermute | solution.py:354
  24.6 1.3 %collective-permute-start.6 = (bf16[256,128]{1,0:T(8,128)(2,1)S(1)}, bf16[256,128]{1,0:T(8,128)(2,1)S(1)}, u32[]{:S(2)}, u32[]{:S(2)}) collective-permute-start(bf16[256,128]{1,0:T(8,128)(2,1)S(1)} %collective-permute-done.1.refs_2_), channel_id=1, source_target_pairs={{0,2},{1,3},{2,0},{3,1},{4,6},{5,7},{6,4},{7,5},{8,10},{9,11},{10,... | collective-permute-start | bytes 196616 | tf_op jit(solution)/shard_map/ppermute | solution.py:354
  25.9 0.7 %collective-permute-start.5 = (bf16[256,128]{1,0:T(8,128)(2,1)S(1)}, bf16[256,128]{1,0:T(8,128)(2,1)S(1)}, u32[]{:S(2)}, u32[]{:S(2)}) collective-permute-start(bf16[256,128]{1,0:T(8,128)(2,1)S(1)} %collective-permute-done.refs_1_), channel_id=1, source_target_pairs={{0,2},{1,3},{2,0},{3,1},{4,6},{5,7},{6,4},{7,5},{8,10},{9,11},{10,... | collective-permute-start | bytes 196616 | tf_op jit(solution)/shard_map/ppermute | solution.py:354
  26.6 2.1 %collective-permute-done.7.refs_4_ = bf16[256,128]{1,0:T(8,128)(2,1)S(1)} collective-permute-done((bf16[256,128]{1,0:T(8,128)(2,1)S(1)}, bf16[256,128]{1,0:T(8,128)(2,1)S(1)}, u32[]{:S(2)}, u32[]{:S(2)}) %collective-permute-start.7) | collective-permute-done | bytes 65568 | tf_op jit(solution)/shard_map/ppermute | solution.py:354
  28.7 1.4 %collective-permute-done.6.refs_3_ = bf16[256,128]{1,0:T(8,128)(2,1)S(1)} collective-permute-done((bf16[256,128]{1,0:T(8,128)(2,1)S(1)}, bf16[256,128]{1,0:T(8,128)(2,1)S(1)}, u32[]{:S(2)}, u32[]{:S(2)}) %collective-permute-start.6) | collective-permute-done | bytes 65568 | tf_op jit(solution)/shard_map/ppermute | solution.py:354
  30.1 1.0 %collective-permute-done.5.refs_2_ = bf16[256,128]{1,0:T(8,128)(2,1)S(1)} collective-permute-done((bf16[256,128]{1,0:T(8,128)(2,1)S(1)}, bf16[256,128]{1,0:T(8,128)(2,1)S(1)}, u32[]{:S(2)}, u32[]{:S(2)}) %collective-permute-start.5) | collective-permute-done | bytes 65568 | tf_op jit(solution)/shard_map/ppermute | solution.py:354
  31.4 1.0 %collective-permute-done.8.refs_5_ = bf16[256,128]{1,0:T(8,128)(2,1)S(1)} collective-permute-done((bf16[256,128]{1,0:T(8,128)(2,1)S(1)}, bf16[256,128]{1,0:T(8,128)(2,1)S(1)}, u32[]{:S(2)}, u32[]{:S(2)}) %collective-permute-start.8) | collective-permute-done | bytes 65568 | tf_op jit(solution)/shard_map/ppermute | solution.py:354
  32.3 7.9 %first_part.1 = (bf16[2,144,128]{2,1,0:T(8,128)(2,1)S(1)}, bf16[2,144,128]{2,1,0:T(8,128)(2,1)S(1)}, bf16[2,144,128]{2,1,0:T(8,128)(2,1)S(1)}, bf16[2,144,128]{2,1,0:T(8,128)(2,1)S(1)}, bf16[8,128,640]{2,1,0:T(8,128)(2,1)S(1)}) custom-call(s32[306]{0:T(512)S(1)} %get-tuple-element.21.meta, bf16[64,5,128,128]{3,2,1,0:T(8,128)(2,1)S(1)} %get-tuple-element.22.tiles, ...), custom_call_target="tpu_custom_call" | custom-call | flops 2013265920 | bytes 5242880 | tf_op jit(solution)/shard_map/first_part/pallas_call | solution.py:226
  40.4 1.4 %collective-permute-start.15 = (bf16[2,144,128]{2,1,0:T(8,128)(2,1)S(1)}, bf16[2,144,128]{2,1,0:T(8,128)(2,1)S(1)}, u32[]{:S(2)}, u32[]{:S(2)}) collective-permute-start(bf16[2,144,128]{2,1,0:T(8,128)(2,1)S(1)} %get-tuple-element.31), channel_id=1, source_target_pairs={{0,2},{1,3},{2,0},{3,1},{4,6},{5,7},{6,4},{7,5},{8,10},{9,11},{10,... | collective-permute-start | bytes 221192 | tf_op jit(solution)/shard_map/ppermute | solution.py:354
  42.2 3.6 %second_part.1 = (bf16[2,144,128]{2,1,0:T(8,128)(2,1)S(1)}, bf16[2,144,128]{2,1,0:T(8,128)(2,1)S(1)}, bf16[2,144,128]{2,1,0:T(8,128)(2,1)S(1)}, bf16[2,144,128]{2,1,0:T(8,128)(2,1)S(1)}) custom-call(s32[306]{0:T(512)S(1)} %get-tuple-element.21.meta, bf16[64,5,128,128]{3,2,1,0:T(8,128)(2,1)S(1)} %get-tuple-element.22.tiles, ...), custom_call_target="tpu_custom_call" | custom-call | flops 10000000000 | bytes 5242880 | tf_op jit(solution)/shard_map/second_part/pallas_call | solution.py:260
  46.2 1.4 %collective-permute-start.12 = (bf16[2,144,128]{2,1,0:T(8,128)(2,1)S(1)}, bf16[2,144,128]{2,1,0:T(8,128)(2,1)S(1)}, u32[]{:S(2)}, u32[]{:S(2)}) collective-permute-start(bf16[2,144,128]{2,1,0:T(8,128)(2,1)S(1)} %get-tuple-element.27), channel_id=1, source_target_pairs={{0,2},{1,3},{2,0},{3,1},{4,6},{5,7},{6,4},{7,5},{8,10},{9,11},{10,... | collective-permute-start | bytes 221192 | tf_op jit(solution)/shard_map/ppermute | solution.py:354
  47.9 2.7 %collective-permute-done.12.refs_2_ = bf16[2,144,128]{2,1,0:T(8,128)(2,1)S(1)} collective-permute-done((bf16[2,144,128]{2,1,0:T(8,128)(2,1)S(1)}, bf16[2,144,128]{2,1,0:T(8,128)(2,1)S(1)}, u32[]{:S(2)}, u32[]{:S(2)}) %collective-permute-start.12) | collective-permute-done | bytes 73760 | tf_op jit(solution)/shard_map/ppermute | solution.py:354
  50.6 1.6 %collective-permute-done.13.refs_3_ = bf16[2,144,128]{2,1,0:T(8,128)(2,1)S(1)} collective-permute-done((bf16[2,144,128]{2,1,0:T(8,128)(2,1)S(1)}, bf16[2,144,128]{2,1,0:T(8,128)(2,1)S(1)}, u32[]{:S(2)}, u32[]{:S(2)}) %collective-permute-start.13) | collective-permute-done | bytes 73760 | tf_op jit(solution)/shard_map/ppermute | solution.py:354
  52.8 3.0 %collective-permute-start.19 = (bf16[256,128]{1,0:T(8,128)(2,1)S(1)}, bf16[256,128]{1,0:T(8,128)(2,1)S(1)}, u32[]{:S(2)}, u32[]{:S(2)}) collective-permute-start(bf16[256,128]{1,0:T(8,128)(2,1)S(1)} %get-tuple-element.36), channel_id=1, source_target_pairs={{0,12},{1,13},{2,14},{3,15},{4,8},{5,9},{6,10},{7,11},{8,4},{9,5},... | collective-permute-start | bytes 196616 | tf_op jit(solution)/shard_map/ppermute | solution.py:354
  56.6 3.3 %collective-permute-done.19.refs_3_ = bf16[256,128]{1,0:T(8,128)(2,1)S(1)} collective-permute-done((bf16[256,128]{1,0:T(8,128)(2,1)S(1)}, bf16[256,128]{1,0:T(8,128)(2,1)S(1)}, u32[]{:S(2)}, u32[]{:S(2)}) %collective-permute-start.19) | collective-permute-done | bytes 65568 | tf_op jit(solution)/shard_map/ppermute | solution.py:354
  59.9 2.9 %collective-permute-done.18.refs_2_ = bf16[256,128]{1,0:T(8,128)(2,1)S(1)} collective-permute-done((bf16[256,128]{1,0:T(8,128)(2,1)S(1)}, bf16[256,128]{1,0:T(8,128)(2,1)S(1)}, u32[]{:S(2)}, u32[]{:S(2)}) %collective-permute-start.18) | collective-permute-done | bytes 65568 | tf_op jit(solution)/shard_map/ppermute | solution.py:354
  62.8 0.7 %total_of.1 = bf16[256,128]{1,0:T(8,128)(2,1)} custom-call(f32[256,128]{1,0:T(8,128)S(1)} %get-tuple-element.34.refs_0_, bf16[256,128]{1,0:T(8,128)(2,1)S(1)} %collective-permute-done.17.refs_1_, bf16[256,128]{1,0:T(8,128)(2,1)S(1)} %collective-permute-done.18.refs_2_, bf16[256,128]{1,0:T(8,128)(2,1)S(1)} %collective-permute-done.19.refs_3_), custom_call_target="tpu_custom_call" | custom-call | tf_op jit(solution)/shard_map/total_of/pallas_call | solution.py:314
  (32 shorter events, 4.8 us)
Async XLA Ops:
  0.0 8.0 %collective-permute-start.2 = (bf16[256,128]{1,0:T(8,128)(2,1)}, bf16[256,128]{1,0:T(8,128)(2,1)S(1)}, u32[]{:S(2)}, u32[]{:S(2)}) collective-permute-start(bf16[256,128]{1,0:T(8,128)(2,1)} %refs_0_.1), channel_id=1, source_target_pairs={{0,12},{1,13},{2,14},{3,15},{4,8},{5,9},{6,10},{7,11},{8,4},{9,5},... | collective-permute-start | bytes 196616 | tf_op jit(solution)/shard_map/ppermute | solution.py:354
  5.0 5.8 %collective-permute-start.1 = (bf16[256,128]{1,0:T(8,128)(2,1)}, bf16[256,128]{1,0:T(8,128)(2,1)S(1)}, u32[]{:S(2)}, u32[]{:S(2)}) collective-permute-start(bf16[256,128]{1,0:T(8,128)(2,1)} %refs_0_.1), channel_id=1, source_target_pairs={{0,8},{1,9},{2,10},{3,11},{4,12},{5,13},{6,14},{7,15},{8,0},{9,1},... | collective-permute-start | bytes 196616 | tf_op jit(solution)/shard_map/ppermute | solution.py:354
  5.1 5.8 %collective-permute-start = (bf16[256,128]{1,0:T(8,128)(2,1)}, bf16[256,128]{1,0:T(8,128)(2,1)S(1)}, u32[]{:S(2)}, u32[]{:S(2)}) collective-permute-start(bf16[256,128]{1,0:T(8,128)(2,1)} %refs_0_.1), channel_id=1, source_target_pairs={{0,4},{1,5},{2,6},{3,7},{4,0},{5,1},{6,2},{7,3},{8,12},{9,13},{10,... | collective-permute-start | bytes 196616 | tf_op jit(solution)/shard_map/ppermute | solution.py:354
  5.6 5.2 %collective-permute-start.3 = (bf16[256,128]{1,0:T(8,128)(2,1)}, bf16[256,128]{1,0:T(8,128)(2,1)S(1)}, u32[]{:S(2)}, u32[]{:S(2)}) collective-permute-start(bf16[256,128]{1,0:T(8,128)(2,1)} %refs_0_.1), channel_id=1, source_target_pairs={{0,2},{1,3},{2,0},{3,1},{4,6},{5,7},{6,4},{7,5},{8,10},{9,11},{10,... | collective-permute-start | bytes 196616 | tf_op jit(solution)/shard_map/ppermute | solution.py:354
  10.9 4.0 %copy-start = (bf16[64,5,128,128]{3,2,1,0:T(8,128)(2,1)S(1)}, bf16[64,5,128,128]{3,2,1,0:T(8,128)(2,1)}, u32[]{:S(2)}) copy-start(bf16[64,5,128,128]{3,2,1,0:T(8,128)(2,1)} %source.1) | copy-start | bytes 31457284
  14.8 0.8 %copy-start.1 = (bf16[256,128]{1,0:T(8,128)(2,1)S(1)}, bf16[256,128]{1,0:T(8,128)(2,1)}, u32[]{:S(2)}) copy-start(bf16[256,128]{1,0:T(8,128)(2,1)} %refs_0_.1) | copy-start | bytes 196612
  15.7 0.7 %copy-start.2 = (s32[64]{0:T(128)S(1)}, s32[64]{0:T(128)}, u32[]{:S(2)}) copy-start(s32[64]{0:T(128)} %block_ref.1) | copy-start | bytes 772
  16.3 0.7 %copy-start.3 = (s32[64]{0:T(128)S(1)}, s32[64]{0:T(128)}, u32[]{:S(2)}) copy-start(s32[64]{0:T(128)} %aux_ref.1) | copy-start | bytes 772
  23.7 8.7 %collective-permute-start.4 = (bf16[5,256,128]{2,1,0:T(8,128)(2,1)S(1)}, bf16[5,256,128]{2,1,0:T(8,128)(2,1)S(1)}, u32[]{:S(2)}, u32[]{:S(2)}) collective-permute-start(bf16[5,256,128]{2,1,0:T(8,128)(2,1)S(1)} %get-tuple-element.23.refs_0_), channel_id=1, source_target_pairs={{0,1},{1,0},{2,3},{3,2},{4,5},{5,4},{6,7},{7,6},{8,9},{9,8},{10,11... | collective-permute-start | bytes 983048 | tf_op jit(solution)/shard_map/ppermute | solution.py:354
  23.8 5.0 %collective-permute-start.7 = (bf16[256,128]{1,0:T(8,128)(2,1)S(1)}, bf16[256,128]{1,0:T(8,128)(2,1)S(1)}, u32[]{:S(2)}, u32[]{:S(2)}) collective-permute-start(bf16[256,128]{1,0:T(8,128)(2,1)S(1)} %collective-permute-done.2.refs_3_), channel_id=1, source_target_pairs={{0,2},{1,3},{2,0},{3,1},{4,6},{5,7},{6,4},{7,5},{8,10},{9,11},{10,... | collective-permute-start | bytes 196616 | tf_op jit(solution)/shard_map/ppermute | solution.py:354
  24.6 5.6 %collective-permute-start.6 = (bf16[256,128]{1,0:T(8,128)(2,1)S(1)}, bf16[256,128]{1,0:T(8,128)(2,1)S(1)}, u32[]{:S(2)}, u32[]{:S(2)}) collective-permute-start(bf16[256,128]{1,0:T(8,128)(2,1)S(1)} %collective-permute-done.1.refs_2_), channel_id=1, source_target_pairs={{0,2},{1,3},{2,0},{3,1},{4,6},{5,7},{6,4},{7,5},{8,10},{9,11},{10,... | collective-permute-start | bytes 196616 | tf_op jit(solution)/shard_map/ppermute | solution.py:354
  25.9 5.2 %collective-permute-start.5 = (bf16[256,128]{1,0:T(8,128)(2,1)S(1)}, bf16[256,128]{1,0:T(8,128)(2,1)S(1)}, u32[]{:S(2)}, u32[]{:S(2)}) collective-permute-start(bf16[256,128]{1,0:T(8,128)(2,1)S(1)} %collective-permute-done.refs_1_), channel_id=1, source_target_pairs={{0,2},{1,3},{2,0},{3,1},{4,6},{5,7},{6,4},{7,5},{8,10},{9,11},{10,... | collective-permute-start | bytes 196616 | tf_op jit(solution)/shard_map/ppermute | solution.py:354
  28.7 2.4 %collective-permute-start.10 = (bf16[256,128]{1,0:T(8,128)(2,1)S(1)}, bf16[256,128]{1,0:T(8,128)(2,1)S(1)}, u32[]{:S(2)}, u32[]{:S(2)}) collective-permute-start(bf16[256,128]{1,0:T(8,128)(2,1)S(1)} %collective-permute-done.7.refs_4_), channel_id=1, source_target_pairs={{0,1},{1,0},{2,3},{3,2},{4,5},{5,4},{6,7},{7,6},{8,9},{9,8},{10,11... | collective-permute-start | bytes 196616 | tf_op jit(solution)/shard_map/ppermute | solution.py:354
  30.1 1.3 %collective-permute-start.9 = (bf16[256,128]{1,0:T(8,128)(2,1)S(1)}, bf16[256,128]{1,0:T(8,128)(2,1)S(1)}, u32[]{:S(2)}, u32[]{:S(2)}) collective-permute-start(bf16[256,128]{1,0:T(8,128)(2,1)S(1)} %collective-permute-done.6.refs_3_), channel_id=1, source_target_pairs={{0,1},{1,0},{2,3},{3,2},{4,5},{5,4},{6,7},{7,6},{8,9},{9,8},{10,11... | collective-permute-start | bytes 196616 | tf_op jit(solution)/shard_map/ppermute | solution.py:354
  31.1 1.3 %collective-permute-start.8 = (bf16[256,128]{1,0:T(8,128)(2,1)S(1)}, bf16[256,128]{1,0:T(8,128)(2,1)S(1)}, u32[]{:S(2)}, u32[]{:S(2)}) collective-permute-start(bf16[256,128]{1,0:T(8,128)(2,1)S(1)} %collective-permute-done.5.refs_2_), channel_id=1, source_target_pairs={{0,1},{1,0},{2,3},{3,2},{4,5},{5,4},{6,7},{7,6},{8,9},{9,8},{10,11... | collective-permute-start | bytes 196616 | tf_op jit(solution)/shard_map/ppermute | solution.py:354
  40.3 7.3 %collective-permute-start.14 = (bf16[2,144,128]{2,1,0:T(8,128)(2,1)S(1)}, bf16[2,144,128]{2,1,0:T(8,128)(2,1)S(1)}, u32[]{:S(2)}, u32[]{:S(2)}) collective-permute-start(bf16[2,144,128]{2,1,0:T(8,128)(2,1)S(1)} %get-tuple-element.30), channel_id=1, source_target_pairs={{0,1},{1,0},{2,3},{3,2},{4,5},{5,4},{6,7},{7,6},{8,9},{9,8},{10,11... | collective-permute-start | bytes 221192 | tf_op jit(solution)/shard_map/ppermute | solution.py:354
  40.4 7.4 %collective-permute-start.15 = (bf16[2,144,128]{2,1,0:T(8,128)(2,1)S(1)}, bf16[2,144,128]{2,1,0:T(8,128)(2,1)S(1)}, u32[]{:S(2)}, u32[]{:S(2)}) collective-permute-start(bf16[2,144,128]{2,1,0:T(8,128)(2,1)S(1)} %get-tuple-element.31), channel_id=1, source_target_pairs={{0,2},{1,3},{2,0},{3,1},{4,6},{5,7},{6,4},{7,5},{8,10},{9,11},{10,... | collective-permute-start | bytes 221192 | tf_op jit(solution)/shard_map/ppermute | solution.py:354
  41.8 5.9 %collective-permute-start.16 = (bf16[2,144,128]{2,1,0:T(8,128)(2,1)S(1)}, bf16[2,144,128]{2,1,0:T(8,128)(2,1)S(1)}, u32[]{:S(2)}, u32[]{:S(2)}) collective-permute-start(bf16[2,144,128]{2,1,0:T(8,128)(2,1)S(1)} %get-tuple-element.32), channel_id=1, source_target_pairs={{0,3},{1,2},{2,1},{3,0},{4,7},{5,6},{6,5},{7,4},{8,11},{9,10},{10,... | collective-permute-start | bytes 221192 | tf_op jit(solution)/shard_map/ppermute | solution.py:354
  45.8 2.1 %collective-permute-start.11 = (bf16[2,144,128]{2,1,0:T(8,128)(2,1)S(1)}, bf16[2,144,128]{2,1,0:T(8,128)(2,1)S(1)}, u32[]{:S(2)}, u32[]{:S(2)}) collective-permute-start(bf16[2,144,128]{2,1,0:T(8,128)(2,1)S(1)} %get-tuple-element.26), channel_id=1, source_target_pairs={{0,1},{1,0},{2,3},{3,2},{4,5},{5,4},{6,7},{7,6},{8,9},{9,8},{10,11... | collective-permute-start | bytes 221192 | tf_op jit(solution)/shard_map/ppermute | solution.py:354
  46.2 4.4 %collective-permute-start.12 = (bf16[2,144,128]{2,1,0:T(8,128)(2,1)S(1)}, bf16[2,144,128]{2,1,0:T(8,128)(2,1)S(1)}, u32[]{:S(2)}, u32[]{:S(2)}) collective-permute-start(bf16[2,144,128]{2,1,0:T(8,128)(2,1)S(1)} %get-tuple-element.27), channel_id=1, source_target_pairs={{0,2},{1,3},{2,0},{3,1},{4,6},{5,7},{6,4},{7,5},{8,10},{9,11},{10,... | collective-permute-start | bytes 221192 | tf_op jit(solution)/shard_map/ppermute | solution.py:354
  47.6 4.5 %collective-permute-start.13 = (bf16[2,144,128]{2,1,0:T(8,128)(2,1)S(1)}, bf16[2,144,128]{2,1,0:T(8,128)(2,1)S(1)}, u32[]{:S(2)}, u32[]{:S(2)}) collective-permute-start(bf16[2,144,128]{2,1,0:T(8,128)(2,1)S(1)} %get-tuple-element.28), channel_id=1, source_target_pairs={{0,3},{1,2},{2,1},{3,0},{4,7},{5,6},{6,5},{7,4},{8,11},{9,10},{10,... | collective-permute-start | bytes 221192 | tf_op jit(solution)/shard_map/ppermute | solution.py:354
  52.2 4.3 %collective-permute-start.17 = (bf16[256,128]{1,0:T(8,128)(2,1)S(1)}, bf16[256,128]{1,0:T(8,128)(2,1)S(1)}, u32[]{:S(2)}, u32[]{:S(2)}) collective-permute-start(bf16[256,128]{1,0:T(8,128)(2,1)S(1)} %get-tuple-element.35), channel_id=1, source_target_pairs={{0,4},{1,5},{2,6},{3,7},{4,0},{5,1},{6,2},{7,3},{8,12},{9,13},{10,... | collective-permute-start | bytes 196616 | tf_op jit(solution)/shard_map/ppermute | solution.py:354
  52.8 7.1 %collective-permute-start.19 = (bf16[256,128]{1,0:T(8,128)(2,1)S(1)}, bf16[256,128]{1,0:T(8,128)(2,1)S(1)}, u32[]{:S(2)}, u32[]{:S(2)}) collective-permute-start(bf16[256,128]{1,0:T(8,128)(2,1)S(1)} %get-tuple-element.36), channel_id=1, source_target_pairs={{0,12},{1,13},{2,14},{3,15},{4,8},{5,9},{6,10},{7,11},{8,4},{9,5},... | collective-permute-start | bytes 196616 | tf_op jit(solution)/shard_map/ppermute | solution.py:354
  55.8 7.0 %collective-permute-start.18 = (bf16[256,128]{1,0:T(8,128)(2,1)S(1)}, bf16[256,128]{1,0:T(8,128)(2,1)S(1)}, u32[]{:S(2)}, u32[]{:S(2)}) collective-permute-start(bf16[256,128]{1,0:T(8,128)(2,1)S(1)} %get-tuple-element.33.refs_4_), channel_id=1, source_target_pairs={{0,8},{1,9},{2,10},{3,11},{4,12},{5,13},{6,14},{7,15},{8,0},{9,1},... | collective-permute-start | bytes 196616 | tf_op jit(solution)/shard_map/ppermute | solution.py:354
  (1 other events, 0.7 us)

commit v5 on v3

v5 whole, which is shorter than its diff:
```python
import functools

import jax
import jax.numpy as jnp
from jax import lax
from jax.experimental import pallas as pl
from jax.experimental.pallas import tpu as pltpu
from jax.sharding import PartitionSpec as P

AB_DEV = 8
CHUNK = 4
UNROLL = 2
AHEAD = 8
FIRST_VMEM = 36
TAIL = 16
PLANE = 4
SPREAD_COST = 10**10
DIRECT = 16


def plan(tile_block, tile_aux, live, basis_order, base, split, n_aux, bb_dev):
    slots = tile_block.shape[0]
    nbb = basis_order.shape[0]
    keys = 2 * AB_DEV
    chunks = slots // CHUNK + keys
    t = lax.iota(jnp.int32, slots)
    alive = t < live[0]
    position = jnp.sum(
        jnp.where(
            basis_order[None, :] == tile_block[:, None], lax.iota(jnp.int32, nbb)[None, :], 0
        ),
        axis=1,
    )
    where_to = jnp.bitwise_xor(position // bb_dev, base)
    which = position % bb_dev
    group = jnp.where(alive, tile_aux + jnp.where(where_to < split, AB_DEV, 0), keys)
    ids = lax.iota(jnp.int32, keys)
    counts = jnp.sum((group[None, :] == ids[:, None]).astype(jnp.int32), axis=1)
    need = (counts + CHUNK - 1) // CHUNK
    ends = jnp.sum(jnp.where(ids[None, :] <= ids[:, None], need[None, :], 0), axis=1)
    rank = jnp.sum(
        ((group[None, :] == group[:, None]) & (t[None, :] < t[:, None])).astype(jnp.int32), axis=1
    )
    start = jnp.sum(jnp.where(group[:, None] > ids[None, :], need[None, :], 0), axis=1)
    place = jnp.where(alive, start * CHUNK + rank, -1)
    q = lax.iota(jnp.int32, chunks * CHUNK)
    hit = place[None, :] == q[:, None]
    lead = place[None, :] == (q // CHUNK * CHUNK)[:, None]
    valid = jnp.any(hit, axis=1)
    slot = jnp.sum(jnp.where(hit, t[None, :], 0), axis=1)
    slot = jnp.where(valid, slot, jnp.sum(jnp.where(lead, t[None, :], 0), axis=1))
    block = jnp.where(valid, jnp.sum(jnp.where(hit, where_to[None, :], 0), axis=1), n_aux)
    gid = jnp.sum(
        (lax.iota(jnp.int32, chunks)[:, None] >= ends[None, :]).astype(jnp.int32), axis=1
    )
    bit = jnp.max(
        jnp.where(
            (where_to[None, :] == lax.iota(jnp.int32, n_aux)[:, None]) & alive[None, :],
            which[None, :],
            0,
        ),
        axis=1,
    )
    gid = gid % AB_DEV
    return slot, block, jnp.concatenate([gid, ends]), bit


def slab(tiles, slot):
    return jnp.concatenate([tiles[slot, p] for p in range(tiles.shape[1])], axis=1)


def apply_fitted(meta, tiles, zb, acc, low, high):
    slot_ref, block_ref, gid_ref, _ = meta
    blk = acc.shape[1]

    @pl.loop(0, (high - low + UNROLL - 1) // UNROLL)
    def _(step):
        for chunk in [low + step * UNROLL + u for u in range(UNROLL)]:
            spots = [chunk * CHUNK + i for i in range(CHUNK)]
            left = jnp.concatenate([slab(tiles, slot_ref[pos]) for pos in spots], axis=0)
            value = jnp.dot(left, zb[gid_ref[chunk]], preferred_element_type=jnp.float32)
            for i, pos in enumerate(spots):
                acc[block_ref[pos]] += value[i * blk : (i + 1) * blk]


def put(bit_ref, acc, m, out_ref, place):
    blk, nocc = acc.shape[1:]
    out_ref[place, :blk, :] = acc[m].astype(out_ref.dtype)
    out_ref[place, blk:, :] = jnp.full((TAIL, nocc), bit_ref[m], jnp.int32).astype(
        jnp.float32
    ).astype(out_ref.dtype)


def first_part(direct, n_aux, meta_arrays, tiles_array, own_array, shards, sources):
    slots, auxb, blk, nocc = tiles_array.shape
    chunks = slots // CHUNK + 2 * AB_DEV
    n_in = len(shards)

    def kernel(slot_ref, block_ref, gid_ref, bit_ref, tiles_hbm, own_hbm, *refs):
        c_refs, out_refs = refs[:n_in], refs[n_in:-8]
        zb, tiles, ct, zacc, acc, own, sems, own_sem = refs[-8:]
        own_copy = pltpu.make_async_copy(own_hbm, own, own_sem)
        own_copy.start()
        far = gid_ref[chunks + AB_DEV - 1]
        total = gid_ref[chunks + 2 * AB_DEV - 1]

        def each(chunk, act):
            for i in range(CHUNK):
                pos = chunk * CHUNK + i
                copy = pltpu.make_async_copy(
                    tiles_hbm.at[slot_ref[pos]], tiles.at[slot_ref[pos]], sems.at[chunk]
                )

                @pl.when(block_ref[pos] < n_aux)
                def _():
                    act(copy)

        @pl.loop(0, jnp.minimum(total, AHEAD))
        def _(chunk):
            each(chunk, lambda copy: copy.start())

        def turn(m, source):
            row = pl.multiple_of(bit_ref[m] * blk, blk)
            ct[m] = source[pl.ds(row, blk), :].T

        if direct:
            for m in range(1, n_aux):
                ref, i = sources[m]
                turn(m, c_refs[ref] if i is None else c_refs[ref].at[i])
        else:
            @pl.loop(0, n_aux)
            def _(m):
                turn(m, c_refs[0].at[m])

        own_copy.wait()
        if direct:
            turn(0, own)
        ct[n_aux] = jnp.zeros((nocc, blk), ct.dtype)
        acc[...] = jnp.zeros(acc.shape, acc.dtype)
        zacc[...] = jnp.zeros(zacc.shape, zacc.dtype)

        @pl.loop(0, (total + UNROLL - 1) // UNROLL)
        def _(step):
            group = [step * UNROLL + u for u in range(UNROLL)]
            for chunk in group:
                @pl.when(chunk + AHEAD < total)
                def _():
                    each(chunk + AHEAD, lambda copy: copy.start())
            for chunk in group:
                each(chunk, lambda copy: copy.wait())
            for chunk in group:
                spots = [chunk * CHUNK + i for i in range(CHUNK)]
                left = jnp.concatenate([ct[block_ref[pos]] for pos in spots], axis=1)
                right = jnp.concatenate([slab(tiles, slot_ref[pos]) for pos in spots], axis=0)
                zacc[gid_ref[chunk]] += jnp.dot(left, right, preferred_element_type=jnp.float32)

        for g in range(AB_DEV):
            for p in range(auxb):
                part = zacc[g, :, p * nocc : (p + 1) * nocc].astype(zb.dtype)
                zb[g, p * nocc : (p + 1) * nocc, :] = part.T
        apply_fitted((slot_ref, block_ref, gid_ref, bit_ref), tiles, zb, acc, 0, far)
        if direct:
            for m in range(n_aux // 2, n_aux):
                put(bit_ref, acc, m, out_refs[m % PLANE], (m - n_aux // 2) // PLANE)
        else:
            @pl.loop(0, n_aux)
            def _(m):
                put(bit_ref, acc, m, out_refs[0], m)

    smem = pl.BlockSpec(memory_space=pltpu.SMEM)
    vmem = pl.BlockSpec(memory_space=pltpu.VMEM)
    if direct:
        shape = (n_aux // PLANE // 2, blk + TAIL, nocc)
        out_shape = [jax.ShapeDtypeStruct(shape, jnp.bfloat16)] * PLANE
    else:
        out_shape = [jax.ShapeDtypeStruct((n_aux, blk + TAIL, nocc), jnp.bfloat16)]
    out_shape = out_shape + [
        jax.ShapeDtypeStruct((AB_DEV, auxb * nocc, nocc), jnp.bfloat16),
        jax.ShapeDtypeStruct(tiles_array.shape, tiles_array.dtype),
    ]
    return pl.pallas_call(
        kernel,
        out_shape=out_shape,
        in_specs=[smem] * 4 + [pl.BlockSpec(memory_space=pl.ANY)] * 2 + [vmem] * n_in,
        out_specs=[vmem] * len(out_shape),
        scratch_shapes=[
            pltpu.VMEM((n_aux + 1, nocc, blk), jnp.bfloat16),
            pltpu.VMEM((AB_DEV, nocc, auxb * nocc), jnp.float32),
            pltpu.VMEM((n_aux + 1, blk, nocc), jnp.float32),
            pltpu.VMEM(own_array.shape, own_array.dtype),
            pltpu.SemaphoreType.DMA((chunks,)),
            pltpu.SemaphoreType.DMA,
        ],
        compiler_params=pltpu.CompilerParams(vmem_limit_bytes=FIRST_VMEM * 1024 * 1024),
        cost_estimate=pl.CostEstimate(
            flops=3 * tiles_array.size * nocc, bytes_accessed=tiles_array.size, transcendentals=0
        ),
        name="first_part",
    )(*meta_arrays, tiles_array, own_array, *shards)


def second_part(n_aux, meta_arrays, tiles_array, fitted):
    slots, auxb, blk, nocc = tiles_array.shape
    chunks = slots // CHUNK + 2 * AB_DEV

    def kernel(slot_ref, block_ref, gid_ref, bit_ref, tiles, zb, *refs):
        out_refs, acc = refs[:-1], refs[-1]
        acc[...] = jnp.zeros(acc.shape, acc.dtype)
        apply_fitted(
            (slot_ref, block_ref, gid_ref, bit_ref),
            tiles,
            zb,
            acc,
            gid_ref[chunks + AB_DEV - 1],
            gid_ref[chunks + 2 * AB_DEV - 1],
        )
        for m in range(n_aux // 2):
            put(bit_ref, acc, m, out_refs[m % PLANE], m // PLANE)

    smem = pl.BlockSpec(memory_space=pltpu.SMEM)
    vmem = pl.BlockSpec(memory_space=pltpu.VMEM)
    shape = (n_aux // PLANE // 2, blk + TAIL, nocc)
    return pl.pallas_call(
        kernel,
        out_shape=[jax.ShapeDtypeStruct(shape, jnp.bfloat16)] * PLANE,
        in_specs=[smem] * 4 + [vmem, vmem],
        out_specs=[vmem] * PLANE,
        scratch_shapes=[pltpu.VMEM((n_aux + 1, blk, nocc), jnp.float32)],
        compiler_params=pltpu.CompilerParams(vmem_limit_bytes=20 * 1024 * 1024),
        cost_estimate=pl.CostEstimate(
            flops=10**10, bytes_accessed=tiles_array.size, transcendentals=0
        ),
        name="second_part",
    )(*meta_arrays, tiles_array, fitted)


def merge(arrays):
    def kernel(*refs):
        for i, ref in enumerate(refs[:-1]):
            refs[-1][i] = ref[...]

    vmem = pl.BlockSpec(memory_space=pltpu.VMEM)
    return pl.pallas_call(
        kernel,
        out_shape=jax.ShapeDtypeStruct((len(arrays),) + arrays[0].shape, arrays[0].dtype),
        in_specs=[vmem] * len(arrays),
        out_specs=vmem,
        compiler_params=pltpu.CompilerParams(vmem_limit_bytes=4 * 1024 * 1024),
        name="merge",
    )(*arrays)


def spread(parts, after, dtypes, blk, bb_dev):
    count, rows, nocc = parts[0].shape

    def kernel(*refs):
        sources, targets = refs[: len(parts)], refs[len(parts) + len(after) :]
        for i in range(count):
            sums = [jnp.zeros((blk, nocc), jnp.float32) for _ in range(bb_dev)]
            for source in sources:
                value = source[i, :blk, :].astype(jnp.float32)
                which = source[i, blk:, :][:1].astype(jnp.float32)
                for b in range(bb_dev):
                    sums[b] = sums[b] + jnp.where(which == b, value, 0.0)
            for b in range(bb_dev):
                targets[i][b * blk : (b + 1) * blk, :] = sums[b].astype(targets[i].dtype)

    vmem = pl.BlockSpec(memory_space=pltpu.VMEM)
    return pl.pallas_call(
        kernel,
        out_shape=[jax.ShapeDtypeStruct((bb_dev * blk, nocc), dtype) for dtype in dtypes],
        in_specs=[vmem] * len(parts) + [pl.BlockSpec(memory_space=pl.ANY)] * len(after),
        out_specs=[vmem] * count,
        compiler_params=pltpu.CompilerParams(vmem_limit_bytes=4 * 1024 * 1024),
        cost_estimate=pl.CostEstimate(
            flops=SPREAD_COST, bytes_accessed=SPREAD_COST // 1000, transcendentals=0
        ),
        name="spread",
    )(*parts, *after)


def total_of(arrays, dtype, cost):
    def kernel(*refs):
        value = refs[0][...].astype(jnp.float32)
        for ref in refs[1:-1]:
            value = value + ref[...].astype(jnp.float32)
        refs[-1][...] = value.astype(refs[-1].dtype)

    vmem = pl.BlockSpec(memory_space=pltpu.VMEM)
    return pl.pallas_call(
        kernel,
        out_shape=jax.ShapeDtypeStruct(arrays[0].shape, dtype),
        in_specs=[vmem] * len(arrays),
        out_specs=vmem,
        compiler_params=pltpu.CompilerParams(vmem_limit_bytes=4 * 1024 * 1024),
        cost_estimate=pl.CostEstimate(flops=cost, bytes_accessed=cost // 1000, transcendentals=0),
        name="total_of",
    )(*arrays)


def owner_sum(parts, blk, bb_dev):
    n_aux, rows, nocc = parts.shape

    def kernel(parts_ref, out_ref):
        sums = [jnp.zeros((blk, nocc), jnp.float32) for _ in range(bb_dev)]
        for s in range(n_aux):
            value = parts_ref[s, :blk, :].astype(jnp.float32)
            which = parts_ref[s, blk:, :][:1].astype(jnp.float32)
            for b in range(bb_dev):
                sums[b] = sums[b] + jnp.where(which == b, value, 0.0)
        for b in range(bb_dev):
            out_ref[b * blk : (b + 1) * blk, :] = sums[b].astype(out_ref.dtype)

    vmem = pl.BlockSpec(memory_space=pltpu.VMEM)
    return pl.pallas_call(
        kernel,
        out_shape=jax.ShapeDtypeStruct((bb_dev * blk, nocc), jnp.bfloat16),
        in_specs=[vmem],
        out_specs=vmem,
        name="owner_sum",
    )(parts)


def on_device(tiles, c_orbitals, basis_order, tile_block, tile_aux, live):
    blk, nocc = tiles.shape[2:]
    n_aux = lax.axis_size("aux")
    bb_dev = basis_order.shape[0] // n_aux
    direct = n_aux == DIRECT

    def swap(array, m):
        return lax.ppermute(array, "aux", [(i, i ^ m) for i in range(n_aux)])

    base = lax.axis_index("aux").astype(jnp.int32) if direct else jnp.int32(0)
    split = n_aux // 2 if direct else 0
    meta = plan(tile_block, tile_aux, live, basis_order, base, split, n_aux, bb_dev)
    if not direct:
        whole = lax.all_gather(c_orbitals, "aux", axis=0, tiled=True)
        shards = [whole.reshape(n_aux, bb_dev * blk, nocc)]
        parts, _, _ = first_part(direct, n_aux, meta, tiles, c_orbitals, shards, None)
        moved = lax.all_to_all(parts, "aux", 0, 0, tiled=True)
        return owner_sum(moved, blk, bb_dev)

    depth = n_aux // PLANE
    half = depth // 2
    column = [c_orbitals] + [None] * (depth - 1)
    for dz in range(depth - 1, 0, -1):
        column[dz] = swap(c_orbitals, dz * PLANE)
    beside = swap(c_orbitals, 2)
    across = swap(c_orbitals, 1)
    early = merge(column[1:] + [beside])
    late = [swap(array, 2) for array in column[1:]]
    shards = [early, swap(early, 1), across] + late + [swap(array, 1) for array in late]
    sources = [None] * n_aux
    for dz in range(1, depth):
        for core in range(2):
            sources[dz * PLANE + core] = (core, dz - 1)
            sources[dz * PLANE + 2 + core] = (2 + dz + core * (depth - 1), None)
    sources[1:PLANE] = [(2, None), (0, depth - 1), (1, depth - 1)]
    *far, fitted, held = first_part(direct, n_aux, meta, tiles, c_orbitals, shards, sources)
    far = [far[0]] + [swap(far[r], r) for r in range(1, PLANE)]
    near = second_part(n_aux, meta, held, fitted)
    near = [near[0]] + [swap(near[r], r) for r in range(1, PLANE)]
    far = spread(far, [], [jnp.bfloat16] * half, blk, bb_dev)
    near = spread(
        near, [far[0]], [jnp.float32] + [jnp.bfloat16] * (half - 1), blk, bb_dev
    )
    far = [swap(far[i], (half + i) * PLANE) for i in range(half)]
    far = total_of(far, jnp.float32, SPREAD_COST)
    near = [near[0]] + [swap(near[dz], dz * PLANE) for dz in range(1, half)]
    return total_of(near + [far], jnp.bfloat16, 0)


def solution(mesh):
    return jax.shard_map(
        on_device,
        mesh=mesh,
        in_specs=(
            P(("grp", "aux"), None, None, None),
            P(("grp", "aux"), None),
            P("grp"),
            P(("grp", "aux")),
            P(("grp", "aux")),
            P(("grp", "aux")),
        ),
        out_specs=P(("grp", "aux"), None),
        check_vma=False,
    )
```

time: 58.2 us -> 50.1 us (0.86)
  local copies, waits for them, and re-layouts: 7.99 us -> 0.84 us
  starting transfers between devices: 21.7 us -> 19.6 us
  waiting for transfers between devices: 13.7 us -> 14.5 us
    unnamed x26 -> x2, local copies, waits for them, and re-layouts: 7.99 us -> 0.84 us
    pallas_call x2, Pallas kernels: 3.45 us -> 0.22 us  [spread(): pl.pallas_call(kernel, out_shape=[jax.ShapeDtypeStruct((bb_dev * blk, noc...]
    pallas_call x2 -> x5, Pallas kernels: 8.09 us -> 11.2 us  [the longest x1 7.91 us: first_part(): pl.pallas_call(kernel, out_shape=out_shape, in_specs=[smem] * 4 + [pl.Blo...]
    ppermute x24 -> x21, starting transfers between devices: 21.7 us -> 19.6 us  [swap(): return lax.ppermute(array, 'aux', [(i, i ^ m) for i in range(n_aux)])]
    ppermute x24 -> x21, waiting for transfers between devices: 13.7 us -> 14.5 us  [swap(): return lax.ppermute(array, 'aux', [(i, i ^ m) for i in range(n_aux)])]
  transfers between devices with their start and end apart: 24 -> 21, of which waited for: 9 -> 10; matrix products, arithmetic and copies ran while one was open for 4% -> 5% of each run, Pallas kernels for 6% -> 6%
where the time goes in v5:
time: 50.1 us; the launch traced here: 49.7 us
  starting transfers between devices  19.6 us (39%)
  waiting for transfers between devices  14.5 us (29%)
  Pallas kernels  11.5 us (23%)
  other arithmetic  2.44 us (5%)
  local copies, waits for them, and re-layouts  0.84 us (2%)
  between operations  0.8 us (2%)
    ppermute x21, starting transfers between devices, swap(): return lax.ppermute(array, 'aux', [(i, i ^ m) for i in range(n_aux)])  19.6 us
    ppermute x21, waiting for transfers between devices, swap(): return lax.ppermute(array, 'aux', [(i, i ^ m) for i in range(n_aux)])  14.5 us
    pallas_call x1, Pallas kernels, first_part(): pl.pallas_call(kernel, out_shape=out_shape, in_specs=[smem] * 4 + [pl.Blo...  7.91 us
    pallas_call x1, Pallas kernels, second_part(): pl.pallas_call(kernel, out_shape=[jax.ShapeDtypeStruct(shape, jnp.bfloat1...  2.64 us
  transfers between devices with their start and end apart: 21, of which 10 were waited for; matrix products, arithmetic and copies ran while one was open for 5% of the time, Pallas kernels for 6%

profile of v5, /device:TPU:0, one launch (start us, length us, event | category | flops | bytes accessed | tf_op | source)
XLA Modules:
  0.0 49.7 jit_solution(5713515602805141291)
XLA Ops:
  0.0 3.0 %collective-permute-start.3 = (bf16[256,128]{1,0:T(8,128)(2,1)}, bf16[256,128]{1,0:T(8,128)(2,1)S(1)}, u32[]{:S(2)}, u32[]{:S(2)}) collective-permute-start(bf16[256,128]{1,0:T(8,128)(2,1)} %own_hbm.1), channel_id=1, source_target_pairs={{0,2},{1,3},{2,0},{3,1},{4,6},{5,7},{6,4},{7,5},{8,10},{9,11},{10,... | collective-permute-start | bytes 196616 | tf_op jit(solution)/shard_map/ppermute | solution.py:331
  3.0 3.6 %collective-permute-start.2 = (bf16[256,128]{1,0:T(8,128)(2,1)}, bf16[256,128]{1,0:T(8,128)(2,1)S(1)}, u32[]{:S(2)}, u32[]{:S(2)}) collective-permute-start(bf16[256,128]{1,0:T(8,128)(2,1)} %own_hbm.1), channel_id=1, source_target_pairs={{0,12},{1,13},{2,14},{3,15},{4,8},{5,9},{6,10},{7,11},{8,4},{9,5},... | collective-permute-start | bytes 196616 | tf_op jit(solution)/shard_map/ppermute | solution.py:331
  6.6 0.8 %collective-permute-start = (bf16[256,128]{1,0:T(8,128)(2,1)}, bf16[256,128]{1,0:T(8,128)(2,1)S(1)}, u32[]{:S(2)}, u32[]{:S(2)}) collective-permute-start(bf16[256,128]{1,0:T(8,128)(2,1)} %own_hbm.1), channel_id=1, source_target_pairs={{0,4},{1,5},{2,6},{3,7},{4,0},{5,1},{6,2},{7,3},{8,12},{9,13},{10,... | collective-permute-start | bytes 196616 | tf_op jit(solution)/shard_map/ppermute | solution.py:331
  8.0 0.8 %select_reduce_fusion.3 = s32[64]{0:T(128)S(1)} fusion(s32[64]{0:T(128)} %param.9, s32[32]{0:T(128)} %param.8), kind=kLoop, calls=%fused_computation.8 | loop fusion | flops 6080 | bytes 640 | tf_op jit(solution)/shard_map/reduce_sum | solution.py:28
  8.8 0.7 %fusion.5 = (s32[64]{0:T(128)S(1)}, s32[64]{0:T(128)S(1)}, s32[64]{0:T(128)S(1)}) fusion(s32[64]{0:T(128)} %param.10, s32[]{:T(128)} %bitcast.3, s32[]{:T(128)S(6)} %axis_index.12, s32[64]{0:T(128)S(1)} %select_reduce_fusion.3), kind=kLoop, calls=%fused_computation.39 | loop fusion | flops 1600 | bytes 1288 | tf_op jit(solution)/shard_map/jit(_where)/select_n | solution.py:36
  10.3 1.9 %collective-permute-done.1.refs_1_ = bf16[256,128]{1,0:T(8,128)(2,1)S(1)} collective-permute-done((bf16[256,128]{1,0:T(8,128)(2,1)}, bf16[256,128]{1,0:T(8,128)(2,1)S(1)}, u32[]{:S(2)}, u32[]{:S(2)}) %collective-permute-start.1) | collective-permute-done | bytes 65568 | tf_op jit(solution)/shard_map/ppermute | solution.py:331
  12.9 1.5 %collective-permute-start.7 = (bf16[256,128]{1,0:T(8,128)(2,1)S(1)}, bf16[256,128]{1,0:T(8,128)(2,1)S(1)}, u32[]{:S(2)}, u32[]{:S(2)}) collective-permute-start(bf16[256,128]{1,0:T(8,128)(2,1)S(1)} %collective-permute-done.1.refs_1_), channel_id=1, source_target_pairs={{0,2},{1,3},{2,0},{3,1},{4,6},{5,7},{6,4},{7,5},{8,10},{9,11},{10,... | collective-permute-start | bytes 196616 | tf_op jit(solution)/shard_map/ppermute | solution.py:331
  15.1 2.2 %collective-permute-done.8.refs_5_ = bf16[256,128]{1,0:T(8,128)(2,1)S(1)} collective-permute-done((bf16[256,128]{1,0:T(8,128)(2,1)S(1)}, bf16[256,128]{1,0:T(8,128)(2,1)S(1)}, u32[]{:S(2)}, u32[]{:S(2)}) %collective-permute-start.8) | collective-permute-done | bytes 65568 | tf_op jit(solution)/shard_map/ppermute | solution.py:331
  17.3 1.4 %collective-permute-done.7.refs_4_ = bf16[256,128]{1,0:T(8,128)(2,1)S(1)} collective-permute-done((bf16[256,128]{1,0:T(8,128)(2,1)S(1)}, bf16[256,128]{1,0:T(8,128)(2,1)S(1)}, u32[]{:S(2)}, u32[]{:S(2)}) %collective-permute-start.7) | collective-permute-done | bytes 65568 | tf_op jit(solution)/shard_map/ppermute | solution.py:331
  18.7 0.9 %collective-permute-done.6.refs_3_ = bf16[256,128]{1,0:T(8,128)(2,1)S(1)} collective-permute-done((bf16[256,128]{1,0:T(8,128)(2,1)S(1)}, bf16[256,128]{1,0:T(8,128)(2,1)S(1)}, u32[]{:S(2)}, u32[]{:S(2)}) %collective-permute-start.6) | collective-permute-done | bytes 65568 | tf_op jit(solution)/shard_map/ppermute | solution.py:331
  20.0 0.9 %collective-permute-done.9.refs_6_ = bf16[256,128]{1,0:T(8,128)(2,1)S(1)} collective-permute-done((bf16[256,128]{1,0:T(8,128)(2,1)S(1)}, bf16[256,128]{1,0:T(8,128)(2,1)S(1)}, u32[]{:S(2)}, u32[]{:S(2)}) %collective-permute-start.9) | collective-permute-done | bytes 65568 | tf_op jit(solution)/shard_map/ppermute | solution.py:331
  20.9 0.8 %copy-done = bf16[256,128]{1,0:T(8,128)(2,1)S(1)} copy-done((bf16[256,128]{1,0:T(8,128)(2,1)S(1)}, bf16[256,128]{1,0:T(8,128)(2,1)}, u32[]{:S(2)}) %copy-start) | copy-done | bytes 65560
  21.8 7.9 %first_part.1 = (bf16[2,144,128]{2,1,0:T(8,128)(2,1)S(1)}, bf16[2,144,128]{2,1,0:T(8,128)(2,1)S(1)}, bf16[2,144,128]{2,1,0:T(8,128)(2,1)S(1)}, bf16[2,144,128]{2...) custom-call(s32[128]{0:T(128)S(1)} %get-tuple-element.40.slot_ref, ...), custom_call_target="tpu_custom_call" | custom-call | flops 2013265920 | bytes 5242880 | tf_op jit(solution)/shard_map/first_part/pallas_call | solution.py:181
  29.7 1.9 %collective-permute-start.15 = (bf16[2,144,128]{2,1,0:T(8,128)(2,1)S(1)}, bf16[2,144,128]{2,1,0:T(8,128)(2,1)S(1)}, u32[]{:S(2)}, u32[]{:S(2)}) collective-permute-start(bf16[2,144,128]{2,1,0:T(8,128)(2,1)S(1)} %get-tuple-element.26), channel_id=1, source_target_pairs={{0,1},{1,0},{2,3},{3,2},{4,5},{5,4},{6,7},{7,6},{8,9},{9,8},{10,11... | collective-permute-start | bytes 221192 | tf_op jit(solution)/shard_map/ppermute | solution.py:331
  31.6 1.5 %collective-permute-start.16 = (bf16[2,144,128]{2,1,0:T(8,128)(2,1)S(1)}, bf16[2,144,128]{2,1,0:T(8,128)(2,1)S(1)}, u32[]{:S(2)}, u32[]{:S(2)}) collective-permute-start(bf16[2,144,128]{2,1,0:T(8,128)(2,1)S(1)} %get-tuple-element.27), channel_id=1, source_target_pairs={{0,2},{1,3},{2,0},{3,1},{4,6},{5,7},{6,4},{7,5},{8,10},{9,11},{10,... | collective-permute-start | bytes 221192 | tf_op jit(solution)/shard_map/ppermute | solution.py:331
  33.1 2.6 %second_part.1 = (bf16[2,144,128]{2,1,0:T(8,128)(2,1)S(1)}, bf16[2,144,128]{2,1,0:T(8,128)(2,1)S(1)}, bf16[2,144,128]{2,1,0:T(8,128)(2,1)S(1)}, bf16[2,144,128]{2,1,0:T(8,128)(2,1)S(1)}) custom-call(s32[128]{0:T(128)S(1)} %get-tuple-element.40.slot_ref, s32[128]{0:T(128)S(1)} %get-tuple-element.39.block_ref, s32[48]{0:T(128)S(1)} %pad_add_fusion.gid_ref, ...), custom_call_target="tpu_custom_call" | custom-call | flops 10000000000 | bytes 5242880 | tf_op jit(solution)/shard_map/second_part/pallas_call | solution.py:223
  35.7 1.2 %collective-permute-start.12 = (bf16[2,144,128]{2,1,0:T(8,128)(2,1)S(1)}, bf16[2,144,128]{2,1,0:T(8,128)(2,1)S(1)}, u32[]{:S(2)}, u32[]{:S(2)}) collective-permute-start(bf16[2,144,128]{2,1,0:T(8,128)(2,1)S(1)} %get-tuple-element.22), channel_id=1, source_target_pairs={{0,1},{1,0},{2,3},{3,2},{4,5},{5,4},{6,7},{7,6},{8,9},{9,8},{10,11... | collective-permute-start | bytes 221192 | tf_op jit(solution)/shard_map/ppermute | solution.py:331
  37.0 1.5 %collective-permute-start.13 = (bf16[2,144,128]{2,1,0:T(8,128)(2,1)S(1)}, bf16[2,144,128]{2,1,0:T(8,128)(2,1)S(1)}, u32[]{:S(2)}, u32[]{:S(2)}) collective-permute-start(bf16[2,144,128]{2,1,0:T(8,128)(2,1)S(1)} %get-tuple-element.23), channel_id=1, source_target_pairs={{0,2},{1,3},{2,0},{3,1},{4,6},{5,7},{6,4},{7,5},{8,10},{9,11},{10,... | collective-permute-start | bytes 221192 | tf_op jit(solution)/shard_map/ppermute | solution.py:331
  38.6 2.5 %collective-permute-start.20 = (bf16[256,128]{1,0:T(8,128)(2,1)S(1)}, bf16[256,128]{1,0:T(8,128)(2,1)S(1)}, u32[]{:S(2)}, u32[]{:S(2)}) collective-permute-start(bf16[256,128]{1,0:T(8,128)(2,1)S(1)} %get-tuple-element.32), channel_id=1, source_target_pairs={{0,12},{1,13},{2,14},{3,15},{4,8},{5,9},{6,10},{7,11},{8,4},{9,5},... | collective-permute-start | bytes 196616 | tf_op jit(solution)/shard_map/ppermute | solution.py:331
  41.1 0.8 %collective-permute-start.19 = (bf16[256,128]{1,0:T(8,128)(2,1)S(1)}, bf16[256,128]{1,0:T(8,128)(2,1)S(1)}, u32[]{:S(2)}, u32[]{:S(2)}) collective-permute-start(bf16[256,128]{1,0:T(8,128)(2,1)S(1)} %get-tuple-element.29.refs_4_), channel_id=1, source_target_pairs={{0,8},{1,9},{2,10},{3,11},{4,12},{5,13},{6,14},{7,15},{8,0},{9,1},... | collective-permute-start | bytes 196616 | tf_op jit(solution)/shard_map/ppermute | solution.py:331
  41.9 1.0 %collective-permute-done.14.refs_3_ = bf16[2,144,128]{2,1,0:T(8,128)(2,1)S(1)} collective-permute-done((bf16[2,144,128]{2,1,0:T(8,128)(2,1)S(1)}, bf16[2,144,128]{2,1,0:T(8,128)(2,1)S(1)}, u32[]{:S(2)}, u32[]{:S(2)}) %collective-permute-start.14) | collective-permute-done | bytes 73760 | tf_op jit(solution)/shard_map/ppermute | solution.py:331
  43.2 1.9 %collective-permute-done.20.refs_1_ = bf16[256,128]{1,0:T(8,128)(2,1)S(1)} collective-permute-done((bf16[256,128]{1,0:T(8,128)(2,1)S(1)}, bf16[256,128]{1,0:T(8,128)(2,1)S(1)}, u32[]{:S(2)}, u32[]{:S(2)}) %collective-permute-start.20) | collective-permute-done | bytes 65568 | tf_op jit(solution)/shard_map/ppermute | solution.py:331
  45.2 3.8 %collective-permute-done.19.refs_0_ = bf16[256,128]{1,0:T(8,128)(2,1)S(1)} collective-permute-done((bf16[256,128]{1,0:T(8,128)(2,1)S(1)}, bf16[256,128]{1,0:T(8,128)(2,1)S(1)}, u32[]{:S(2)}, u32[]{:S(2)}) %collective-permute-start.19) | collective-permute-done | bytes 65568 | tf_op jit(solution)/shard_map/ppermute | solution.py:331
  49.0 0.7 %total_of.3 = bf16[256,128]{1,0:T(8,128)(2,1)} custom-call(f32[256,128]{1,0:T(8,128)S(1)} %get-tuple-element.30.refs_0_, bf16[256,128]{1,0:T(8,128)(2,1)S(1)} %collective-permute-done.18.refs_1_, f32[256,128]{1,0:T(8,128)S(1)} %total_of.2.refs_2_), custom_call_target="tpu_custom_call" | custom-call | tf_op jit(solution)/shard_map/total_of/pallas_call | solution.py:290
  (44 shorter events, 2.9 us)
Async XLA Ops:
  0.0 10.3 %collective-permute-start.3 = (bf16[256,128]{1,0:T(8,128)(2,1)}, bf16[256,128]{1,0:T(8,128)(2,1)S(1)}, u32[]{:S(2)}, u32[]{:S(2)}) collective-permute-start(bf16[256,128]{1,0:T(8,128)(2,1)} %own_hbm.1), channel_id=1, source_target_pairs={{0,2},{1,3},{2,0},{3,1},{4,6},{5,7},{6,4},{7,5},{8,10},{9,11},{10,... | collective-permute-start | bytes 196616 | tf_op jit(solution)/shard_map/ppermute | solution.py:331
  3.0 7.3 %collective-permute-start.2 = (bf16[256,128]{1,0:T(8,128)(2,1)}, bf16[256,128]{1,0:T(8,128)(2,1)S(1)}, u32[]{:S(2)}, u32[]{:S(2)}) collective-permute-start(bf16[256,128]{1,0:T(8,128)(2,1)} %own_hbm.1), channel_id=1, source_target_pairs={{0,12},{1,13},{2,14},{3,15},{4,8},{5,9},{6,10},{7,11},{8,4},{9,5},... | collective-permute-start | bytes 196616 | tf_op jit(solution)/shard_map/ppermute | solution.py:331
  6.6 5.6 %collective-permute-start.1 = (bf16[256,128]{1,0:T(8,128)(2,1)}, bf16[256,128]{1,0:T(8,128)(2,1)S(1)}, u32[]{:S(2)}, u32[]{:S(2)}) collective-permute-start(bf16[256,128]{1,0:T(8,128)(2,1)} %own_hbm.1), channel_id=1, source_target_pairs={{0,8},{1,9},{2,10},{3,11},{4,12},{5,13},{6,14},{7,15},{8,0},{9,1},... | collective-permute-start | bytes 196616 | tf_op jit(solution)/shard_map/ppermute | solution.py:331
  6.6 5.7 %collective-permute-start = (bf16[256,128]{1,0:T(8,128)(2,1)}, bf16[256,128]{1,0:T(8,128)(2,1)S(1)}, u32[]{:S(2)}, u32[]{:S(2)}) collective-permute-start(bf16[256,128]{1,0:T(8,128)(2,1)} %own_hbm.1), channel_id=1, source_target_pairs={{0,4},{1,5},{2,6},{3,7},{4,0},{5,1},{6,2},{7,3},{8,12},{9,13},{10,... | collective-permute-start | bytes 196616 | tf_op jit(solution)/shard_map/ppermute | solution.py:331
  7.4 12.4 %collective-permute-start.5 = (bf16[256,128]{1,0:T(8,128)(2,1)}, bf16[256,128]{1,0:T(8,128)(2,1)S(1)}, u32[]{:S(2)}, u32[]{:S(2)}) collective-permute-start(bf16[256,128]{1,0:T(8,128)(2,1)} %own_hbm.1), channel_id=1, source_target_pairs={{0,1},{1,0},{2,3},{3,2},{4,5},{5,4},{6,7},{7,6},{8,9},{9,8},{10,11... | collective-permute-start | bytes 196616 | tf_op jit(solution)/shard_map/ppermute | solution.py:331
  12.3 8.7 %collective-permute-start.4 = (bf16[4,256,128]{2,1,0:T(8,128)(2,1)S(1)}, bf16[4,256,128]{2,1,0:T(8,128)(2,1)S(1)}, u32[]{:S(2)}, u32[]{:S(2)}) collective-permute-start(bf16[4,256,128]{2,1,0:T(8,128)(2,1)S(1)} %merge.1.refs_0_), channel_id=1, source_target_pairs={{0,1},{1,0},{2,3},{3,2},{4,5},{5,4},{6,7},{7,6},{8,9},{9,8},{10,11... | collective-permute-start | bytes 786440 | tf_op jit(solution)/shard_map/ppermute | solution.py:331
  12.4 5.0 %collective-permute-start.8 = (bf16[256,128]{1,0:T(8,128)(2,1)S(1)}, bf16[256,128]{1,0:T(8,128)(2,1)S(1)}, u32[]{:S(2)}, u32[]{:S(2)}) collective-permute-start(bf16[256,128]{1,0:T(8,128)(2,1)S(1)} %collective-permute-done.2.refs_2_), channel_id=1, source_target_pairs={{0,2},{1,3},{2,0},{3,1},{4,6},{5,7},{6,4},{7,5},{8,10},{9,11},{10,... | collective-permute-start | bytes 196616 | tf_op jit(solution)/shard_map/ppermute | solution.py:331
  12.9 5.8 %collective-permute-start.7 = (bf16[256,128]{1,0:T(8,128)(2,1)S(1)}, bf16[256,128]{1,0:T(8,128)(2,1)S(1)}, u32[]{:S(2)}, u32[]{:S(2)}) collective-permute-start(bf16[256,128]{1,0:T(8,128)(2,1)S(1)} %collective-permute-done.1.refs_1_), channel_id=1, source_target_pairs={{0,2},{1,3},{2,0},{3,1},{4,6},{5,7},{6,4},{7,5},{8,10},{9,11},{10,... | collective-permute-start | bytes 196616 | tf_op jit(solution)/shard_map/ppermute | solution.py:331
  14.5 5.2 %collective-permute-start.6 = (bf16[256,128]{1,0:T(8,128)(2,1)S(1)}, bf16[256,128]{1,0:T(8,128)(2,1)S(1)}, u32[]{:S(2)}, u32[]{:S(2)}) collective-permute-start(bf16[256,128]{1,0:T(8,128)(2,1)S(1)} %collective-permute-done.refs_0_), channel_id=1, source_target_pairs={{0,2},{1,3},{2,0},{3,1},{4,6},{5,7},{6,4},{7,5},{8,10},{9,11},{10,... | collective-permute-start | bytes 196616 | tf_op jit(solution)/shard_map/ppermute | solution.py:331
  17.3 2.4 %collective-permute-start.11 = (bf16[256,128]{1,0:T(8,128)(2,1)S(1)}, bf16[256,128]{1,0:T(8,128)(2,1)S(1)}, u32[]{:S(2)}, u32[]{:S(2)}) collective-permute-start(bf16[256,128]{1,0:T(8,128)(2,1)S(1)} %collective-permute-done.8.refs_5_), channel_id=1, source_target_pairs={{0,1},{1,0},{2,3},{3,2},{4,5},{5,4},{6,7},{7,6},{8,9},{9,8},{10,11... | collective-permute-start | bytes 196616 | tf_op jit(solution)/shard_map/ppermute | solution.py:331
  18.7 1.3 %collective-permute-start.10 = (bf16[256,128]{1,0:T(8,128)(2,1)S(1)}, bf16[256,128]{1,0:T(8,128)(2,1)S(1)}, u32[]{:S(2)}, u32[]{:S(2)}) collective-permute-start(bf16[256,128]{1,0:T(8,128)(2,1)S(1)} %collective-permute-done.7.refs_4_), channel_id=1, source_target_pairs={{0,1},{1,0},{2,3},{3,2},{4,5},{5,4},{6,7},{7,6},{8,9},{9,8},{10,11... | collective-permute-start | bytes 196616 | tf_op jit(solution)/shard_map/ppermute | solution.py:331
  19.7 1.3 %collective-permute-start.9 = (bf16[256,128]{1,0:T(8,128)(2,1)S(1)}, bf16[256,128]{1,0:T(8,128)(2,1)S(1)}, u32[]{:S(2)}, u32[]{:S(2)}) collective-permute-start(bf16[256,128]{1,0:T(8,128)(2,1)S(1)} %collective-permute-done.6.refs_3_), channel_id=1, source_target_pairs={{0,1},{1,0},{2,3},{3,2},{4,5},{5,4},{6,7},{7,6},{8,9},{9,8},{10,11... | collective-permute-start | bytes 196616 | tf_op jit(solution)/shard_map/ppermute | solution.py:331
  20.9 0.8 %copy-start = (bf16[256,128]{1,0:T(8,128)(2,1)S(1)}, bf16[256,128]{1,0:T(8,128)(2,1)}, u32[]{:S(2)}) copy-start(bf16[256,128]{1,0:T(8,128)(2,1)} %own_hbm.1) | copy-start | bytes 196612
  29.7 8.8 %collective-permute-start.15 = (bf16[2,144,128]{2,1,0:T(8,128)(2,1)S(1)}, bf16[2,144,128]{2,1,0:T(8,128)(2,1)S(1)}, u32[]{:S(2)}, u32[]{:S(2)}) collective-permute-start(bf16[2,144,128]{2,1,0:T(8,128)(2,1)S(1)} %get-tuple-element.26), channel_id=1, source_target_pairs={{0,1},{1,0},{2,3},{3,2},{4,5},{5,4},{6,7},{7,6},{8,9},{9,8},{10,11... | collective-permute-start | bytes 221192 | tf_op jit(solution)/shard_map/ppermute | solution.py:331
  31.6 6.8 %collective-permute-start.16 = (bf16[2,144,128]{2,1,0:T(8,128)(2,1)S(1)}, bf16[2,144,128]{2,1,0:T(8,128)(2,1)S(1)}, u32[]{:S(2)}, u32[]{:S(2)}) collective-permute-start(bf16[2,144,128]{2,1,0:T(8,128)(2,1)S(1)} %get-tuple-element.27), channel_id=1, source_target_pairs={{0,2},{1,3},{2,0},{3,1},{4,6},{5,7},{6,4},{7,5},{8,10},{9,11},{10,... | collective-permute-start | bytes 221192 | tf_op jit(solution)/shard_map/ppermute | solution.py:331
  33.1 5.4 %collective-permute-start.17 = (bf16[2,144,128]{2,1,0:T(8,128)(2,1)S(1)}, bf16[2,144,128]{2,1,0:T(8,128)(2,1)S(1)}, u32[]{:S(2)}, u32[]{:S(2)}) collective-permute-start(bf16[2,144,128]{2,1,0:T(8,128)(2,1)S(1)} %get-tuple-element.28), channel_id=1, source_target_pairs={{0,3},{1,2},{2,1},{3,0},{4,7},{5,6},{6,5},{7,4},{8,11},{9,10},{10,... | collective-permute-start | bytes 221192 | tf_op jit(solution)/shard_map/ppermute | solution.py:331
  35.7 6.2 %collective-permute-start.12 = (bf16[2,144,128]{2,1,0:T(8,128)(2,1)S(1)}, bf16[2,144,128]{2,1,0:T(8,128)(2,1)S(1)}, u32[]{:S(2)}, u32[]{:S(2)}) collective-permute-start(bf16[2,144,128]{2,1,0:T(8,128)(2,1)S(1)} %get-tuple-element.22), channel_id=1, source_target_pairs={{0,1},{1,0},{2,3},{3,2},{4,5},{5,4},{6,7},{7,6},{8,9},{9,8},{10,11... | collective-permute-start | bytes 221192 | tf_op jit(solution)/shard_map/ppermute | solution.py:331
  37.0 5.0 %collective-permute-start.13 = (bf16[2,144,128]{2,1,0:T(8,128)(2,1)S(1)}, bf16[2,144,128]{2,1,0:T(8,128)(2,1)S(1)}, u32[]{:S(2)}, u32[]{:S(2)}) collective-permute-start(bf16[2,144,128]{2,1,0:T(8,128)(2,1)S(1)} %get-tuple-element.23), channel_id=1, source_target_pairs={{0,2},{1,3},{2,0},{3,1},{4,6},{5,7},{6,4},{7,5},{8,10},{9,11},{10,... | collective-permute-start | bytes 221192 | tf_op jit(solution)/shard_map/ppermute | solution.py:331
  38.5 4.5 %collective-permute-start.14 = (bf16[2,144,128]{2,1,0:T(8,128)(2,1)S(1)}, bf16[2,144,128]{2,1,0:T(8,128)(2,1)S(1)}, u32[]{:S(2)}, u32[]{:S(2)}) collective-permute-start(bf16[2,144,128]{2,1,0:T(8,128)(2,1)S(1)} %get-tuple-element.24), channel_id=1, source_target_pairs={{0,3},{1,2},{2,1},{3,0},{4,7},{5,6},{6,5},{7,4},{8,11},{9,10},{10,... | collective-permute-start | bytes 221192 | tf_op jit(solution)/shard_map/ppermute | solution.py:331
  38.6 6.6 %collective-permute-start.20 = (bf16[256,128]{1,0:T(8,128)(2,1)S(1)}, bf16[256,128]{1,0:T(8,128)(2,1)S(1)}, u32[]{:S(2)}, u32[]{:S(2)}) collective-permute-start(bf16[256,128]{1,0:T(8,128)(2,1)S(1)} %get-tuple-element.32), channel_id=1, source_target_pairs={{0,12},{1,13},{2,14},{3,15},{4,8},{5,9},{6,10},{7,11},{8,4},{9,5},... | collective-permute-start | bytes 196616 | tf_op jit(solution)/shard_map/ppermute | solution.py:331
  41.1 7.8 %collective-permute-start.19 = (bf16[256,128]{1,0:T(8,128)(2,1)S(1)}, bf16[256,128]{1,0:T(8,128)(2,1)S(1)}, u32[]{:S(2)}, u32[]{:S(2)}) collective-permute-start(bf16[256,128]{1,0:T(8,128)(2,1)S(1)} %get-tuple-element.29.refs_4_), channel_id=1, source_target_pairs={{0,8},{1,9},{2,10},{3,11},{4,12},{5,13},{6,14},{7,15},{8,0},{9,1},... | collective-permute-start | bytes 196616 | tf_op jit(solution)/shard_map/ppermute | solution.py:331
  43.1 5.9 %collective-permute-start.18 = (bf16[256,128]{1,0:T(8,128)(2,1)S(1)}, bf16[256,128]{1,0:T(8,128)(2,1)S(1)}, u32[]{:S(2)}, u32[]{:S(2)}) collective-permute-start(bf16[256,128]{1,0:T(8,128)(2,1)S(1)} %get-tuple-element.31), channel_id=1, source_target_pairs={{0,4},{1,5},{2,6},{3,7},{4,0},{5,1},{6,2},{7,3},{8,12},{9,13},{10,... | collective-permute-start | bytes 196616 | tf_op jit(solution)/shard_map/ppermute | solution.py:331

commit v6 on v5

v6 whole, which is shorter than its diff:
```python
import functools

import jax
import jax.numpy as jnp
from jax import lax
from jax.experimental import pallas as pl
from jax.experimental.pallas import tpu as pltpu
from jax.sharding import PartitionSpec as P

AB_DEV = 8
CHUNK = 4
UNROLL = 2
LOADS = 8
BEGIN_VMEM = 40
TAIL = 16
PLANE = 4
SPREAD_COST = 10**10
DIRECT = 16


def owners_of(tile_block, basis_order, base, bb_dev):
    nbb = basis_order.shape[0]
    position = jnp.sum(
        jnp.where(
            basis_order[None, :] == tile_block[:, None], lax.iota(jnp.int32, nbb)[None, :], 0
        ),
        axis=1,
    )
    return jnp.bitwise_xor(position // bb_dev, base), position % bb_dev


def chunk_lists(where_to, later, alive, tile_aux, n_aux):
    slots = where_to.shape[0]
    keys = 2 * AB_DEV
    chunks = slots // CHUNK + keys
    t = lax.iota(jnp.int32, slots)
    group = jnp.where(alive, tile_aux + jnp.where(later, AB_DEV, 0), keys)
    ids = lax.iota(jnp.int32, keys)
    counts = jnp.sum((group[None, :] == ids[:, None]).astype(jnp.int32), axis=1)
    need = (counts + CHUNK - 1) // CHUNK
    ends = jnp.sum(jnp.where(ids[None, :] <= ids[:, None], need[None, :], 0), axis=1)
    rank = jnp.sum(
        ((group[None, :] == group[:, None]) & (t[None, :] < t[:, None])).astype(jnp.int32), axis=1
    )
    start = jnp.sum(jnp.where(group[:, None] > ids[None, :], need[None, :], 0), axis=1)
    place = jnp.where(alive, start * CHUNK + rank, -1)
    q = lax.iota(jnp.int32, chunks * CHUNK)
    hit = place[None, :] == q[:, None]
    lead = place[None, :] == (q // CHUNK * CHUNK)[:, None]
    valid = jnp.any(hit, axis=1)
    slot = jnp.sum(jnp.where(hit, t[None, :], 0), axis=1)
    slot = jnp.where(valid, slot, jnp.sum(jnp.where(lead, t[None, :], 0), axis=1))
    block = jnp.where(valid, jnp.sum(jnp.where(hit, where_to[None, :], 0), axis=1), n_aux)
    gid = jnp.sum(
        (lax.iota(jnp.int32, chunks)[:, None] >= ends[None, :]).astype(jnp.int32), axis=1
    )
    return slot, block, jnp.concatenate([gid % AB_DEV, ends])


def bits_of(where_to, which, alive, n_aux):
    return jnp.max(
        jnp.where(
            (where_to[None, :] == lax.iota(jnp.int32, n_aux)[:, None]) & alive[None, :],
            which[None, :],
            0,
        ),
        axis=1,
    )


def slab(tiles, slot):
    return jnp.concatenate([tiles[slot, p] for p in range(tiles.shape[1])], axis=1)


def chunk_ends(gid_ref, slots):
    chunks = slots // CHUNK + 2 * AB_DEV
    return gid_ref[chunks + AB_DEV - 1], gid_ref[chunks + 2 * AB_DEV - 1]


def turn(ct, bit_ref, m, source):
    blk = ct.shape[2]
    row = pl.multiple_of(bit_ref[m] * blk, blk)
    ct[m] = source[pl.ds(row, blk), :].T


def fit(lists, tiles, ct, zacc, low, high):
    slot_ref, block_ref, gid_ref = lists

    @pl.loop(0, (high - low + UNROLL - 1) // UNROLL)
    def _(step):
        for chunk in [low + step * UNROLL + u for u in range(UNROLL)]:
            keep = jnp.where(chunk < high, 0, ct.shape[0] - 1)
            spots = [chunk * CHUNK + i for i in range(CHUNK)]
            left = jnp.concatenate(
                [ct[jnp.maximum(block_ref[pos], keep)] for pos in spots], axis=1
            )
            right = jnp.concatenate([slab(tiles, slot_ref[pos]) for pos in spots], axis=0)
            zacc[gid_ref[chunk]] += jnp.dot(left, right, preferred_element_type=jnp.float32)


def apply_fitted(lists, tiles, zb, acc, low, high):
    slot_ref, block_ref, gid_ref = lists
    blk = acc.shape[1]

    @pl.loop(0, (high - low + UNROLL - 1) // UNROLL)
    def _(step):
        for chunk in [low + step * UNROLL + u for u in range(UNROLL)]:
            spots = [chunk * CHUNK + i for i in range(CHUNK)]
            left = jnp.concatenate([slab(tiles, slot_ref[pos]) for pos in spots], axis=0)
            value = jnp.dot(left, zb[gid_ref[chunk]], preferred_element_type=jnp.float32)
            for i, pos in enumerate(spots):
                acc[block_ref[pos]] += value[i * blk : (i + 1) * blk]


def begin(n_aux, lists, bit, tiles_array, own_array, shards, sources):
    slots, auxb, blk, nocc = tiles_array.shape
    n_in = len(shards)
    step = slots // LOADS

    def kernel(slot_ref, block_ref, gid_ref, bit_ref, tiles_hbm, own_hbm, *refs):
        c_refs, (tiles, zacc, ct, own, sems, own_sem) = refs[:n_in], refs[n_in:]
        own_copy = pltpu.make_async_copy(own_hbm, own, own_sem)
        own_copy.start()
        copies = [
            pltpu.make_async_copy(
                tiles_hbm.at[pl.ds(i * step, step)], tiles.at[pl.ds(i * step, step)], sems.at[i]
            )
            for i in range(LOADS)
        ]
        for copy in copies:
            copy.start()
        zacc[...] = jnp.zeros(zacc.shape, zacc.dtype)
        ct[n_aux] = jnp.zeros((nocc, blk), ct.dtype)
        for m, (ref, i) in sources:
            turn(ct, bit_ref, m, c_refs[ref] if i is None else c_refs[ref].at[i])
        own_copy.wait()
        turn(ct, bit_ref, 0, own)
        for copy in copies:
            copy.wait()
        early, _ = chunk_ends(gid_ref, slots)
        fit((slot_ref, block_ref, gid_ref), tiles, ct, zacc, 0, early)

    smem = pl.BlockSpec(memory_space=pltpu.SMEM)
    vmem = pl.BlockSpec(memory_space=pltpu.VMEM)
    hbm = pl.BlockSpec(memory_space=pl.ANY)
    return pl.pallas_call(
        kernel,
        out_shape=[
            jax.ShapeDtypeStruct(tiles_array.shape, tiles_array.dtype),
            jax.ShapeDtypeStruct((AB_DEV, nocc, auxb * nocc), jnp.float32),
        ],
        in_specs=[smem] * 4 + [hbm] * 2 + [vmem] * n_in,
        out_specs=[vmem] * 2,
        scratch_shapes=[
            pltpu.VMEM((n_aux + 1, nocc, blk), jnp.bfloat16),
            pltpu.VMEM(own_array.shape, own_array.dtype),
            pltpu.SemaphoreType.DMA((LOADS,)),
            pltpu.SemaphoreType.DMA,
        ],
        compiler_params=pltpu.CompilerParams(vmem_limit_bytes=BEGIN_VMEM * 1024 * 1024),
        cost_estimate=pl.CostEstimate(
            flops=2 * tiles_array.size * nocc, bytes_accessed=tiles_array.size, transcendentals=0
        ),
        name="begin",
    )(*lists, bit, tiles_array, own_array, *shards)


def put(bit_ref, acc, m, out_ref, place):
    blk, nocc = acc.shape[1:]
    out_ref[place, :blk, :] = acc[m].astype(out_ref.dtype)
    out_ref[place, blk:, :] = jnp.full((TAIL, nocc), bit_ref[m], jnp.int32).astype(
        jnp.float32
    ).astype(out_ref.dtype)


def clear_and_fit(n_aux, ct, acc):
    ct[n_aux] = jnp.zeros(ct.shape[1:], ct.dtype)
    acc[...] = jnp.zeros(acc.shape, acc.dtype)


def round_fitted(zacc, zb):
    groups, nocc, wide = zacc.shape
    for g in range(groups):
        for p in range(wide // nocc):
            part = zacc[g, :, p * nocc : (p + 1) * nocc].astype(zb.dtype)
            zb[g, p * nocc : (p + 1) * nocc, :] = part.T


def first_part(n_aux, fit_lists, lists, bit, tiles_array, partial_fit, shards, sources):
    slots, auxb, blk, nocc = tiles_array.shape
    n_in = len(shards)

    def kernel(*refs):
        fit_refs, refs = refs[:3], refs[3:]
        list_refs, bit_ref, tiles, partial_ref = refs[:3], refs[3], refs[4], refs[5]
        c_refs, out_refs = refs[6 : 6 + n_in], refs[6 + n_in : -4]
        zb, ct, zacc, acc = refs[-4:]
        clear_and_fit(n_aux, ct, acc)
        zacc[...] = partial_ref[...]
        for m, (ref, i) in sources:
            turn(ct, bit_ref, m, c_refs[ref] if i is None else c_refs[ref].at[i])
        fit(fit_refs, tiles, ct, zacc, *chunk_ends(fit_refs[2], slots))
        round_fitted(zacc, zb)
        far, _ = chunk_ends(list_refs[2], slots)
        apply_fitted(list_refs, tiles, zb, acc, 0, far)
        for m in range(n_aux // 2, n_aux):
            put(bit_ref, acc, m, out_refs[m % PLANE], (m - n_aux // 2) // PLANE)

    smem = pl.BlockSpec(memory_space=pltpu.SMEM)
    vmem = pl.BlockSpec(memory_space=pltpu.VMEM)
    shape = (n_aux // PLANE // 2, blk + TAIL, nocc)
    out_shape = [jax.ShapeDtypeStruct(shape, jnp.bfloat16)] * PLANE
    out_shape = out_shape + [jax.ShapeDtypeStruct((AB_DEV, auxb * nocc, nocc), jnp.bfloat16)]
    return pl.pallas_call(
        kernel,
        out_shape=out_shape,
        in_specs=[smem] * 7 + [vmem] * (2 + n_in),
        out_specs=[vmem] * len(out_shape),
        scratch_shapes=[
            pltpu.VMEM((n_aux + 1, nocc, blk), jnp.bfloat16),
            pltpu.VMEM((AB_DEV, nocc, auxb * nocc), jnp.float32),
            pltpu.VMEM((n_aux + 1, blk, nocc), jnp.float32),
        ],
        compiler_params=pltpu.CompilerParams(vmem_limit_bytes=20 * 1024 * 1024),
        cost_estimate=pl.CostEstimate(
            flops=3 * tiles_array.size * nocc, bytes_accessed=tiles_array.size, transcendentals=0
        ),
        name="first_part",
    )(*fit_lists, *lists, bit, tiles_array, partial_fit, *shards)


def second_part(n_aux, lists, bit, tiles_array, fitted):
    slots, auxb, blk, nocc = tiles_array.shape

    def kernel(slot_ref, block_ref, gid_ref, bit_ref, tiles, zb, *refs):
        out_refs, acc = refs[:-1], refs[-1]
        acc[...] = jnp.zeros(acc.shape, acc.dtype)
        apply_fitted(
            (slot_ref, block_ref, gid_ref), tiles, zb, acc, *chunk_ends(gid_ref, slots)
        )
        for m in range(n_aux // 2):
            put(bit_ref, acc, m, out_refs[m % PLANE], m // PLANE)

    smem = pl.BlockSpec(memory_space=pltpu.SMEM)
    vmem = pl.BlockSpec(memory_space=pltpu.VMEM)
    shape = (n_aux // PLANE // 2, blk + TAIL, nocc)
    return pl.pallas_call(
        kernel,
        out_shape=[jax.ShapeDtypeStruct(shape, jnp.bfloat16)] * PLANE,
        in_specs=[smem] * 4 + [vmem, vmem],
        out_specs=[vmem] * PLANE,
        scratch_shapes=[pltpu.VMEM((n_aux + 1, blk, nocc), jnp.float32)],
        compiler_params=pltpu.CompilerParams(vmem_limit_bytes=20 * 1024 * 1024),
        cost_estimate=pl.CostEstimate(
            flops=10**10, bytes_accessed=tiles_array.size, transcendentals=0
        ),
        name="second_part",
    )(*lists, bit, tiles_array, fitted)


def all_in_one(n_aux, lists, bit, tiles_array, whole):
    slots, auxb, blk, nocc = tiles_array.shape

    def kernel(slot_ref, block_ref, gid_ref, bit_ref, tiles, c_ref, out_ref, ct, zacc, zb, acc):
        lists = (slot_ref, block_ref, gid_ref)
        clear_and_fit(n_aux, ct, acc)
        zacc[...] = jnp.zeros(zacc.shape, zacc.dtype)

        @pl.loop(0, n_aux)
        def _(m):
            turn(ct, bit_ref, m, c_ref.at[m])

        _, total = chunk_ends(gid_ref, slots)
        fit(lists, tiles, ct, zacc, 0, total)
        round_fitted(zacc, zb)
        apply_fitted(lists, tiles, zb, acc, 0, total)

        @pl.loop(0, n_aux)
        def _(m):
            put(bit_ref, acc, m, out_ref, m)

    smem = pl.BlockSpec(memory_space=pltpu.SMEM)
    vmem = pl.BlockSpec(memory_space=pltpu.VMEM)
    return pl.pallas_call(
        kernel,
        out_shape=jax.ShapeDtypeStruct((n_aux, blk + TAIL, nocc), jnp.bfloat16),
        in_specs=[smem] * 4 + [vmem] * 2,
        out_specs=vmem,
        scratch_shapes=[
            pltpu.VMEM((n_aux + 1, nocc, blk), jnp.bfloat16),
            pltpu.VMEM((AB_DEV, nocc, auxb * nocc), jnp.float32),
            pltpu.VMEM((AB_DEV, auxb * nocc, nocc), jnp.bfloat16),
            pltpu.VMEM((n_aux + 1, blk, nocc), jnp.float32),
        ],
        compiler_params=pltpu.CompilerParams(vmem_limit_bytes=46 * 1024 * 1024),
        name="all_in_one",
    )(*lists, bit, tiles_array, whole)


def merge(arrays, after):
    def kernel(*refs):
        for i, ref in enumerate(refs[: len(arrays)]):
            refs[-1][i] = ref[...]

    vmem = pl.BlockSpec(memory_space=pltpu.VMEM)
    return pl.pallas_call(
        kernel,
        out_shape=jax.ShapeDtypeStruct((len(arrays),) + arrays[0].shape, arrays[0].dtype),
        in_specs=[vmem] * len(arrays) + [pl.BlockSpec(memory_space=pl.ANY)] * len(after),
        out_specs=vmem,
        compiler_params=pltpu.CompilerParams(vmem_limit_bytes=4 * 1024 * 1024),
        name="merge",
    )(*arrays, *after)


def spread(parts, after, dtypes, blk, bb_dev):
    count, rows, nocc = parts[0].shape

    def kernel(*refs):
        sources, targets = refs[: len(parts)], refs[len(parts) + len(after) :]
        for i in range(count):
            sums = [jnp.zeros((blk, nocc), jnp.float32) for _ in range(bb_dev)]
            for source in sources:
                value = source[i, :blk, :].astype(jnp.float32)
                which = source[i, blk:, :][:1].astype(jnp.float32)
                for b in range(bb_dev):
                    sums[b] = sums[b] + jnp.where(which == b, value, 0.0)
            for b in range(bb_dev):
                targets[i][b * blk : (b + 1) * blk, :] = sums[b].astype(targets[i].dtype)

    vmem = pl.BlockSpec(memory_space=pltpu.VMEM)
    return pl.pallas_call(
        kernel,
        out_shape=[jax.ShapeDtypeStruct((bb_dev * blk, nocc), dtype) for dtype in dtypes],
        in_specs=[vmem] * len(parts) + [pl.BlockSpec(memory_space=pl.ANY)] * len(after),
        out_specs=[vmem] * count,
        compiler_params=pltpu.CompilerParams(vmem_limit_bytes=4 * 1024 * 1024),
        cost_estimate=pl.CostEstimate(
            flops=SPREAD_COST, bytes_accessed=SPREAD_COST // 1000, transcendentals=0
        ),
        name="spread",
    )(*parts, *after)


def total_of(arrays, dtype, cost):
    def kernel(*refs):
        value = refs[0][...].astype(jnp.float32)
        for ref in refs[1:-1]:
            value = value + ref[...].astype(jnp.float32)
        refs[-1][...] = value.astype(refs[-1].dtype)

    vmem = pl.BlockSpec(memory_space=pltpu.VMEM)
    return pl.pallas_call(
        kernel,
        out_shape=jax.ShapeDtypeStruct(arrays[0].shape, dtype),
        in_specs=[vmem] * len(arrays),
        out_specs=vmem,
        compiler_params=pltpu.CompilerParams(vmem_limit_bytes=4 * 1024 * 1024),
        cost_estimate=pl.CostEstimate(flops=cost, bytes_accessed=cost // 1000, transcendentals=0),
        name="total_of",
    )(*arrays)


def owner_sum(parts, blk, bb_dev):
    n_aux, rows, nocc = parts.shape

    def kernel(parts_ref, out_ref):
        sums = [jnp.zeros((blk, nocc), jnp.float32) for _ in range(bb_dev)]
        for s in range(n_aux):
            value = parts_ref[s, :blk, :].astype(jnp.float32)
            which = parts_ref[s, blk:, :][:1].astype(jnp.float32)
            for b in range(bb_dev):
                sums[b] = sums[b] + jnp.where(which == b, value, 0.0)
        for b in range(bb_dev):
            out_ref[b * blk : (b + 1) * blk, :] = sums[b].astype(out_ref.dtype)

    vmem = pl.BlockSpec(memory_space=pltpu.VMEM)
    return pl.pallas_call(
        kernel,
        out_shape=jax.ShapeDtypeStruct((bb_dev * blk, nocc), jnp.bfloat16),
        in_specs=[vmem],
        out_specs=vmem,
        name="owner_sum",
    )(parts)


def on_device(tiles, c_orbitals, basis_order, tile_block, tile_aux, live):
    blk, nocc = tiles.shape[2:]
    n_aux = lax.axis_size("aux")
    bb_dev = basis_order.shape[0] // n_aux
    direct = n_aux == DIRECT

    def swap(array, m):
        return lax.ppermute(array, "aux", [(i, i ^ m) for i in range(n_aux)])

    base = lax.axis_index("aux").astype(jnp.int32) if direct else jnp.int32(0)
    alive = lax.iota(jnp.int32, tile_block.shape[0]) < live[0]
    where_to, which = owners_of(tile_block, basis_order, base, bb_dev)
    bit = bits_of(where_to, which, alive, n_aux)
    if not direct:
        lists = chunk_lists(where_to, where_to < 0, alive, tile_aux, n_aux)
        whole = lax.all_gather(c_orbitals, "aux", axis=0, tiled=True)
        whole = whole.reshape(n_aux, bb_dev * blk, nocc)
        parts = all_in_one(n_aux, lists, bit, tiles, whole)
        moved = lax.all_to_all(parts, "aux", 0, 0, tiled=True)
        return owner_sum(moved, blk, bb_dev)

    depth = n_aux // PLANE
    half = depth // 2
    last = (where_to >= PLANE) & (where_to % PLANE >= 2)
    fit_lists = chunk_lists(where_to, last, alive, tile_aux, n_aux)
    lists = chunk_lists(where_to, where_to < n_aux // 2, alive, tile_aux, n_aux)
    column = [c_orbitals] + [None] * (depth - 1)
    for dz in range(depth - 1, 0, -1):
        column[dz] = swap(c_orbitals, dz * PLANE)
    beside = swap(c_orbitals, 2)
    across = swap(c_orbitals, 1)
    early = merge(column[1:] + [beside], [])
    late = [swap(array, 2) for array in column[1:]]
    early_from = [(1, (2, None)), (2, (0, depth - 1)), (3, (1, depth - 1))]
    late_from = []
    for dz in range(1, depth):
        for core in range(2):
            early_from.append((dz * PLANE + core, (core, dz - 1)))
            late_from.append((dz * PLANE + 2 + core, (core, dz - 1)))
    held, partial_fit = begin(
        n_aux,
        fit_lists,
        bit,
        tiles,
        c_orbitals,
        [early, swap(early, 1), across],
        early_from,
    )
    late = merge(late, [partial_fit])
    *far, fitted = first_part(
        n_aux, fit_lists, lists, bit, held, partial_fit, [late, swap(late, 1)], late_from
    )
    far = [far[0]] + [swap(far[r], r) for r in range(1, PLANE)]
    near = second_part(n_aux, lists, bit, held, fitted)
    near = [near[0]] + [swap(near[r], r) for r in range(1, PLANE)]
    far = spread(far, [], [jnp.bfloat16] * half, blk, bb_dev)
    near = spread(
        near, [far[0]], [jnp.float32] + [jnp.bfloat16] * (half - 1), blk, bb_dev
    )
    far = [swap(far[i], (half + i) * PLANE) for i in range(half)]
    far = total_of(far, jnp.float32, SPREAD_COST)
    near = [near[0]] + [swap(near[dz], dz * PLANE) for dz in range(1, half)]
    return total_of(near + [far], jnp.bfloat16, 0)


def solution(mesh):
    return jax.shard_map(
        on_device,
        mesh=mesh,
        in_specs=(
            P(("grp", "aux"), None, None, None),
            P(("grp", "aux"), None),
            P("grp"),
            P(("grp", "aux")),
            P(("grp", "aux")),
            P(("grp", "aux")),
        ),
        out_specs=P(("grp", "aux"), None),
        check_vma=False,
    )
```

time: 50.1 us -> 49.1 us (0.980)
  waiting for transfers between devices: 14.5 us -> 8.05 us
  Pallas kernels: 11.5 us -> 16.4 us
  other arithmetic: 2.44 us -> 3.9 us
  starting transfers between devices: 19.6 us -> 18.6 us
    ppermute x21 -> x19, waiting for transfers between devices: 14.5 us -> 8.05 us  [swap(): return lax.ppermute(array, 'aux', [(i, i ^ m) for i in range(n_aux)])]
    pallas_call x1 -> x2, Pallas kernels: 7.91 us -> 12.3 us  [the longest x1 7.02 us: begin(): pl.pallas_call(kernel, out_shape=[jax.ShapeDtypeStruct(tiles_array.shape,...]
    ppermute x21 -> x19, starting transfers between devices: 19.6 us -> 18.6 us  [swap(): return lax.ppermute(array, 'aux', [(i, i ^ m) for i in range(n_aux)])]
    select_n x5 -> x9, other arithmetic: 0.7 us -> 1.41 us  [the longest x2 1.35 us: chunk_lists(): group = jnp.where(alive, tile_aux + jnp.where(later, AB_DEV, 0), keys)]
    reduce_sum x7 -> x12, other arithmetic: 1.44 us -> 2.03 us  [the longest x1 0.76 us: owners_of(): jnp.sum(jnp.where(basis_order[None, :] == tile_block[:, None], lax.iota(j...]
    pallas_call x1, Pallas kernels: 2.64 us -> 3.16 us  [second_part(): pl.pallas_call(kernel, out_shape=[jax.ShapeDtypeStruct(shape, jnp.bfloat1...]
  transfers between devices with their start and end apart: 21 -> 19, of which waited for: 10 -> 7; matrix products, arithmetic and copies ran while one was open for 5% -> 8% of each run, Pallas kernels for 6% -> 21%
where the time goes in v6:
time: 49.1 us; the launch traced here: 48.6 us
  starting transfers between devices  18.6 us (38%)
  Pallas kernels  16.4 us (33%)
  waiting for transfers between devices  8.05 us (16%)
  other arithmetic  3.9 us (8%)
  local copies, waits for them, and re-layouts  0.84 us (2%)
  between operations  0.82 us (2%)
    ppermute x19, starting transfers between devices, swap(): return lax.ppermute(array, 'aux', [(i, i ^ m) for i in range(n_aux)])  18.6 us
    ppermute x19, waiting for transfers between devices, swap(): return lax.ppermute(array, 'aux', [(i, i ^ m) for i in range(n_aux)])  8.05 us
    pallas_call x1, Pallas kernels, begin(): pl.pallas_call(kernel, out_shape=[jax.ShapeDtypeStruct(tiles_array.shape,...  7.02 us
    pallas_call x1, Pallas kernels, first_part(): pl.pallas_call(kernel, out_shape=out_shape, in_specs=[smem] * 7 + [vmem]...  5.28 us
    pallas_call x1, Pallas kernels, second_part(): pl.pallas_call(kernel, out_shape=[jax.ShapeDtypeStruct(shape, jnp.bfloat1...  3.16 us
    select_n x2, other arithmetic, chunk_lists(): group = jnp.where(alive, tile_aux + jnp.where(later, AB_DEV, 0), keys)  1.35 us
  transfers between devices with their start and end apart: 19, of which 7 were waited for; matrix products, arithmetic and copies ran while one was open for 8% of the time, Pallas kernels for 21%

profile of v6, /device:TPU:0, one launch (start us, length us, event | category | flops | bytes accessed | tf_op | source)
XLA Modules:
  0.0 48.6 jit_solution(1948834533765119296)
XLA Ops:
  0.0 3.0 %collective-permute-start.3 = (bf16[256,128]{1,0:T(8,128)(2,1)}, bf16[256,128]{1,0:T(8,128)(2,1)S(1)}, u32[]{:S(2)}, u32[]{:S(2)}) collective-permute-start(bf16[256,128]{1,0:T(8,128)(2,1)} %own_hbm.1), channel_id=1, source_target_pairs={{0,2},{1,3},{2,0},{3,1},{4,6},{5,7},{6,4},{7,5},{8,10},{9,11},{10,... | collective-permute-start | bytes 196616 | tf_op jit(solution)/shard_map/ppermute | solution.py:394
  3.0 3.6 %collective-permute-start.2 = (bf16[256,128]{1,0:T(8,128)(2,1)}, bf16[256,128]{1,0:T(8,128)(2,1)S(1)}, u32[]{:S(2)}, u32[]{:S(2)}) collective-permute-start(bf16[256,128]{1,0:T(8,128)(2,1)} %own_hbm.1), channel_id=1, source_target_pairs={{0,12},{1,13},{2,14},{3,15},{4,8},{5,9},{6,10},{7,11},{8,4},{9,5},... | collective-permute-start | bytes 196616 | tf_op jit(solution)/shard_map/ppermute | solution.py:394
  6.6 0.8 %collective-permute-start = (bf16[256,128]{1,0:T(8,128)(2,1)}, bf16[256,128]{1,0:T(8,128)(2,1)S(1)}, u32[]{:S(2)}, u32[]{:S(2)}) collective-permute-start(bf16[256,128]{1,0:T(8,128)(2,1)} %own_hbm.1), channel_id=1, source_target_pairs={{0,4},{1,5},{2,6},{3,7},{4,0},{5,1},{6,2},{7,3},{8,12},{9,13},{10,... | collective-permute-start | bytes 196616 | tf_op jit(solution)/shard_map/ppermute | solution.py:394
  8.0 0.8 %select_reduce_fusion.6 = s32[64]{0:T(128)S(1)} fusion(s32[64]{0:T(128)} %param.9, s32[32]{0:T(128)} %param.8), kind=kLoop, calls=%fused_computation.15 | loop fusion | flops 6080 | bytes 640 | tf_op jit(solution)/shard_map/reduce_sum | solution.py:23
  8.8 0.7 %fusion.11 = (s32[64]{0:T(128)S(1)}, s32[64]{0:T(128)S(1)}, s32[64]{0:T(128)S(1)}) fusion(s32[64]{0:T(128)} %param.10, s32[]{:T(128)} %bitcast.3, s32[]{:T(128)S(6)} %axis_index.12, s32[64]{0:T(128)S(1)} %select_reduce_fusion.6), kind=kLoop, calls=%fused_computation.68 | loop fusion | flops 2432 | bytes 1288 | tf_op jit(solution)/shard_map/jit(_where)/select_n | solution.py:37
  10.0 0.7 %fusion.7 = (s32[64]{0:T(128)S(1)}, s32[64]{0:T(128)S(1)}) fusion(s32[64]{0:T(128)} %param.10, s32[64]{0:T(128)S(1)} %get-tuple-element.42, s32[]{:T(128)} %bitcast.2, s32[64]{0:T(128)S(1)} %convert_reduce_fusion, s32[64]{0:T(128)S(1)} %select_reduce_fusion.8), kind=kLoop, calls=%fused_computation.64 | loop fusion | flops 512 | bytes 1540 | tf_op jit(solution)/shard_map/jit(_where)/select_n | solution.py:37
  12.6 0.5 %collective-permute-start.8 = (bf16[256,128]{1,0:T(8,128)(2,1)S(1)}, bf16[256,128]{1,0:T(8,128)(2,1)S(1)}, u32[]{:S(2)}, u32[]{:S(2)}) collective-permute-start(bf16[256,128]{1,0:T(8,128)(2,1)S(1)} %collective-permute-done.2.refs_2_), channel_id=1, source_target_pairs={{0,2},{1,3},{2,0},{3,1},{4,6},{5,7},{6,4},{7,5},{8,10},{9,11},{10,... | collective-permute-start | bytes 196616 | tf_op jit(solution)/shard_map/ppermute | solution.py:394
  13.1 1.5 %collective-permute-start.7 = (bf16[256,128]{1,0:T(8,128)(2,1)S(1)}, bf16[256,128]{1,0:T(8,128)(2,1)S(1)}, u32[]{:S(2)}, u32[]{:S(2)}) collective-permute-start(bf16[256,128]{1,0:T(8,128)(2,1)S(1)} %collective-permute-done.1.refs_1_), channel_id=1, source_target_pairs={{0,2},{1,3},{2,0},{3,1},{4,6},{5,7},{6,4},{7,5},{8,10},{9,11},{10,... | collective-permute-start | bytes 196616 | tf_op jit(solution)/shard_map/ppermute | solution.py:394
  15.1 0.8 %copy-done = bf16[256,128]{1,0:T(8,128)(2,1)S(1)} copy-done((bf16[256,128]{1,0:T(8,128)(2,1)S(1)}, bf16[256,128]{1,0:T(8,128)(2,1)}, u32[]{:S(2)}) %copy-start) | copy-done | bytes 65560
  16.0 7.0 %begin.1 = (bf16[64,5,128,128]{3,2,1,0:T(8,128)(2,1)S(1)}, f32[8,128,640]{2,1,0:T(8,128)S(1)}) custom-call(s32[128]{0:T(128)S(1)} %get-tuple-element.44.slot_ref.refs_0_, s32[128]{0:T(128)S(1)} %get-tuple-element.43.block_ref.refs_1_, s32[48]{0:T(128)S(1)} %pad_add_fusion.1.gid_ref.refs_2_, s32[16]{0:T(128)S(1)} %select_reduce_fusion.9.bit_ref.refs_6_, ...), custom_call_target="tpu_custom_call" | custom-call | flops 1342177280 | bytes 5242880 | tf_op jit(solution)/shard_map/begin/pallas_call | solution.py:146
  23.2 1.4 %collective-permute-done.9.refs_10_ = bf16[3,256,128]{2,1,0:T(8,128)(2,1)S(1)} collective-permute-done((bf16[3,256,128]{2,1,0:T(8,128)(2,1)S(1)}, bf16[3,256,128]{2,1,0:T(8,128)(2,1)S(1)}, u32[]{:S(2)}, u32[]{:S(2)}) %collective-permute-start.9) | collective-permute-done | bytes 196640 | tf_op jit(solution)/shard_map/ppermute | solution.py:394
  24.6 5.3 %first_part.1 = (bf16[2,144,128]{2,1,0:T(8,128)(2,1)S(1)}, bf16[2,144,128]{2,1,0:T(8,128)(2,1)S(1)}, bf16[2,144,128]{2,1,0:T(8,128)(2,1)S(1)}, bf16[2,144,128]{2,1,0:T(8,128)(2,1)S(1)}, bf16[8,640,128]{2,1,0:T(8,128)(2,1)S(1)}) custom-call(s32[128]{0:T(128)S(1)} %get-tuple-element.44.slot_ref.refs_0_, s32[128]{0:T(128)S(1)} %get-tuple-element.43.block_ref.refs_1_, ...), custom_call_target="tpu_custom_call" | custom-call | flops 2013265920 | bytes 5242880 | tf_op jit(solution)/shard_map/first_part/pallas_call | solution.py:214
  29.9 1.1 %collective-permute-start.13 = (bf16[2,144,128]{2,1,0:T(8,128)(2,1)S(1)}, bf16[2,144,128]{2,1,0:T(8,128)(2,1)S(1)}, u32[]{:S(2)}, u32[]{:S(2)}) collective-permute-start(bf16[2,144,128]{2,1,0:T(8,128)(2,1)S(1)} %get-tuple-element.28), channel_id=1, source_target_pairs={{0,1},{1,0},{2,3},{3,2},{4,5},{5,4},{6,7},{7,6},{8,9},{9,8},{10,11... | collective-permute-start | bytes 221192 | tf_op jit(solution)/shard_map/ppermute | solution.py:394
  30.9 0.7 %collective-permute-start.14 = (bf16[2,144,128]{2,1,0:T(8,128)(2,1)S(1)}, bf16[2,144,128]{2,1,0:T(8,128)(2,1)S(1)}, u32[]{:S(2)}, u32[]{:S(2)}) collective-permute-start(bf16[2,144,128]{2,1,0:T(8,128)(2,1)S(1)} %get-tuple-element.29), channel_id=1, source_target_pairs={{0,2},{1,3},{2,0},{3,1},{4,6},{5,7},{6,4},{7,5},{8,10},{9,11},{10,... | collective-permute-start | bytes 221192 | tf_op jit(solution)/shard_map/ppermute | solution.py:394
  31.6 0.8 %collective-permute-start.15 = (bf16[2,144,128]{2,1,0:T(8,128)(2,1)S(1)}, bf16[2,144,128]{2,1,0:T(8,128)(2,1)S(1)}, u32[]{:S(2)}, u32[]{:S(2)}) collective-permute-start(bf16[2,144,128]{2,1,0:T(8,128)(2,1)S(1)} %get-tuple-element.30), channel_id=1, source_target_pairs={{0,3},{1,2},{2,1},{3,0},{4,7},{5,6},{6,5},{7,4},{8,11},{9,10},{10,... | collective-permute-start | bytes 221192 | tf_op jit(solution)/shard_map/ppermute | solution.py:394
  32.4 3.2 %second_part.1 = (bf16[2,144,128]{2,1,0:T(8,128)(2,1)S(1)}, bf16[2,144,128]{2,1,0:T(8,128)(2,1)S(1)}, bf16[2,144,128]{2,1,0:T(8,128)(2,1)S(1)}, bf16[2,144,128]{2,1,0:T(8,128)(2,1)S(1)}) custom-call(s32[128]{0:T(128)S(1)} %get-tuple-element.47.refs_3_.slot_ref, s32[128]{0:T(128)S(1)} %get-tuple-element.46.refs_4_.block_ref, ...), custom_call_target="tpu_custom_call" | custom-call | flops 10000000000 | bytes 5242880 | tf_op jit(solution)/shard_map/second_part/pallas_call | solution.py:247
  35.5 1.3 %collective-permute-start.10 = (bf16[2,144,128]{2,1,0:T(8,128)(2,1)S(1)}, bf16[2,144,128]{2,1,0:T(8,128)(2,1)S(1)}, u32[]{:S(2)}, u32[]{:S(2)}) collective-permute-start(bf16[2,144,128]{2,1,0:T(8,128)(2,1)S(1)} %get-tuple-element.24), channel_id=1, source_target_pairs={{0,1},{1,0},{2,3},{3,2},{4,5},{5,4},{6,7},{7,6},{8,9},{9,8},{10,11... | collective-permute-start | bytes 221192 | tf_op jit(solution)/shard_map/ppermute | solution.py:394
  37.0 1.3 %collective-permute-start.12 = (bf16[2,144,128]{2,1,0:T(8,128)(2,1)S(1)}, bf16[2,144,128]{2,1,0:T(8,128)(2,1)S(1)}, u32[]{:S(2)}, u32[]{:S(2)}) collective-permute-start(bf16[2,144,128]{2,1,0:T(8,128)(2,1)S(1)} %get-tuple-element.26), channel_id=1, source_target_pairs={{0,3},{1,2},{2,1},{3,0},{4,7},{5,6},{6,5},{7,4},{8,11},{9,10},{10,... | collective-permute-start | bytes 221192 | tf_op jit(solution)/shard_map/ppermute | solution.py:394
  38.4 2.1 %collective-permute-start.18 = (bf16[256,128]{1,0:T(8,128)(2,1)S(1)}, bf16[256,128]{1,0:T(8,128)(2,1)S(1)}, u32[]{:S(2)}, u32[]{:S(2)}) collective-permute-start(bf16[256,128]{1,0:T(8,128)(2,1)S(1)} %get-tuple-element.34), channel_id=1, source_target_pairs={{0,12},{1,13},{2,14},{3,15},{4,8},{5,9},{6,10},{7,11},{8,4},{9,5},... | collective-permute-start | bytes 196616 | tf_op jit(solution)/shard_map/ppermute | solution.py:394
  40.5 1.3 %collective-permute-done.11.refs_2_ = bf16[2,144,128]{2,1,0:T(8,128)(2,1)S(1)} collective-permute-done((bf16[2,144,128]{2,1,0:T(8,128)(2,1)S(1)}, bf16[2,144,128]{2,1,0:T(8,128)(2,1)S(1)}, u32[]{:S(2)}, u32[]{:S(2)}) %collective-permute-start.11) | collective-permute-done | bytes 73760 | tf_op jit(solution)/shard_map/ppermute | solution.py:394
  42.0 1.2 %collective-permute-start.16 = (bf16[256,128]{1,0:T(8,128)(2,1)S(1)}, bf16[256,128]{1,0:T(8,128)(2,1)S(1)}, u32[]{:S(2)}, u32[]{:S(2)}) collective-permute-start(bf16[256,128]{1,0:T(8,128)(2,1)S(1)} %get-tuple-element.33), channel_id=1, source_target_pairs={{0,4},{1,5},{2,6},{3,7},{4,0},{5,1},{6,2},{7,3},{8,12},{9,13},{10,... | collective-permute-start | bytes 196616 | tf_op jit(solution)/shard_map/ppermute | solution.py:394
  43.2 2.1 %collective-permute-done.18.refs_1_ = bf16[256,128]{1,0:T(8,128)(2,1)S(1)} collective-permute-done((bf16[256,128]{1,0:T(8,128)(2,1)S(1)}, bf16[256,128]{1,0:T(8,128)(2,1)S(1)}, u32[]{:S(2)}, u32[]{:S(2)}) %collective-permute-start.18) | collective-permute-done | bytes 65568 | tf_op jit(solution)/shard_map/ppermute | solution.py:394
  45.3 2.6 %collective-permute-done.17.refs_0_ = bf16[256,128]{1,0:T(8,128)(2,1)S(1)} collective-permute-done((bf16[256,128]{1,0:T(8,128)(2,1)S(1)}, bf16[256,128]{1,0:T(8,128)(2,1)S(1)}, u32[]{:S(2)}, u32[]{:S(2)}) %collective-permute-start.17) | collective-permute-done | bytes 65568 | tf_op jit(solution)/shard_map/ppermute | solution.py:394
  48.0 0.6 %total_of.3 = bf16[256,128]{1,0:T(8,128)(2,1)} custom-call(f32[256,128]{1,0:T(8,128)S(1)} %get-tuple-element.32.refs_0_, bf16[256,128]{1,0:T(8,128)(2,1)S(1)} %collective-permute-done.16.refs_1_, f32[256,128]{1,0:T(8,128)S(1)} %total_of.2.refs_2_), custom_call_target="tpu_custom_call" | custom-call | tf_op jit(solution)/shard_map/total_of/pallas_call | solution.py:353
  (53 shorter events, 3.6 us)
Async XLA Ops:
  0.0 11.7 %collective-permute-start.3 = (bf16[256,128]{1,0:T(8,128)(2,1)}, bf16[256,128]{1,0:T(8,128)(2,1)S(1)}, u32[]{:S(2)}, u32[]{:S(2)}) collective-permute-start(bf16[256,128]{1,0:T(8,128)(2,1)} %own_hbm.1), channel_id=1, source_target_pairs={{0,2},{1,3},{2,0},{3,1},{4,6},{5,7},{6,4},{7,5},{8,10},{9,11},{10,... | collective-permute-start | bytes 196616 | tf_op jit(solution)/shard_map/ppermute | solution.py:394
  3.0 8.8 %collective-permute-start.2 = (bf16[256,128]{1,0:T(8,128)(2,1)}, bf16[256,128]{1,0:T(8,128)(2,1)S(1)}, u32[]{:S(2)}, u32[]{:S(2)}) collective-permute-start(bf16[256,128]{1,0:T(8,128)(2,1)} %own_hbm.1), channel_id=1, source_target_pairs={{0,12},{1,13},{2,14},{3,15},{4,8},{5,9},{6,10},{7,11},{8,4},{9,5},... | collective-permute-start | bytes 196616 | tf_op jit(solution)/shard_map/ppermute | solution.py:394
  6.6 5.6 %collective-permute-start.1 = (bf16[256,128]{1,0:T(8,128)(2,1)}, bf16[256,128]{1,0:T(8,128)(2,1)S(1)}, u32[]{:S(2)}, u32[]{:S(2)}) collective-permute-start(bf16[256,128]{1,0:T(8,128)(2,1)} %own_hbm.1), channel_id=1, source_target_pairs={{0,8},{1,9},{2,10},{3,11},{4,12},{5,13},{6,14},{7,15},{8,0},{9,1},... | collective-permute-start | bytes 196616 | tf_op jit(solution)/shard_map/ppermute | solution.py:394
  6.6 5.7 %collective-permute-start = (bf16[256,128]{1,0:T(8,128)(2,1)}, bf16[256,128]{1,0:T(8,128)(2,1)S(1)}, u32[]{:S(2)}, u32[]{:S(2)}) collective-permute-start(bf16[256,128]{1,0:T(8,128)(2,1)} %own_hbm.1), channel_id=1, source_target_pairs={{0,4},{1,5},{2,6},{3,7},{4,0},{5,1},{6,2},{7,3},{8,12},{9,13},{10,... | collective-permute-start | bytes 196616 | tf_op jit(solution)/shard_map/ppermute | solution.py:394
  7.4 7.8 %collective-permute-start.5 = (bf16[256,128]{1,0:T(8,128)(2,1)}, bf16[256,128]{1,0:T(8,128)(2,1)S(1)}, u32[]{:S(2)}, u32[]{:S(2)}) collective-permute-start(bf16[256,128]{1,0:T(8,128)(2,1)} %own_hbm.1), channel_id=1, source_target_pairs={{0,1},{1,0},{2,3},{3,2},{4,5},{5,4},{6,7},{7,6},{8,9},{9,8},{10,11... | collective-permute-start | bytes 196616 | tf_op jit(solution)/shard_map/ppermute | solution.py:394
  12.3 2.9 %collective-permute-start.4 = (bf16[4,256,128]{2,1,0:T(8,128)(2,1)S(1)}, bf16[4,256,128]{2,1,0:T(8,128)(2,1)S(1)}, u32[]{:S(2)}, u32[]{:S(2)}) collective-permute-start(bf16[4,256,128]{2,1,0:T(8,128)(2,1)S(1)} %merge.2.refs_0_), channel_id=1, source_target_pairs={{0,1},{1,0},{2,3},{3,2},{4,5},{5,4},{6,7},{7,6},{8,9},{9,8},{10,11... | collective-permute-start | bytes 786440 | tf_op jit(solution)/shard_map/ppermute | solution.py:394
  12.6 10.4 %collective-permute-start.8 = (bf16[256,128]{1,0:T(8,128)(2,1)S(1)}, bf16[256,128]{1,0:T(8,128)(2,1)S(1)}, u32[]{:S(2)}, u32[]{:S(2)}) collective-permute-start(bf16[256,128]{1,0:T(8,128)(2,1)S(1)} %collective-permute-done.2.refs_2_), channel_id=1, source_target_pairs={{0,2},{1,3},{2,0},{3,1},{4,6},{5,7},{6,4},{7,5},{8,10},{9,11},{10,... | collective-permute-start | bytes 196616 | tf_op jit(solution)/shard_map/ppermute | solution.py:394
  13.1 9.9 %collective-permute-start.7 = (bf16[256,128]{1,0:T(8,128)(2,1)S(1)}, bf16[256,128]{1,0:T(8,128)(2,1)S(1)}, u32[]{:S(2)}, u32[]{:S(2)}) collective-permute-start(bf16[256,128]{1,0:T(8,128)(2,1)S(1)} %collective-permute-done.1.refs_1_), channel_id=1, source_target_pairs={{0,2},{1,3},{2,0},{3,1},{4,6},{5,7},{6,4},{7,5},{8,10},{9,11},{10,... | collective-permute-start | bytes 196616 | tf_op jit(solution)/shard_map/ppermute | solution.py:394
  14.6 8.4 %collective-permute-start.6 = (bf16[256,128]{1,0:T(8,128)(2,1)S(1)}, bf16[256,128]{1,0:T(8,128)(2,1)S(1)}, u32[]{:S(2)}, u32[]{:S(2)}) collective-permute-start(bf16[256,128]{1,0:T(8,128)(2,1)S(1)} %collective-permute-done.refs_0_), channel_id=1, source_target_pairs={{0,2},{1,3},{2,0},{3,1},{4,6},{5,7},{6,4},{7,5},{8,10},{9,11},{10,... | collective-permute-start | bytes 196616 | tf_op jit(solution)/shard_map/ppermute | solution.py:394
  15.1 0.8 %copy-start = (bf16[256,128]{1,0:T(8,128)(2,1)S(1)}, bf16[256,128]{1,0:T(8,128)(2,1)}, u32[]{:S(2)}) copy-start(bf16[256,128]{1,0:T(8,128)(2,1)} %own_hbm.1) | copy-start | bytes 196612
  23.1 1.5 %collective-permute-start.9 = (bf16[3,256,128]{2,1,0:T(8,128)(2,1)S(1)}, bf16[3,256,128]{2,1,0:T(8,128)(2,1)S(1)}, u32[]{:S(2)}, u32[]{:S(2)}) collective-permute-start(bf16[3,256,128]{2,1,0:T(8,128)(2,1)S(1)} %merge.3.refs_9_), channel_id=1, source_target_pairs={{0,1},{1,0},{2,3},{3,2},{4,5},{5,4},{6,7},{7,6},{8,9},{9,8},{10,11... | collective-permute-start | bytes 589832 | tf_op jit(solution)/shard_map/ppermute | solution.py:394
  29.9 7.1 %collective-permute-start.13 = (bf16[2,144,128]{2,1,0:T(8,128)(2,1)S(1)}, bf16[2,144,128]{2,1,0:T(8,128)(2,1)S(1)}, u32[]{:S(2)}, u32[]{:S(2)}) collective-permute-start(bf16[2,144,128]{2,1,0:T(8,128)(2,1)S(1)} %get-tuple-element.28), channel_id=1, source_target_pairs={{0,1},{1,0},{2,3},{3,2},{4,5},{5,4},{6,7},{7,6},{8,9},{9,8},{10,11... | collective-permute-start | bytes 221192 | tf_op jit(solution)/shard_map/ppermute | solution.py:394
  30.9 7.3 %collective-permute-start.14 = (bf16[2,144,128]{2,1,0:T(8,128)(2,1)S(1)}, bf16[2,144,128]{2,1,0:T(8,128)(2,1)S(1)}, u32[]{:S(2)}, u32[]{:S(2)}) collective-permute-start(bf16[2,144,128]{2,1,0:T(8,128)(2,1)S(1)} %get-tuple-element.29), channel_id=1, source_target_pairs={{0,2},{1,3},{2,0},{3,1},{4,6},{5,7},{6,4},{7,5},{8,10},{9,11},{10,... | collective-permute-start | bytes 221192 | tf_op jit(solution)/shard_map/ppermute | solution.py:394
  31.6 6.7 %collective-permute-start.15 = (bf16[2,144,128]{2,1,0:T(8,128)(2,1)S(1)}, bf16[2,144,128]{2,1,0:T(8,128)(2,1)S(1)}, u32[]{:S(2)}, u32[]{:S(2)}) collective-permute-start(bf16[2,144,128]{2,1,0:T(8,128)(2,1)S(1)} %get-tuple-element.30), channel_id=1, source_target_pairs={{0,3},{1,2},{2,1},{3,0},{4,7},{5,6},{6,5},{7,4},{8,11},{9,10},{10,... | collective-permute-start | bytes 221192 | tf_op jit(solution)/shard_map/ppermute | solution.py:394
  35.5 5.0 %collective-permute-start.10 = (bf16[2,144,128]{2,1,0:T(8,128)(2,1)S(1)}, bf16[2,144,128]{2,1,0:T(8,128)(2,1)S(1)}, u32[]{:S(2)}, u32[]{:S(2)}) collective-permute-start(bf16[2,144,128]{2,1,0:T(8,128)(2,1)S(1)} %get-tuple-element.24), channel_id=1, source_target_pairs={{0,1},{1,0},{2,3},{3,2},{4,5},{5,4},{6,7},{7,6},{8,9},{9,8},{10,11... | collective-permute-start | bytes 221192 | tf_op jit(solution)/shard_map/ppermute | solution.py:394
  36.8 5.0 %collective-permute-start.11 = (bf16[2,144,128]{2,1,0:T(8,128)(2,1)S(1)}, bf16[2,144,128]{2,1,0:T(8,128)(2,1)S(1)}, u32[]{:S(2)}, u32[]{:S(2)}) collective-permute-start(bf16[2,144,128]{2,1,0:T(8,128)(2,1)S(1)} %get-tuple-element.25), channel_id=1, source_target_pairs={{0,2},{1,3},{2,0},{3,1},{4,6},{5,7},{6,4},{7,5},{8,10},{9,11},{10,... | collective-permute-start | bytes 221192 | tf_op jit(solution)/shard_map/ppermute | solution.py:394
  37.0 4.9 %collective-permute-start.12 = (bf16[2,144,128]{2,1,0:T(8,128)(2,1)S(1)}, bf16[2,144,128]{2,1,0:T(8,128)(2,1)S(1)}, u32[]{:S(2)}, u32[]{:S(2)}) collective-permute-start(bf16[2,144,128]{2,1,0:T(8,128)(2,1)S(1)} %get-tuple-element.26), channel_id=1, source_target_pairs={{0,3},{1,2},{2,1},{3,0},{4,7},{5,6},{6,5},{7,4},{8,11},{9,10},{10,... | collective-permute-start | bytes 221192 | tf_op jit(solution)/shard_map/ppermute | solution.py:394
  38.4 6.9 %collective-permute-start.18 = (bf16[256,128]{1,0:T(8,128)(2,1)S(1)}, bf16[256,128]{1,0:T(8,128)(2,1)S(1)}, u32[]{:S(2)}, u32[]{:S(2)}) collective-permute-start(bf16[256,128]{1,0:T(8,128)(2,1)S(1)} %get-tuple-element.34), channel_id=1, source_target_pairs={{0,12},{1,13},{2,14},{3,15},{4,8},{5,9},{6,10},{7,11},{8,4},{9,5},... | collective-permute-start | bytes 196616 | tf_op jit(solution)/shard_map/ppermute | solution.py:394
  40.5 7.3 %collective-permute-start.17 = (bf16[256,128]{1,0:T(8,128)(2,1)S(1)}, bf16[256,128]{1,0:T(8,128)(2,1)S(1)}, u32[]{:S(2)}, u32[]{:S(2)}) collective-permute-start(bf16[256,128]{1,0:T(8,128)(2,1)S(1)} %get-tuple-element.31.refs_4_), channel_id=1, source_target_pairs={{0,8},{1,9},{2,10},{3,11},{4,12},{5,13},{6,14},{7,15},{8,0},{9,1},... | collective-permute-start | bytes 196616 | tf_op jit(solution)/shard_map/ppermute | solution.py:394
  42.0 6.0 %collective-permute-start.16 = (bf16[256,128]{1,0:T(8,128)(2,1)S(1)}, bf16[256,128]{1,0:T(8,128)(2,1)S(1)}, u32[]{:S(2)}, u32[]{:S(2)}) collective-permute-start(bf16[256,128]{1,0:T(8,128)(2,1)S(1)} %get-tuple-element.33), channel_id=1, source_target_pairs={{0,4},{1,5},{2,6},{3,7},{4,0},{5,1},{6,2},{7,3},{8,12},{9,13},{10,... | collective-permute-start | bytes 196616 | tf_op jit(solution)/shard_map/ppermute | solution.py:394

commit v7 on v6

--- a/solution.py
+++ b/solution.py
@@ -10,8 +10,6 @@
 AB_DEV = 8
 CHUNK = 4
 UNROLL = 2
-LOADS = 8
-BEGIN_VMEM = 40
 TAIL = 16
 PLANE = 4
 SPREAD_COST = 10**10
@@ -115,49 +113,26 @@
 def begin(n_aux, lists, bit, tiles_array, own_array, shards, sources):
     slots, auxb, blk, nocc = tiles_array.shape
     n_in = len(shards)
-    step = slots // LOADS
-
-    def kernel(slot_ref, block_ref, gid_ref, bit_ref, tiles_hbm, own_hbm, *refs):
-        c_refs, (tiles, zacc, ct, own, sems, own_sem) = refs[:n_in], refs[n_in:]
-        own_copy = pltpu.make_async_copy(own_hbm, own, own_sem)
-        own_copy.start()
-        copies = [
-            pltpu.make_async_copy(
-                tiles_hbm.at[pl.ds(i * step, step)], tiles.at[pl.ds(i * step, step)], sems.at[i]
-            )
-            for i in range(LOADS)
-        ]
-        for copy in copies:
-            copy.start()
+
+    def kernel(slot_ref, block_ref, gid_ref, bit_ref, tiles, own, *refs):
+        c_refs, (zacc, ct) = refs[:n_in], refs[n_in:]
         zacc[...] = jnp.zeros(zacc.shape, zacc.dtype)
         ct[n_aux] = jnp.zeros((nocc, blk), ct.dtype)
+        turn(ct, bit_ref, 0, own)
         for m, (ref, i) in sources:
             turn(ct, bit_ref, m, c_refs[ref] if i is None else c_refs[ref].at[i])
-        own_copy.wait()
-        turn(ct, bit_ref, 0, own)
-        for copy in copies:
-            copy.wait()
         early, _ = chunk_ends(gid_ref, slots)
         fit((slot_ref, block_ref, gid_ref), tiles, ct, zacc, 0, early)
 
     smem = pl.BlockSpec(memory_space=pltpu.SMEM)
     vmem = pl.BlockSpec(memory_space=pltpu.VMEM)
-    hbm = pl.BlockSpec(memory_space=pl.ANY)
-    return pl.pallas_call(
-        kernel,
-        out_shape=[
-            jax.ShapeDtypeStruct(tiles_array.shape, tiles_array.dtype),
-            jax.ShapeDtypeStruct((AB_DEV, nocc, auxb * nocc), jnp.float32),
-        ],
-        in_specs=[smem] * 4 + [hbm] * 2 + [vmem] * n_in,
-        out_specs=[vmem] * 2,
-        scratch_shapes=[
-            pltpu.VMEM((n_aux + 1, nocc, blk), jnp.bfloat16),
-            pltpu.VMEM(own_array.shape, own_array.dtype),
-            pltpu.SemaphoreType.DMA((LOADS,)),
-            pltpu.SemaphoreType.DMA,
-        ],
-        compiler_params=pltpu.CompilerParams(vmem_limit_bytes=BEGIN_VMEM * 1024 * 1024),
+    return pl.pallas_call(
+        kernel,
+        out_shape=jax.ShapeDtypeStruct((AB_DEV, nocc, auxb * nocc), jnp.float32),
+        in_specs=[smem] * 4 + [vmem] * (2 + n_in),
+        out_specs=vmem,
+        scratch_shapes=[pltpu.VMEM((n_aux + 1, nocc, blk), jnp.bfloat16)],
+        compiler_params=pltpu.CompilerParams(vmem_limit_bytes=20 * 1024 * 1024),
         cost_estimate=pl.CostEstimate(
             flops=2 * tiles_array.size * nocc, bytes_accessed=tiles_array.size, transcendentals=0
         ),
@@ -297,7 +272,7 @@
     )(*lists, bit, tiles_array, whole)
 
 
-def merge(arrays, after):
+def merge(arrays, after, cost):
     def kernel(*refs):
         for i, ref in enumerate(refs[: len(arrays)]):
             refs[-1][i] = ref[...]
@@ -309,6 +284,7 @@
         in_specs=[vmem] * len(arrays) + [pl.BlockSpec(memory_space=pl.ANY)] * len(after),
         out_specs=vmem,
         compiler_params=pltpu.CompilerParams(vmem_limit_bytes=4 * 1024 * 1024),
+        cost_estimate=pl.CostEstimate(flops=cost, bytes_accessed=cost // 1000, transcendentals=0),
         name="merge",
     )(*arrays, *after)
 
@@ -415,7 +391,7 @@
         column[dz] = swap(c_orbitals, dz * PLANE)
     beside = swap(c_orbitals, 2)
     across = swap(c_orbitals, 1)
-    early = merge(column[1:] + [beside], [])
+    early = merge(column[1:] + [beside], [], SPREAD_COST)
     late = [swap(array, 2) for array in column[1:]]
     early_from = [(1, (2, None)), (2, (0, depth - 1)), (3, (1, depth - 1))]
     late_from = []
@@ -423,7 +399,7 @@
         for core in range(2):
             early_from.append((dz * PLANE + core, (core, dz - 1)))
             late_from.append((dz * PLANE + 2 + core, (core, dz - 1)))
-    held, partial_fit = begin(
+    partial_fit = begin(
         n_aux,
         fit_lists,
         bit,
@@ -432,12 +408,12 @@
         [early, swap(early, 1), across],
         early_from,
     )
-    late = merge(late, [partial_fit])
+    late = merge(late, [partial_fit], 0)
     *far, fitted = first_part(
-        n_aux, fit_lists, lists, bit, held, partial_fit, [late, swap(late, 1)], late_from
+        n_aux, fit_lists, lists, bit, tiles, partial_fit, [late, swap(late, 1)], late_from
     )
     far = [far[0]] + [swap(far[r], r) for r in range(1, PLANE)]
-    near = second_part(n_aux, lists, bit, held, fitted)
+    near = second_part(n_aux, lists, bit, tiles, fitted)
     near = [near[0]] + [swap(near[r], r) for r in range(1, PLANE)]
     far = spread(far, [], [jnp.bfloat16] * half, blk, bb_dev)
     near = spread(

time: 49.1 us -> 45.4 us (0.925); the launches traced: 48.6 us -> 45.5 us
  Pallas kernels: 16.4 us -> 13.8 us
    pallas_call x1, Pallas kernels: 7.02 us -> 3.53 us  [begin(): pl.pallas_call(kernel, out_shape=jax.ShapeDtypeStruct((AB_DEV, nocc, auxb...]
    pallas_call x1, Pallas kernels: 5.28 us -> 6.17 us  [first_part(): pl.pallas_call(kernel, out_shape=out_shape, in_specs=[smem] * 7 + [vmem]...]
  transfers between devices with their start and end apart: 19 -> 19, of which waited for: 7 -> 8; matrix products, arithmetic and copies ran while one was open for 8% -> 9% of each run, Pallas kernels for 21% -> 15%
where the time goes in v7:
time: 45.4 us; the launch traced here: 45.5 us
  starting transfers between devices  18.7 us (41%)
  Pallas kernels  13.8 us (30%)
  waiting for transfers between devices  7.69 us (17%)
  other arithmetic  3.9 us (9%)
  between operations  0.87 us (2%)
  local copies, waits for them, and re-layouts  0.58 us (1%)
    ppermute x19, starting transfers between devices, swap(): return lax.ppermute(array, 'aux', [(i, i ^ m) for i in range(n_aux)])  18.7 us
    ppermute x19, waiting for transfers between devices, swap(): return lax.ppermute(array, 'aux', [(i, i ^ m) for i in range(n_aux)])  7.69 us
    pallas_call x1, Pallas kernels, first_part(): pl.pallas_call(kernel, out_shape=out_shape, in_specs=[smem] * 7 + [vmem]...  6.17 us
    pallas_call x1, Pallas kernels, begin(): pl.pallas_call(kernel, out_shape=jax.ShapeDtypeStruct((AB_DEV, nocc, auxb...  3.53 us
    pallas_call x1, Pallas kernels, second_part(): pl.pallas_call(kernel, out_shape=[jax.ShapeDtypeStruct(shape, jnp.bfloat1...  3.14 us
    select_n x2, other arithmetic, chunk_lists(): group = jnp.where(alive, tile_aux + jnp.where(later, AB_DEV, 0), keys)  1.35 us
  transfers between devices with their start and end apart: 19, of which 8 were waited for; matrix products, arithmetic and copies ran while one was open for 9% of the time, Pallas kernels for 15%

profile of v7, /device:TPU:0, one launch (start us, length us, event | category | flops | bytes accessed | tf_op | source)
XLA Modules:
  0.0 45.5 jit_solution(8211208128246221298)
XLA Ops:
  0.0 3.0 %collective-permute-start.3 = (bf16[256,128]{1,0:T(8,128)(2,1)}, bf16[256,128]{1,0:T(8,128)(2,1)S(1)}, u32[]{:S(2)}, u32[]{:S(2)}) collective-permute-start(bf16[256,128]{1,0:T(8,128)(2,1)} %own.1), channel_id=1, source_target_pairs={{0,2},{1,3},{2,0},{3,1},{4,6},{5,7},{6,4},{7,5},{8,10},{9,11},{10,... | collective-permute-start | bytes 196616 | tf_op jit(solution)/shard_map/ppermute | solution.py:370
  3.0 3.6 %collective-permute-start.2 = (bf16[256,128]{1,0:T(8,128)(2,1)}, bf16[256,128]{1,0:T(8,128)(2,1)S(1)}, u32[]{:S(2)}, u32[]{:S(2)}) collective-permute-start(bf16[256,128]{1,0:T(8,128)(2,1)} %own.1), channel_id=1, source_target_pairs={{0,12},{1,13},{2,14},{3,15},{4,8},{5,9},{6,10},{7,11},{8,4},{9,5},... | collective-permute-start | bytes 196616 | tf_op jit(solution)/shard_map/ppermute | solution.py:370
  6.6 0.8 %collective-permute-start = (bf16[256,128]{1,0:T(8,128)(2,1)}, bf16[256,128]{1,0:T(8,128)(2,1)S(1)}, u32[]{:S(2)}, u32[]{:S(2)}) collective-permute-start(bf16[256,128]{1,0:T(8,128)(2,1)} %own.1), channel_id=1, source_target_pairs={{0,4},{1,5},{2,6},{3,7},{4,0},{5,1},{6,2},{7,3},{8,12},{9,13},{10,... | collective-permute-start | bytes 196616 | tf_op jit(solution)/shard_map/ppermute | solution.py:370
  8.0 0.8 %select_reduce_fusion.6 = s32[64]{0:T(128)S(1)} fusion(s32[64]{0:T(128)} %param.9, s32[32]{0:T(128)} %param.8), kind=kLoop, calls=%fused_computation.15 | loop fusion | flops 6080 | bytes 640 | tf_op jit(solution)/shard_map/reduce_sum | solution.py:21
  8.8 0.7 %fusion.11 = (s32[64]{0:T(128)S(1)}, s32[64]{0:T(128)S(1)}, s32[64]{0:T(128)S(1)}) fusion(s32[64]{0:T(128)} %param.10, s32[]{:T(128)} %bitcast.3, s32[]{:T(128)S(6)} %axis_index.12, s32[64]{0:T(128)S(1)} %select_reduce_fusion.6), kind=kLoop, calls=%fused_computation.68 | loop fusion | flops 2432 | bytes 1288 | tf_op jit(solution)/shard_map/jit(_where)/select_n | solution.py:35
  10.0 0.7 %fusion.7 = (s32[64]{0:T(128)S(1)}, s32[64]{0:T(128)S(1)}) fusion(s32[64]{0:T(128)} %param.10, s32[64]{0:T(128)S(1)} %get-tuple-element.38, s32[]{:T(128)} %bitcast.2, s32[64]{0:T(128)S(1)} %convert_reduce_fusion, s32[64]{0:T(128)S(1)} %select_reduce_fusion.8), kind=kLoop, calls=%fused_computation.64 | loop fusion | flops 512 | bytes 1540 | tf_op jit(solution)/shard_map/jit(_where)/select_n | solution.py:35
  11.8 0.4 collective-permute-done.1.refs_1_
  12.7 0.4 collective-permute-start.8
  13.1 1.6 %collective-permute-start.7 = (bf16[256,128]{1,0:T(8,128)(2,1)S(1)}, bf16[256,128]{1,0:T(8,128)(2,1)S(1)}, u32[]{:S(2)}, u32[]{:S(2)}) collective-permute-start(bf16[256,128]{1,0:T(8,128)(2,1)S(1)} %collective-permute-done.1.refs_1_), channel_id=1, source_target_pairs={{0,2},{1,3},{2,0},{3,1},{4,6},{5,7},{6,4},{7,5},{8,10},{9,11},{10,... | collective-permute-start | bytes 196616 | tf_op jit(solution)/shard_map/ppermute | solution.py:370
  14.7 0.4 collective-permute-start.6
  15.1 0.6 %slice-done.2 = s8[2097152]{0:T(1024)(128)(4,1)S(1)} async-done(((s8[10485760]{0:T(1024)(128)(4,1)}), s8[2097152]{0:T(1024)(128)(4,1)S(1)}, s32[]{:S(2)}) %slice-start.2) | async-done | bytes 2097176
  15.7 3.5 %begin.1.refs_3_.refs_8_ = f32[8,128,640]{2,1,0:T(8,128)S(1)} custom-call(s32[128]{0:T(128)S(1)} %get-tuple-element.40.slot_ref.refs_0_, s32[128]{0:T(128)S(1)} %get-tuple-element.39.block_ref.refs_1_, s32[48]{0:T(128)S(1)} %pad_add_fusion.1.gid_ref.refs_2_, s32[16]{0:T(128)S(1)} %select_reduce_fusion.9.bit_ref.refs_6_, ...), custom_call_target="tpu_custom_call" | custom-call | flops 1342177280 | bytes 5242880 | tf_op jit(solution)/shard_map/begin/pallas_call | solution.py:129
  19.3 0.6 %collective-permute-done.6.refs_0_ = bf16[256,128]{1,0:T(8,128)(2,1)S(1)} collective-permute-done((bf16[256,128]{1,0:T(8,128)(2,1)S(1)}, bf16[256,128]{1,0:T(8,128)(2,1)S(1)}, u32[]{:S(2)}, u32[]{:S(2)}) %collective-permute-start.6) | collective-permute-done | bytes 65568 | tf_op jit(solution)/shard_map/ppermute | solution.py:370
  20.0 1.4 %collective-permute-done.9.refs_10_ = bf16[3,256,128]{2,1,0:T(8,128)(2,1)S(1)} collective-permute-done((bf16[3,256,128]{2,1,0:T(8,128)(2,1)S(1)}, bf16[3,256,128]{2,1,0:T(8,128)(2,1)S(1)}, u32[]{:S(2)}, u32[]{:S(2)}) %collective-permute-start.9) | collective-permute-done | bytes 196640 | tf_op jit(solution)/shard_map/ppermute | solution.py:370
  21.4 6.2 %first_part.1 = (bf16[2,144,128]{2,1,0:T(8,128)(2,1)S(1)}, bf16[2,144,128]{2,1,0:T(8,128)(2,1)S(1)}, bf16[2,144,128]{2,1,0:T(8,128)(2,1)S(1)}, bf16[2,144,128]{2,1,0:T(8,128)(2,1)S(1)}, bf16[8,640,128]{2,1,0:T(8,128)(2,1)S(1)}) custom-call(s32[128]{0:T(128)S(1)} %get-tuple-element.40.slot_ref.refs_0_, s32[128]{0:T(128)S(1)} %get-tuple-element.39.block_ref.refs_1_, ...), custom_call_target="tpu_custom_call" | custom-call | flops 2013265920 | bytes 5242880 | tf_op jit(solution)/shard_map/first_part/pallas_call | solution.py:189
  27.9 1.7 %collective-permute-start.15 = (bf16[2,144,128]{2,1,0:T(8,128)(2,1)S(1)}, bf16[2,144,128]{2,1,0:T(8,128)(2,1)S(1)}, u32[]{:S(2)}, u32[]{:S(2)}) collective-permute-start(bf16[2,144,128]{2,1,0:T(8,128)(2,1)S(1)} %get-tuple-element.26), channel_id=1, source_target_pairs={{0,3},{1,2},{2,1},{3,0},{4,7},{5,6},{6,5},{7,4},{8,11},{9,10},{10,... | collective-permute-start | bytes 221192 | tf_op jit(solution)/shard_map/ppermute | solution.py:370
  29.6 3.1 %second_part.1 = (bf16[2,144,128]{2,1,0:T(8,128)(2,1)S(1)}, bf16[2,144,128]{2,1,0:T(8,128)(2,1)S(1)}, bf16[2,144,128]{2,1,0:T(8,128)(2,1)S(1)}, bf16[2,144,128]{2,1,0:T(8,128)(2,1)S(1)}) custom-call(s32[128]{0:T(128)S(1)} %get-tuple-element.43.refs_3_.slot_ref, s32[128]{0:T(128)S(1)} %get-tuple-element.42.refs_4_.block_ref, ...), custom_call_target="tpu_custom_call" | custom-call | flops 10000000000 | bytes 5242880 | tf_op jit(solution)/shard_map/second_part/pallas_call | solution.py:222
  32.7 0.9 %collective-permute-start.10 = (bf16[2,144,128]{2,1,0:T(8,128)(2,1)S(1)}, bf16[2,144,128]{2,1,0:T(8,128)(2,1)S(1)}, u32[]{:S(2)}, u32[]{:S(2)}) collective-permute-start(bf16[2,144,128]{2,1,0:T(8,128)(2,1)S(1)} %get-tuple-element.20), channel_id=1, source_target_pairs={{0,1},{1,0},{2,3},{3,2},{4,5},{5,4},{6,7},{7,6},{8,9},{9,8},{10,11... | collective-permute-start | bytes 221192 | tf_op jit(solution)/shard_map/ppermute | solution.py:370
  33.6 1.4 %collective-permute-start.12 = (bf16[2,144,128]{2,1,0:T(8,128)(2,1)S(1)}, bf16[2,144,128]{2,1,0:T(8,128)(2,1)S(1)}, u32[]{:S(2)}, u32[]{:S(2)}) collective-permute-start(bf16[2,144,128]{2,1,0:T(8,128)(2,1)S(1)} %get-tuple-element.22), channel_id=1, source_target_pairs={{0,3},{1,2},{2,1},{3,0},{4,7},{5,6},{6,5},{7,4},{8,11},{9,10},{10,... | collective-permute-start | bytes 221192 | tf_op jit(solution)/shard_map/ppermute | solution.py:370
  35.2 3.3 %collective-permute-start.18 = (bf16[256,128]{1,0:T(8,128)(2,1)S(1)}, bf16[256,128]{1,0:T(8,128)(2,1)S(1)}, u32[]{:S(2)}, u32[]{:S(2)}) collective-permute-start(bf16[256,128]{1,0:T(8,128)(2,1)S(1)} %get-tuple-element.30), channel_id=1, source_target_pairs={{0,12},{1,13},{2,14},{3,15},{4,8},{5,9},{6,10},{7,11},{8,4},{9,5},... | collective-permute-start | bytes 196616 | tf_op jit(solution)/shard_map/ppermute | solution.py:370
  38.8 1.0 %collective-permute-start.16 = (bf16[256,128]{1,0:T(8,128)(2,1)S(1)}, bf16[256,128]{1,0:T(8,128)(2,1)S(1)}, u32[]{:S(2)}, u32[]{:S(2)}) collective-permute-start(bf16[256,128]{1,0:T(8,128)(2,1)S(1)} %get-tuple-element.29), channel_id=1, source_target_pairs={{0,4},{1,5},{2,6},{3,7},{4,0},{5,1},{6,2},{7,3},{8,12},{9,13},{10,... | collective-permute-start | bytes 196616 | tf_op jit(solution)/shard_map/ppermute | solution.py:370
  39.8 2.2 %collective-permute-done.18.refs_1_ = bf16[256,128]{1,0:T(8,128)(2,1)S(1)} collective-permute-done((bf16[256,128]{1,0:T(8,128)(2,1)S(1)}, bf16[256,128]{1,0:T(8,128)(2,1)S(1)}, u32[]{:S(2)}, u32[]{:S(2)}) %collective-permute-start.18) | collective-permute-done | bytes 65568 | tf_op jit(solution)/shard_map/ppermute | solution.py:370
  42.0 2.7 %collective-permute-done.17.refs_0_ = bf16[256,128]{1,0:T(8,128)(2,1)S(1)} collective-permute-done((bf16[256,128]{1,0:T(8,128)(2,1)S(1)}, bf16[256,128]{1,0:T(8,128)(2,1)S(1)}, u32[]{:S(2)}, u32[]{:S(2)}) %collective-permute-start.17) | collective-permute-done | bytes 65568 | tf_op jit(solution)/shard_map/ppermute | solution.py:370
  44.8 0.6 %total_of.3 = bf16[256,128]{1,0:T(8,128)(2,1)} custom-call(f32[256,128]{1,0:T(8,128)S(1)} %get-tuple-element.28.refs_0_, bf16[256,128]{1,0:T(8,128)(2,1)S(1)} %collective-permute-done.16.refs_1_, f32[256,128]{1,0:T(8,128)S(1)} %total_of.2.refs_2_), custom_call_target="tpu_custom_call" | custom-call | tf_op jit(solution)/shard_map/total_of/pallas_call | solution.py:329
  (60 shorter events, 3.0 us)
Async XLA Ops:
  0.0 11.8 %collective-permute-start.3 = (bf16[256,128]{1,0:T(8,128)(2,1)}, bf16[256,128]{1,0:T(8,128)(2,1)S(1)}, u32[]{:S(2)}, u32[]{:S(2)}) collective-permute-start(bf16[256,128]{1,0:T(8,128)(2,1)} %own.1), channel_id=1, source_target_pairs={{0,2},{1,3},{2,0},{3,1},{4,6},{5,7},{6,4},{7,5},{8,10},{9,11},{10,... | collective-permute-start | bytes 196616 | tf_op jit(solution)/shard_map/ppermute | solution.py:370
  3.0 8.8 %collective-permute-start.2 = (bf16[256,128]{1,0:T(8,128)(2,1)}, bf16[256,128]{1,0:T(8,128)(2,1)S(1)}, u32[]{:S(2)}, u32[]{:S(2)}) collective-permute-start(bf16[256,128]{1,0:T(8,128)(2,1)} %own.1), channel_id=1, source_target_pairs={{0,12},{1,13},{2,14},{3,15},{4,8},{5,9},{6,10},{7,11},{8,4},{9,5},... | collective-permute-start | bytes 196616 | tf_op jit(solution)/shard_map/ppermute | solution.py:370
  6.6 5.6 %collective-permute-start.1 = (bf16[256,128]{1,0:T(8,128)(2,1)}, bf16[256,128]{1,0:T(8,128)(2,1)S(1)}, u32[]{:S(2)}, u32[]{:S(2)}) collective-permute-start(bf16[256,128]{1,0:T(8,128)(2,1)} %own.1), channel_id=1, source_target_pairs={{0,8},{1,9},{2,10},{3,11},{4,12},{5,13},{6,14},{7,15},{8,0},{9,1},... | collective-permute-start | bytes 196616 | tf_op jit(solution)/shard_map/ppermute | solution.py:370
  6.6 5.7 %collective-permute-start = (bf16[256,128]{1,0:T(8,128)(2,1)}, bf16[256,128]{1,0:T(8,128)(2,1)S(1)}, u32[]{:S(2)}, u32[]{:S(2)}) collective-permute-start(bf16[256,128]{1,0:T(8,128)(2,1)} %own.1), channel_id=1, source_target_pairs={{0,4},{1,5},{2,6},{3,7},{4,0},{5,1},{6,2},{7,3},{8,12},{9,13},{10,... | collective-permute-start | bytes 196616 | tf_op jit(solution)/shard_map/ppermute | solution.py:370
  7.4 7.8 %collective-permute-start.5 = (bf16[256,128]{1,0:T(8,128)(2,1)}, bf16[256,128]{1,0:T(8,128)(2,1)S(1)}, u32[]{:S(2)}, u32[]{:S(2)}) collective-permute-start(bf16[256,128]{1,0:T(8,128)(2,1)} %own.1), channel_id=1, source_target_pairs={{0,1},{1,0},{2,3},{3,2},{4,5},{5,4},{6,7},{7,6},{8,9},{9,8},{10,11... | collective-permute-start | bytes 196616 | tf_op jit(solution)/shard_map/ppermute | solution.py:370
  11.6 3.5 %slice-start = ((s8[10485760]{0:T(1024)(128)(4,1)}), s8[4194304]{0:T(1024)(128)(4,1)S(1)}, s32[]{:S(2)}) async-start(s8[10485760]{0:T(1024)(128)(4,1)} %bitcast.5), calls=%async_computation | async-start | bytes 8388608
  11.7 3.4 %slice-start.1 = ((s8[10485760]{0:T(1024)(128)(4,1)}), s8[4194304]{0:T(1024)(128)(4,1)S(1)}, s32[]{:S(2)}) async-start(s8[10485760]{0:T(1024)(128)(4,1)} %bitcast.5), calls=%async_computation.1 | async-start | bytes 8388608
  11.7 4.0 %slice-start.2 = ((s8[10485760]{0:T(1024)(128)(4,1)}), s8[2097152]{0:T(1024)(128)(4,1)S(1)}, s32[]{:S(2)}) async-start(s8[10485760]{0:T(1024)(128)(4,1)} %bitcast.5), calls=%async_computation.2 | async-start | bytes 4194304
  11.8 3.9 %copy-start = (bf16[256,128]{1,0:T(8,128)(2,1)S(1)}, bf16[256,128]{1,0:T(8,128)(2,1)}, u32[]{:S(2)}) copy-start(bf16[256,128]{1,0:T(8,128)(2,1)} %own.1) | copy-start | bytes 196612
  12.3 2.9 %collective-permute-start.4 = (bf16[4,256,128]{2,1,0:T(8,128)(2,1)S(1)}, bf16[4,256,128]{2,1,0:T(8,128)(2,1)S(1)}, u32[]{:S(2)}, u32[]{:S(2)}) collective-permute-start(bf16[4,256,128]{2,1,0:T(8,128)(2,1)S(1)} %merge.2.refs_0_), channel_id=1, source_target_pairs={{0,1},{1,0},{2,3},{3,2},{4,5},{5,4},{6,7},{7,6},{8,9},{9,8},{10,11... | collective-permute-start | bytes 786440 | tf_op jit(solution)/shard_map/ppermute | solution.py:370
  12.7 6.6 %collective-permute-start.8 = (bf16[256,128]{1,0:T(8,128)(2,1)S(1)}, bf16[256,128]{1,0:T(8,128)(2,1)S(1)}, u32[]{:S(2)}, u32[]{:S(2)}) collective-permute-start(bf16[256,128]{1,0:T(8,128)(2,1)S(1)} %collective-permute-done.2.refs_2_), channel_id=1, source_target_pairs={{0,2},{1,3},{2,0},{3,1},{4,6},{5,7},{6,4},{7,5},{8,10},{9,11},{10,... | collective-permute-start | bytes 196616 | tf_op jit(solution)/shard_map/ppermute | solution.py:370
  13.1 6.2 %collective-permute-start.7 = (bf16[256,128]{1,0:T(8,128)(2,1)S(1)}, bf16[256,128]{1,0:T(8,128)(2,1)S(1)}, u32[]{:S(2)}, u32[]{:S(2)}) collective-permute-start(bf16[256,128]{1,0:T(8,128)(2,1)S(1)} %collective-permute-done.1.refs_1_), channel_id=1, source_target_pairs={{0,2},{1,3},{2,0},{3,1},{4,6},{5,7},{6,4},{7,5},{8,10},{9,11},{10,... | collective-permute-start | bytes 196616 | tf_op jit(solution)/shard_map/ppermute | solution.py:370
  14.7 5.2 %collective-permute-start.6 = (bf16[256,128]{1,0:T(8,128)(2,1)S(1)}, bf16[256,128]{1,0:T(8,128)(2,1)S(1)}, u32[]{:S(2)}, u32[]{:S(2)}) collective-permute-start(bf16[256,128]{1,0:T(8,128)(2,1)S(1)} %collective-permute-done.refs_0_), channel_id=1, source_target_pairs={{0,2},{1,3},{2,0},{3,1},{4,6},{5,7},{6,4},{7,5},{8,10},{9,11},{10,... | collective-permute-start | bytes 196616 | tf_op jit(solution)/shard_map/ppermute | solution.py:370
  19.9 1.5 %collective-permute-start.9 = (bf16[3,256,128]{2,1,0:T(8,128)(2,1)S(1)}, bf16[3,256,128]{2,1,0:T(8,128)(2,1)S(1)}, u32[]{:S(2)}, u32[]{:S(2)}) collective-permute-start(bf16[3,256,128]{2,1,0:T(8,128)(2,1)S(1)} %merge.3.refs_9_), channel_id=1, source_target_pairs={{0,1},{1,0},{2,3},{3,2},{4,5},{5,4},{6,7},{7,6},{8,9},{9,8},{10,11... | collective-permute-start | bytes 589832 | tf_op jit(solution)/shard_map/ppermute | solution.py:370
  27.6 6.0 %collective-permute-start.13 = (bf16[2,144,128]{2,1,0:T(8,128)(2,1)S(1)}, bf16[2,144,128]{2,1,0:T(8,128)(2,1)S(1)}, u32[]{:S(2)}, u32[]{:S(2)}) collective-permute-start(bf16[2,144,128]{2,1,0:T(8,128)(2,1)S(1)} %get-tuple-element.24), channel_id=1, source_target_pairs={{0,1},{1,0},{2,3},{3,2},{4,5},{5,4},{6,7},{7,6},{8,9},{9,8},{10,11... | collective-permute-start | bytes 221192 | tf_op jit(solution)/shard_map/ppermute | solution.py:370
  27.7 7.4 %collective-permute-start.14 = (bf16[2,144,128]{2,1,0:T(8,128)(2,1)S(1)}, bf16[2,144,128]{2,1,0:T(8,128)(2,1)S(1)}, u32[]{:S(2)}, u32[]{:S(2)}) collective-permute-start(bf16[2,144,128]{2,1,0:T(8,128)(2,1)S(1)} %get-tuple-element.25), channel_id=1, source_target_pairs={{0,2},{1,3},{2,0},{3,1},{4,6},{5,7},{6,4},{7,5},{8,10},{9,11},{10,... | collective-permute-start | bytes 221192 | tf_op jit(solution)/shard_map/ppermute | solution.py:370
  27.9 7.2 %collective-permute-start.15 = (bf16[2,144,128]{2,1,0:T(8,128)(2,1)S(1)}, bf16[2,144,128]{2,1,0:T(8,128)(2,1)S(1)}, u32[]{:S(2)}, u32[]{:S(2)}) collective-permute-start(bf16[2,144,128]{2,1,0:T(8,128)(2,1)S(1)} %get-tuple-element.26), channel_id=1, source_target_pairs={{0,3},{1,2},{2,1},{3,0},{4,7},{5,6},{6,5},{7,4},{8,11},{9,10},{10,... | collective-permute-start | bytes 221192 | tf_op jit(solution)/shard_map/ppermute | solution.py:370
  32.7 5.8 %collective-permute-start.10 = (bf16[2,144,128]{2,1,0:T(8,128)(2,1)S(1)}, bf16[2,144,128]{2,1,0:T(8,128)(2,1)S(1)}, u32[]{:S(2)}, u32[]{:S(2)}) collective-permute-start(bf16[2,144,128]{2,1,0:T(8,128)(2,1)S(1)} %get-tuple-element.20), channel_id=1, source_target_pairs={{0,1},{1,0},{2,3},{3,2},{4,5},{5,4},{6,7},{7,6},{8,9},{9,8},{10,11... | collective-permute-start | bytes 221192 | tf_op jit(solution)/shard_map/ppermute | solution.py:370
  33.6 5.0 %collective-permute-start.11 = (bf16[2,144,128]{2,1,0:T(8,128)(2,1)S(1)}, bf16[2,144,128]{2,1,0:T(8,128)(2,1)S(1)}, u32[]{:S(2)}, u32[]{:S(2)}) collective-permute-start(bf16[2,144,128]{2,1,0:T(8,128)(2,1)S(1)} %get-tuple-element.21), channel_id=1, source_target_pairs={{0,2},{1,3},{2,0},{3,1},{4,6},{5,7},{6,4},{7,5},{8,10},{9,11},{10,... | collective-permute-start | bytes 221192 | tf_op jit(solution)/shard_map/ppermute | solution.py:370
  33.6 5.0 %collective-permute-start.12 = (bf16[2,144,128]{2,1,0:T(8,128)(2,1)S(1)}, bf16[2,144,128]{2,1,0:T(8,128)(2,1)S(1)}, u32[]{:S(2)}, u32[]{:S(2)}) collective-permute-start(bf16[2,144,128]{2,1,0:T(8,128)(2,1)S(1)} %get-tuple-element.22), channel_id=1, source_target_pairs={{0,3},{1,2},{2,1},{3,0},{4,7},{5,6},{6,5},{7,4},{8,11},{9,10},{10,... | collective-permute-start | bytes 221192 | tf_op jit(solution)/shard_map/ppermute | solution.py:370
  35.2 6.8 %collective-permute-start.18 = (bf16[256,128]{1,0:T(8,128)(2,1)S(1)}, bf16[256,128]{1,0:T(8,128)(2,1)S(1)}, u32[]{:S(2)}, u32[]{:S(2)}) collective-permute-start(bf16[256,128]{1,0:T(8,128)(2,1)S(1)} %get-tuple-element.30), channel_id=1, source_target_pairs={{0,12},{1,13},{2,14},{3,15},{4,8},{5,9},{6,10},{7,11},{8,4},{9,5},... | collective-permute-start | bytes 196616 | tf_op jit(solution)/shard_map/ppermute | solution.py:370
  38.5 6.2 %collective-permute-start.17 = (bf16[256,128]{1,0:T(8,128)(2,1)S(1)}, bf16[256,128]{1,0:T(8,128)(2,1)S(1)}, u32[]{:S(2)}, u32[]{:S(2)}) collective-permute-start(bf16[256,128]{1,0:T(8,128)(2,1)S(1)} %get-tuple-element.27.refs_4_), channel_id=1, source_target_pairs={{0,8},{1,9},{2,10},{3,11},{4,12},{5,13},{6,14},{7,15},{8,0},{9,1},... | collective-permute-start | bytes 196616 | tf_op jit(solution)/shard_map/ppermute | solution.py:370
  38.8 6.1 %collective-permute-start.16 = (bf16[256,128]{1,0:T(8,128)(2,1)S(1)}, bf16[256,128]{1,0:T(8,128)(2,1)S(1)}, u32[]{:S(2)}, u32[]{:S(2)}) collective-permute-start(bf16[256,128]{1,0:T(8,128)(2,1)S(1)} %get-tuple-element.29), channel_id=1, source_target_pairs={{0,4},{1,5},{2,6},{3,7},{4,0},{5,1},{6,2},{7,3},{8,12},{9,13},{10,... | collective-permute-start | bytes 196616 | tf_op jit(solution)/shard_map/ppermute | solution.py:370

commit v8 on v7

--- a/solution.py
+++ b/solution.py
@@ -16,7 +16,7 @@
 DIRECT = 16
 
 
-def owners_of(tile_block, basis_order, base, bb_dev):
+def pack_slots(tile_block, tile_aux, live, basis_order, base, bb_dev):
     nbb = basis_order.shape[0]
     position = jnp.sum(
         jnp.where(
@@ -24,7 +24,16 @@
         ),
         axis=1,
     )
-    return jnp.bitwise_xor(position // bb_dev, base), position % bb_dev
+    owner = jnp.bitwise_xor(position // bb_dev, base)
+    alive = (lax.iota(jnp.int32, tile_block.shape[0]) < live[0]).astype(jnp.int32)
+    return ((owner * bb_dev + position % bb_dev) * AB_DEV + tile_aux) * 2 + alive
+
+
+def unpack_slots(packed, bb_dev):
+    rest = packed // 2
+    tile_aux = rest % AB_DEV
+    rest = rest // AB_DEV
+    return rest // bb_dev, rest % bb_dev, tile_aux, packed % 2 == 1
 
 
 def chunk_lists(where_to, later, alive, tile_aux, n_aux):
@@ -110,12 +119,13 @@
                 acc[block_ref[pos]] += value[i * blk : (i + 1) * blk]
 
 
-def begin(n_aux, lists, bit, tiles_array, own_array, shards, sources):
+def begin(n_aux, lists, bit, packed, tiles_array, own_array, shards, sources):
     slots, auxb, blk, nocc = tiles_array.shape
     n_in = len(shards)
 
-    def kernel(slot_ref, block_ref, gid_ref, bit_ref, tiles, own, *refs):
-        c_refs, (zacc, ct) = refs[:n_in], refs[n_in:]
+    def kernel(slot_ref, block_ref, gid_ref, bit_ref, packed_ref, tiles, own, *refs):
+        c_refs, (zacc, passed, ct) = refs[:n_in], refs[n_in:]
+        passed[...] = packed_ref[...]
         zacc[...] = jnp.zeros(zacc.shape, zacc.dtype)
         ct[n_aux] = jnp.zeros((nocc, blk), ct.dtype)
         turn(ct, bit_ref, 0, own)
@@ -128,16 +138,19 @@
     vmem = pl.BlockSpec(memory_space=pltpu.VMEM)
     return pl.pallas_call(
         kernel,
-        out_shape=jax.ShapeDtypeStruct((AB_DEV, nocc, auxb * nocc), jnp.float32),
-        in_specs=[smem] * 4 + [vmem] * (2 + n_in),
-        out_specs=vmem,
+        out_shape=[
+            jax.ShapeDtypeStruct((AB_DEV, nocc, auxb * nocc), jnp.float32),
+            jax.ShapeDtypeStruct(packed.shape, packed.dtype),
+        ],
+        in_specs=[smem] * 4 + [vmem] * (3 + n_in),
+        out_specs=[vmem] * 2,
         scratch_shapes=[pltpu.VMEM((n_aux + 1, nocc, blk), jnp.bfloat16)],
         compiler_params=pltpu.CompilerParams(vmem_limit_bytes=20 * 1024 * 1024),
         cost_estimate=pl.CostEstimate(
             flops=2 * tiles_array.size * nocc, bytes_accessed=tiles_array.size, transcendentals=0
         ),
         name="begin",
-    )(*lists, bit, tiles_array, own_array, *shards)
+    )(*lists, bit, packed, tiles_array, own_array, *shards)
 
 
 def put(bit_ref, acc, m, out_ref, place):
@@ -148,7 +161,7 @@
     ).astype(out_ref.dtype)
 
 
-def clear_and_fit(n_aux, ct, acc):
+def clear(n_aux, ct, acc):
     ct[n_aux] = jnp.zeros(ct.shape[1:], ct.dtype)
     acc[...] = jnp.zeros(acc.shape, acc.dtype)
 
@@ -167,11 +180,10 @@
 
     def kernel(*refs):
         fit_refs, refs = refs[:3], refs[3:]
-        list_refs, bit_ref, tiles, partial_ref = refs[:3], refs[3], refs[4], refs[5]
+        list_refs, bit_ref, tiles = refs[:3], refs[3], refs[4]
         c_refs, out_refs = refs[6 : 6 + n_in], refs[6 + n_in : -4]
-        zb, ct, zacc, acc = refs[-4:]
-        clear_and_fit(n_aux, ct, acc)
-        zacc[...] = partial_ref[...]
+        zb, zacc, ct, acc = refs[-4:]
+        clear(n_aux, ct, acc)
         for m, (ref, i) in sources:
             turn(ct, bit_ref, m, c_refs[ref] if i is None else c_refs[ref].at[i])
         fit(fit_refs, tiles, ct, zacc, *chunk_ends(fit_refs[2], slots))
@@ -185,7 +197,10 @@
     vmem = pl.BlockSpec(memory_space=pltpu.VMEM)
     shape = (n_aux // PLANE // 2, blk + TAIL, nocc)
     out_shape = [jax.ShapeDtypeStruct(shape, jnp.bfloat16)] * PLANE
-    out_shape = out_shape + [jax.ShapeDtypeStruct((AB_DEV, auxb * nocc, nocc), jnp.bfloat16)]
+    out_shape = out_shape + [
+        jax.ShapeDtypeStruct((AB_DEV, auxb * nocc, nocc), jnp.bfloat16),
+        jax.ShapeDtypeStruct(partial_fit.shape, partial_fit.dtype),
+    ]
     return pl.pallas_call(
         kernel,
         out_shape=out_shape,
@@ -193,9 +208,9 @@
         out_specs=[vmem] * len(out_shape),
         scratch_shapes=[
             pltpu.VMEM((n_aux + 1, nocc, blk), jnp.bfloat16),
-            pltpu.VMEM((AB_DEV, nocc, auxb * nocc), jnp.float32),
             pltpu.VMEM((n_aux + 1, blk, nocc), jnp.float32),
         ],
+        input_output_aliases={8: PLANE + 1},
         compiler_params=pltpu.CompilerParams(vmem_limit_bytes=20 * 1024 * 1024),
         cost_estimate=pl.CostEstimate(
             flops=3 * tiles_array.size * nocc, bytes_accessed=tiles_array.size, transcendentals=0
@@ -238,7 +253,7 @@
 
     def kernel(slot_ref, block_ref, gid_ref, bit_ref, tiles, c_ref, out_ref, ct, zacc, zb, acc):
         lists = (slot_ref, block_ref, gid_ref)
-        clear_and_fit(n_aux, ct, acc)
+        clear(n_aux, ct, acc)
         zacc[...] = jnp.zeros(zacc.shape, zacc.dtype)
 
         @pl.loop(0, n_aux)
@@ -272,6 +287,21 @@
     )(*lists, bit, tiles_array, whole)
 
 
+def gate(array, after):
+    def kernel(source, _, target):
+        target[...] = source[...]
+
+    vmem = pl.BlockSpec(memory_space=pltpu.VMEM)
+    return pl.pallas_call(
+        kernel,
+        out_shape=jax.ShapeDtypeStruct(array.shape, array.dtype),
+        in_specs=[vmem, pl.BlockSpec(memory_space=pl.ANY)],
+        out_specs=vmem,
+        compiler_params=pltpu.CompilerParams(vmem_limit_bytes=4 * 1024 * 1024),
+        name="gate",
+    )(array, after)
+
+
 def merge(arrays, after, cost):
     def kernel(*refs):
         for i, ref in enumerate(refs[: len(arrays)]):
@@ -370,11 +400,11 @@
         return lax.ppermute(array, "aux", [(i, i ^ m) for i in range(n_aux)])
 
     base = lax.axis_index("aux").astype(jnp.int32) if direct else jnp.int32(0)
-    alive = lax.iota(jnp.int32, tile_block.shape[0]) < live[0]
-    where_to, which = owners_of(tile_block, basis_order, base, bb_dev)
+    packed = pack_slots(tile_block, tile_aux, live, basis_order, base, bb_dev)
+    where_to, which, group, alive = unpack_slots(packed, bb_dev)
     bit = bits_of(where_to, which, alive, n_aux)
     if not direct:
-        lists = chunk_lists(where_to, where_to < 0, alive, tile_aux, n_aux)
+        lists = chunk_lists(where_to, where_to < 0, alive, group, n_aux)
         whole = lax.all_gather(c_orbitals, "aux", axis=0, tiled=True)
         whole = whole.reshape(n_aux, bb_dev * blk, nocc)
         parts = all_in_one(n_aux, lists, bit, tiles, whole)
@@ -384,32 +414,26 @@
     depth = n_aux // PLANE
     half = depth // 2
     last = (where_to >= PLANE) & (where_to % PLANE >= 2)
-    fit_lists = chunk_lists(where_to, last, alive, tile_aux, n_aux)
-    lists = chunk_lists(where_to, where_to < n_aux // 2, alive, tile_aux, n_aux)
-    column = [c_orbitals] + [None] * (depth - 1)
-    for dz in range(depth - 1, 0, -1):
-        column[dz] = swap(c_orbitals, dz * PLANE)
+    fit_lists = chunk_lists(where_to, last, alive, group, n_aux)
+    column = [swap(c_orbitals, dz * PLANE) for dz in range(depth - 1, 0, -1)]
     beside = swap(c_orbitals, 2)
     across = swap(c_orbitals, 1)
-    early = merge(column[1:] + [beside], [], SPREAD_COST)
-    late = [swap(array, 2) for array in column[1:]]
-    early_from = [(1, (2, None)), (2, (0, depth - 1)), (3, (1, depth - 1))]
+    column = merge(column, [], SPREAD_COST)
+    late = swap(column, 2)
+    early = [column, swap(column, 1), across, beside, swap(beside, 1)]
+    early_from = [(1, (2, None)), (2, (3, None)), (3, (4, None))]
     late_from = []
     for dz in range(1, depth):
         for core in range(2):
-            early_from.append((dz * PLANE + core, (core, dz - 1)))
-            late_from.append((dz * PLANE + 2 + core, (core, dz - 1)))
-    partial_fit = begin(
-        n_aux,
-        fit_lists,
-        bit,
-        tiles,
-        c_orbitals,
-        [early, swap(early, 1), across],
-        early_from,
-    )
-    late = merge(late, [partial_fit], 0)
-    *far, fitted = first_part(
+            early_from.append((dz * PLANE + core, (core, depth - 1 - dz)))
+            late_from.append((dz * PLANE + 2 + core, (core, depth - 1 - dz)))
+    partial_fit, packed = begin(
+        n_aux, fit_lists, bit, packed, tiles, c_orbitals, early, early_from
+    )
+    late = gate(late, partial_fit)
+    where_to, _, group, alive = unpack_slots(packed, bb_dev)
+    lists = chunk_lists(where_to, where_to < n_aux // 2, alive, group, n_aux)
+    *far, fitted, _ = first_part(
         n_aux, fit_lists, lists, bit, tiles, partial_fit, [late, swap(late, 1)], late_from
     )
     far = [far[0]] + [swap(far[r], r) for r in range(1, PLANE)]

time: 45.4 us -> 45.2 us (level)
  waiting for transfers between devices: 7.69 us -> 10.2 us
  Pallas kernels: 13.8 us -> 12.3 us
  starting transfers between devices: 18.7 us -> 18.1 us
  other arithmetic: 3.9 us -> 3.38 us
  local copies, waits for them, and re-layouts: 0.58 us -> 0.06 us
    ppermute x19 -> x18, waiting for transfers between devices: 7.69 us -> 10.2 us  [swap(): return lax.ppermute(array, 'aux', [(i, i ^ m) for i in range(n_aux)])]
    select_n x2, other arithmetic: 1.35 us -> 0.04 us  [chunk_lists(): group = jnp.where(alive, tile_aux + jnp.where(later, AB_DEV, 0), keys)]
    pallas_call x1, Pallas kernels: 6.17 us -> 5.14 us  [first_part(): pl.pallas_call(kernel, out_shape=out_shape, in_specs=[smem] * 7 + [vmem]...]
    select_n x0 -> x2, other arithmetic: none -> 0.7 us  [the longest x1 0.69 us: unpack_slots(): return (rest // bb_dev, rest % bb_dev, tile_aux, packed % 2 == 1)]
    ppermute x19 -> x18, starting transfers between devices: 18.7 us -> 18.1 us  [swap(): return lax.ppermute(array, 'aux', [(i, i ^ m) for i in range(n_aux)])]
    unnamed x8, local copies, waits for them, and re-layouts: 0.58 us -> 0.06 us
    pallas_call x1 -> x2, Pallas kernels: 3.53 us -> 3.17 us  [the longest x1 3.16 us: begin(): pl.pallas_call(kernel, out_shape=[jax.ShapeDtypeStruct((AB_DEV, nocc, aux...]
  transfers between devices with their start and end apart: 19 -> 18, of which waited for: 8 -> 7; matrix products, arithmetic and copies ran while one was open for 9% -> 7% of each run, Pallas kernels for 15% -> 15%
where the time goes in v8:
time: 45.2 us; the launch traced here: 45.1 us
  starting transfers between devices  18.1 us (40%)
  Pallas kernels  12.3 us (27%)
  waiting for transfers between devices  10.2 us (23%)
  other arithmetic  3.38 us (7%)
  between operations  0.9 us (2%)
    ppermute x18, starting transfers between devices, swap(): return lax.ppermute(array, 'aux', [(i, i ^ m) for i in range(n_aux)])  18.1 us
    ppermute x18, waiting for transfers between devices, swap(): return lax.ppermute(array, 'aux', [(i, i ^ m) for i in range(n_aux)])  10.2 us
    pallas_call x1, Pallas kernels, first_part(): pl.pallas_call(kernel, out_shape=out_shape, in_specs=[smem] * 7 + [vmem]...  5.14 us
    pallas_call x1, Pallas kernels, begin(): pl.pallas_call(kernel, out_shape=[jax.ShapeDtypeStruct((AB_DEV, nocc, aux...  3.16 us
    pallas_call x1, Pallas kernels, second_part(): pl.pallas_call(kernel, out_shape=[jax.ShapeDtypeStruct(shape, jnp.bfloat1...  3.14 us
  transfers between devices with their start and end apart: 18, of which 7 were waited for; matrix products, arithmetic and copies ran while one was open for 7% of the time, Pallas kernels for 15%

profile of v8, /device:TPU:0, one launch (start us, length us, event | category | flops | bytes accessed | tf_op | source)
XLA Modules:
  0.0 45.1 jit_solution(5233725478579675465)
XLA Ops:
  0.0 0.5 %collective-permute-start.4 = (bf16[256,128]{1,0:T(8,128)(2,1)}, bf16[256,128]{1,0:T(8,128)(2,1)S(1)}, u32[]{:S(2)}, u32[]{:S(2)}) collective-permute-start(bf16[256,128]{1,0:T(8,128)(2,1)} %own.1), channel_id=1, source_target_pairs={{0,1},{1,0},{2,3},{3,2},{4,5},{5,4},{6,7},{7,6},{8,9},{9,8},{10,11... | collective-permute-start | bytes 196616 | tf_op jit(solution)/shard_map/ppermute | solution.py:400
  0.5 2.6 %collective-permute-start.2 = (bf16[256,128]{1,0:T(8,128)(2,1)}, bf16[256,128]{1,0:T(8,128)(2,1)S(1)}, u32[]{:S(2)}, u32[]{:S(2)}) collective-permute-start(bf16[256,128]{1,0:T(8,128)(2,1)} %own.1), channel_id=1, source_target_pairs={{0,4},{1,5},{2,6},{3,7},{4,0},{5,1},{6,2},{7,3},{8,12},{9,13},{10,... | collective-permute-start | bytes 196616 | tf_op jit(solution)/shard_map/ppermute | solution.py:400
  3.0 2.6 %collective-permute-start.1 = (bf16[256,128]{1,0:T(8,128)(2,1)}, bf16[256,128]{1,0:T(8,128)(2,1)S(1)}, u32[]{:S(2)}, u32[]{:S(2)}) collective-permute-start(bf16[256,128]{1,0:T(8,128)(2,1)} %own.1), channel_id=1, source_target_pairs={{0,8},{1,9},{2,10},{3,11},{4,12},{5,13},{6,14},{7,15},{8,0},{9,1},... | collective-permute-start | bytes 196616 | tf_op jit(solution)/shard_map/ppermute | solution.py:400
  5.6 1.7 %collective-permute-start.5 = (bf16[256,128]{1,0:T(8,128)(2,1)}, bf16[256,128]{1,0:T(8,128)(2,1)S(1)}, u32[]{:S(2)}, u32[]{:S(2)}) collective-permute-start(bf16[256,128]{1,0:T(8,128)(2,1)} %own.1), channel_id=1, source_target_pairs={{0,2},{1,3},{2,0},{3,1},{4,6},{5,7},{6,4},{7,5},{8,10},{9,11},{10,... | collective-permute-start | bytes 196616 | tf_op jit(solution)/shard_map/ppermute | solution.py:400
  8.0 0.8 %select_reduce_fusion.6 = s32[64]{0:T(128)S(1)} fusion(s32[64]{0:T(128)} %param.9, s32[32]{0:T(128)} %param.8), kind=kLoop, calls=%fused_computation.15 | loop fusion | flops 6080 | bytes 640 | tf_op jit(solution)/shard_map/reduce_sum | solution.py:21
  8.8 0.7 %and_select_fusion.7 = (s32[64]{0:T(128)S(1)}, s32[64]{0:T(128)S(1)}, s32[64]{0:T(128)S(1)}, s32[64]{0:T(128)S(1)}) fusion(s32[]{:T(128)} %bitcast.1, s32[64]{0:T(128)} %param.10, s32[]{:T(128)S(6)} %axis_index.12, s32[64]{0:T(128)S(1)} %select_reduce_fusion.6), kind=kLoop, calls=%fused_computation.48 | loop fusion | flops 4416 | bytes 1544 | tf_op jit(solution)/shard_map/jit(remainder)/select_n | solution.py:36
  10.4 1.5 %collective-permute-done.refs_0_ = bf16[256,128]{1,0:T(8,128)(2,1)S(1)} collective-permute-done((bf16[256,128]{1,0:T(8,128)(2,1)}, bf16[256,128]{1,0:T(8,128)(2,1)S(1)}, u32[]{:S(2)}, u32[]{:S(2)}) %collective-permute-start) | collective-permute-done | bytes 65568 | tf_op jit(solution)/shard_map/ppermute | solution.py:400
  12.2 0.6 %collective-permute-start.6 = (bf16[256,128]{1,0:T(8,128)(2,1)S(1)}, bf16[256,128]{1,0:T(8,128)(2,1)S(1)}, u32[]{:S(2)}, u32[]{:S(2)}) collective-permute-start(bf16[256,128]{1,0:T(8,128)(2,1)S(1)} %collective-permute-done.5.refs_3_), channel_id=1, source_target_pairs={{0,1},{1,0},{2,3},{3,2},{4,5},{5,4},{6,7},{7,6},{8,9},{9,8},{10,11... | collective-permute-start | bytes 196616 | tf_op jit(solution)/shard_map/ppermute | solution.py:400
  12.8 1.5 %collective-permute-start.7 = (bf16[3,256,128]{2,1,0:T(8,128)(2,1)S(1)}, bf16[3,256,128]{2,1,0:T(8,128)(2,1)S(1)}, u32[]{:S(2)}, u32[]{:S(2)}) collective-permute-start(bf16[3,256,128]{2,1,0:T(8,128)(2,1)S(1)} %merge.1.refs_0_), channel_id=1, source_target_pairs={{0,2},{1,3},{2,0},{3,1},{4,6},{5,7},{6,4},{7,5},{8,10},{9,11},{10,... | collective-permute-start | bytes 589832 | tf_op jit(solution)/shard_map/ppermute | solution.py:400
  14.4 3.2 %begin.1 = (f32[8,128,640]{2,1,0:T(8,128)S(1)}, s32[64]{0:T(128)S(1)}) custom-call(s32[128]{0:T(128)S(1)} %get-tuple-element.55.slot_ref.refs_0_, s32[128]{0:T(128)S(1)} %get-tuple-element.54.block_ref.refs_1_, s32[48]{0:T(128)S(1)} %pad_add_fusion.gid_ref.refs_2_, s32[16]{0:T(128)S(1)} %select_reduce_fusion.9.bit_ref.refs_6_, ...), custom_call_target="tpu_custom_call" | custom-call | flops 1342177280 | bytes 5242880 | tf_op jit(solution)/shard_map/begin/pallas_call | solution.py:139
  18.5 1.1 %collective-permute-done.7.source = bf16[3,256,128]{2,1,0:T(8,128)(2,1)S(1)} collective-permute-done((bf16[3,256,128]{2,1,0:T(8,128)(2,1)S(1)}, bf16[3,256,128]{2,1,0:T(8,128)(2,1)S(1)}, u32[]{:S(2)}, u32[]{:S(2)}) %collective-permute-start.7) | collective-permute-done | bytes 196640 | tf_op jit(solution)/shard_map/ppermute | solution.py:400
  19.7 1.4 %collective-permute-done.8.refs_10_ = bf16[3,256,128]{2,1,0:T(8,128)(2,1)S(1)} collective-permute-done((bf16[3,256,128]{2,1,0:T(8,128)(2,1)S(1)}, bf16[3,256,128]{2,1,0:T(8,128)(2,1)S(1)}, u32[]{:S(2)}, u32[]{:S(2)}) %collective-permute-start.8) | collective-permute-done | bytes 196640 | tf_op jit(solution)/shard_map/ppermute | solution.py:400
  21.2 5.1 %first_part.1 = (bf16[2,144,128]{2,1,0:T(8,128)(2,1)S(1)}, bf16[2,144,128]{2,1,0:T(8,128)(2,1)S(1)}, bf16[2,144,128]{2,1,0:T(8,128)(2,1)S(1)}, bf16[2,144,128]{2...) custom-call(s32[128]{0:T(128)S(1)} %get-tuple-element.55.slot_ref.re, ...), custom_call_target="tpu_custom_call", output_to_operand_aliasing={{5}: (8, {})} | custom-call | flops 2013265920 | bytes 5242880 | tf_op jit(solution)/shard_map/first_part/pallas_call | solution.py:204
  26.3 1.1 %collective-permute-start.12 = (bf16[2,144,128]{2,1,0:T(8,128)(2,1)S(1)}, bf16[2,144,128]{2,1,0:T(8,128)(2,1)S(1)}, u32[]{:S(2)}, u32[]{:S(2)}) collective-permute-start(bf16[2,144,128]{2,1,0:T(8,128)(2,1)S(1)} %get-tuple-element.28), channel_id=1, source_target_pairs={{0,1},{1,0},{2,3},{3,2},{4,5},{5,4},{6,7},{7,6},{8,9},{9,8},{10,11... | collective-permute-start | bytes 221192 | tf_op jit(solution)/shard_map/ppermute | solution.py:400
  27.6 1.2 %collective-permute-start.14 = (bf16[2,144,128]{2,1,0:T(8,128)(2,1)S(1)}, bf16[2,144,128]{2,1,0:T(8,128)(2,1)S(1)}, u32[]{:S(2)}, u32[]{:S(2)}) collective-permute-start(bf16[2,144,128]{2,1,0:T(8,128)(2,1)S(1)} %get-tuple-element.30), channel_id=1, source_target_pairs={{0,3},{1,2},{2,1},{3,0},{4,7},{5,6},{6,5},{7,4},{8,11},{9,10},{10,... | collective-permute-start | bytes 221192 | tf_op jit(solution)/shard_map/ppermute | solution.py:400
  28.8 3.1 %second_part.1 = (bf16[2,144,128]{2,1,0:T(8,128)(2,1)S(1)}, bf16[2,144,128]{2,1,0:T(8,128)(2,1)S(1)}, bf16[2,144,128]{2,1,0:T(8,128)(2,1)S(1)}, bf16[2,144,128]{2,1,0:T(8,128)(2,1)S(1)}) custom-call(s32[128]{0:T(128)S(1)} %get-tuple-element.53.refs_3_.slot_ref, s32[128]{0:T(128)S(1)} %get-tuple-element.52.refs_4_.block_ref, ...), custom_call_target="tpu_custom_call" | custom-call | flops 10000000000 | bytes 5242880 | tf_op jit(solution)/shard_map/second_part/pallas_call | solution.py:237
  32.0 1.3 %collective-permute-start.9 = (bf16[2,144,128]{2,1,0:T(8,128)(2,1)S(1)}, bf16[2,144,128]{2,1,0:T(8,128)(2,1)S(1)}, u32[]{:S(2)}, u32[]{:S(2)}) collective-permute-start(bf16[2,144,128]{2,1,0:T(8,128)(2,1)S(1)} %get-tuple-element.24), channel_id=1, source_target_pairs={{0,1},{1,0},{2,3},{3,2},{4,5},{5,4},{6,7},{7,6},{8,9},{9,8},{10,11... | collective-permute-start | bytes 221192 | tf_op jit(solution)/shard_map/ppermute | solution.py:400
  33.2 1.4 %collective-permute-start.11 = (bf16[2,144,128]{2,1,0:T(8,128)(2,1)S(1)}, bf16[2,144,128]{2,1,0:T(8,128)(2,1)S(1)}, u32[]{:S(2)}, u32[]{:S(2)}) collective-permute-start(bf16[2,144,128]{2,1,0:T(8,128)(2,1)S(1)} %get-tuple-element.26), channel_id=1, source_target_pairs={{0,3},{1,2},{2,1},{3,0},{4,7},{5,6},{6,5},{7,4},{8,11},{9,10},{10,... | collective-permute-start | bytes 221192 | tf_op jit(solution)/shard_map/ppermute | solution.py:400
  34.8 2.3 %collective-permute-start.17 = (bf16[256,128]{1,0:T(8,128)(2,1)S(1)}, bf16[256,128]{1,0:T(8,128)(2,1)S(1)}, u32[]{:S(2)}, u32[]{:S(2)}) collective-permute-start(bf16[256,128]{1,0:T(8,128)(2,1)S(1)} %get-tuple-element.34), channel_id=1, source_target_pairs={{0,12},{1,13},{2,14},{3,15},{4,8},{5,9},{6,10},{7,11},{8,4},{9,5},... | collective-permute-start | bytes 196616 | tf_op jit(solution)/shard_map/ppermute | solution.py:400
  37.1 1.2 %collective-permute-done.10.refs_2_ = bf16[2,144,128]{2,1,0:T(8,128)(2,1)S(1)} collective-permute-done((bf16[2,144,128]{2,1,0:T(8,128)(2,1)S(1)}, bf16[2,144,128]{2,1,0:T(8,128)(2,1)S(1)}, u32[]{:S(2)}, u32[]{:S(2)}) %collective-permute-start.10) | collective-permute-done | bytes 73760 | tf_op jit(solution)/shard_map/ppermute | solution.py:400
  38.4 1.0 %collective-permute-start.15 = (bf16[256,128]{1,0:T(8,128)(2,1)S(1)}, bf16[256,128]{1,0:T(8,128)(2,1)S(1)}, u32[]{:S(2)}, u32[]{:S(2)}) collective-permute-start(bf16[256,128]{1,0:T(8,128)(2,1)S(1)} %get-tuple-element.33), channel_id=1, source_target_pairs={{0,4},{1,5},{2,6},{3,7},{4,0},{5,1},{6,2},{7,3},{8,12},{9,13},{10,... | collective-permute-start | bytes 196616 | tf_op jit(solution)/shard_map/ppermute | solution.py:400
  39.4 2.3 %collective-permute-done.17.refs_1_ = bf16[256,128]{1,0:T(8,128)(2,1)S(1)} collective-permute-done((bf16[256,128]{1,0:T(8,128)(2,1)S(1)}, bf16[256,128]{1,0:T(8,128)(2,1)S(1)}, u32[]{:S(2)}, u32[]{:S(2)}) %collective-permute-start.17) | collective-permute-done | bytes 65568 | tf_op jit(solution)/shard_map/ppermute | solution.py:400
  41.7 2.6 %collective-permute-done.16.refs_0_ = bf16[256,128]{1,0:T(8,128)(2,1)S(1)} collective-permute-done((bf16[256,128]{1,0:T(8,128)(2,1)S(1)}, bf16[256,128]{1,0:T(8,128)(2,1)S(1)}, u32[]{:S(2)}, u32[]{:S(2)}) %collective-permute-start.16) | collective-permute-done | bytes 65568 | tf_op jit(solution)/shard_map/ppermute | solution.py:400
  44.4 0.6 %total_of.3 = bf16[256,128]{1,0:T(8,128)(2,1)} custom-call(f32[256,128]{1,0:T(8,128)S(1)} %get-tuple-element.32.refs_0_, bf16[256,128]{1,0:T(8,128)(2,1)S(1)} %collective-permute-done.15.refs_1_, f32[256,128]{1,0:T(8,128)S(1)} %total_of.2.refs_2_), custom_call_target="tpu_custom_call" | custom-call | tf_op jit(solution)/shard_map/total_of/pallas_call | solution.py:359
  (61 shorter events, 2.8 us)
Async XLA Ops:
  0.0 14.3 %collective-permute-start.4 = (bf16[256,128]{1,0:T(8,128)(2,1)}, bf16[256,128]{1,0:T(8,128)(2,1)S(1)}, u32[]{:S(2)}, u32[]{:S(2)}) collective-permute-start(bf16[256,128]{1,0:T(8,128)(2,1)} %own.1), channel_id=1, source_target_pairs={{0,1},{1,0},{2,3},{3,2},{4,5},{5,4},{6,7},{7,6},{8,9},{9,8},{10,11... | collective-permute-start | bytes 196616 | tf_op jit(solution)/shard_map/ppermute | solution.py:400
  0.5 9.9 %collective-permute-start.2 = (bf16[256,128]{1,0:T(8,128)(2,1)}, bf16[256,128]{1,0:T(8,128)(2,1)S(1)}, u32[]{:S(2)}, u32[]{:S(2)}) collective-permute-start(bf16[256,128]{1,0:T(8,128)(2,1)} %own.1), channel_id=1, source_target_pairs={{0,4},{1,5},{2,6},{3,7},{4,0},{5,1},{6,2},{7,3},{8,12},{9,13},{10,... | collective-permute-start | bytes 196616 | tf_op jit(solution)/shard_map/ppermute | solution.py:400
  3.0 7.4 %collective-permute-start.1 = (bf16[256,128]{1,0:T(8,128)(2,1)}, bf16[256,128]{1,0:T(8,128)(2,1)S(1)}, u32[]{:S(2)}, u32[]{:S(2)}) collective-permute-start(bf16[256,128]{1,0:T(8,128)(2,1)} %own.1), channel_id=1, source_target_pairs={{0,8},{1,9},{2,10},{3,11},{4,12},{5,13},{6,14},{7,15},{8,0},{9,1},... | collective-permute-start | bytes 196616 | tf_op jit(solution)/shard_map/ppermute | solution.py:400
  5.6 6.3 %collective-permute-start = (bf16[256,128]{1,0:T(8,128)(2,1)}, bf16[256,128]{1,0:T(8,128)(2,1)S(1)}, u32[]{:S(2)}, u32[]{:S(2)}) collective-permute-start(bf16[256,128]{1,0:T(8,128)(2,1)} %own.1), channel_id=1, source_target_pairs={{0,12},{1,13},{2,14},{3,15},{4,8},{5,9},{6,10},{7,11},{8,4},{9,5},... | collective-permute-start | bytes 196616 | tf_op jit(solution)/shard_map/ppermute | solution.py:400
  5.6 6.5 %collective-permute-start.5 = (bf16[256,128]{1,0:T(8,128)(2,1)}, bf16[256,128]{1,0:T(8,128)(2,1)S(1)}, u32[]{:S(2)}, u32[]{:S(2)}) collective-permute-start(bf16[256,128]{1,0:T(8,128)(2,1)} %own.1), channel_id=1, source_target_pairs={{0,2},{1,3},{2,0},{3,1},{4,6},{5,7},{6,4},{7,5},{8,10},{9,11},{10,... | collective-permute-start | bytes 196616 | tf_op jit(solution)/shard_map/ppermute | solution.py:400
  10.3 4.0 %slice-start = ((s8[10485760]{0:T(1024)(128)(4,1)}), s8[4194304]{0:T(1024)(128)(4,1)S(1)}, s32[]{:S(2)}) async-start(s8[10485760]{0:T(1024)(128)(4,1)} %bitcast.2), calls=%async_computation | async-start | bytes 8388608
  10.3 4.0 %slice-start.1 = ((s8[10485760]{0:T(1024)(128)(4,1)}), s8[4194304]{0:T(1024)(128)(4,1)S(1)}, s32[]{:S(2)}) async-start(s8[10485760]{0:T(1024)(128)(4,1)} %bitcast.2), calls=%async_computation.1 | async-start | bytes 8388608
  10.4 4.0 %slice-start.2 = ((s8[10485760]{0:T(1024)(128)(4,1)}), s8[2097152]{0:T(1024)(128)(4,1)S(1)}, s32[]{:S(2)}) async-start(s8[10485760]{0:T(1024)(128)(4,1)} %bitcast.2), calls=%async_computation.2 | async-start | bytes 4194304
  10.4 4.0 %copy-start = (bf16[256,128]{1,0:T(8,128)(2,1)S(1)}, bf16[256,128]{1,0:T(8,128)(2,1)}, u32[]{:S(2)}) copy-start(bf16[256,128]{1,0:T(8,128)(2,1)} %own.1) | copy-start | bytes 196612
  12.0 2.4 %collective-permute-start.3 = (bf16[3,256,128]{2,1,0:T(8,128)(2,1)S(1)}, bf16[3,256,128]{2,1,0:T(8,128)(2,1)S(1)}, u32[]{:S(2)}, u32[]{:S(2)}) collective-permute-start(bf16[3,256,128]{2,1,0:T(8,128)(2,1)S(1)} %merge.1.refs_0_), channel_id=1, source_target_pairs={{0,1},{1,0},{2,3},{3,2},{4,5},{5,4},{6,7},{7,6},{8,9},{9,8},{10,11... | collective-permute-start | bytes 589832 | tf_op jit(solution)/shard_map/ppermute | solution.py:400
  12.2 2.2 %collective-permute-start.6 = (bf16[256,128]{1,0:T(8,128)(2,1)S(1)}, bf16[256,128]{1,0:T(8,128)(2,1)S(1)}, u32[]{:S(2)}, u32[]{:S(2)}) collective-permute-start(bf16[256,128]{1,0:T(8,128)(2,1)S(1)} %collective-permute-done.5.refs_3_), channel_id=1, source_target_pairs={{0,1},{1,0},{2,3},{3,2},{4,5},{5,4},{6,7},{7,6},{8,9},{9,8},{10,11... | collective-permute-start | bytes 196616 | tf_op jit(solution)/shard_map/ppermute | solution.py:400
  12.8 6.8 %collective-permute-start.7 = (bf16[3,256,128]{2,1,0:T(8,128)(2,1)S(1)}, bf16[3,256,128]{2,1,0:T(8,128)(2,1)S(1)}, u32[]{:S(2)}, u32[]{:S(2)}) collective-permute-start(bf16[3,256,128]{2,1,0:T(8,128)(2,1)S(1)} %merge.1.refs_0_), channel_id=1, source_target_pairs={{0,2},{1,3},{2,0},{3,1},{4,6},{5,7},{6,4},{7,5},{8,10},{9,11},{10,... | collective-permute-start | bytes 589832 | tf_op jit(solution)/shard_map/ppermute | solution.py:400
  19.7 1.5 %collective-permute-start.8 = (bf16[3,256,128]{2,1,0:T(8,128)(2,1)S(1)}, bf16[3,256,128]{2,1,0:T(8,128)(2,1)S(1)}, u32[]{:S(2)}, u32[]{:S(2)}) collective-permute-start(bf16[3,256,128]{2,1,0:T(8,128)(2,1)S(1)} %gate.1.refs_9_), channel_id=1, source_target_pairs={{0,1},{1,0},{2,3},{3,2},{4,5},{5,4},{6,7},{7,6},{8,9},{9,8},{10,11... | collective-permute-start | bytes 589832 | tf_op jit(solution)/shard_map/ppermute | solution.py:400
  26.3 6.9 %collective-permute-start.12 = (bf16[2,144,128]{2,1,0:T(8,128)(2,1)S(1)}, bf16[2,144,128]{2,1,0:T(8,128)(2,1)S(1)}, u32[]{:S(2)}, u32[]{:S(2)}) collective-permute-start(bf16[2,144,128]{2,1,0:T(8,128)(2,1)S(1)} %get-tuple-element.28), channel_id=1, source_target_pairs={{0,1},{1,0},{2,3},{3,2},{4,5},{5,4},{6,7},{7,6},{8,9},{9,8},{10,11... | collective-permute-start | bytes 221192 | tf_op jit(solution)/shard_map/ppermute | solution.py:400
  27.4 7.3 %collective-permute-start.13 = (bf16[2,144,128]{2,1,0:T(8,128)(2,1)S(1)}, bf16[2,144,128]{2,1,0:T(8,128)(2,1)S(1)}, u32[]{:S(2)}, u32[]{:S(2)}) collective-permute-start(bf16[2,144,128]{2,1,0:T(8,128)(2,1)S(1)} %get-tuple-element.29), channel_id=1, source_target_pairs={{0,2},{1,3},{2,0},{3,1},{4,6},{5,7},{6,4},{7,5},{8,10},{9,11},{10,... | collective-permute-start | bytes 221192 | tf_op jit(solution)/shard_map/ppermute | solution.py:400
  27.6 7.0 %collective-permute-start.14 = (bf16[2,144,128]{2,1,0:T(8,128)(2,1)S(1)}, bf16[2,144,128]{2,1,0:T(8,128)(2,1)S(1)}, u32[]{:S(2)}, u32[]{:S(2)}) collective-permute-start(bf16[2,144,128]{2,1,0:T(8,128)(2,1)S(1)} %get-tuple-element.30), channel_id=1, source_target_pairs={{0,3},{1,2},{2,1},{3,0},{4,7},{5,6},{6,5},{7,4},{8,11},{9,10},{10,... | collective-permute-start | bytes 221192 | tf_op jit(solution)/shard_map/ppermute | solution.py:400
  32.0 5.1 %collective-permute-start.9 = (bf16[2,144,128]{2,1,0:T(8,128)(2,1)S(1)}, bf16[2,144,128]{2,1,0:T(8,128)(2,1)S(1)}, u32[]{:S(2)}, u32[]{:S(2)}) collective-permute-start(bf16[2,144,128]{2,1,0:T(8,128)(2,1)S(1)} %get-tuple-element.24), channel_id=1, source_target_pairs={{0,1},{1,0},{2,3},{3,2},{4,5},{5,4},{6,7},{7,6},{8,9},{9,8},{10,11... | collective-permute-start | bytes 221192 | tf_op jit(solution)/shard_map/ppermute | solution.py:400
  33.2 5.0 %collective-permute-start.10 = (bf16[2,144,128]{2,1,0:T(8,128)(2,1)S(1)}, bf16[2,144,128]{2,1,0:T(8,128)(2,1)S(1)}, u32[]{:S(2)}, u32[]{:S(2)}) collective-permute-start(bf16[2,144,128]{2,1,0:T(8,128)(2,1)S(1)} %get-tuple-element.25), channel_id=1, source_target_pairs={{0,2},{1,3},{2,0},{3,1},{4,6},{5,7},{6,4},{7,5},{8,10},{9,11},{10,... | collective-permute-start | bytes 221192 | tf_op jit(solution)/shard_map/ppermute | solution.py:400
  33.2 5.0 %collective-permute-start.11 = (bf16[2,144,128]{2,1,0:T(8,128)(2,1)S(1)}, bf16[2,144,128]{2,1,0:T(8,128)(2,1)S(1)}, u32[]{:S(2)}, u32[]{:S(2)}) collective-permute-start(bf16[2,144,128]{2,1,0:T(8,128)(2,1)S(1)} %get-tuple-element.26), channel_id=1, source_target_pairs={{0,3},{1,2},{2,1},{3,0},{4,7},{5,6},{6,5},{7,4},{8,11},{9,10},{10,... | collective-permute-start | bytes 221192 | tf_op jit(solution)/shard_map/ppermute | solution.py:400
  34.8 6.9 %collective-permute-start.17 = (bf16[256,128]{1,0:T(8,128)(2,1)S(1)}, bf16[256,128]{1,0:T(8,128)(2,1)S(1)}, u32[]{:S(2)}, u32[]{:S(2)}) collective-permute-start(bf16[256,128]{1,0:T(8,128)(2,1)S(1)} %get-tuple-element.34), channel_id=1, source_target_pairs={{0,12},{1,13},{2,14},{3,15},{4,8},{5,9},{6,10},{7,11},{8,4},{9,5},... | collective-permute-start | bytes 196616 | tf_op jit(solution)/shard_map/ppermute | solution.py:400
  37.1 7.2 %collective-permute-start.16 = (bf16[256,128]{1,0:T(8,128)(2,1)S(1)}, bf16[256,128]{1,0:T(8,128)(2,1)S(1)}, u32[]{:S(2)}, u32[]{:S(2)}) collective-permute-start(bf16[256,128]{1,0:T(8,128)(2,1)S(1)} %get-tuple-element.31.refs_4_), channel_id=1, source_target_pairs={{0,8},{1,9},{2,10},{3,11},{4,12},{5,13},{6,14},{7,15},{8,0},{9,1},... | collective-permute-start | bytes 196616 | tf_op jit(solution)/shard_map/ppermute | solution.py:400
  38.4 6.0 %collective-permute-start.15 = (bf16[256,128]{1,0:T(8,128)(2,1)S(1)}, bf16[256,128]{1,0:T(8,128)(2,1)S(1)}, u32[]{:S(2)}, u32[]{:S(2)}) collective-permute-start(bf16[256,128]{1,0:T(8,128)(2,1)S(1)} %get-tuple-element.33), channel_id=1, source_target_pairs={{0,4},{1,5},{2,6},{3,7},{4,0},{5,1},{6,2},{7,3},{8,12},{9,13},{10,... | collective-permute-start | bytes 196616 | tf_op jit(solution)/shard_map/ppermute | solution.py:400

commit v9 on v8

--- a/solution.py
+++ b/solution.py
@@ -114,7 +114,12 @@
         for chunk in [low + step * UNROLL + u for u in range(UNROLL)]:
             spots = [chunk * CHUNK + i for i in range(CHUNK)]
             left = jnp.concatenate([slab(tiles, slot_ref[pos]) for pos in spots], axis=0)
-            value = jnp.dot(left, zb[gid_ref[chunk]], preferred_element_type=jnp.float32)
+            value = lax.dot_general(
+                left,
+                zb[gid_ref[chunk]],
+                (((1,), (1,)), ((), ())),
+                preferred_element_type=jnp.float32,
+            )
             for i, pos in enumerate(spots):
                 acc[block_ref[pos]] += value[i * blk : (i + 1) * blk]
 
@@ -167,11 +172,8 @@
 
 
 def round_fitted(zacc, zb):
-    groups, nocc, wide = zacc.shape
-    for g in range(groups):
-        for p in range(wide // nocc):
-            part = zacc[g, :, p * nocc : (p + 1) * nocc].astype(zb.dtype)
-            zb[g, p * nocc : (p + 1) * nocc, :] = part.T
+    for g in range(zacc.shape[0]):
+        zb[g] = zacc[g].astype(zb.dtype)
 
 
 def first_part(n_aux, fit_lists, lists, bit, tiles_array, partial_fit, shards, sources):
@@ -198,7 +200,7 @@
     shape = (n_aux // PLANE // 2, blk + TAIL, nocc)
     out_shape = [jax.ShapeDtypeStruct(shape, jnp.bfloat16)] * PLANE
     out_shape = out_shape + [
-        jax.ShapeDtypeStruct((AB_DEV, auxb * nocc, nocc), jnp.bfloat16),
+        jax.ShapeDtypeStruct((AB_DEV, nocc, auxb * nocc), jnp.bfloat16),
         jax.ShapeDtypeStruct(partial_fit.shape, partial_fit.dtype),
     ]
     return pl.pallas_call(
@@ -279,7 +281,7 @@
         scratch_shapes=[
             pltpu.VMEM((n_aux + 1, nocc, blk), jnp.bfloat16),
             pltpu.VMEM((AB_DEV, nocc, auxb * nocc), jnp.float32),
-            pltpu.VMEM((AB_DEV, auxb * nocc, nocc), jnp.bfloat16),
+            pltpu.VMEM((AB_DEV, nocc, auxb * nocc), jnp.bfloat16),
             pltpu.VMEM((n_aux + 1, blk, nocc), jnp.float32),
         ],
         compiler_params=pltpu.CompilerParams(vmem_limit_bytes=46 * 1024 * 1024),
@@ -287,19 +289,25 @@
     )(*lists, bit, tiles_array, whole)
 
 
-def gate(array, after):
-    def kernel(source, _, target):
-        target[...] = source[...]
-
-    vmem = pl.BlockSpec(memory_space=pltpu.VMEM)
-    return pl.pallas_call(
-        kernel,
-        out_shape=jax.ShapeDtypeStruct(array.shape, array.dtype),
-        in_specs=[vmem, pl.BlockSpec(memory_space=pl.ANY)],
+def gate(arrays, after):
+    counts = [array.shape[0] if array.ndim == 3 else 1 for array in arrays]
+
+    def kernel(*refs):
+        target, place = refs[-1], 0
+        for ref, count in zip(refs, counts):
+            value = ref[...]
+            target[place : place + count] = value.reshape((count,) + value.shape[-2:])
+            place += count
+
+    vmem = pl.BlockSpec(memory_space=pltpu.VMEM)
+    return pl.pallas_call(
+        kernel,
+        out_shape=jax.ShapeDtypeStruct((sum(counts),) + arrays[0].shape[-2:], arrays[0].dtype),
+        in_specs=[vmem] * len(arrays) + [pl.BlockSpec(memory_space=pl.ANY)],
         out_specs=vmem,
         compiler_params=pltpu.CompilerParams(vmem_limit_bytes=4 * 1024 * 1024),
         name="gate",
-    )(array, after)
+    )(*arrays, after)
 
 
 def merge(arrays, after, cost):
@@ -413,24 +421,32 @@
 
     depth = n_aux // PLANE
     half = depth // 2
-    last = (where_to >= PLANE) & (where_to % PLANE >= 2)
+    side = where_to % PLANE >= 2
+    last = (where_to >= 3 * PLANE) | ((where_to >= PLANE) & side)
     fit_lists = chunk_lists(where_to, last, alive, group, n_aux)
-    column = [swap(c_orbitals, dz * PLANE) for dz in range(depth - 1, 0, -1)]
+    two = swap(c_orbitals, 2 * PLANE)
+    one = swap(c_orbitals, PLANE)
     beside = swap(c_orbitals, 2)
     across = swap(c_orbitals, 1)
-    column = merge(column, [], SPREAD_COST)
-    late = swap(column, 2)
-    early = [column, swap(column, 1), across, beside, swap(beside, 1)]
+    three = swap(two, PLANE)
+    pair = merge([one, two], [], SPREAD_COST)
+    pair_beside = swap(pair, 2)
+    three_beside = swap(three, 2)
+    early = [pair, swap(pair, 1), across, beside, swap(beside, 1)]
     early_from = [(1, (2, None)), (2, (3, None)), (3, (4, None))]
     late_from = []
-    for dz in range(1, depth):
-        for core in range(2):
-            early_from.append((dz * PLANE + core, (core, depth - 1 - dz)))
-            late_from.append((dz * PLANE + 2 + core, (core, depth - 1 - dz)))
+    for core in range(2):
+        early_from += [(PLANE + core, (core, 0)), (2 * PLANE + core, (core, 1))]
+        late_from += [
+            (PLANE + 2 + core, (core, 0)),
+            (2 * PLANE + 2 + core, (core, 1)),
+            (3 * PLANE + core, (core, 2)),
+            (3 * PLANE + 2 + core, (core, 3)),
+        ]
     partial_fit, packed = begin(
         n_aux, fit_lists, bit, packed, tiles, c_orbitals, early, early_from
     )
-    late = gate(late, partial_fit)
+    late = gate([pair_beside, three, three_beside], partial_fit)
     where_to, _, group, alive = unpack_slots(packed, bb_dev)
     lists = chunk_lists(where_to, where_to < n_aux // 2, alive, group, n_aux)
     *far, fitted, _ = first_part(

time: 45.2 us -> 45.1 us (level)
  Pallas kernels: 12.3 us -> 13.6 us
  starting transfers between devices: 18.1 us -> 17.1 us
    pallas_call x1, Pallas kernels: 5.14 us -> 6.23 us  [first_part(): pl.pallas_call(kernel, out_shape=out_shape, in_specs=[smem] * 7 + [vmem]...]
    ppermute x18 -> x19, starting transfers between devices: 18.1 us -> 17.1 us  [swap(): return lax.ppermute(array, 'aux', [(i, i ^ m) for i in range(n_aux)])]
    pallas_call x1, Pallas kernels: 3.14 us -> 3.69 us  [second_part(): pl.pallas_call(kernel, out_shape=[jax.ShapeDtypeStruct(shape, jnp.bfloat1...]
    ppermute x18 -> x19, waiting for transfers between devices: 10.2 us -> 10.2 us  [swap(): return lax.ppermute(array, 'aux', [(i, i ^ m) for i in range(n_aux)])]
  transfers between devices with their start and end apart: 18 -> 19, of which waited for: 7 -> 7; matrix products, arithmetic and copies ran while one was open for 7% -> 7% of each run, Pallas kernels for 15% -> 15%
where the time goes in v9:
time: 45.1 us; the launch traced here: 45.2 us
  starting transfers between devices  17.1 us (38%)
  Pallas kernels  13.6 us (30%)
  waiting for transfers between devices  10.2 us (23%)
  other arithmetic  3.38 us (7%)
  between operations  0.92 us (2%)
    ppermute x19, starting transfers between devices, swap(): return lax.ppermute(array, 'aux', [(i, i ^ m) for i in range(n_aux)])  17.1 us
    ppermute x19, waiting for transfers between devices, swap(): return lax.ppermute(array, 'aux', [(i, i ^ m) for i in range(n_aux)])  10.2 us
    pallas_call x1, Pallas kernels, first_part(): pl.pallas_call(kernel, out_shape=out_shape, in_specs=[smem] * 7 + [vmem]...  6.23 us
    pallas_call x1, Pallas kernels, second_part(): pl.pallas_call(kernel, out_shape=[jax.ShapeDtypeStruct(shape, jnp.bfloat1...  3.69 us
    pallas_call x1, Pallas kernels, begin(): pl.pallas_call(kernel, out_shape=[jax.ShapeDtypeStruct((AB_DEV, nocc, aux...  2.71 us
  transfers between devices with their start and end apart: 19, of which 7 were waited for; matrix products, arithmetic and copies ran while one was open for 7% of the time, Pallas kernels for 15%

profile of v9, /device:TPU:0, one launch (start us, length us, event | category | flops | bytes accessed | tf_op | source)
XLA Modules:
  0.0 45.2 jit_solution(525897128323619484)
XLA Ops:
  0.0 0.5 %collective-permute-start.3 = (bf16[256,128]{1,0:T(8,128)(2,1)}, bf16[256,128]{1,0:T(8,128)(2,1)S(1)}, u32[]{:S(2)}, u32[]{:S(2)}) collective-permute-start(bf16[256,128]{1,0:T(8,128)(2,1)} %own.1), channel_id=1, source_target_pairs={{0,1},{1,0},{2,3},{3,2},{4,5},{5,4},{6,7},{7,6},{8,9},{9,8},{10,11... | collective-permute-start | bytes 196616 | tf_op jit(solution)/shard_map/ppermute | solution.py:408
  0.5 3.6 %collective-permute-start.1 = (bf16[256,128]{1,0:T(8,128)(2,1)}, bf16[256,128]{1,0:T(8,128)(2,1)S(1)}, u32[]{:S(2)}, u32[]{:S(2)}) collective-permute-start(bf16[256,128]{1,0:T(8,128)(2,1)} %own.1), channel_id=1, source_target_pairs={{0,8},{1,9},{2,10},{3,11},{4,12},{5,13},{6,14},{7,15},{8,0},{9,1},... | collective-permute-start | bytes 196616 | tf_op jit(solution)/shard_map/ppermute | solution.py:408
  4.0 1.6 %collective-permute-start = (bf16[256,128]{1,0:T(8,128)(2,1)}, bf16[256,128]{1,0:T(8,128)(2,1)S(1)}, u32[]{:S(2)}, u32[]{:S(2)}) collective-permute-start(bf16[256,128]{1,0:T(8,128)(2,1)} %own.1), channel_id=1, source_target_pairs={{0,4},{1,5},{2,6},{3,7},{4,0},{5,1},{6,2},{7,3},{8,12},{9,13},{10,... | collective-permute-start | bytes 196616 | tf_op jit(solution)/shard_map/ppermute | solution.py:408
  5.6 1.5 %collective-permute-start.4 = (bf16[256,128]{1,0:T(8,128)(2,1)}, bf16[256,128]{1,0:T(8,128)(2,1)S(1)}, u32[]{:S(2)}, u32[]{:S(2)}) collective-permute-start(bf16[256,128]{1,0:T(8,128)(2,1)} %own.1), channel_id=1, source_target_pairs={{0,2},{1,3},{2,0},{3,1},{4,6},{5,7},{6,4},{7,5},{8,10},{9,11},{10,... | collective-permute-start | bytes 196616 | tf_op jit(solution)/shard_map/ppermute | solution.py:408
  7.8 0.8 %select_reduce_fusion.6 = s32[64]{0:T(128)S(1)} fusion(s32[64]{0:T(128)} %param.9, s32[32]{0:T(128)} %param.8), kind=kLoop, calls=%fused_computation.15 | loop fusion | flops 6080 | bytes 640 | tf_op jit(solution)/shard_map/reduce_sum | solution.py:21
  8.6 0.7 %and_select_fusion.7 = (s32[64]{0:T(128)S(1)}, s32[64]{0:T(128)S(1)}, s32[64]{0:T(128)S(1)}, s32[64]{0:T(128)S(1)}) fusion(s32[]{:T(128)} %bitcast.1, s32[64]{0:T(128)} %param.10, s32[]{:T(128)S(6)} %axis_index.12, s32[64]{0:T(128)S(1)} %select_reduce_fusion.6), kind=kLoop, calls=%fused_computation.48 | loop fusion | flops 4416 | bytes 1544 | tf_op jit(solution)/shard_map/jit(remainder)/select_n | solution.py:36
  10.4 0.5 %collective-permute-start.7 = (bf16[256,128]{1,0:T(8,128)(2,1)S(1)}, bf16[256,128]{1,0:T(8,128)(2,1)S(1)}, u32[]{:S(2)}, u32[]{:S(2)}) collective-permute-start(bf16[256,128]{1,0:T(8,128)(2,1)S(1)} %collective-permute-done.1.refs_1_), channel_id=1, source_target_pairs={{0,4},{1,5},{2,6},{3,7},{4,0},{5,1},{6,2},{7,3},{8,12},{9,13},{10,... | collective-permute-start | bytes 196616 | tf_op jit(solution)/shard_map/ppermute | solution.py:408
  11.2 1.0 %collective-permute-start.6 = (bf16[2,256,128]{2,1,0:T(8,128)(2,1)S(1)}, bf16[2,256,128]{2,1,0:T(8,128)(2,1)S(1)}, u32[]{:S(2)}, u32[]{:S(2)}) collective-permute-start(bf16[2,256,128]{2,1,0:T(8,128)(2,1)S(1)} %merge.1.refs_0_), channel_id=1, source_target_pairs={{0,2},{1,3},{2,0},{3,1},{4,6},{5,7},{6,4},{7,5},{8,10},{9,11},{10,... | collective-permute-start | bytes 393224 | tf_op jit(solution)/shard_map/ppermute | solution.py:408
  12.3 2.7 %collective-permute-done.7.refs_1_ = bf16[256,128]{1,0:T(8,128)(2,1)S(1)} collective-permute-done((bf16[256,128]{1,0:T(8,128)(2,1)S(1)}, bf16[256,128]{1,0:T(8,128)(2,1)S(1)}, u32[]{:S(2)}, u32[]{:S(2)}) %collective-permute-start.7) | collective-permute-done | bytes 65568 | tf_op jit(solution)/shard_map/ppermute | solution.py:408
  15.0 0.5 %collective-permute-start.8 = (bf16[256,128]{1,0:T(8,128)(2,1)S(1)}, bf16[256,128]{1,0:T(8,128)(2,1)S(1)}, u32[]{:S(2)}, u32[]{:S(2)}) collective-permute-start(bf16[256,128]{1,0:T(8,128)(2,1)S(1)} %collective-permute-done.7.refs_1_), channel_id=1, source_target_pairs={{0,2},{1,3},{2,0},{3,1},{4,6},{5,7},{6,4},{7,5},{8,10},{9,11},{10,... | collective-permute-start | bytes 196616 | tf_op jit(solution)/shard_map/ppermute | solution.py:408
  15.5 2.7 %begin.1 = (f32[8,128,640]{2,1,0:T(8,128)S(1)}, s32[64]{0:T(128)S(1)}) custom-call(s32[128]{0:T(128)S(1)} %get-tuple-element.55.slot_ref.refs_0_, s32[128]{0:T(128)S(1)} %get-tuple-element.54.block_ref.refs_1_, s32[48]{0:T(128)S(1)} %pad_add_fusion.gid_ref.refs_2_, s32[16]{0:T(128)S(1)} %select_reduce_fusion.9.bit_ref.refs_6_, ...), custom_call_target="tpu_custom_call" | custom-call | flops 1342177280 | bytes 5242880 | tf_op jit(solution)/shard_map/begin/pallas_call | solution.py:144
  19.4 1.4 %collective-permute-done.9.refs_10_ = bf16[4,256,128]{2,1,0:T(8,128)(2,1)S(1)} collective-permute-done((bf16[4,256,128]{2,1,0:T(8,128)(2,1)S(1)}, bf16[4,256,128]{2,1,0:T(8,128)(2,1)S(1)}, u32[]{:S(2)}, u32[]{:S(2)}) %collective-permute-start.9) | collective-permute-done | bytes 262176 | tf_op jit(solution)/shard_map/ppermute | solution.py:408
  20.9 6.2 %first_part.1 = (bf16[2,144,128]{2,1,0:T(8,128)(2,1)S(1)}, bf16[2,144,128]{2,1,0:T(8,128)(2,1)S(1)}, bf16[2,144,128]{2,1,0:T(8,128)(2,1)S(1)}, bf16[2,144,128]{2...) custom-call(s32[128]{0:T(128)S(1)} %get-tuple-element.55.slot_ref.re, ...), custom_call_target="tpu_custom_call", output_to_operand_aliasing={{5}: (8, {})} | custom-call | flops 2013265920 | bytes 5242880 | tf_op jit(solution)/shard_map/first_part/pallas_call | solution.py:206
  27.2 1.2 %collective-permute-start.14 = (bf16[2,144,128]{2,1,0:T(8,128)(2,1)S(1)}, bf16[2,144,128]{2,1,0:T(8,128)(2,1)S(1)}, u32[]{:S(2)}, u32[]{:S(2)}) collective-permute-start(bf16[2,144,128]{2,1,0:T(8,128)(2,1)S(1)} %get-tuple-element.29), channel_id=1, source_target_pairs={{0,2},{1,3},{2,0},{3,1},{4,6},{5,7},{6,4},{7,5},{8,10},{9,11},{10,... | collective-permute-start | bytes 221192 | tf_op jit(solution)/shard_map/ppermute | solution.py:408
  28.3 0.7 %collective-permute-start.15 = (bf16[2,144,128]{2,1,0:T(8,128)(2,1)S(1)}, bf16[2,144,128]{2,1,0:T(8,128)(2,1)S(1)}, u32[]{:S(2)}, u32[]{:S(2)}) collective-permute-start(bf16[2,144,128]{2,1,0:T(8,128)(2,1)S(1)} %get-tuple-element.30), channel_id=1, source_target_pairs={{0,3},{1,2},{2,1},{3,0},{4,7},{5,6},{6,5},{7,4},{8,11},{9,10},{10,... | collective-permute-start | bytes 221192 | tf_op jit(solution)/shard_map/ppermute | solution.py:408
  29.0 3.7 %second_part.1 = (bf16[2,144,128]{2,1,0:T(8,128)(2,1)S(1)}, bf16[2,144,128]{2,1,0:T(8,128)(2,1)S(1)}, bf16[2,144,128]{2,1,0:T(8,128)(2,1)S(1)}, bf16[2,144,128]{2,1,0:T(8,128)(2,1)S(1)}) custom-call(s32[128]{0:T(128)S(1)} %get-tuple-element.53.refs_3_.slot_ref, s32[128]{0:T(128)S(1)} %get-tuple-element.52.refs_4_.block_ref, ...), custom_call_target="tpu_custom_call" | custom-call | flops 10000000000 | bytes 5242880 | tf_op jit(solution)/shard_map/second_part/pallas_call | solution.py:239
  32.7 0.4 collective-permute-start.10
  33.1 1.1 %collective-permute-start.11 = (bf16[2,144,128]{2,1,0:T(8,128)(2,1)S(1)}, bf16[2,144,128]{2,1,0:T(8,128)(2,1)S(1)}, u32[]{:S(2)}, u32[]{:S(2)}) collective-permute-start(bf16[2,144,128]{2,1,0:T(8,128)(2,1)S(1)} %get-tuple-element.25), channel_id=1, source_target_pairs={{0,2},{1,3},{2,0},{3,1},{4,6},{5,7},{6,4},{7,5},{8,10},{9,11},{10,... | collective-permute-start | bytes 221192 | tf_op jit(solution)/shard_map/ppermute | solution.py:408
  34.8 3.1 %collective-permute-start.18 = (bf16[256,128]{1,0:T(8,128)(2,1)S(1)}, bf16[256,128]{1,0:T(8,128)(2,1)S(1)}, u32[]{:S(2)}, u32[]{:S(2)}) collective-permute-start(bf16[256,128]{1,0:T(8,128)(2,1)S(1)} %get-tuple-element.34), channel_id=1, source_target_pairs={{0,12},{1,13},{2,14},{3,15},{4,8},{5,9},{6,10},{7,11},{8,4},{9,5},... | collective-permute-start | bytes 196616 | tf_op jit(solution)/shard_map/ppermute | solution.py:408
  37.9 0.8 %collective-permute-done.12.refs_3_ = bf16[2,144,128]{2,1,0:T(8,128)(2,1)S(1)} collective-permute-done((bf16[2,144,128]{2,1,0:T(8,128)(2,1)S(1)}, bf16[2,144,128]{2,1,0:T(8,128)(2,1)S(1)}, u32[]{:S(2)}, u32[]{:S(2)}) %collective-permute-start.12) | collective-permute-done | bytes 73760 | tf_op jit(solution)/shard_map/ppermute | solution.py:408
  38.9 0.6 %collective-permute-start.16 = (bf16[256,128]{1,0:T(8,128)(2,1)S(1)}, bf16[256,128]{1,0:T(8,128)(2,1)S(1)}, u32[]{:S(2)}, u32[]{:S(2)}) collective-permute-start(bf16[256,128]{1,0:T(8,128)(2,1)S(1)} %get-tuple-element.33), channel_id=1, source_target_pairs={{0,4},{1,5},{2,6},{3,7},{4,0},{5,1},{6,2},{7,3},{8,12},{9,13},{10,... | collective-permute-start | bytes 196616 | tf_op jit(solution)/shard_map/ppermute | solution.py:408
  39.4 2.2 %collective-permute-done.18.refs_1_ = bf16[256,128]{1,0:T(8,128)(2,1)S(1)} collective-permute-done((bf16[256,128]{1,0:T(8,128)(2,1)S(1)}, bf16[256,128]{1,0:T(8,128)(2,1)S(1)}, u32[]{:S(2)}, u32[]{:S(2)}) %collective-permute-start.18) | collective-permute-done | bytes 65568 | tf_op jit(solution)/shard_map/ppermute | solution.py:408
  41.6 2.6 %collective-permute-done.17.refs_0_ = bf16[256,128]{1,0:T(8,128)(2,1)S(1)} collective-permute-done((bf16[256,128]{1,0:T(8,128)(2,1)S(1)}, bf16[256,128]{1,0:T(8,128)(2,1)S(1)}, u32[]{:S(2)}, u32[]{:S(2)}) %collective-permute-start.17) | collective-permute-done | bytes 65568 | tf_op jit(solution)/shard_map/ppermute | solution.py:408
  44.5 0.6 %total_of.3 = bf16[256,128]{1,0:T(8,128)(2,1)} custom-call(f32[256,128]{1,0:T(8,128)S(1)} %get-tuple-element.32.refs_0_, bf16[256,128]{1,0:T(8,128)(2,1)S(1)} %collective-permute-done.16.refs_1_, f32[256,128]{1,0:T(8,128)S(1)} %total_of.2.refs_2_), custom_call_target="tpu_custom_call" | custom-call | tf_op jit(solution)/shard_map/total_of/pallas_call | solution.py:367
  (63 shorter events, 3.5 us)
Async XLA Ops:
  0.0 15.5 %collective-permute-start.3 = (bf16[256,128]{1,0:T(8,128)(2,1)}, bf16[256,128]{1,0:T(8,128)(2,1)S(1)}, u32[]{:S(2)}, u32[]{:S(2)}) collective-permute-start(bf16[256,128]{1,0:T(8,128)(2,1)} %own.1), channel_id=1, source_target_pairs={{0,1},{1,0},{2,3},{3,2},{4,5},{5,4},{6,7},{7,6},{8,9},{9,8},{10,11... | collective-permute-start | bytes 196616 | tf_op jit(solution)/shard_map/ppermute | solution.py:408
  0.5 9.7 %collective-permute-start.1 = (bf16[256,128]{1,0:T(8,128)(2,1)}, bf16[256,128]{1,0:T(8,128)(2,1)S(1)}, u32[]{:S(2)}, u32[]{:S(2)}) collective-permute-start(bf16[256,128]{1,0:T(8,128)(2,1)} %own.1), channel_id=1, source_target_pairs={{0,8},{1,9},{2,10},{3,11},{4,12},{5,13},{6,14},{7,15},{8,0},{9,1},... | collective-permute-start | bytes 196616 | tf_op jit(solution)/shard_map/ppermute | solution.py:408
  4.0 6.1 %collective-permute-start = (bf16[256,128]{1,0:T(8,128)(2,1)}, bf16[256,128]{1,0:T(8,128)(2,1)S(1)}, u32[]{:S(2)}, u32[]{:S(2)}) collective-permute-start(bf16[256,128]{1,0:T(8,128)(2,1)} %own.1), channel_id=1, source_target_pairs={{0,4},{1,5},{2,6},{3,7},{4,0},{5,1},{6,2},{7,3},{8,12},{9,13},{10,... | collective-permute-start | bytes 196616 | tf_op jit(solution)/shard_map/ppermute | solution.py:408
  5.6 5.3 %collective-permute-start.4 = (bf16[256,128]{1,0:T(8,128)(2,1)}, bf16[256,128]{1,0:T(8,128)(2,1)S(1)}, u32[]{:S(2)}, u32[]{:S(2)}) collective-permute-start(bf16[256,128]{1,0:T(8,128)(2,1)} %own.1), channel_id=1, source_target_pairs={{0,2},{1,3},{2,0},{3,1},{4,6},{5,7},{6,4},{7,5},{8,10},{9,11},{10,... | collective-permute-start | bytes 196616 | tf_op jit(solution)/shard_map/ppermute | solution.py:408
  10.1 5.4 %slice-start = ((s8[10485760]{0:T(1024)(128)(4,1)}), s8[4194304]{0:T(1024)(128)(4,1)S(1)}, s32[]{:S(2)}) async-start(s8[10485760]{0:T(1024)(128)(4,1)} %bitcast.2), calls=%async_computation | async-start | bytes 8388608
  10.1 5.4 %slice-start.1 = ((s8[10485760]{0:T(1024)(128)(4,1)}), s8[4194304]{0:T(1024)(128)(4,1)S(1)}, s32[]{:S(2)}) async-start(s8[10485760]{0:T(1024)(128)(4,1)} %bitcast.2), calls=%async_computation.1 | async-start | bytes 8388608
  10.1 5.4 %slice-start.2 = ((s8[10485760]{0:T(1024)(128)(4,1)}), s8[2097152]{0:T(1024)(128)(4,1)S(1)}, s32[]{:S(2)}) async-start(s8[10485760]{0:T(1024)(128)(4,1)} %bitcast.2), calls=%async_computation.2 | async-start | bytes 4194304
  10.2 5.4 %copy-start = (bf16[256,128]{1,0:T(8,128)(2,1)S(1)}, bf16[256,128]{1,0:T(8,128)(2,1)}, u32[]{:S(2)}) copy-start(bf16[256,128]{1,0:T(8,128)(2,1)} %own.1) | copy-start | bytes 196612
  10.2 5.3 %collective-permute-start.2 = (bf16[2,256,128]{2,1,0:T(8,128)(2,1)S(1)}, bf16[2,256,128]{2,1,0:T(8,128)(2,1)S(1)}, u32[]{:S(2)}, u32[]{:S(2)}) collective-permute-start(bf16[2,256,128]{2,1,0:T(8,128)(2,1)S(1)} %merge.1.refs_0_), channel_id=1, source_target_pairs={{0,1},{1,0},{2,3},{3,2},{4,5},{5,4},{6,7},{7,6},{8,9},{9,8},{10,11... | collective-permute-start | bytes 393224 | tf_op jit(solution)/shard_map/ppermute | solution.py:408
  10.4 4.6 %collective-permute-start.7 = (bf16[256,128]{1,0:T(8,128)(2,1)S(1)}, bf16[256,128]{1,0:T(8,128)(2,1)S(1)}, u32[]{:S(2)}, u32[]{:S(2)}) collective-permute-start(bf16[256,128]{1,0:T(8,128)(2,1)S(1)} %collective-permute-done.1.refs_1_), channel_id=1, source_target_pairs={{0,4},{1,5},{2,6},{3,7},{4,0},{5,1},{6,2},{7,3},{8,12},{9,13},{10,... | collective-permute-start | bytes 196616 | tf_op jit(solution)/shard_map/ppermute | solution.py:408
  10.9 4.6 %collective-permute-start.5 = (bf16[256,128]{1,0:T(8,128)(2,1)S(1)}, bf16[256,128]{1,0:T(8,128)(2,1)S(1)}, u32[]{:S(2)}, u32[]{:S(2)}) collective-permute-start(bf16[256,128]{1,0:T(8,128)(2,1)S(1)} %collective-permute-done.4.refs_3_), channel_id=1, source_target_pairs={{0,1},{1,0},{2,3},{3,2},{4,5},{5,4},{6,7},{7,6},{8,9},{9,8},{10,11... | collective-permute-start | bytes 196616 | tf_op jit(solution)/shard_map/ppermute | solution.py:408
  11.2 8.0 %collective-permute-start.6 = (bf16[2,256,128]{2,1,0:T(8,128)(2,1)S(1)}, bf16[2,256,128]{2,1,0:T(8,128)(2,1)S(1)}, u32[]{:S(2)}, u32[]{:S(2)}) collective-permute-start(bf16[2,256,128]{2,1,0:T(8,128)(2,1)S(1)} %merge.1.refs_0_), channel_id=1, source_target_pairs={{0,2},{1,3},{2,0},{3,1},{4,6},{5,7},{6,4},{7,5},{8,10},{9,11},{10,... | collective-permute-start | bytes 393224 | tf_op jit(solution)/shard_map/ppermute | solution.py:408
  15.0 4.3 %collective-permute-start.8 = (bf16[256,128]{1,0:T(8,128)(2,1)S(1)}, bf16[256,128]{1,0:T(8,128)(2,1)S(1)}, u32[]{:S(2)}, u32[]{:S(2)}) collective-permute-start(bf16[256,128]{1,0:T(8,128)(2,1)S(1)} %collective-permute-done.7.refs_1_), channel_id=1, source_target_pairs={{0,2},{1,3},{2,0},{3,1},{4,6},{5,7},{6,4},{7,5},{8,10},{9,11},{10,... | collective-permute-start | bytes 196616 | tf_op jit(solution)/shard_map/ppermute | solution.py:408
  19.3 1.6 %collective-permute-start.9 = (bf16[4,256,128]{2,1,0:T(8,128)(2,1)S(1)}, bf16[4,256,128]{2,1,0:T(8,128)(2,1)S(1)}, u32[]{:S(2)}, u32[]{:S(2)}) collective-permute-start(bf16[4,256,128]{2,1,0:T(8,128)(2,1)S(1)} %gate.1.refs_9_), channel_id=1, source_target_pairs={{0,1},{1,0},{2,3},{3,2},{4,5},{5,4},{6,7},{7,6},{8,9},{9,8},{10,11... | collective-permute-start | bytes 786440 | tf_op jit(solution)/shard_map/ppermute | solution.py:408
  27.1 7.2 %collective-permute-start.13 = (bf16[2,144,128]{2,1,0:T(8,128)(2,1)S(1)}, bf16[2,144,128]{2,1,0:T(8,128)(2,1)S(1)}, u32[]{:S(2)}, u32[]{:S(2)}) collective-permute-start(bf16[2,144,128]{2,1,0:T(8,128)(2,1)S(1)} %get-tuple-element.28), channel_id=1, source_target_pairs={{0,1},{1,0},{2,3},{3,2},{4,5},{5,4},{6,7},{7,6},{8,9},{9,8},{10,11... | collective-permute-start | bytes 221192 | tf_op jit(solution)/shard_map/ppermute | solution.py:408
  27.2 7.5 %collective-permute-start.14 = (bf16[2,144,128]{2,1,0:T(8,128)(2,1)S(1)}, bf16[2,144,128]{2,1,0:T(8,128)(2,1)S(1)}, u32[]{:S(2)}, u32[]{:S(2)}) collective-permute-start(bf16[2,144,128]{2,1,0:T(8,128)(2,1)S(1)} %get-tuple-element.29), channel_id=1, source_target_pairs={{0,2},{1,3},{2,0},{3,1},{4,6},{5,7},{6,4},{7,5},{8,10},{9,11},{10,... | collective-permute-start | bytes 221192 | tf_op jit(solution)/shard_map/ppermute | solution.py:408
  28.3 6.3 %collective-permute-start.15 = (bf16[2,144,128]{2,1,0:T(8,128)(2,1)S(1)}, bf16[2,144,128]{2,1,0:T(8,128)(2,1)S(1)}, u32[]{:S(2)}, u32[]{:S(2)}) collective-permute-start(bf16[2,144,128]{2,1,0:T(8,128)(2,1)S(1)} %get-tuple-element.30), channel_id=1, source_target_pairs={{0,3},{1,2},{2,1},{3,0},{4,7},{5,6},{6,5},{7,4},{8,11},{9,10},{10,... | collective-permute-start | bytes 221192 | tf_op jit(solution)/shard_map/ppermute | solution.py:408
  32.7 5.2 %collective-permute-start.10 = (bf16[2,144,128]{2,1,0:T(8,128)(2,1)S(1)}, bf16[2,144,128]{2,1,0:T(8,128)(2,1)S(1)}, u32[]{:S(2)}, u32[]{:S(2)}) collective-permute-start(bf16[2,144,128]{2,1,0:T(8,128)(2,1)S(1)} %get-tuple-element.24), channel_id=1, source_target_pairs={{0,1},{1,0},{2,3},{3,2},{4,5},{5,4},{6,7},{7,6},{8,9},{9,8},{10,11... | collective-permute-start | bytes 221192 | tf_op jit(solution)/shard_map/ppermute | solution.py:408
  33.1 4.8 %collective-permute-start.11 = (bf16[2,144,128]{2,1,0:T(8,128)(2,1)S(1)}, bf16[2,144,128]{2,1,0:T(8,128)(2,1)S(1)}, u32[]{:S(2)}, u32[]{:S(2)}) collective-permute-start(bf16[2,144,128]{2,1,0:T(8,128)(2,1)S(1)} %get-tuple-element.25), channel_id=1, source_target_pairs={{0,2},{1,3},{2,0},{3,1},{4,6},{5,7},{6,4},{7,5},{8,10},{9,11},{10,... | collective-permute-start | bytes 221192 | tf_op jit(solution)/shard_map/ppermute | solution.py:408
  34.3 4.5 %collective-permute-start.12 = (bf16[2,144,128]{2,1,0:T(8,128)(2,1)S(1)}, bf16[2,144,128]{2,1,0:T(8,128)(2,1)S(1)}, u32[]{:S(2)}, u32[]{:S(2)}) collective-permute-start(bf16[2,144,128]{2,1,0:T(8,128)(2,1)S(1)} %get-tuple-element.26), channel_id=1, source_target_pairs={{0,3},{1,2},{2,1},{3,0},{4,7},{5,6},{6,5},{7,4},{8,11},{9,10},{10,... | collective-permute-start | bytes 221192 | tf_op jit(solution)/shard_map/ppermute | solution.py:408
  34.8 6.8 %collective-permute-start.18 = (bf16[256,128]{1,0:T(8,128)(2,1)S(1)}, bf16[256,128]{1,0:T(8,128)(2,1)S(1)}, u32[]{:S(2)}, u32[]{:S(2)}) collective-permute-start(bf16[256,128]{1,0:T(8,128)(2,1)S(1)} %get-tuple-element.34), channel_id=1, source_target_pairs={{0,12},{1,13},{2,14},{3,15},{4,8},{5,9},{6,10},{7,11},{8,4},{9,5},... | collective-permute-start | bytes 196616 | tf_op jit(solution)/shard_map/ppermute | solution.py:408
  37.9 6.3 %collective-permute-start.17 = (bf16[256,128]{1,0:T(8,128)(2,1)S(1)}, bf16[256,128]{1,0:T(8,128)(2,1)S(1)}, u32[]{:S(2)}, u32[]{:S(2)}) collective-permute-start(bf16[256,128]{1,0:T(8,128)(2,1)S(1)} %get-tuple-element.31.refs_4_), channel_id=1, source_target_pairs={{0,8},{1,9},{2,10},{3,11},{4,12},{5,13},{6,14},{7,15},{8,0},{9,1},... | collective-permute-start | bytes 196616 | tf_op jit(solution)/shard_map/ppermute | solution.py:408
  38.9 5.7 %collective-permute-start.16 = (bf16[256,128]{1,0:T(8,128)(2,1)S(1)}, bf16[256,128]{1,0:T(8,128)(2,1)S(1)}, u32[]{:S(2)}, u32[]{:S(2)}) collective-permute-start(bf16[256,128]{1,0:T(8,128)(2,1)S(1)} %get-tuple-element.33), channel_id=1, source_target_pairs={{0,4},{1,5},{2,6},{3,7},{4,0},{5,1},{6,2},{7,3},{8,12},{9,13},{10,... | collective-permute-start | bytes 196616 | tf_op jit(solution)/shard_map/ppermute | solution.py:408

commit v10 on v9

--- a/solution.py
+++ b/solution.py
@@ -192,12 +192,12 @@
         round_fitted(zacc, zb)
         far, _ = chunk_ends(list_refs[2], slots)
         apply_fitted(list_refs, tiles, zb, acc, 0, far)
-        for m in range(n_aux // 2, n_aux):
-            put(bit_ref, acc, m, out_refs[m % PLANE], (m - n_aux // 2) // PLANE)
+        for m in range(PLANE, n_aux):
+            put(bit_ref, acc, m, out_refs[m % PLANE], m // PLANE - 1)
 
     smem = pl.BlockSpec(memory_space=pltpu.SMEM)
     vmem = pl.BlockSpec(memory_space=pltpu.VMEM)
-    shape = (n_aux // PLANE // 2, blk + TAIL, nocc)
+    shape = (n_aux // PLANE - 1, blk + TAIL, nocc)
     out_shape = [jax.ShapeDtypeStruct(shape, jnp.bfloat16)] * PLANE
     out_shape = out_shape + [
         jax.ShapeDtypeStruct((AB_DEV, nocc, auxb * nocc), jnp.bfloat16),
@@ -230,12 +230,12 @@
         apply_fitted(
             (slot_ref, block_ref, gid_ref), tiles, zb, acc, *chunk_ends(gid_ref, slots)
         )
-        for m in range(n_aux // 2):
-            put(bit_ref, acc, m, out_refs[m % PLANE], m // PLANE)
+        for m in range(PLANE):
+            put(bit_ref, acc, m, out_refs[m], 0)
 
     smem = pl.BlockSpec(memory_space=pltpu.SMEM)
     vmem = pl.BlockSpec(memory_space=pltpu.VMEM)
-    shape = (n_aux // PLANE // 2, blk + TAIL, nocc)
+    shape = (1, blk + TAIL, nocc)
     return pl.pallas_call(
         kernel,
         out_shape=[jax.ShapeDtypeStruct(shape, jnp.bfloat16)] * PLANE,
@@ -327,52 +327,59 @@
     )(*arrays, *after)
 
 
-def spread(parts, after, dtypes, blk, bb_dev):
+def placed_sum(sources, i, blk, bb_dev):
+    nocc = sources[0].shape[2]
+    sums = [jnp.zeros((blk, nocc), jnp.float32) for _ in range(bb_dev)]
+    for source in sources:
+        value = source[i, :blk, :].astype(jnp.float32)
+        which = source[i, blk:, :][:1].astype(jnp.float32)
+        for b in range(bb_dev):
+            sums[b] = sums[b] + jnp.where(which == b, value, 0.0)
+    return sums
+
+
+def spread(parts, blk, bb_dev):
     count, rows, nocc = parts[0].shape
 
     def kernel(*refs):
-        sources, targets = refs[: len(parts)], refs[len(parts) + len(after) :]
+        sources, targets = refs[: len(parts)], refs[len(parts) :]
         for i in range(count):
-            sums = [jnp.zeros((blk, nocc), jnp.float32) for _ in range(bb_dev)]
-            for source in sources:
-                value = source[i, :blk, :].astype(jnp.float32)
-                which = source[i, blk:, :][:1].astype(jnp.float32)
-                for b in range(bb_dev):
-                    sums[b] = sums[b] + jnp.where(which == b, value, 0.0)
-            for b in range(bb_dev):
-                targets[i][b * blk : (b + 1) * blk, :] = sums[b].astype(targets[i].dtype)
-
-    vmem = pl.BlockSpec(memory_space=pltpu.VMEM)
-    return pl.pallas_call(
-        kernel,
-        out_shape=[jax.ShapeDtypeStruct((bb_dev * blk, nocc), dtype) for dtype in dtypes],
-        in_specs=[vmem] * len(parts) + [pl.BlockSpec(memory_space=pl.ANY)] * len(after),
+            for b, value in enumerate(placed_sum(sources, i, blk, bb_dev)):
+                targets[i][b * blk : (b + 1) * blk, :] = value.astype(targets[i].dtype)
+
+    vmem = pl.BlockSpec(memory_space=pltpu.VMEM)
+    return pl.pallas_call(
+        kernel,
+        out_shape=[jax.ShapeDtypeStruct((bb_dev * blk, nocc), jnp.bfloat16)] * count,
+        in_specs=[vmem] * len(parts),
         out_specs=[vmem] * count,
         compiler_params=pltpu.CompilerParams(vmem_limit_bytes=4 * 1024 * 1024),
         cost_estimate=pl.CostEstimate(
             flops=SPREAD_COST, bytes_accessed=SPREAD_COST // 1000, transcendentals=0
         ),
         name="spread",
-    )(*parts, *after)
-
-
-def total_of(arrays, dtype, cost):
+    )(*parts)
+
+
+def total_of(parts, arrays, blk, bb_dev):
+    nocc = parts[0].shape[2]
+
     def kernel(*refs):
-        value = refs[0][...].astype(jnp.float32)
-        for ref in refs[1:-1]:
-            value = value + ref[...].astype(jnp.float32)
-        refs[-1][...] = value.astype(refs[-1].dtype)
-
-    vmem = pl.BlockSpec(memory_space=pltpu.VMEM)
-    return pl.pallas_call(
-        kernel,
-        out_shape=jax.ShapeDtypeStruct(arrays[0].shape, dtype),
-        in_specs=[vmem] * len(arrays),
+        sources, others, target = refs[: len(parts)], refs[len(parts) : -1], refs[-1]
+        for b, value in enumerate(placed_sum(sources, 0, blk, bb_dev)):
+            for other in others:
+                value = value + other[b * blk : (b + 1) * blk, :].astype(jnp.float32)
+            target[b * blk : (b + 1) * blk, :] = value.astype(target.dtype)
+
+    vmem = pl.BlockSpec(memory_space=pltpu.VMEM)
+    return pl.pallas_call(
+        kernel,
+        out_shape=jax.ShapeDtypeStruct((bb_dev * blk, nocc), jnp.bfloat16),
+        in_specs=[vmem] * (len(parts) + len(arrays)),
         out_specs=vmem,
         compiler_params=pltpu.CompilerParams(vmem_limit_bytes=4 * 1024 * 1024),
-        cost_estimate=pl.CostEstimate(flops=cost, bytes_accessed=cost // 1000, transcendentals=0),
         name="total_of",
-    )(*arrays)
+    )(*parts, *arrays)
 
 
 def owner_sum(parts, blk, bb_dev):
@@ -420,7 +427,6 @@
         return owner_sum(moved, blk, bb_dev)
 
     depth = n_aux // PLANE
-    half = depth // 2
     side = where_to % PLANE >= 2
     last = (where_to >= 3 * PLANE) | ((where_to >= PLANE) & side)
     fit_lists = chunk_lists(where_to, last, alive, group, n_aux)
@@ -428,7 +434,7 @@
     one = swap(c_orbitals, PLANE)
     beside = swap(c_orbitals, 2)
     across = swap(c_orbitals, 1)
-    three = swap(two, PLANE)
+    three = swap(c_orbitals, 3 * PLANE)
     pair = merge([one, two], [], SPREAD_COST)
     pair_beside = swap(pair, 2)
     three_beside = swap(three, 2)
@@ -448,21 +454,16 @@
     )
     late = gate([pair_beside, three, three_beside], partial_fit)
     where_to, _, group, alive = unpack_slots(packed, bb_dev)
-    lists = chunk_lists(where_to, where_to < n_aux // 2, alive, group, n_aux)
+    lists = chunk_lists(where_to, where_to < PLANE, alive, group, n_aux)
     *far, fitted, _ = first_part(
         n_aux, fit_lists, lists, bit, tiles, partial_fit, [late, swap(late, 1)], late_from
     )
     far = [far[0]] + [swap(far[r], r) for r in range(1, PLANE)]
     near = second_part(n_aux, lists, bit, tiles, fitted)
     near = [near[0]] + [swap(near[r], r) for r in range(1, PLANE)]
-    far = spread(far, [], [jnp.bfloat16] * half, blk, bb_dev)
-    near = spread(
-        near, [far[0]], [jnp.float32] + [jnp.bfloat16] * (half - 1), blk, bb_dev
-    )
-    far = [swap(far[i], (half + i) * PLANE) for i in range(half)]
-    far = total_of(far, jnp.float32, SPREAD_COST)
-    near = [near[0]] + [swap(near[dz], dz * PLANE) for dz in range(1, half)]
-    return total_of(near + [far], jnp.bfloat16, 0)
+    far = spread(far, blk, bb_dev)
+    far = [swap(far[dz - 1], dz * PLANE) for dz in range(depth - 1, 0, -1)]
+    return total_of(near, far, blk, bb_dev)
 
 
 def solution(mesh):

time: 45.1 us -> 44.6 us (0.989); the launches traced: 45.2 us -> 44.1 us
  Pallas kernels: 13.6 us -> 11.3 us
  starting transfers between devices: 17.1 us -> 17.8 us
    pallas_call x1, Pallas kernels: 3.69 us -> 2.16 us  [second_part(): pl.pallas_call(kernel, out_shape=[jax.ShapeDtypeStruct(shape, jnp.bfloat1...]
    pallas_call x1, Pallas kernels: 6.23 us -> 5.47 us  [first_part(): pl.pallas_call(kernel, out_shape=out_shape, in_specs=[smem] * 7 + [vmem]...]
    ppermute x19, starting transfers between devices: 17.1 us -> 17.8 us  [swap(): return lax.ppermute(array, 'aux', [(i, i ^ m) for i in range(n_aux)])]
  transfers between devices with their start and end apart: 19 -> 19, of which waited for: 7 -> 8; matrix products, arithmetic and copies ran while one was open for 7% -> 8% of each run, Pallas kernels for 15% -> 11%
where the time goes in v10:
time: 44.6 us; the launch traced here: 44.1 us
  starting transfers between devices  17.8 us (40%)
  Pallas kernels  11.3 us (25%)
  waiting for transfers between devices  10.3 us (23%)
  other arithmetic  3.38 us (8%)
  between operations  0.89 us (2%)
  local copies, waits for them, and re-layouts  0.47 us (1%)
    ppermute x19, starting transfers between devices, swap(): return lax.ppermute(array, 'aux', [(i, i ^ m) for i in range(n_aux)])  17.8 us
    ppermute x19, waiting for transfers between devices, swap(): return lax.ppermute(array, 'aux', [(i, i ^ m) for i in range(n_aux)])  10.3 us
    pallas_call x1, Pallas kernels, first_part(): pl.pallas_call(kernel, out_shape=out_shape, in_specs=[smem] * 7 + [vmem]...  5.47 us
    pallas_call x1, Pallas kernels, begin(): pl.pallas_call(kernel, out_shape=[jax.ShapeDtypeStruct((AB_DEV, nocc, aux...  2.71 us
    pallas_call x1, Pallas kernels, second_part(): pl.pallas_call(kernel, out_shape=[jax.ShapeDtypeStruct(shape, jnp.bfloat1...  2.16 us
  transfers between devices with their start and end apart: 19, of which 8 were waited for; matrix products, arithmetic and copies ran while one was open for 8% of the time, Pallas kernels for 11%

profile of v10, /device:TPU:0, one launch (start us, length us, event | category | flops | bytes accessed | tf_op | source)
XLA Modules:
  0.0 44.1 jit_solution(4689468987163972001)
XLA Ops:
  0.0 3.0 %collective-permute-start.4 = (bf16[256,128]{1,0:T(8,128)(2,1)}, bf16[256,128]{1,0:T(8,128)(2,1)S(1)}, u32[]{:S(2)}, u32[]{:S(2)}) collective-permute-start(bf16[256,128]{1,0:T(8,128)(2,1)} %own.1), channel_id=1, source_target_pairs={{0,2},{1,3},{2,0},{3,1},{4,6},{5,7},{6,4},{7,5},{8,10},{9,11},{10,... | collective-permute-start | bytes 196616 | tf_op jit(solution)/shard_map/ppermute | solution.py:415
  3.0 2.6 %collective-permute-start.1 = (bf16[256,128]{1,0:T(8,128)(2,1)}, bf16[256,128]{1,0:T(8,128)(2,1)S(1)}, u32[]{:S(2)}, u32[]{:S(2)}) collective-permute-start(bf16[256,128]{1,0:T(8,128)(2,1)} %own.1), channel_id=1, source_target_pairs={{0,8},{1,9},{2,10},{3,11},{4,12},{5,13},{6,14},{7,15},{8,0},{9,1},... | collective-permute-start | bytes 196616 | tf_op jit(solution)/shard_map/ppermute | solution.py:415
  5.6 1.6 %collective-permute-start = (bf16[256,128]{1,0:T(8,128)(2,1)}, bf16[256,128]{1,0:T(8,128)(2,1)S(1)}, u32[]{:S(2)}, u32[]{:S(2)}) collective-permute-start(bf16[256,128]{1,0:T(8,128)(2,1)} %own.1), channel_id=1, source_target_pairs={{0,4},{1,5},{2,6},{3,7},{4,0},{5,1},{6,2},{7,3},{8,12},{9,13},{10,... | collective-permute-start | bytes 196616 | tf_op jit(solution)/shard_map/ppermute | solution.py:415
  8.0 0.8 %select_reduce_fusion.6 = s32[64]{0:T(128)S(1)} fusion(s32[64]{0:T(128)} %param.9, s32[32]{0:T(128)} %param.8), kind=kLoop, calls=%fused_computation.15 | loop fusion | flops 6080 | bytes 640 | tf_op jit(solution)/shard_map/reduce_sum | solution.py:21
  8.8 0.7 %and_select_fusion.7 = (s32[64]{0:T(128)S(1)}, s32[64]{0:T(128)S(1)}, s32[64]{0:T(128)S(1)}, s32[64]{0:T(128)S(1)}) fusion(s32[]{:T(128)} %bitcast.1, s32[64]{0:T(128)} %param.10, s32[]{:T(128)S(6)} %axis_index.12, s32[64]{0:T(128)S(1)} %select_reduce_fusion.6), kind=kLoop, calls=%fused_computation.48 | loop fusion | flops 4416 | bytes 1544 | tf_op jit(solution)/shard_map/jit(remainder)/select_n | solution.py:36
  10.6 0.6 %collective-permute-start.5 = (bf16[256,128]{1,0:T(8,128)(2,1)S(1)}, bf16[256,128]{1,0:T(8,128)(2,1)S(1)}, u32[]{:S(2)}, u32[]{:S(2)}) collective-permute-start(bf16[256,128]{1,0:T(8,128)(2,1)S(1)} %collective-permute-done.4.refs_3_), channel_id=1, source_target_pairs={{0,1},{1,0},{2,3},{3,2},{4,5},{5,4},{6,7},{7,6},{8,9},{9,8},{10,11... | collective-permute-start | bytes 196616 | tf_op jit(solution)/shard_map/ppermute | solution.py:415
  11.6 1.8 %collective-permute-done.7.refs_1_ = bf16[256,128]{1,0:T(8,128)(2,1)S(1)} collective-permute-done((bf16[256,128]{1,0:T(8,128)(2,1)}, bf16[256,128]{1,0:T(8,128)(2,1)S(1)}, u32[]{:S(2)}, u32[]{:S(2)}) %collective-permute-start.7) | collective-permute-done | bytes 65568 | tf_op jit(solution)/shard_map/ppermute | solution.py:415
  13.4 0.5 %collective-permute-start.8 = (bf16[256,128]{1,0:T(8,128)(2,1)S(1)}, bf16[256,128]{1,0:T(8,128)(2,1)S(1)}, u32[]{:S(2)}, u32[]{:S(2)}) collective-permute-start(bf16[256,128]{1,0:T(8,128)(2,1)S(1)} %collective-permute-done.7.refs_1_), channel_id=1, source_target_pairs={{0,2},{1,3},{2,0},{3,1},{4,6},{5,7},{6,4},{7,5},{8,10},{9,11},{10,... | collective-permute-start | bytes 196616 | tf_op jit(solution)/shard_map/ppermute | solution.py:415
  14.0 0.4 %slice-done.2 = s8[2097152]{0:T(1024)(128)(4,1)S(1)} async-done(((s8[10485760]{0:T(1024)(128)(4,1)}), s8[2097152]{0:T(1024)(128)(4,1)S(1)}, s32[]{:S(2)}) %slice-start.2) | async-done | bytes 2097176
  14.4 2.7 %begin.1 = (f32[8,128,640]{2,1,0:T(8,128)S(1)}, s32[64]{0:T(128)S(1)}) custom-call(s32[128]{0:T(128)S(1)} %get-tuple-element.53.slot_ref.refs_0_, s32[128]{0:T(128)S(1)} %get-tuple-element.52.block_ref.refs_1_, s32[48]{0:T(128)S(1)} %pad_add_fusion.gid_ref.refs_2_, s32[16]{0:T(128)S(1)} %select_reduce_fusion.9.bit_ref.refs_6_, ...), custom_call_target="tpu_custom_call" | custom-call | flops 1342177280 | bytes 5242880 | tf_op jit(solution)/shard_map/begin/pallas_call | solution.py:144
  18.3 1.4 %collective-permute-done.9.refs_10_ = bf16[4,256,128]{2,1,0:T(8,128)(2,1)S(1)} collective-permute-done((bf16[4,256,128]{2,1,0:T(8,128)(2,1)S(1)}, bf16[4,256,128]{2,1,0:T(8,128)(2,1)S(1)}, u32[]{:S(2)}, u32[]{:S(2)}) %collective-permute-start.9) | collective-permute-done | bytes 262176 | tf_op jit(solution)/shard_map/ppermute | solution.py:415
  19.7 5.5 %first_part.1 = (bf16[3,144,128]{2,1,0:T(8,128)(2,1)S(1)}, bf16[3,144,128]{2,1,0:T(8,128)(2,1)S(1)}, bf16[3,144,128]{2,1,0:T(8,128)(2,1)S(1)}, bf16[3,144,128]{2...) custom-call(s32[128]{0:T(128)S(1)} %get-tuple-element.53.slot_ref.re, ...), custom_call_target="tpu_custom_call", output_to_operand_aliasing={{5}: (8, {})} | custom-call | flops 2013265920 | bytes 5242880 | tf_op jit(solution)/shard_map/first_part/pallas_call | solution.py:206
  25.2 0.6 %collective-permute-start.13 = (bf16[3,144,128]{2,1,0:T(8,128)(2,1)S(1)}, bf16[3,144,128]{2,1,0:T(8,128)(2,1)S(1)}, u32[]{:S(2)}, u32[]{:S(2)}) collective-permute-start(bf16[3,144,128]{2,1,0:T(8,128)(2,1)S(1)} %get-tuple-element.27), channel_id=1, source_target_pairs={{0,1},{1,0},{2,3},{3,2},{4,5},{5,4},{6,7},{7,6},{8,9},{9,8},{10,11... | collective-permute-start | bytes 331784 | tf_op jit(solution)/shard_map/ppermute | solution.py:415
  25.8 1.8 %collective-permute-start.14 = (bf16[3,144,128]{2,1,0:T(8,128)(2,1)S(1)}, bf16[3,144,128]{2,1,0:T(8,128)(2,1)S(1)}, u32[]{:S(2)}, u32[]{:S(2)}) collective-permute-start(bf16[3,144,128]{2,1,0:T(8,128)(2,1)S(1)} %get-tuple-element.28), channel_id=1, source_target_pairs={{0,2},{1,3},{2,0},{3,1},{4,6},{5,7},{6,4},{7,5},{8,10},{9,11},{10,... | collective-permute-start | bytes 331784 | tf_op jit(solution)/shard_map/ppermute | solution.py:415
  27.7 2.2 %second_part.1 = (bf16[1,144,128]{2,1,0:T(8,128)(2,1)S(1)}, bf16[1,144,128]{2,1,0:T(8,128)(2,1)S(1)}, bf16[1,144,128]{2,1,0:T(8,128)(2,1)S(1)}, bf16[1,144,128]{2,1,0:T(8,128)(2,1)S(1)}) custom-call(s32[128]{0:T(128)S(1)} %get-tuple-element.51.refs_3_.slot_ref, s32[128]{0:T(128)S(1)} %get-tuple-element.50.refs_4_.block_ref, ...), custom_call_target="tpu_custom_call" | custom-call | flops 10000000000 | bytes 5242880 | tf_op jit(solution)/shard_map/second_part/pallas_call | solution.py:239
  30.2 1.5 %collective-permute-done.14.refs_2_ = bf16[3,144,128]{2,1,0:T(8,128)(2,1)S(1)} collective-permute-done((bf16[3,144,128]{2,1,0:T(8,128)(2,1)S(1)}, bf16[3,144,128]{2,1,0:T(8,128)(2,1)S(1)}, u32[]{:S(2)}, u32[]{:S(2)}) %collective-permute-start.14) | collective-permute-done | bytes 110624 | tf_op jit(solution)/shard_map/ppermute | solution.py:415
  31.6 1.7 %collective-permute-done.15.refs_3_ = bf16[3,144,128]{2,1,0:T(8,128)(2,1)S(1)} collective-permute-done((bf16[3,144,128]{2,1,0:T(8,128)(2,1)S(1)}, bf16[3,144,128]{2,1,0:T(8,128)(2,1)S(1)}, u32[]{:S(2)}, u32[]{:S(2)}) %collective-permute-start.15) | collective-permute-done | bytes 110624 | tf_op jit(solution)/shard_map/ppermute | solution.py:415
  33.5 3.9 %collective-permute-start.16 = (bf16[256,128]{1,0:T(8,128)(2,1)S(1)}, bf16[256,128]{1,0:T(8,128)(2,1)S(1)}, u32[]{:S(2)}, u32[]{:S(2)}) collective-permute-start(bf16[256,128]{1,0:T(8,128)(2,1)S(1)} %get-tuple-element.30), channel_id=1, source_target_pairs={{0,12},{1,13},{2,14},{3,15},{4,8},{5,9},{6,10},{7,11},{8,4},{9,5},... | collective-permute-start | bytes 196616 | tf_op jit(solution)/shard_map/ppermute | solution.py:415
  37.3 0.6 %collective-permute-start.18 = (bf16[256,128]{1,0:T(8,128)(2,1)S(1)}, bf16[256,128]{1,0:T(8,128)(2,1)S(1)}, u32[]{:S(2)}, u32[]{:S(2)}) collective-permute-start(bf16[256,128]{1,0:T(8,128)(2,1)S(1)} %get-tuple-element.32), channel_id=1, source_target_pairs={{0,4},{1,5},{2,6},{3,7},{4,0},{5,1},{6,2},{7,3},{8,12},{9,13},{10,... | collective-permute-start | bytes 196616 | tf_op jit(solution)/shard_map/ppermute | solution.py:415
  38.0 1.6 %collective-permute-start.11 = (bf16[1,144,128]{2,1,0:T(8,128)(2,1)S(1)}, bf16[1,144,128]{2,1,0:T(8,128)(2,1)S(1)}, u32[]{:S(2)}, u32[]{:S(2)}) collective-permute-start(bf16[1,144,128]{2,1,0:T(8,128)(2,1)S(1)} %get-tuple-element.24), channel_id=1, source_target_pairs={{0,2},{1,3},{2,0},{3,1},{4,6},{5,7},{6,4},{7,5},{8,10},{9,11},{10,... | collective-permute-start | bytes 110600 | tf_op jit(solution)/shard_map/ppermute | solution.py:415
  39.6 2.3 %collective-permute-done.11.refs_2_ = bf16[1,144,128]{2,1,0:T(8,128)(2,1)S(1)} collective-permute-done((bf16[1,144,128]{2,1,0:T(8,128)(2,1)S(1)}, bf16[1,144,128]{2,1,0:T(8,128)(2,1)S(1)}, u32[]{:S(2)}, u32[]{:S(2)}) %collective-permute-start.11) | collective-permute-done | bytes 36896 | tf_op jit(solution)/shard_map/ppermute | solution.py:415
  41.9 1.0 %collective-permute-done.12.refs_3_ = bf16[1,144,128]{2,1,0:T(8,128)(2,1)S(1)} collective-permute-done((bf16[1,144,128]{2,1,0:T(8,128)(2,1)S(1)}, bf16[1,144,128]{2,1,0:T(8,128)(2,1)S(1)}, u32[]{:S(2)}, u32[]{:S(2)}) %collective-permute-start.12) | collective-permute-done | bytes 36896 | tf_op jit(solution)/shard_map/ppermute | solution.py:415
  43.0 0.5 %collective-permute-done.17.refs_5_ = bf16[256,128]{1,0:T(8,128)(2,1)S(1)} collective-permute-done((bf16[256,128]{1,0:T(8,128)(2,1)S(1)}, bf16[256,128]{1,0:T(8,128)(2,1)S(1)}, u32[]{:S(2)}, u32[]{:S(2)}) %collective-permute-start.17) | collective-permute-done | bytes 65568 | tf_op jit(solution)/shard_map/ppermute | solution.py:415
  43.4 0.7 %total_of.1 = bf16[256,128]{1,0:T(8,128)(2,1)} custom-call(bf16[1,144,128]{2,1,0:T(8,128)(2,1)S(1)} %get-tuple-element.22.refs_0_, bf16[1,144,128]{2,1,0:T(8,128)(2,1)S(1)} %collective-permute-done.10.refs_1_, bf16[1,144,128]{2,1,0:T(8,128)(2,1)S(1)} %collective-permute-done.11.refs_2_, bf16[1,144,128]{2,1,0:T(8,128)(2,1)S(1)} %collective-permute-done.12.refs_3_, ...), custom_call_target="tpu_custom_call" | custom-call | tf_op jit(solution)/shard_map/total_of/pallas_call | solution.py:375
  (61 shorter events, 3.4 us)
Async XLA Ops:
  0.0 10.6 %collective-permute-start.4 = (bf16[256,128]{1,0:T(8,128)(2,1)}, bf16[256,128]{1,0:T(8,128)(2,1)S(1)}, u32[]{:S(2)}, u32[]{:S(2)}) collective-permute-start(bf16[256,128]{1,0:T(8,128)(2,1)} %own.1), channel_id=1, source_target_pairs={{0,2},{1,3},{2,0},{3,1},{4,6},{5,7},{6,4},{7,5},{8,10},{9,11},{10,... | collective-permute-start | bytes 196616 | tf_op jit(solution)/shard_map/ppermute | solution.py:415
  3.0 11.0 %collective-permute-start.3 = (bf16[256,128]{1,0:T(8,128)(2,1)}, bf16[256,128]{1,0:T(8,128)(2,1)S(1)}, u32[]{:S(2)}, u32[]{:S(2)}) collective-permute-start(bf16[256,128]{1,0:T(8,128)(2,1)} %own.1), channel_id=1, source_target_pairs={{0,1},{1,0},{2,3},{3,2},{4,5},{5,4},{6,7},{7,6},{8,9},{9,8},{10,11... | collective-permute-start | bytes 196616 | tf_op jit(solution)/shard_map/ppermute | solution.py:415
  3.0 7.4 %collective-permute-start.1 = (bf16[256,128]{1,0:T(8,128)(2,1)}, bf16[256,128]{1,0:T(8,128)(2,1)S(1)}, u32[]{:S(2)}, u32[]{:S(2)}) collective-permute-start(bf16[256,128]{1,0:T(8,128)(2,1)} %own.1), channel_id=1, source_target_pairs={{0,8},{1,9},{2,10},{3,11},{4,12},{5,13},{6,14},{7,15},{8,0},{9,1},... | collective-permute-start | bytes 196616 | tf_op jit(solution)/shard_map/ppermute | solution.py:415
  5.6 4.8 %collective-permute-start = (bf16[256,128]{1,0:T(8,128)(2,1)}, bf16[256,128]{1,0:T(8,128)(2,1)S(1)}, u32[]{:S(2)}, u32[]{:S(2)}) collective-permute-start(bf16[256,128]{1,0:T(8,128)(2,1)} %own.1), channel_id=1, source_target_pairs={{0,4},{1,5},{2,6},{3,7},{4,0},{5,1},{6,2},{7,3},{8,12},{9,13},{10,... | collective-permute-start | bytes 196616 | tf_op jit(solution)/shard_map/ppermute | solution.py:415
  7.1 6.3 %collective-permute-start.7 = (bf16[256,128]{1,0:T(8,128)(2,1)}, bf16[256,128]{1,0:T(8,128)(2,1)S(1)}, u32[]{:S(2)}, u32[]{:S(2)}) collective-permute-start(bf16[256,128]{1,0:T(8,128)(2,1)} %own.1), channel_id=1, source_target_pairs={{0,12},{1,13},{2,14},{3,15},{4,8},{5,9},{6,10},{7,11},{8,4},{9,5},... | collective-permute-start | bytes 196616 | tf_op jit(solution)/shard_map/ppermute | solution.py:415
  10.3 3.6 %slice-start = ((s8[10485760]{0:T(1024)(128)(4,1)}), s8[4194304]{0:T(1024)(128)(4,1)S(1)}, s32[]{:S(2)}) async-start(s8[10485760]{0:T(1024)(128)(4,1)} %bitcast.2), calls=%async_computation | async-start | bytes 8388608
  10.4 3.6 %slice-start.1 = ((s8[10485760]{0:T(1024)(128)(4,1)}), s8[4194304]{0:T(1024)(128)(4,1)S(1)}, s32[]{:S(2)}) async-start(s8[10485760]{0:T(1024)(128)(4,1)} %bitcast.2), calls=%async_computation.1 | async-start | bytes 8388608
  10.4 4.0 %slice-start.2 = ((s8[10485760]{0:T(1024)(128)(4,1)}), s8[2097152]{0:T(1024)(128)(4,1)S(1)}, s32[]{:S(2)}) async-start(s8[10485760]{0:T(1024)(128)(4,1)} %bitcast.2), calls=%async_computation.2 | async-start | bytes 4194304
  10.4 4.0 %copy-start = (bf16[256,128]{1,0:T(8,128)(2,1)S(1)}, bf16[256,128]{1,0:T(8,128)(2,1)}, u32[]{:S(2)}) copy-start(bf16[256,128]{1,0:T(8,128)(2,1)} %own.1) | copy-start | bytes 196612
  10.4 3.5 %collective-permute-start.2 = (bf16[2,256,128]{2,1,0:T(8,128)(2,1)S(1)}, bf16[2,256,128]{2,1,0:T(8,128)(2,1)S(1)}, u32[]{:S(2)}, u32[]{:S(2)}) collective-permute-start(bf16[2,256,128]{2,1,0:T(8,128)(2,1)S(1)} %merge.1.refs_0_), channel_id=1, source_target_pairs={{0,1},{1,0},{2,3},{3,2},{4,5},{5,4},{6,7},{7,6},{8,9},{9,8},{10,11... | collective-permute-start | bytes 393224 | tf_op jit(solution)/shard_map/ppermute | solution.py:415
  10.6 3.3 %collective-permute-start.5 = (bf16[256,128]{1,0:T(8,128)(2,1)S(1)}, bf16[256,128]{1,0:T(8,128)(2,1)S(1)}, u32[]{:S(2)}, u32[]{:S(2)}) collective-permute-start(bf16[256,128]{1,0:T(8,128)(2,1)S(1)} %collective-permute-done.4.refs_3_), channel_id=1, source_target_pairs={{0,1},{1,0},{2,3},{3,2},{4,5},{5,4},{6,7},{7,6},{8,9},{9,8},{10,11... | collective-permute-start | bytes 196616 | tf_op jit(solution)/shard_map/ppermute | solution.py:415
  11.3 6.8 %collective-permute-start.6 = (bf16[2,256,128]{2,1,0:T(8,128)(2,1)S(1)}, bf16[2,256,128]{2,1,0:T(8,128)(2,1)S(1)}, u32[]{:S(2)}, u32[]{:S(2)}) collective-permute-start(bf16[2,256,128]{2,1,0:T(8,128)(2,1)S(1)} %merge.1.refs_0_), channel_id=1, source_target_pairs={{0,2},{1,3},{2,0},{3,1},{4,6},{5,7},{6,4},{7,5},{8,10},{9,11},{10,... | collective-permute-start | bytes 393224 | tf_op jit(solution)/shard_map/ppermute | solution.py:415
  13.4 4.7 %collective-permute-start.8 = (bf16[256,128]{1,0:T(8,128)(2,1)S(1)}, bf16[256,128]{1,0:T(8,128)(2,1)S(1)}, u32[]{:S(2)}, u32[]{:S(2)}) collective-permute-start(bf16[256,128]{1,0:T(8,128)(2,1)S(1)} %collective-permute-done.7.refs_1_), channel_id=1, source_target_pairs={{0,2},{1,3},{2,0},{3,1},{4,6},{5,7},{6,4},{7,5},{8,10},{9,11},{10,... | collective-permute-start | bytes 196616 | tf_op jit(solution)/shard_map/ppermute | solution.py:415
  18.1 1.6 %collective-permute-start.9 = (bf16[4,256,128]{2,1,0:T(8,128)(2,1)S(1)}, bf16[4,256,128]{2,1,0:T(8,128)(2,1)S(1)}, u32[]{:S(2)}, u32[]{:S(2)}) collective-permute-start(bf16[4,256,128]{2,1,0:T(8,128)(2,1)S(1)} %gate.1.refs_9_), channel_id=1, source_target_pairs={{0,1},{1,0},{2,3},{3,2},{4,5},{5,4},{6,7},{7,6},{8,9},{9,8},{10,11... | collective-permute-start | bytes 786440 | tf_op jit(solution)/shard_map/ppermute | solution.py:415
  25.2 5.0 %collective-permute-start.13 = (bf16[3,144,128]{2,1,0:T(8,128)(2,1)S(1)}, bf16[3,144,128]{2,1,0:T(8,128)(2,1)S(1)}, u32[]{:S(2)}, u32[]{:S(2)}) collective-permute-start(bf16[3,144,128]{2,1,0:T(8,128)(2,1)S(1)} %get-tuple-element.27), channel_id=1, source_target_pairs={{0,1},{1,0},{2,3},{3,2},{4,5},{5,4},{6,7},{7,6},{8,9},{9,8},{10,11... | collective-permute-start | bytes 331784 | tf_op jit(solution)/shard_map/ppermute | solution.py:415
  25.8 5.8 %collective-permute-start.14 = (bf16[3,144,128]{2,1,0:T(8,128)(2,1)S(1)}, bf16[3,144,128]{2,1,0:T(8,128)(2,1)S(1)}, u32[]{:S(2)}, u32[]{:S(2)}) collective-permute-start(bf16[3,144,128]{2,1,0:T(8,128)(2,1)S(1)} %get-tuple-element.28), channel_id=1, source_target_pairs={{0,2},{1,3},{2,0},{3,1},{4,6},{5,7},{6,4},{7,5},{8,10},{9,11},{10,... | collective-permute-start | bytes 331784 | tf_op jit(solution)/shard_map/ppermute | solution.py:415
  27.6 5.7 %collective-permute-start.15 = (bf16[3,144,128]{2,1,0:T(8,128)(2,1)S(1)}, bf16[3,144,128]{2,1,0:T(8,128)(2,1)S(1)}, u32[]{:S(2)}, u32[]{:S(2)}) collective-permute-start(bf16[3,144,128]{2,1,0:T(8,128)(2,1)S(1)} %get-tuple-element.29), channel_id=1, source_target_pairs={{0,3},{1,2},{2,1},{3,0},{4,7},{5,6},{6,5},{7,4},{8,11},{9,10},{10,... | collective-permute-start | bytes 331784 | tf_op jit(solution)/shard_map/ppermute | solution.py:415
  29.9 9.7 %collective-permute-start.10 = (bf16[1,144,128]{2,1,0:T(8,128)(2,1)S(1)}, bf16[1,144,128]{2,1,0:T(8,128)(2,1)S(1)}, u32[]{:S(2)}, u32[]{:S(2)}) collective-permute-start(bf16[1,144,128]{2,1,0:T(8,128)(2,1)S(1)} %get-tuple-element.23), channel_id=1, source_target_pairs={{0,1},{1,0},{2,3},{3,2},{4,5},{5,4},{6,7},{7,6},{8,9},{9,8},{10,11... | collective-permute-start | bytes 110600 | tf_op jit(solution)/shard_map/ppermute | solution.py:415
  33.5 9.5 %collective-permute-start.16 = (bf16[256,128]{1,0:T(8,128)(2,1)S(1)}, bf16[256,128]{1,0:T(8,128)(2,1)S(1)}, u32[]{:S(2)}, u32[]{:S(2)}) collective-permute-start(bf16[256,128]{1,0:T(8,128)(2,1)S(1)} %get-tuple-element.30), channel_id=1, source_target_pairs={{0,12},{1,13},{2,14},{3,15},{4,8},{5,9},{6,10},{7,11},{8,4},{9,5},... | collective-permute-start | bytes 196616 | tf_op jit(solution)/shard_map/ppermute | solution.py:415
  37.3 6.1 %collective-permute-start.17 = (bf16[256,128]{1,0:T(8,128)(2,1)S(1)}, bf16[256,128]{1,0:T(8,128)(2,1)S(1)}, u32[]{:S(2)}, u32[]{:S(2)}) collective-permute-start(bf16[256,128]{1,0:T(8,128)(2,1)S(1)} %get-tuple-element.31), channel_id=1, source_target_pairs={{0,8},{1,9},{2,10},{3,11},{4,12},{5,13},{6,14},{7,15},{8,0},{9,1},... | collective-permute-start | bytes 196616 | tf_op jit(solution)/shard_map/ppermute | solution.py:415
  37.3 6.1 %collective-permute-start.18 = (bf16[256,128]{1,0:T(8,128)(2,1)S(1)}, bf16[256,128]{1,0:T(8,128)(2,1)S(1)}, u32[]{:S(2)}, u32[]{:S(2)}) collective-permute-start(bf16[256,128]{1,0:T(8,128)(2,1)S(1)} %get-tuple-element.32), channel_id=1, source_target_pairs={{0,4},{1,5},{2,6},{3,7},{4,0},{5,1},{6,2},{7,3},{8,12},{9,13},{10,... | collective-permute-start | bytes 196616 | tf_op jit(solution)/shard_map/ppermute | solution.py:415
  38.0 4.0 %collective-permute-start.11 = (bf16[1,144,128]{2,1,0:T(8,128)(2,1)S(1)}, bf16[1,144,128]{2,1,0:T(8,128)(2,1)S(1)}, u32[]{:S(2)}, u32[]{:S(2)}) collective-permute-start(bf16[1,144,128]{2,1,0:T(8,128)(2,1)S(1)} %get-tuple-element.24), channel_id=1, source_target_pairs={{0,2},{1,3},{2,0},{3,1},{4,6},{5,7},{6,4},{7,5},{8,10},{9,11},{10,... | collective-permute-start | bytes 110600 | tf_op jit(solution)/shard_map/ppermute | solution.py:415
  39.6 3.4 %collective-permute-start.12 = (bf16[1,144,128]{2,1,0:T(8,128)(2,1)S(1)}, bf16[1,144,128]{2,1,0:T(8,128)(2,1)S(1)}, u32[]{:S(2)}, u32[]{:S(2)}) collective-permute-start(bf16[1,144,128]{2,1,0:T(8,128)(2,1)S(1)} %get-tuple-element.25), channel_id=1, source_target_pairs={{0,3},{1,2},{2,1},{3,0},{4,7},{5,6},{6,5},{7,4},{8,11},{9,10},{10,... | collective-permute-start | bytes 110600 | tf_op jit(solution)/shard_map/ppermute | solution.py:415

commit v11 on v10

--- a/solution.py
+++ b/solution.py
@@ -9,7 +9,7 @@
 
 AB_DEV = 8
 CHUNK = 4
-UNROLL = 2
+UNROLL = 4
 TAIL = 16
 PLANE = 4
 SPREAD_COST = 10**10
@@ -90,28 +90,37 @@
     ct[m] = source[pl.ds(row, blk), :].T
 
 
+def sweep(low, high, body):
+    whole = (high - low) // UNROLL
+
+    @pl.loop(0, whole)
+    def _(step):
+        body([low + step * UNROLL + u for u in range(UNROLL)])
+
+    @pl.loop(low + whole * UNROLL, high)
+    def _(chunk):
+        body([chunk])
+
+
 def fit(lists, tiles, ct, zacc, low, high):
     slot_ref, block_ref, gid_ref = lists
 
-    @pl.loop(0, (high - low + UNROLL - 1) // UNROLL)
-    def _(step):
-        for chunk in [low + step * UNROLL + u for u in range(UNROLL)]:
-            keep = jnp.where(chunk < high, 0, ct.shape[0] - 1)
+    def body(group):
+        for chunk in group:
             spots = [chunk * CHUNK + i for i in range(CHUNK)]
-            left = jnp.concatenate(
-                [ct[jnp.maximum(block_ref[pos], keep)] for pos in spots], axis=1
-            )
+            left = jnp.concatenate([ct[block_ref[pos]] for pos in spots], axis=1)
             right = jnp.concatenate([slab(tiles, slot_ref[pos]) for pos in spots], axis=0)
             zacc[gid_ref[chunk]] += jnp.dot(left, right, preferred_element_type=jnp.float32)
+
+    sweep(low, high, body)
 
 
 def apply_fitted(lists, tiles, zb, acc, low, high):
     slot_ref, block_ref, gid_ref = lists
     blk = acc.shape[1]
 
-    @pl.loop(0, (high - low + UNROLL - 1) // UNROLL)
-    def _(step):
-        for chunk in [low + step * UNROLL + u for u in range(UNROLL)]:
+    def body(group):
+        for chunk in group:
             spots = [chunk * CHUNK + i for i in range(CHUNK)]
             left = jnp.concatenate([slab(tiles, slot_ref[pos]) for pos in spots], axis=0)
             value = lax.dot_general(
@@ -122,6 +131,8 @@
             )
             for i, pos in enumerate(spots):
                 acc[block_ref[pos]] += value[i * blk : (i + 1) * blk]
+
+    sweep(low, high, body)
 
 
 def begin(n_aux, lists, bit, packed, tiles_array, own_array, shards, sources):
@@ -221,10 +232,10 @@
     )(*fit_lists, *lists, bit, tiles_array, partial_fit, *shards)
 
 
-def second_part(n_aux, lists, bit, tiles_array, fitted):
+def second_part(n_aux, lists, bit, tiles_array, fitted, after):
     slots, auxb, blk, nocc = tiles_array.shape
 
-    def kernel(slot_ref, block_ref, gid_ref, bit_ref, tiles, zb, *refs):
+    def kernel(slot_ref, block_ref, gid_ref, bit_ref, tiles, zb, _, *refs):
         out_refs, acc = refs[:-1], refs[-1]
         acc[...] = jnp.zeros(acc.shape, acc.dtype)
         apply_fitted(
@@ -239,7 +250,7 @@
     return pl.pallas_call(
         kernel,
         out_shape=[jax.ShapeDtypeStruct(shape, jnp.bfloat16)] * PLANE,
-        in_specs=[smem] * 4 + [vmem, vmem],
+        in_specs=[smem] * 4 + [vmem, vmem, pl.BlockSpec(memory_space=pl.ANY)],
         out_specs=[vmem] * PLANE,
         scratch_shapes=[pltpu.VMEM((n_aux + 1, blk, nocc), jnp.float32)],
         compiler_params=pltpu.CompilerParams(vmem_limit_bytes=20 * 1024 * 1024),
@@ -247,7 +258,7 @@
             flops=10**10, bytes_accessed=tiles_array.size, transcendentals=0
         ),
         name="second_part",
-    )(*lists, bit, tiles_array, fitted)
+    )(*lists, bit, tiles_array, fitted, after)
 
 
 def all_in_one(n_aux, lists, bit, tiles_array, whole):
@@ -338,7 +349,7 @@
     return sums
 
 
-def spread(parts, blk, bb_dev):
+def spread(parts, dtype, blk, bb_dev):
     count, rows, nocc = parts[0].shape
 
     def kernel(*refs):
@@ -350,7 +361,7 @@
     vmem = pl.BlockSpec(memory_space=pltpu.VMEM)
     return pl.pallas_call(
         kernel,
-        out_shape=[jax.ShapeDtypeStruct((bb_dev * blk, nocc), jnp.bfloat16)] * count,
+        out_shape=[jax.ShapeDtypeStruct((bb_dev * blk, nocc), dtype)] * count,
         in_specs=[vmem] * len(parts),
         out_specs=[vmem] * count,
         compiler_params=pltpu.CompilerParams(vmem_limit_bytes=4 * 1024 * 1024),
@@ -361,25 +372,22 @@
     )(*parts)
 
 
-def total_of(parts, arrays, blk, bb_dev):
-    nocc = parts[0].shape[2]
-
+def total_of(arrays):
     def kernel(*refs):
-        sources, others, target = refs[: len(parts)], refs[len(parts) : -1], refs[-1]
-        for b, value in enumerate(placed_sum(sources, 0, blk, bb_dev)):
-            for other in others:
-                value = value + other[b * blk : (b + 1) * blk, :].astype(jnp.float32)
-            target[b * blk : (b + 1) * blk, :] = value.astype(target.dtype)
-
-    vmem = pl.BlockSpec(memory_space=pltpu.VMEM)
-    return pl.pallas_call(
-        kernel,
-        out_shape=jax.ShapeDtypeStruct((bb_dev * blk, nocc), jnp.bfloat16),
-        in_specs=[vmem] * (len(parts) + len(arrays)),
+        value = refs[0][...].astype(jnp.float32)
+        for ref in refs[1:-1]:
+            value = value + ref[...].astype(jnp.float32)
+        refs[-1][...] = value.astype(refs[-1].dtype)
+
+    vmem = pl.BlockSpec(memory_space=pltpu.VMEM)
+    return pl.pallas_call(
+        kernel,
+        out_shape=jax.ShapeDtypeStruct(arrays[0].shape, jnp.bfloat16),
+        in_specs=[vmem] * len(arrays),
         out_specs=vmem,
         compiler_params=pltpu.CompilerParams(vmem_limit_bytes=4 * 1024 * 1024),
         name="total_of",
-    )(*parts, *arrays)
+    )(*arrays)
 
 
 def owner_sum(parts, blk, bb_dev):
@@ -459,11 +467,12 @@
         n_aux, fit_lists, lists, bit, tiles, partial_fit, [late, swap(late, 1)], late_from
     )
     far = [far[0]] + [swap(far[r], r) for r in range(1, PLANE)]
-    near = second_part(n_aux, lists, bit, tiles, fitted)
+    near = second_part(n_aux, lists, bit, tiles, fitted, far[1])
     near = [near[0]] + [swap(near[r], r) for r in range(1, PLANE)]
-    far = spread(far, blk, bb_dev)
+    far = spread(far, jnp.bfloat16, blk, bb_dev)
     far = [swap(far[dz - 1], dz * PLANE) for dz in range(depth - 1, 0, -1)]
-    return total_of(near, far, blk, bb_dev)
+    near = spread(near, jnp.float32, blk, bb_dev)
+    return total_of(list(near) + far)
 
 
 def solution(mesh):

time: 44.6 us -> 43.7 us (0.980)
  waiting for transfers between devices: 10.3 us -> 9.4 us
  starting transfers between devices: 17.8 us -> 17.2 us
  Pallas kernels: 11.3 us -> 11.9 us
    ppermute x19, waiting for transfers between devices: 10.3 us -> 9.4 us  [swap(): return lax.ppermute(array, 'aux', [(i, i ^ m) for i in range(n_aux)])]
    ppermute x19, starting transfers between devices: 17.8 us -> 17.2 us  [swap(): return lax.ppermute(array, 'aux', [(i, i ^ m) for i in range(n_aux)])]
  transfers between devices with their start and end apart: 19 -> 19, of which waited for: 8 -> 7; matrix products, arithmetic and copies ran while one was open for 8% -> 8% of each run, Pallas kernels for 11% -> 12%
where the time goes in v11:
time: 43.7 us; the launch traced here: 43.4 us
  starting transfers between devices  17.2 us (39%)
  Pallas kernels  11.9 us (27%)
  waiting for transfers between devices  9.4 us (22%)
  other arithmetic  3.38 us (8%)
  between operations  0.91 us (2%)
  local copies, waits for them, and re-layouts  0.47 us (1%)
    ppermute x19, starting transfers between devices, swap(): return lax.ppermute(array, 'aux', [(i, i ^ m) for i in range(n_aux)])  17.2 us
    ppermute x19, waiting for transfers between devices, swap(): return lax.ppermute(array, 'aux', [(i, i ^ m) for i in range(n_aux)])  9.4 us
    pallas_call x1, Pallas kernels, first_part(): pl.pallas_call(kernel, out_shape=out_shape, in_specs=[smem] * 7 + [vmem]...  5.91 us
    pallas_call x1, Pallas kernels, begin(): pl.pallas_call(kernel, out_shape=[jax.ShapeDtypeStruct((AB_DEV, nocc, aux...  2.61 us
    pallas_call x1, Pallas kernels, second_part(): pl.pallas_call(kernel, out_shape=[jax.ShapeDtypeStruct(shape, jnp.bfloat1...  2.51 us
  transfers between devices with their start and end apart: 19, of which 7 were waited for; matrix products, arithmetic and copies ran while one was open for 8% of the time, Pallas kernels for 12%

profile of v11, /device:TPU:0, one launch (start us, length us, event | category | flops | bytes accessed | tf_op | source)
XLA Modules:
  0.0 43.4 jit_solution(12593105222524552289)
XLA Ops:
  0.0 3.0 %collective-permute-start.4 = (bf16[256,128]{1,0:T(8,128)(2,1)}, bf16[256,128]{1,0:T(8,128)(2,1)S(1)}, u32[]{:S(2)}, u32[]{:S(2)}) collective-permute-start(bf16[256,128]{1,0:T(8,128)(2,1)} %own.1), channel_id=1, source_target_pairs={{0,2},{1,3},{2,0},{3,1},{4,6},{5,7},{6,4},{7,5},{8,10},{9,11},{10,... | collective-permute-start | bytes 196616 | tf_op jit(solution)/shard_map/ppermute | solution.py:423
  3.0 2.6 %collective-permute-start.1 = (bf16[256,128]{1,0:T(8,128)(2,1)}, bf16[256,128]{1,0:T(8,128)(2,1)S(1)}, u32[]{:S(2)}, u32[]{:S(2)}) collective-permute-start(bf16[256,128]{1,0:T(8,128)(2,1)} %own.1), channel_id=1, source_target_pairs={{0,8},{1,9},{2,10},{3,11},{4,12},{5,13},{6,14},{7,15},{8,0},{9,1},... | collective-permute-start | bytes 196616 | tf_op jit(solution)/shard_map/ppermute | solution.py:423
  5.6 1.6 %collective-permute-start = (bf16[256,128]{1,0:T(8,128)(2,1)}, bf16[256,128]{1,0:T(8,128)(2,1)S(1)}, u32[]{:S(2)}, u32[]{:S(2)}) collective-permute-start(bf16[256,128]{1,0:T(8,128)(2,1)} %own.1), channel_id=1, source_target_pairs={{0,4},{1,5},{2,6},{3,7},{4,0},{5,1},{6,2},{7,3},{8,12},{9,13},{10,... | collective-permute-start | bytes 196616 | tf_op jit(solution)/shard_map/ppermute | solution.py:423
  8.0 0.8 %select_reduce_fusion.6 = s32[64]{0:T(128)S(1)} fusion(s32[64]{0:T(128)} %param.9, s32[32]{0:T(128)} %param.8), kind=kLoop, calls=%fused_computation.15 | loop fusion | flops 6080 | bytes 640 | tf_op jit(solution)/shard_map/reduce_sum | solution.py:21
  8.8 0.7 %and_select_fusion.7 = (s32[64]{0:T(128)S(1)}, s32[64]{0:T(128)S(1)}, s32[64]{0:T(128)S(1)}, s32[64]{0:T(128)S(1)}) fusion(s32[]{:T(128)} %bitcast.1, s32[64]{0:T(128)} %param.10, s32[]{:T(128)S(6)} %axis_index.12, s32[64]{0:T(128)S(1)} %select_reduce_fusion.6), kind=kLoop, calls=%fused_computation.48 | loop fusion | flops 4416 | bytes 1544 | tf_op jit(solution)/shard_map/jit(remainder)/select_n | solution.py:36
  10.6 0.6 %collective-permute-start.5 = (bf16[256,128]{1,0:T(8,128)(2,1)S(1)}, bf16[256,128]{1,0:T(8,128)(2,1)S(1)}, u32[]{:S(2)}, u32[]{:S(2)}) collective-permute-start(bf16[256,128]{1,0:T(8,128)(2,1)S(1)} %collective-permute-done.4.refs_3_), channel_id=1, source_target_pairs={{0,1},{1,0},{2,3},{3,2},{4,5},{5,4},{6,7},{7,6},{8,9},{9,8},{10,11... | collective-permute-start | bytes 196616 | tf_op jit(solution)/shard_map/ppermute | solution.py:423
  11.3 0.4 collective-permute-start.6
  11.6 1.8 %collective-permute-done.7.refs_1_ = bf16[256,128]{1,0:T(8,128)(2,1)S(1)} collective-permute-done((bf16[256,128]{1,0:T(8,128)(2,1)}, bf16[256,128]{1,0:T(8,128)(2,1)S(1)}, u32[]{:S(2)}, u32[]{:S(2)}) %collective-permute-start.7) | collective-permute-done | bytes 65568 | tf_op jit(solution)/shard_map/ppermute | solution.py:423
  13.4 0.5 %collective-permute-start.8 = (bf16[256,128]{1,0:T(8,128)(2,1)S(1)}, bf16[256,128]{1,0:T(8,128)(2,1)S(1)}, u32[]{:S(2)}, u32[]{:S(2)}) collective-permute-start(bf16[256,128]{1,0:T(8,128)(2,1)S(1)} %collective-permute-done.7.refs_1_), channel_id=1, source_target_pairs={{0,2},{1,3},{2,0},{3,1},{4,6},{5,7},{6,4},{7,5},{8,10},{9,11},{10,... | collective-permute-start | bytes 196616 | tf_op jit(solution)/shard_map/ppermute | solution.py:423
  14.0 0.4 %slice-done.2 = s8[2097152]{0:T(1024)(128)(4,1)S(1)} async-done(((s8[10485760]{0:T(1024)(128)(4,1)}), s8[2097152]{0:T(1024)(128)(4,1)S(1)}, s32[]{:S(2)}) %slice-start.2) | async-done | bytes 2097176
  14.4 2.6 %begin.1 = (f32[8,128,640]{2,1,0:T(8,128)S(1)}, s32[64]{0:T(128)S(1)}) custom-call(s32[128]{0:T(128)S(1)} %get-tuple-element.53.slot_ref.refs_0_, s32[128]{0:T(128)S(1)} %get-tuple-element.52.block_ref.refs_1_, s32[48]{0:T(128)S(1)} %pad_add_fusion.gid_ref.refs_2_, s32[16]{0:T(128)S(1)} %select_reduce_fusion.9.bit_ref.refs_6_, ...), custom_call_target="tpu_custom_call" | custom-call | flops 1342177280 | bytes 5242880 | tf_op jit(solution)/shard_map/begin/pallas_call | solution.py:155
  18.3 1.4 %collective-permute-done.9.refs_10_ = bf16[4,256,128]{2,1,0:T(8,128)(2,1)S(1)} collective-permute-done((bf16[4,256,128]{2,1,0:T(8,128)(2,1)S(1)}, bf16[4,256,128]{2,1,0:T(8,128)(2,1)S(1)}, u32[]{:S(2)}, u32[]{:S(2)}) %collective-permute-start.9) | collective-permute-done | bytes 262176 | tf_op jit(solution)/shard_map/ppermute | solution.py:423
  19.7 5.9 %first_part.1 = (bf16[3,144,128]{2,1,0:T(8,128)(2,1)S(1)}, bf16[3,144,128]{2,1,0:T(8,128)(2,1)S(1)}, bf16[3,144,128]{2,1,0:T(8,128)(2,1)S(1)}, bf16[3,144,128]{2...) custom-call(s32[128]{0:T(128)S(1)} %get-tuple-element.53.slot_ref.re, ...), custom_call_target="tpu_custom_call", output_to_operand_aliasing={{5}: (8, {})} | custom-call | flops 2013265920 | bytes 5242880 | tf_op jit(solution)/shard_map/first_part/pallas_call | solution.py:217
  25.7 0.8 %collective-permute-start.14 = (bf16[3,144,128]{2,1,0:T(8,128)(2,1)S(1)}, bf16[3,144,128]{2,1,0:T(8,128)(2,1)S(1)}, u32[]{:S(2)}, u32[]{:S(2)}) collective-permute-start(bf16[3,144,128]{2,1,0:T(8,128)(2,1)S(1)} %get-tuple-element.28), channel_id=1, source_target_pairs={{0,2},{1,3},{2,0},{3,1},{4,6},{5,7},{6,4},{7,5},{8,10},{9,11},{10,... | collective-permute-start | bytes 331784 | tf_op jit(solution)/shard_map/ppermute | solution.py:423
  26.5 1.1 %collective-permute-start.15 = (bf16[3,144,128]{2,1,0:T(8,128)(2,1)S(1)}, bf16[3,144,128]{2,1,0:T(8,128)(2,1)S(1)}, u32[]{:S(2)}, u32[]{:S(2)}) collective-permute-start(bf16[3,144,128]{2,1,0:T(8,128)(2,1)S(1)} %get-tuple-element.29), channel_id=1, source_target_pairs={{0,3},{1,2},{2,1},{3,0},{4,7},{5,6},{6,5},{7,4},{8,11},{9,10},{10,... | collective-permute-start | bytes 331784 | tf_op jit(solution)/shard_map/ppermute | solution.py:423
  27.6 2.5 %second_part.1 = (bf16[1,144,128]{2,1,0:T(8,128)(2,1)S(1)}, bf16[1,144,128]{2,1,0:T(8,128)(2,1)S(1)}, bf16[1,144,128]{2,1,0:T(8,128)(2,1)S(1)}, bf16[1,144,128]{2,1,0:T(8,128)(2,1)S(1)}) custom-call(s32[128]{0:T(128)S(1)} %get-tuple-element.51.refs_3_.slot_ref, s32[128]{0:T(128)S(1)} %get-tuple-element.50.refs_4_.block_ref, ...), custom_call_target="tpu_custom_call" | custom-call | flops 10000000000 | bytes 5242880 | tf_op jit(solution)/shard_map/second_part/pallas_call | solution.py:250
  30.2 1.1 %collective-permute-start.12 = (bf16[1,144,128]{2,1,0:T(8,128)(2,1)S(1)}, bf16[1,144,128]{2,1,0:T(8,128)(2,1)S(1)}, u32[]{:S(2)}, u32[]{:S(2)}) collective-permute-start(bf16[1,144,128]{2,1,0:T(8,128)(2,1)S(1)} %get-tuple-element.25), channel_id=1, source_target_pairs={{0,2},{1,3},{2,0},{3,1},{4,6},{5,7},{6,4},{7,5},{8,10},{9,11},{10,... | collective-permute-start | bytes 110600 | tf_op jit(solution)/shard_map/ppermute | solution.py:423
  31.3 0.8 %collective-permute-start.13 = (bf16[1,144,128]{2,1,0:T(8,128)(2,1)S(1)}, bf16[1,144,128]{2,1,0:T(8,128)(2,1)S(1)}, u32[]{:S(2)}, u32[]{:S(2)}) collective-permute-start(bf16[1,144,128]{2,1,0:T(8,128)(2,1)S(1)} %get-tuple-element.26), channel_id=1, source_target_pairs={{0,3},{1,2},{2,1},{3,0},{4,7},{5,6},{6,5},{7,4},{8,11},{9,10},{10,... | collective-permute-start | bytes 110600 | tf_op jit(solution)/shard_map/ppermute | solution.py:423
  32.0 1.1 %collective-permute-done.15.refs_3_ = bf16[3,144,128]{2,1,0:T(8,128)(2,1)S(1)} collective-permute-done((bf16[3,144,128]{2,1,0:T(8,128)(2,1)S(1)}, bf16[3,144,128]{2,1,0:T(8,128)(2,1)S(1)}, u32[]{:S(2)}, u32[]{:S(2)}) %collective-permute-start.15) | collective-permute-done | bytes 110624 | tf_op jit(solution)/shard_map/ppermute | solution.py:423
  33.3 3.4 %collective-permute-start.16 = (bf16[256,128]{1,0:T(8,128)(2,1)S(1)}, bf16[256,128]{1,0:T(8,128)(2,1)S(1)}, u32[]{:S(2)}, u32[]{:S(2)}) collective-permute-start(bf16[256,128]{1,0:T(8,128)(2,1)S(1)} %get-tuple-element.30), channel_id=1, source_target_pairs={{0,12},{1,13},{2,14},{3,15},{4,8},{5,9},{6,10},{7,11},{8,4},{9,5},... | collective-permute-start | bytes 196616 | tf_op jit(solution)/shard_map/ppermute | solution.py:423
  36.7 1.0 %collective-permute-start.18 = (bf16[256,128]{1,0:T(8,128)(2,1)S(1)}, bf16[256,128]{1,0:T(8,128)(2,1)S(1)}, u32[]{:S(2)}, u32[]{:S(2)}) collective-permute-start(bf16[256,128]{1,0:T(8,128)(2,1)S(1)} %get-tuple-element.32), channel_id=1, source_target_pairs={{0,4},{1,5},{2,6},{3,7},{4,0},{5,1},{6,2},{7,3},{8,12},{9,13},{10,... | collective-permute-start | bytes 196616 | tf_op jit(solution)/shard_map/ppermute | solution.py:423
  37.8 2.2 %collective-permute-done.16.refs_1_ = bf16[256,128]{1,0:T(8,128)(2,1)S(1)} collective-permute-done((bf16[256,128]{1,0:T(8,128)(2,1)S(1)}, bf16[256,128]{1,0:T(8,128)(2,1)S(1)}, u32[]{:S(2)}, u32[]{:S(2)}) %collective-permute-start.16) | collective-permute-done | bytes 65568 | tf_op jit(solution)/shard_map/ppermute | solution.py:423
  40.0 2.5 %collective-permute-done.17.refs_2_ = bf16[256,128]{1,0:T(8,128)(2,1)S(1)} collective-permute-done((bf16[256,128]{1,0:T(8,128)(2,1)S(1)}, bf16[256,128]{1,0:T(8,128)(2,1)S(1)}, u32[]{:S(2)}, u32[]{:S(2)}) %collective-permute-start.17) | collective-permute-done | bytes 65568 | tf_op jit(solution)/shard_map/ppermute | solution.py:423
  42.7 0.7 %total_of.1 = bf16[256,128]{1,0:T(8,128)(2,1)} custom-call(f32[256,128]{1,0:T(8,128)S(1)} %spread.2.refs_0_, bf16[256,128]{1,0:T(8,128)(2,1)S(1)} %collective-permute-done.16.refs_1_, bf16[256,128]{1,0:T(8,128)(2,1)S(1)} %collective-permute-done.17.refs_2_, bf16[256,128]{1,0:T(8,128)(2,1)S(1)} %collective-permute-done.18.refs_3_), custom_call_target="tpu_custom_call" | custom-call | tf_op jit(solution)/shard_map/total_of/pallas_call | solution.py:383
  (62 shorter events, 3.1 us)
Async XLA Ops:
  0.0 10.6 %collective-permute-start.4 = (bf16[256,128]{1,0:T(8,128)(2,1)}, bf16[256,128]{1,0:T(8,128)(2,1)S(1)}, u32[]{:S(2)}, u32[]{:S(2)}) collective-permute-start(bf16[256,128]{1,0:T(8,128)(2,1)} %own.1), channel_id=1, source_target_pairs={{0,2},{1,3},{2,0},{3,1},{4,6},{5,7},{6,4},{7,5},{8,10},{9,11},{10,... | collective-permute-start | bytes 196616 | tf_op jit(solution)/shard_map/ppermute | solution.py:423
  3.0 11.0 %collective-permute-start.3 = (bf16[256,128]{1,0:T(8,128)(2,1)}, bf16[256,128]{1,0:T(8,128)(2,1)S(1)}, u32[]{:S(2)}, u32[]{:S(2)}) collective-permute-start(bf16[256,128]{1,0:T(8,128)(2,1)} %own.1), channel_id=1, source_target_pairs={{0,1},{1,0},{2,3},{3,2},{4,5},{5,4},{6,7},{7,6},{8,9},{9,8},{10,11... | collective-permute-start | bytes 196616 | tf_op jit(solution)/shard_map/ppermute | solution.py:423
  3.0 7.4 %collective-permute-start.1 = (bf16[256,128]{1,0:T(8,128)(2,1)}, bf16[256,128]{1,0:T(8,128)(2,1)S(1)}, u32[]{:S(2)}, u32[]{:S(2)}) collective-permute-start(bf16[256,128]{1,0:T(8,128)(2,1)} %own.1), channel_id=1, source_target_pairs={{0,8},{1,9},{2,10},{3,11},{4,12},{5,13},{6,14},{7,15},{8,0},{9,1},... | collective-permute-start | bytes 196616 | tf_op jit(solution)/shard_map/ppermute | solution.py:423
  5.6 4.8 %collective-permute-start = (bf16[256,128]{1,0:T(8,128)(2,1)}, bf16[256,128]{1,0:T(8,128)(2,1)S(1)}, u32[]{:S(2)}, u32[]{:S(2)}) collective-permute-start(bf16[256,128]{1,0:T(8,128)(2,1)} %own.1), channel_id=1, source_target_pairs={{0,4},{1,5},{2,6},{3,7},{4,0},{5,1},{6,2},{7,3},{8,12},{9,13},{10,... | collective-permute-start | bytes 196616 | tf_op jit(solution)/shard_map/ppermute | solution.py:423
  7.1 6.3 %collective-permute-start.7 = (bf16[256,128]{1,0:T(8,128)(2,1)}, bf16[256,128]{1,0:T(8,128)(2,1)S(1)}, u32[]{:S(2)}, u32[]{:S(2)}) collective-permute-start(bf16[256,128]{1,0:T(8,128)(2,1)} %own.1), channel_id=1, source_target_pairs={{0,12},{1,13},{2,14},{3,15},{4,8},{5,9},{6,10},{7,11},{8,4},{9,5},... | collective-permute-start | bytes 196616 | tf_op jit(solution)/shard_map/ppermute | solution.py:423
  10.3 3.6 %slice-start = ((s8[10485760]{0:T(1024)(128)(4,1)}), s8[4194304]{0:T(1024)(128)(4,1)S(1)}, s32[]{:S(2)}) async-start(s8[10485760]{0:T(1024)(128)(4,1)} %bitcast.2), calls=%async_computation | async-start | bytes 8388608
  10.4 3.6 %slice-start.1 = ((s8[10485760]{0:T(1024)(128)(4,1)}), s8[4194304]{0:T(1024)(128)(4,1)S(1)}, s32[]{:S(2)}) async-start(s8[10485760]{0:T(1024)(128)(4,1)} %bitcast.2), calls=%async_computation.1 | async-start | bytes 8388608
  10.4 4.0 %slice-start.2 = ((s8[10485760]{0:T(1024)(128)(4,1)}), s8[2097152]{0:T(1024)(128)(4,1)S(1)}, s32[]{:S(2)}) async-start(s8[10485760]{0:T(1024)(128)(4,1)} %bitcast.2), calls=%async_computation.2 | async-start | bytes 4194304
  10.4 4.0 %copy-start = (bf16[256,128]{1,0:T(8,128)(2,1)S(1)}, bf16[256,128]{1,0:T(8,128)(2,1)}, u32[]{:S(2)}) copy-start(bf16[256,128]{1,0:T(8,128)(2,1)} %own.1) | copy-start | bytes 196612
  10.4 3.5 %collective-permute-start.2 = (bf16[2,256,128]{2,1,0:T(8,128)(2,1)S(1)}, bf16[2,256,128]{2,1,0:T(8,128)(2,1)S(1)}, u32[]{:S(2)}, u32[]{:S(2)}) collective-permute-start(bf16[2,256,128]{2,1,0:T(8,128)(2,1)S(1)} %merge.1.refs_0_), channel_id=1, source_target_pairs={{0,1},{1,0},{2,3},{3,2},{4,5},{5,4},{6,7},{7,6},{8,9},{9,8},{10,11... | collective-permute-start | bytes 393224 | tf_op jit(solution)/shard_map/ppermute | solution.py:423
  10.6 3.3 %collective-permute-start.5 = (bf16[256,128]{1,0:T(8,128)(2,1)S(1)}, bf16[256,128]{1,0:T(8,128)(2,1)S(1)}, u32[]{:S(2)}, u32[]{:S(2)}) collective-permute-start(bf16[256,128]{1,0:T(8,128)(2,1)S(1)} %collective-permute-done.4.refs_3_), channel_id=1, source_target_pairs={{0,1},{1,0},{2,3},{3,2},{4,5},{5,4},{6,7},{7,6},{8,9},{9,8},{10,11... | collective-permute-start | bytes 196616 | tf_op jit(solution)/shard_map/ppermute | solution.py:423
  11.3 6.8 %collective-permute-start.6 = (bf16[2,256,128]{2,1,0:T(8,128)(2,1)S(1)}, bf16[2,256,128]{2,1,0:T(8,128)(2,1)S(1)}, u32[]{:S(2)}, u32[]{:S(2)}) collective-permute-start(bf16[2,256,128]{2,1,0:T(8,128)(2,1)S(1)} %merge.1.refs_0_), channel_id=1, source_target_pairs={{0,2},{1,3},{2,0},{3,1},{4,6},{5,7},{6,4},{7,5},{8,10},{9,11},{10,... | collective-permute-start | bytes 393224 | tf_op jit(solution)/shard_map/ppermute | solution.py:423
  13.4 4.7 %collective-permute-start.8 = (bf16[256,128]{1,0:T(8,128)(2,1)S(1)}, bf16[256,128]{1,0:T(8,128)(2,1)S(1)}, u32[]{:S(2)}, u32[]{:S(2)}) collective-permute-start(bf16[256,128]{1,0:T(8,128)(2,1)S(1)} %collective-permute-done.7.refs_1_), channel_id=1, source_target_pairs={{0,2},{1,3},{2,0},{3,1},{4,6},{5,7},{6,4},{7,5},{8,10},{9,11},{10,... | collective-permute-start | bytes 196616 | tf_op jit(solution)/shard_map/ppermute | solution.py:423
  18.1 1.6 %collective-permute-start.9 = (bf16[4,256,128]{2,1,0:T(8,128)(2,1)S(1)}, bf16[4,256,128]{2,1,0:T(8,128)(2,1)S(1)}, u32[]{:S(2)}, u32[]{:S(2)}) collective-permute-start(bf16[4,256,128]{2,1,0:T(8,128)(2,1)S(1)} %gate.1.refs_9_), channel_id=1, source_target_pairs={{0,1},{1,0},{2,3},{3,2},{4,5},{5,4},{6,7},{7,6},{8,9},{9,8},{10,11... | collective-permute-start | bytes 786440 | tf_op jit(solution)/shard_map/ppermute | solution.py:423
  25.6 1.9 %collective-permute-start.10 = (bf16[3,144,128]{2,1,0:T(8,128)(2,1)S(1)}, bf16[3,144,128]{2,1,0:T(8,128)(2,1)S(1)}, u32[]{:S(2)}, u32[]{:S(2)}) collective-permute-start(bf16[3,144,128]{2,1,0:T(8,128)(2,1)S(1)} %get-tuple-element.22), channel_id=1, source_target_pairs={{0,1},{1,0},{2,3},{3,2},{4,5},{5,4},{6,7},{7,6},{8,9},{9,8},{10,11... | collective-permute-start | bytes 331784 | tf_op jit(solution)/shard_map/ppermute | solution.py:423
  25.7 6.3 %collective-permute-start.14 = (bf16[3,144,128]{2,1,0:T(8,128)(2,1)S(1)}, bf16[3,144,128]{2,1,0:T(8,128)(2,1)S(1)}, u32[]{:S(2)}, u32[]{:S(2)}) collective-permute-start(bf16[3,144,128]{2,1,0:T(8,128)(2,1)S(1)} %get-tuple-element.28), channel_id=1, source_target_pairs={{0,2},{1,3},{2,0},{3,1},{4,6},{5,7},{6,4},{7,5},{8,10},{9,11},{10,... | collective-permute-start | bytes 331784 | tf_op jit(solution)/shard_map/ppermute | solution.py:423
  26.5 6.6 %collective-permute-start.15 = (bf16[3,144,128]{2,1,0:T(8,128)(2,1)S(1)}, bf16[3,144,128]{2,1,0:T(8,128)(2,1)S(1)}, u32[]{:S(2)}, u32[]{:S(2)}) collective-permute-start(bf16[3,144,128]{2,1,0:T(8,128)(2,1)S(1)} %get-tuple-element.29), channel_id=1, source_target_pairs={{0,3},{1,2},{2,1},{3,0},{4,7},{5,6},{6,5},{7,4},{8,11},{9,10},{10,... | collective-permute-start | bytes 331784 | tf_op jit(solution)/shard_map/ppermute | solution.py:423
  30.1 6.6 %collective-permute-start.11 = (bf16[1,144,128]{2,1,0:T(8,128)(2,1)S(1)}, bf16[1,144,128]{2,1,0:T(8,128)(2,1)S(1)}, u32[]{:S(2)}, u32[]{:S(2)}) collective-permute-start(bf16[1,144,128]{2,1,0:T(8,128)(2,1)S(1)} %get-tuple-element.24), channel_id=1, source_target_pairs={{0,1},{1,0},{2,3},{3,2},{4,5},{5,4},{6,7},{7,6},{8,9},{9,8},{10,11... | collective-permute-start | bytes 110600 | tf_op jit(solution)/shard_map/ppermute | solution.py:423
  30.2 7.6 %collective-permute-start.12 = (bf16[1,144,128]{2,1,0:T(8,128)(2,1)S(1)}, bf16[1,144,128]{2,1,0:T(8,128)(2,1)S(1)}, u32[]{:S(2)}, u32[]{:S(2)}) collective-permute-start(bf16[1,144,128]{2,1,0:T(8,128)(2,1)S(1)} %get-tuple-element.25), channel_id=1, source_target_pairs={{0,2},{1,3},{2,0},{3,1},{4,6},{5,7},{6,4},{7,5},{8,10},{9,11},{10,... | collective-permute-start | bytes 110600 | tf_op jit(solution)/shard_map/ppermute | solution.py:423
  31.3 6.5 %collective-permute-start.13 = (bf16[1,144,128]{2,1,0:T(8,128)(2,1)S(1)}, bf16[1,144,128]{2,1,0:T(8,128)(2,1)S(1)}, u32[]{:S(2)}, u32[]{:S(2)}) collective-permute-start(bf16[1,144,128]{2,1,0:T(8,128)(2,1)S(1)} %get-tuple-element.26), channel_id=1, source_target_pairs={{0,3},{1,2},{2,1},{3,0},{4,7},{5,6},{6,5},{7,4},{8,11},{9,10},{10,... | collective-permute-start | bytes 110600 | tf_op jit(solution)/shard_map/ppermute | solution.py:423
  33.3 6.8 %collective-permute-start.16 = (bf16[256,128]{1,0:T(8,128)(2,1)S(1)}, bf16[256,128]{1,0:T(8,128)(2,1)S(1)}, u32[]{:S(2)}, u32[]{:S(2)}) collective-permute-start(bf16[256,128]{1,0:T(8,128)(2,1)S(1)} %get-tuple-element.30), channel_id=1, source_target_pairs={{0,12},{1,13},{2,14},{3,15},{4,8},{5,9},{6,10},{7,11},{8,4},{9,5},... | collective-permute-start | bytes 196616 | tf_op jit(solution)/shard_map/ppermute | solution.py:423
  36.7 5.9 %collective-permute-start.17 = (bf16[256,128]{1,0:T(8,128)(2,1)S(1)}, bf16[256,128]{1,0:T(8,128)(2,1)S(1)}, u32[]{:S(2)}, u32[]{:S(2)}) collective-permute-start(bf16[256,128]{1,0:T(8,128)(2,1)S(1)} %get-tuple-element.31), channel_id=1, source_target_pairs={{0,8},{1,9},{2,10},{3,11},{4,12},{5,13},{6,14},{7,15},{8,0},{9,1},... | collective-permute-start | bytes 196616 | tf_op jit(solution)/shard_map/ppermute | solution.py:423
  36.7 6.0 %collective-permute-start.18 = (bf16[256,128]{1,0:T(8,128)(2,1)S(1)}, bf16[256,128]{1,0:T(8,128)(2,1)S(1)}, u32[]{:S(2)}, u32[]{:S(2)}) collective-permute-start(bf16[256,128]{1,0:T(8,128)(2,1)S(1)} %get-tuple-element.32), channel_id=1, source_target_pairs={{0,4},{1,5},{2,6},{3,7},{4,0},{5,1},{6,2},{7,3},{8,12},{9,13},{10,... | collective-permute-start | bytes 196616 | tf_op jit(solution)/shard_map/ppermute | solution.py:423

commit v12 on v11

--- a/solution.py
+++ b/solution.py
@@ -8,8 +8,8 @@
 from jax.sharding import PartitionSpec as P
 
 AB_DEV = 8
-CHUNK = 4
-UNROLL = 4
+CHUNK = 2
+TURNS = (8, 2, 1)
 TAIL = 16
 PLANE = 4
 SPREAD_COST = 10**10
@@ -17,16 +17,15 @@
 
 
 def pack_slots(tile_block, tile_aux, live, basis_order, base, bb_dev):
-    nbb = basis_order.shape[0]
-    position = jnp.sum(
-        jnp.where(
-            basis_order[None, :] == tile_block[:, None], lax.iota(jnp.int32, nbb)[None, :], 0
-        ),
-        axis=1,
-    )
-    owner = jnp.bitwise_xor(position // bb_dev, base)
-    alive = (lax.iota(jnp.int32, tile_block.shape[0]) < live[0]).astype(jnp.int32)
-    return ((owner * bb_dev + position % bb_dev) * AB_DEV + tile_aux) * 2 + alive
+    slots, nbb = tile_block.shape[0], basis_order.shape[0]
+    k = lax.broadcasted_iota(jnp.int32, (slots, nbb), 1)
+    owner = jnp.bitwise_xor(k // bb_dev, base)
+    alive = lax.broadcasted_iota(jnp.int32, (slots, nbb), 0) < live[None, :]
+    value = ((owner * bb_dev + k % bb_dev) * AB_DEV + tile_aux[:, None]) * 2
+    value = value + alive.astype(jnp.int32)
+    return jnp.sum(
+        jnp.where(basis_order[None, :] == tile_block[:, None], value, 0), axis=1
+    )
 
 
 def unpack_slots(packed, bb_dev):
@@ -91,15 +90,14 @@
 
 
 def sweep(low, high, body):
-    whole = (high - low) // UNROLL
-
-    @pl.loop(0, whole)
-    def _(step):
-        body([low + step * UNROLL + u for u in range(UNROLL)])
-
-    @pl.loop(low + whole * UNROLL, high)
-    def _(chunk):
-        body([chunk])
+    for size in TURNS:
+        whole = (high - low) // size
+
+        @pl.loop(0, whole)
+        def _(step, low=low, size=size):
+            body([low + step * size + u for u in range(size)])
+
+        low = low + whole * size
 
 
 def fit(lists, tiles, ct, zacc, low, high):
@@ -423,7 +421,18 @@
         return lax.ppermute(array, "aux", [(i, i ^ m) for i in range(n_aux)])
 
     base = lax.axis_index("aux").astype(jnp.int32) if direct else jnp.int32(0)
-    packed = pack_slots(tile_block, tile_aux, live, basis_order, base, bb_dev)
+    slots, nbb = tile_block.shape[0], basis_order.shape[0]
+    index = lax.optimization_barrier(
+        jnp.concatenate([tile_block, tile_aux, basis_order, live])
+    )
+    packed = pack_slots(
+        index[:slots],
+        index[slots : 2 * slots],
+        index[2 * slots + nbb :],
+        index[2 * slots : 2 * slots + nbb],
+        base,
+        bb_dev,
+    )
     where_to, which, group, alive = unpack_slots(packed, bb_dev)
     bit = bits_of(where_to, which, alive, n_aux)
     if not direct:

time: 43.7 us -> 44.5 us (1.018)
  local copies, waits for them, and re-layouts: 0.47 us -> 1.76 us
  Pallas kernels: 11.9 us -> 10.7 us
  waiting for transfers between devices: 9.4 us -> 9.95 us
    concatenate x0 -> x1, other arithmetic: none -> 0.77 us  [on_device(): jnp.concatenate([tile_block, tile_aux, basis_order, live])]
    select_n x1, other arithmetic: 0.69 us -> 0.03 us  [unpack_slots(): return (rest // bb_dev, rest % bb_dev, tile_aux, packed % 2 == 1)]
    slice x0 -> x3, local copies, waits for them, and re-layouts: none -> 0.66 us  [the longest x1 0.58 us: on_device(): index[2 * slots + nbb:]]
    convert_element_type x0 -> x1, other arithmetic: none -> 0.65 us  [pack_slots(): value = value + alive.astype(jnp.int32)]
    pallas_call x1, Pallas kernels: 2.51 us -> 1.86 us  [second_part(): pl.pallas_call(kernel, out_shape=[jax.ShapeDtypeStruct(shape, jnp.bfloat1...]
    reduce_sum x1, other arithmetic: 0.76 us -> 0.12 us  [pack_slots(): jnp.sum(jnp.where(basis_order[None, :] == tile_block[:, None], value, 0),...]
    unnamed x8, local copies, waits for them, and re-layouts: 0.47 us -> 1.1 us
    pallas_call x1, Pallas kernels: 5.91 us -> 5.33 us  [first_part(): pl.pallas_call(kernel, out_shape=out_shape, in_specs=[smem] * 7 + [vmem]...]
  transfers between devices with their start and end apart: 19 -> 19, of which waited for: 7 -> 8; matrix products, arithmetic and copies ran while one was open for 8% -> 9% of each run, Pallas kernels for 12% -> 11%
where the time goes in v12:
time: 44.5 us; the launch traced here: 44.2 us
  starting transfers between devices  17.5 us (39%)
  Pallas kernels  10.7 us (24%)
  waiting for transfers between devices  9.95 us (22%)
  other arithmetic  3.51 us (8%)
  local copies, waits for them, and re-layouts  1.76 us (4%)
  between operations  0.91 us (2%)
    ppermute x19, starting transfers between devices, swap(): return lax.ppermute(array, 'aux', [(i, i ^ m) for i in range(n_aux)])  17.5 us
    ppermute x19, waiting for transfers between devices, swap(): return lax.ppermute(array, 'aux', [(i, i ^ m) for i in range(n_aux)])  9.95 us
    pallas_call x1, Pallas kernels, first_part(): pl.pallas_call(kernel, out_shape=out_shape, in_specs=[smem] * 7 + [vmem]...  5.33 us
    pallas_call x1, Pallas kernels, begin(): pl.pallas_call(kernel, out_shape=[jax.ShapeDtypeStruct((AB_DEV, nocc, aux...  2.56 us
    pallas_call x1, Pallas kernels, second_part(): pl.pallas_call(kernel, out_shape=[jax.ShapeDtypeStruct(shape, jnp.bfloat1...  1.86 us
    unnamed x8, local copies, waits for them, and re-layouts  1.1 us
  transfers between devices with their start and end apart: 19, of which 8 were waited for; matrix products, arithmetic and copies ran while one was open for 9% of the time, Pallas kernels for 11%

profile of v12, /device:TPU:0, one launch (start us, length us, event | category | flops | bytes accessed | tf_op | source)
XLA Modules:
  0.0 44.2 jit_solution(8636829727114337052)
XLA Ops:
  0.0 3.0 %collective-permute-start.4 = (bf16[256,128]{1,0:T(8,128)(2,1)}, bf16[256,128]{1,0:T(8,128)(2,1)S(1)}, u32[]{:S(2)}, u32[]{:S(2)}) collective-permute-start(bf16[256,128]{1,0:T(8,128)(2,1)} %own.1), channel_id=1, source_target_pairs={{0,2},{1,3},{2,0},{3,1},{4,6},{5,7},{6,4},{7,5},{8,10},{9,11},{10,... | collective-permute-start | bytes 196616 | tf_op jit(solution)/shard_map/ppermute | solution.py:421
  3.0 2.6 %collective-permute-start.1 = (bf16[256,128]{1,0:T(8,128)(2,1)}, bf16[256,128]{1,0:T(8,128)(2,1)S(1)}, u32[]{:S(2)}, u32[]{:S(2)}) collective-permute-start(bf16[256,128]{1,0:T(8,128)(2,1)} %own.1), channel_id=1, source_target_pairs={{0,8},{1,9},{2,10},{3,11},{4,12},{5,13},{6,14},{7,15},{8,0},{9,1},... | collective-permute-start | bytes 196616 | tf_op jit(solution)/shard_map/ppermute | solution.py:421
  5.6 1.6 %collective-permute-start = (bf16[256,128]{1,0:T(8,128)(2,1)}, bf16[256,128]{1,0:T(8,128)(2,1)S(1)}, u32[]{:S(2)}, u32[]{:S(2)}) collective-permute-start(bf16[256,128]{1,0:T(8,128)(2,1)} %own.1), channel_id=1, source_target_pairs={{0,4},{1,5},{2,6},{3,7},{4,0},{5,1},{6,2},{7,3},{8,12},{9,13},{10,... | collective-permute-start | bytes 196616 | tf_op jit(solution)/shard_map/ppermute | solution.py:421
  8.0 0.8 %pad_add_fusion = s32[161]{0:T(256)S(1)} fusion(s32[1]{0:T(128)S(6)} %copy.9, s32[32]{0:T(128)} %param.8, s32[64]{0:T(128)} %param.10, s32[64]{0:T(128)} %param.9), kind=kLoop, calls=%fused_computation.88 | loop fusion | flops 483 | bytes 1288 | tf_op jit(solution)/shard_map/concatenate | solution.py:426
  8.8 0.6 %slice.15 = s32[1]{0:T(128)} slice(s32[161]{0:T(256)S(1)} %pad_add_fusion), slice={[160:161]} | slice | bytes 8 | tf_op jit(solution)/shard_map/slice | solution.py:431
  9.5 0.6 %compare_convert_fusion = s32[64]{0:T(128)S(1)} fusion(s32[]{:T(128)} %bitcast), kind=kLoop, calls=%fused_computation.59 | loop fusion | flops 128 | bytes 260 | tf_op jit(solution)/shard_map/convert_element_type | solution.py:25
  11.4 0.6 %collective-permute-start.5 = (bf16[256,128]{1,0:T(8,128)(2,1)S(1)}, bf16[256,128]{1,0:T(8,128)(2,1)S(1)}, u32[]{:S(2)}, u32[]{:S(2)}) collective-permute-start(bf16[256,128]{1,0:T(8,128)(2,1)S(1)} %collective-permute-done.4.refs_3_), channel_id=1, source_target_pairs={{0,1},{1,0},{2,3},{3,2},{4,5},{5,4},{6,7},{7,6},{8,9},{9,8},{10,11... | collective-permute-start | bytes 196616 | tf_op jit(solution)/shard_map/ppermute | solution.py:421
  12.4 1.1 %collective-permute-done.7.refs_1_ = bf16[256,128]{1,0:T(8,128)(2,1)S(1)} collective-permute-done((bf16[256,128]{1,0:T(8,128)(2,1)}, bf16[256,128]{1,0:T(8,128)(2,1)S(1)}, u32[]{:S(2)}, u32[]{:S(2)}) %collective-permute-start.7) | collective-permute-done | bytes 65568 | tf_op jit(solution)/shard_map/ppermute | solution.py:421
  13.4 0.7 %collective-permute-start.8 = (bf16[256,128]{1,0:T(8,128)(2,1)S(1)}, bf16[256,128]{1,0:T(8,128)(2,1)S(1)}, u32[]{:S(2)}, u32[]{:S(2)}) collective-permute-start(bf16[256,128]{1,0:T(8,128)(2,1)S(1)} %collective-permute-done.7.refs_1_), channel_id=1, source_target_pairs={{0,2},{1,3},{2,0},{3,1},{4,6},{5,7},{6,4},{7,5},{8,10},{9,11},{10,... | collective-permute-start | bytes 196616 | tf_op jit(solution)/shard_map/ppermute | solution.py:421
  14.6 0.6 %slice-done.2 = s8[2097152]{0:T(1024)(128)(4,1)S(1)} async-done(((s8[10485760]{0:T(1024)(128)(4,1)}), s8[2097152]{0:T(1024)(128)(4,1)S(1)}, s32[]{:S(2)}) %slice-start.2) | async-done | bytes 2097176
  15.2 2.6 %begin.1 = (f32[8,128,640]{2,1,0:T(8,128)S(1)}, s32[64]{0:T(128)S(1)}) custom-call(s32[96]{0:T(128)S(1)} %get-tuple-element.54.slot_ref.refs_0_, s32[96]{0:T(128)S(1)} %get-tuple-element.53.block_ref.refs_1_, s32[64]{0:T(128)S(1)} %pad_add_fusion.1.gid_ref.refs_2_, s32[16]{0:T(128)S(1)} %select_reduce_fusion.9.bit_ref.refs_6_, ...), custom_call_target="tpu_custom_call" | custom-call | flops 1342177280 | bytes 5242880 | tf_op jit(solution)/shard_map/begin/pallas_call | solution.py:153
  19.1 1.4 %collective-permute-done.9.refs_10_ = bf16[4,256,128]{2,1,0:T(8,128)(2,1)S(1)} collective-permute-done((bf16[4,256,128]{2,1,0:T(8,128)(2,1)S(1)}, bf16[4,256,128]{2,1,0:T(8,128)(2,1)S(1)}, u32[]{:S(2)}, u32[]{:S(2)}) %collective-permute-start.9) | collective-permute-done | bytes 262176 | tf_op jit(solution)/shard_map/ppermute | solution.py:421
  20.5 5.3 %first_part.1 = (bf16[3,144,128]{2,1,0:T(8,128)(2,1)S(1)}, bf16[3,144,128]{2,1,0:T(8,128)(2,1)S(1)}, bf16[3,144,128]{2,1,0:T(8,128)(2,1)S(1)}, bf16[3,144,128]{2...) custom-call(s32[96]{0:T(128)S(1)} %get-tuple-element.54.slot_ref.ref, ...), custom_call_target="tpu_custom_call", output_to_operand_aliasing={{5}: (8, {})} | custom-call | flops 2013265920 | bytes 5242880 | tf_op jit(solution)/shard_map/first_part/pallas_call | solution.py:215
  25.9 0.7 %collective-permute-start.14 = (bf16[3,144,128]{2,1,0:T(8,128)(2,1)S(1)}, bf16[3,144,128]{2,1,0:T(8,128)(2,1)S(1)}, u32[]{:S(2)}, u32[]{:S(2)}) collective-permute-start(bf16[3,144,128]{2,1,0:T(8,128)(2,1)S(1)} %get-tuple-element.28), channel_id=1, source_target_pairs={{0,2},{1,3},{2,0},{3,1},{4,6},{5,7},{6,4},{7,5},{8,10},{9,11},{10,... | collective-permute-start | bytes 331784 | tf_op jit(solution)/shard_map/ppermute | solution.py:421
  26.6 1.2 %collective-permute-start.15 = (bf16[3,144,128]{2,1,0:T(8,128)(2,1)S(1)}, bf16[3,144,128]{2,1,0:T(8,128)(2,1)S(1)}, u32[]{:S(2)}, u32[]{:S(2)}) collective-permute-start(bf16[3,144,128]{2,1,0:T(8,128)(2,1)S(1)} %get-tuple-element.29), channel_id=1, source_target_pairs={{0,3},{1,2},{2,1},{3,0},{4,7},{5,6},{6,5},{7,4},{8,11},{9,10},{10,... | collective-permute-start | bytes 331784 | tf_op jit(solution)/shard_map/ppermute | solution.py:421
  27.8 1.9 %second_part.1 = (bf16[1,144,128]{2,1,0:T(8,128)(2,1)S(1)}, bf16[1,144,128]{2,1,0:T(8,128)(2,1)S(1)}, bf16[1,144,128]{2,1,0:T(8,128)(2,1)S(1)}, bf16[1,144,128]{2,1,0:T(8,128)(2,1)S(1)}) custom-call(s32[96]{0:T(128)S(1)} %get-tuple-element.52.refs_3_.slot_ref, s32[96]{0:T(128)S(1)} %get-tuple-element.51.refs_4_.block_ref, ...), custom_call_target="tpu_custom_call" | custom-call | flops 10000000000 | bytes 5242880 | tf_op jit(solution)/shard_map/second_part/pallas_call | solution.py:248
  29.9 0.8 %collective-permute-start.12 = (bf16[1,144,128]{2,1,0:T(8,128)(2,1)S(1)}, bf16[1,144,128]{2,1,0:T(8,128)(2,1)S(1)}, u32[]{:S(2)}, u32[]{:S(2)}) collective-permute-start(bf16[1,144,128]{2,1,0:T(8,128)(2,1)S(1)} %get-tuple-element.25), channel_id=1, source_target_pairs={{0,2},{1,3},{2,0},{3,1},{4,6},{5,7},{6,4},{7,5},{8,10},{9,11},{10,... | collective-permute-start | bytes 110600 | tf_op jit(solution)/shard_map/ppermute | solution.py:421
  30.7 0.9 %collective-permute-start.13 = (bf16[1,144,128]{2,1,0:T(8,128)(2,1)S(1)}, bf16[1,144,128]{2,1,0:T(8,128)(2,1)S(1)}, u32[]{:S(2)}, u32[]{:S(2)}) collective-permute-start(bf16[1,144,128]{2,1,0:T(8,128)(2,1)S(1)} %get-tuple-element.26), channel_id=1, source_target_pairs={{0,3},{1,2},{2,1},{3,0},{4,7},{5,6},{6,5},{7,4},{8,11},{9,10},{10,... | collective-permute-start | bytes 110600 | tf_op jit(solution)/shard_map/ppermute | solution.py:421
  31.9 1.5 %collective-permute-done.15.refs_3_ = bf16[3,144,128]{2,1,0:T(8,128)(2,1)S(1)} collective-permute-done((bf16[3,144,128]{2,1,0:T(8,128)(2,1)S(1)}, bf16[3,144,128]{2,1,0:T(8,128)(2,1)S(1)}, u32[]{:S(2)}, u32[]{:S(2)}) %collective-permute-start.15) | collective-permute-done | bytes 110624 | tf_op jit(solution)/shard_map/ppermute | solution.py:421
  33.5 3.9 %collective-permute-start.16 = (bf16[256,128]{1,0:T(8,128)(2,1)S(1)}, bf16[256,128]{1,0:T(8,128)(2,1)S(1)}, u32[]{:S(2)}, u32[]{:S(2)}) collective-permute-start(bf16[256,128]{1,0:T(8,128)(2,1)S(1)} %get-tuple-element.30), channel_id=1, source_target_pairs={{0,12},{1,13},{2,14},{3,15},{4,8},{5,9},{6,10},{7,11},{8,4},{9,5},... | collective-permute-start | bytes 196616 | tf_op jit(solution)/shard_map/ppermute | solution.py:421
  37.4 0.6 %collective-permute-start.18 = (bf16[256,128]{1,0:T(8,128)(2,1)S(1)}, bf16[256,128]{1,0:T(8,128)(2,1)S(1)}, u32[]{:S(2)}, u32[]{:S(2)}) collective-permute-start(bf16[256,128]{1,0:T(8,128)(2,1)S(1)} %get-tuple-element.32), channel_id=1, source_target_pairs={{0,4},{1,5},{2,6},{3,7},{4,0},{5,1},{6,2},{7,3},{8,12},{9,13},{10,... | collective-permute-start | bytes 196616 | tf_op jit(solution)/shard_map/ppermute | solution.py:421
  38.1 2.0 %collective-permute-done.16.refs_1_ = bf16[256,128]{1,0:T(8,128)(2,1)S(1)} collective-permute-done((bf16[256,128]{1,0:T(8,128)(2,1)S(1)}, bf16[256,128]{1,0:T(8,128)(2,1)S(1)}, u32[]{:S(2)}, u32[]{:S(2)}) %collective-permute-start.16) | collective-permute-done | bytes 65568 | tf_op jit(solution)/shard_map/ppermute | solution.py:421
  40.1 3.2 %collective-permute-done.17.refs_2_ = bf16[256,128]{1,0:T(8,128)(2,1)S(1)} collective-permute-done((bf16[256,128]{1,0:T(8,128)(2,1)S(1)}, bf16[256,128]{1,0:T(8,128)(2,1)S(1)}, u32[]{:S(2)}, u32[]{:S(2)}) %collective-permute-start.17) | collective-permute-done | bytes 65568 | tf_op jit(solution)/shard_map/ppermute | solution.py:421
  43.6 0.7 %total_of.1 = bf16[256,128]{1,0:T(8,128)(2,1)} custom-call(f32[256,128]{1,0:T(8,128)S(1)} %spread.2.refs_0_, bf16[256,128]{1,0:T(8,128)(2,1)S(1)} %collective-permute-done.16.refs_1_, bf16[256,128]{1,0:T(8,128)(2,1)S(1)} %collective-permute-done.17.refs_2_, bf16[256,128]{1,0:T(8,128)(2,1)S(1)} %collective-permute-done.18.refs_3_), custom_call_target="tpu_custom_call" | custom-call | tf_op jit(solution)/shard_map/total_of/pallas_call | solution.py:381
  (70 shorter events, 4.6 us)
Async XLA Ops:
  0.0 11.4 %collective-permute-start.4 = (bf16[256,128]{1,0:T(8,128)(2,1)}, bf16[256,128]{1,0:T(8,128)(2,1)S(1)}, u32[]{:S(2)}, u32[]{:S(2)}) collective-permute-start(bf16[256,128]{1,0:T(8,128)(2,1)} %own.1), channel_id=1, source_target_pairs={{0,2},{1,3},{2,0},{3,1},{4,6},{5,7},{6,4},{7,5},{8,10},{9,11},{10,... | collective-permute-start | bytes 196616 | tf_op jit(solution)/shard_map/ppermute | solution.py:421
  3.0 11.1 %collective-permute-start.3 = (bf16[256,128]{1,0:T(8,128)(2,1)}, bf16[256,128]{1,0:T(8,128)(2,1)S(1)}, u32[]{:S(2)}, u32[]{:S(2)}) collective-permute-start(bf16[256,128]{1,0:T(8,128)(2,1)} %own.1), channel_id=1, source_target_pairs={{0,1},{1,0},{2,3},{3,2},{4,5},{5,4},{6,7},{7,6},{8,9},{9,8},{10,11... | collective-permute-start | bytes 196616 | tf_op jit(solution)/shard_map/ppermute | solution.py:421
  3.0 8.2 %collective-permute-start.1 = (bf16[256,128]{1,0:T(8,128)(2,1)}, bf16[256,128]{1,0:T(8,128)(2,1)S(1)}, u32[]{:S(2)}, u32[]{:S(2)}) collective-permute-start(bf16[256,128]{1,0:T(8,128)(2,1)} %own.1), channel_id=1, source_target_pairs={{0,8},{1,9},{2,10},{3,11},{4,12},{5,13},{6,14},{7,15},{8,0},{9,1},... | collective-permute-start | bytes 196616 | tf_op jit(solution)/shard_map/ppermute | solution.py:421
  5.6 5.6 %collective-permute-start = (bf16[256,128]{1,0:T(8,128)(2,1)}, bf16[256,128]{1,0:T(8,128)(2,1)S(1)}, u32[]{:S(2)}, u32[]{:S(2)}) collective-permute-start(bf16[256,128]{1,0:T(8,128)(2,1)} %own.1), channel_id=1, source_target_pairs={{0,4},{1,5},{2,6},{3,7},{4,0},{5,1},{6,2},{7,3},{8,12},{9,13},{10,... | collective-permute-start | bytes 196616 | tf_op jit(solution)/shard_map/ppermute | solution.py:421
  7.1 6.3 %collective-permute-start.7 = (bf16[256,128]{1,0:T(8,128)(2,1)}, bf16[256,128]{1,0:T(8,128)(2,1)S(1)}, u32[]{:S(2)}, u32[]{:S(2)}) collective-permute-start(bf16[256,128]{1,0:T(8,128)(2,1)} %own.1), channel_id=1, source_target_pairs={{0,12},{1,13},{2,14},{3,15},{4,8},{5,9},{6,10},{7,11},{8,4},{9,5},... | collective-permute-start | bytes 196616 | tf_op jit(solution)/shard_map/ppermute | solution.py:421
  11.1 3.0 %slice-start = ((s8[10485760]{0:T(1024)(128)(4,1)}), s8[4194304]{0:T(1024)(128)(4,1)S(1)}, s32[]{:S(2)}) async-start(s8[10485760]{0:T(1024)(128)(4,1)} %bitcast.1), calls=%async_computation | async-start | bytes 8388608
  11.1 3.4 %slice-start.1 = ((s8[10485760]{0:T(1024)(128)(4,1)}), s8[4194304]{0:T(1024)(128)(4,1)S(1)}, s32[]{:S(2)}) async-start(s8[10485760]{0:T(1024)(128)(4,1)} %bitcast.1), calls=%async_computation.1 | async-start | bytes 8388608
  11.2 4.0 %slice-start.2 = ((s8[10485760]{0:T(1024)(128)(4,1)}), s8[2097152]{0:T(1024)(128)(4,1)S(1)}, s32[]{:S(2)}) async-start(s8[10485760]{0:T(1024)(128)(4,1)} %bitcast.1), calls=%async_computation.2 | async-start | bytes 4194304
  11.2 4.0 %copy-start = (bf16[256,128]{1,0:T(8,128)(2,1)S(1)}, bf16[256,128]{1,0:T(8,128)(2,1)}, u32[]{:S(2)}) copy-start(bf16[256,128]{1,0:T(8,128)(2,1)} %own.1) | copy-start | bytes 196612
  11.2 2.9 %collective-permute-start.2 = (bf16[2,256,128]{2,1,0:T(8,128)(2,1)S(1)}, bf16[2,256,128]{2,1,0:T(8,128)(2,1)S(1)}, u32[]{:S(2)}, u32[]{:S(2)}) collective-permute-start(bf16[2,256,128]{2,1,0:T(8,128)(2,1)S(1)} %merge.1.refs_0_), channel_id=1, source_target_pairs={{0,1},{1,0},{2,3},{3,2},{4,5},{5,4},{6,7},{7,6},{8,9},{9,8},{10,11... | collective-permute-start | bytes 393224 | tf_op jit(solution)/shard_map/ppermute | solution.py:421
  11.4 2.7 %collective-permute-start.5 = (bf16[256,128]{1,0:T(8,128)(2,1)S(1)}, bf16[256,128]{1,0:T(8,128)(2,1)S(1)}, u32[]{:S(2)}, u32[]{:S(2)}) collective-permute-start(bf16[256,128]{1,0:T(8,128)(2,1)S(1)} %collective-permute-done.4.refs_3_), channel_id=1, source_target_pairs={{0,1},{1,0},{2,3},{3,2},{4,5},{5,4},{6,7},{7,6},{8,9},{9,8},{10,11... | collective-permute-start | bytes 196616 | tf_op jit(solution)/shard_map/ppermute | solution.py:421
  12.1 6.8 %collective-permute-start.6 = (bf16[2,256,128]{2,1,0:T(8,128)(2,1)S(1)}, bf16[2,256,128]{2,1,0:T(8,128)(2,1)S(1)}, u32[]{:S(2)}, u32[]{:S(2)}) collective-permute-start(bf16[2,256,128]{2,1,0:T(8,128)(2,1)S(1)} %merge.1.refs_0_), channel_id=1, source_target_pairs={{0,2},{1,3},{2,0},{3,1},{4,6},{5,7},{6,4},{7,5},{8,10},{9,11},{10,... | collective-permute-start | bytes 393224 | tf_op jit(solution)/shard_map/ppermute | solution.py:421
  13.4 5.5 %collective-permute-start.8 = (bf16[256,128]{1,0:T(8,128)(2,1)S(1)}, bf16[256,128]{1,0:T(8,128)(2,1)S(1)}, u32[]{:S(2)}, u32[]{:S(2)}) collective-permute-start(bf16[256,128]{1,0:T(8,128)(2,1)S(1)} %collective-permute-done.7.refs_1_), channel_id=1, source_target_pairs={{0,2},{1,3},{2,0},{3,1},{4,6},{5,7},{6,4},{7,5},{8,10},{9,11},{10,... | collective-permute-start | bytes 196616 | tf_op jit(solution)/shard_map/ppermute | solution.py:421
  18.9 1.6 %collective-permute-start.9 = (bf16[4,256,128]{2,1,0:T(8,128)(2,1)S(1)}, bf16[4,256,128]{2,1,0:T(8,128)(2,1)S(1)}, u32[]{:S(2)}, u32[]{:S(2)}) collective-permute-start(bf16[4,256,128]{2,1,0:T(8,128)(2,1)S(1)} %gate.1.refs_9_), channel_id=1, source_target_pairs={{0,1},{1,0},{2,3},{3,2},{4,5},{5,4},{6,7},{7,6},{8,9},{9,8},{10,11... | collective-permute-start | bytes 786440 | tf_op jit(solution)/shard_map/ppermute | solution.py:421
  25.9 1.9 %collective-permute-start.10 = (bf16[3,144,128]{2,1,0:T(8,128)(2,1)S(1)}, bf16[3,144,128]{2,1,0:T(8,128)(2,1)S(1)}, u32[]{:S(2)}, u32[]{:S(2)}) collective-permute-start(bf16[3,144,128]{2,1,0:T(8,128)(2,1)S(1)} %get-tuple-element.22), channel_id=1, source_target_pairs={{0,1},{1,0},{2,3},{3,2},{4,5},{5,4},{6,7},{7,6},{8,9},{9,8},{10,11... | collective-permute-start | bytes 331784 | tf_op jit(solution)/shard_map/ppermute | solution.py:421
  25.9 5.9 %collective-permute-start.14 = (bf16[3,144,128]{2,1,0:T(8,128)(2,1)S(1)}, bf16[3,144,128]{2,1,0:T(8,128)(2,1)S(1)}, u32[]{:S(2)}, u32[]{:S(2)}) collective-permute-start(bf16[3,144,128]{2,1,0:T(8,128)(2,1)S(1)} %get-tuple-element.28), channel_id=1, source_target_pairs={{0,2},{1,3},{2,0},{3,1},{4,6},{5,7},{6,4},{7,5},{8,10},{9,11},{10,... | collective-permute-start | bytes 331784 | tf_op jit(solution)/shard_map/ppermute | solution.py:421
  26.6 6.7 %collective-permute-start.15 = (bf16[3,144,128]{2,1,0:T(8,128)(2,1)S(1)}, bf16[3,144,128]{2,1,0:T(8,128)(2,1)S(1)}, u32[]{:S(2)}, u32[]{:S(2)}) collective-permute-start(bf16[3,144,128]{2,1,0:T(8,128)(2,1)S(1)} %get-tuple-element.29), channel_id=1, source_target_pairs={{0,3},{1,2},{2,1},{3,0},{4,7},{5,6},{6,5},{7,4},{8,11},{9,10},{10,... | collective-permute-start | bytes 331784 | tf_op jit(solution)/shard_map/ppermute | solution.py:421
  29.7 7.7 %collective-permute-start.11 = (bf16[1,144,128]{2,1,0:T(8,128)(2,1)S(1)}, bf16[1,144,128]{2,1,0:T(8,128)(2,1)S(1)}, u32[]{:S(2)}, u32[]{:S(2)}) collective-permute-start(bf16[1,144,128]{2,1,0:T(8,128)(2,1)S(1)} %get-tuple-element.24), channel_id=1, source_target_pairs={{0,1},{1,0},{2,3},{3,2},{4,5},{5,4},{6,7},{7,6},{8,9},{9,8},{10,11... | collective-permute-start | bytes 110600 | tf_op jit(solution)/shard_map/ppermute | solution.py:421
  29.9 8.2 %collective-permute-start.12 = (bf16[1,144,128]{2,1,0:T(8,128)(2,1)S(1)}, bf16[1,144,128]{2,1,0:T(8,128)(2,1)S(1)}, u32[]{:S(2)}, u32[]{:S(2)}) collective-permute-start(bf16[1,144,128]{2,1,0:T(8,128)(2,1)S(1)} %get-tuple-element.25), channel_id=1, source_target_pairs={{0,2},{1,3},{2,0},{3,1},{4,6},{5,7},{6,4},{7,5},{8,10},{9,11},{10,... | collective-permute-start | bytes 110600 | tf_op jit(solution)/shard_map/ppermute | solution.py:421
  30.7 7.4 %collective-permute-start.13 = (bf16[1,144,128]{2,1,0:T(8,128)(2,1)S(1)}, bf16[1,144,128]{2,1,0:T(8,128)(2,1)S(1)}, u32[]{:S(2)}, u32[]{:S(2)}) collective-permute-start(bf16[1,144,128]{2,1,0:T(8,128)(2,1)S(1)} %get-tuple-element.26), channel_id=1, source_target_pairs={{0,3},{1,2},{2,1},{3,0},{4,7},{5,6},{6,5},{7,4},{8,11},{9,10},{10,... | collective-permute-start | bytes 110600 | tf_op jit(solution)/shard_map/ppermute | solution.py:421
  33.5 6.6 %collective-permute-start.16 = (bf16[256,128]{1,0:T(8,128)(2,1)S(1)}, bf16[256,128]{1,0:T(8,128)(2,1)S(1)}, u32[]{:S(2)}, u32[]{:S(2)}) collective-permute-start(bf16[256,128]{1,0:T(8,128)(2,1)S(1)} %get-tuple-element.30), channel_id=1, source_target_pairs={{0,12},{1,13},{2,14},{3,15},{4,8},{5,9},{6,10},{7,11},{8,4},{9,5},... | collective-permute-start | bytes 196616 | tf_op jit(solution)/shard_map/ppermute | solution.py:421
  37.4 5.9 %collective-permute-start.17 = (bf16[256,128]{1,0:T(8,128)(2,1)S(1)}, bf16[256,128]{1,0:T(8,128)(2,1)S(1)}, u32[]{:S(2)}, u32[]{:S(2)}) collective-permute-start(bf16[256,128]{1,0:T(8,128)(2,1)S(1)} %get-tuple-element.31), channel_id=1, source_target_pairs={{0,8},{1,9},{2,10},{3,11},{4,12},{5,13},{6,14},{7,15},{8,0},{9,1},... | collective-permute-start | bytes 196616 | tf_op jit(solution)/shard_map/ppermute | solution.py:421
  37.4 6.2 %collective-permute-start.18 = (bf16[256,128]{1,0:T(8,128)(2,1)S(1)}, bf16[256,128]{1,0:T(8,128)(2,1)S(1)}, u32[]{:S(2)}, u32[]{:S(2)}) collective-permute-start(bf16[256,128]{1,0:T(8,128)(2,1)S(1)} %get-tuple-element.32), channel_id=1, source_target_pairs={{0,4},{1,5},{2,6},{3,7},{4,0},{5,1},{6,2},{7,3},{8,12},{9,13},{10,... | collective-permute-start | bytes 196616 | tf_op jit(solution)/shard_map/ppermute | solution.py:421

commit v13 on v11

--- a/solution.py
+++ b/solution.py
@@ -8,8 +8,8 @@
 from jax.sharding import PartitionSpec as P
 
 AB_DEV = 8
-CHUNK = 4
-UNROLL = 4
+CHUNK = 2
+TURNS = (8, 2, 1)
 TAIL = 16
 PLANE = 4
 SPREAD_COST = 10**10
@@ -91,15 +91,14 @@
 
 
 def sweep(low, high, body):
-    whole = (high - low) // UNROLL
-
-    @pl.loop(0, whole)
-    def _(step):
-        body([low + step * UNROLL + u for u in range(UNROLL)])
-
-    @pl.loop(low + whole * UNROLL, high)
-    def _(chunk):
-        body([chunk])
+    for size in TURNS:
+        whole = (high - low) // size
+
+        @pl.loop(0, whole)
+        def _(step, low=low, size=size):
+            body([low + step * size + u for u in range(size)])
+
+        low = low + whole * size
 
 
 def fit(lists, tiles, ct, zacc, low, high):

time: 43.7 us -> 44 us (level)
  Pallas kernels: 11.9 us -> 8.54 us
  waiting for transfers between devices: 9.4 us -> 12.3 us
  starting transfers between devices: 17.2 us -> 18.4 us
    ppermute x19, waiting for transfers between devices: 9.4 us -> 12.3 us  [swap(): return lax.ppermute(array, 'aux', [(i, i ^ m) for i in range(n_aux)])]
    pallas_call x1, Pallas kernels: 5.91 us -> 4.2 us  [first_part(): pl.pallas_call(kernel, out_shape=out_shape, in_specs=[smem] * 7 + [vmem]...]
    ppermute x19, starting transfers between devices: 17.2 us -> 18.4 us  [swap(): return lax.ppermute(array, 'aux', [(i, i ^ m) for i in range(n_aux)])]
    pallas_call x1, Pallas kernels: 2.51 us -> 1.59 us  [second_part(): pl.pallas_call(kernel, out_shape=[jax.ShapeDtypeStruct(shape, jnp.bfloat1...]
    pallas_call x1, Pallas kernels: 2.61 us -> 1.84 us  [begin(): pl.pallas_call(kernel, out_shape=[jax.ShapeDtypeStruct((AB_DEV, nocc, aux...]
  transfers between devices with their start and end apart: 19 -> 19, of which waited for: 7 -> 6; matrix products, arithmetic and copies ran while one was open for 8% -> 8% of each run, Pallas kernels for 12% -> 8%
where the time goes in v13:
time: 44 us
  starting transfers between devices  18.4 us (42%)
  waiting for transfers between devices  12.3 us (28%)
  Pallas kernels  8.54 us (19%)
  other arithmetic  3.39 us (8%)
  between operations  0.89 us (2%)
  local copies, waits for them, and re-layouts  0.48 us (1%)
    ppermute x19, starting transfers between devices, swap(): return lax.ppermute(array, 'aux', [(i, i ^ m) for i in range(n_aux)])  18.4 us
    ppermute x19, waiting for transfers between devices, swap(): return lax.ppermute(array, 'aux', [(i, i ^ m) for i in range(n_aux)])  12.3 us
    pallas_call x1, Pallas kernels, first_part(): pl.pallas_call(kernel, out_shape=out_shape, in_specs=[smem] * 7 + [vmem]...  4.2 us
    pallas_call x1, Pallas kernels, begin(): pl.pallas_call(kernel, out_shape=[jax.ShapeDtypeStruct((AB_DEV, nocc, aux...  1.84 us
    pallas_call x1, Pallas kernels, second_part(): pl.pallas_call(kernel, out_shape=[jax.ShapeDtypeStruct(shape, jnp.bfloat1...  1.59 us
  transfers between devices with their start and end apart: 19, of which 6 were waited for; matrix products, arithmetic and copies ran while one was open for 8% of the time, Pallas kernels for 8%

profile of v13, /device:TPU:0, one launch (start us, length us, event | category | flops | bytes accessed | tf_op | source)
XLA Modules:
  0.0 44.0 jit_solution(733346183655771113)
XLA Ops:
  0.0 3.0 %collective-permute-start.4 = (bf16[256,128]{1,0:T(8,128)(2,1)}, bf16[256,128]{1,0:T(8,128)(2,1)S(1)}, u32[]{:S(2)}, u32[]{:S(2)}) collective-permute-start(bf16[256,128]{1,0:T(8,128)(2,1)} %own.1), channel_id=1, source_target_pairs={{0,2},{1,3},{2,0},{3,1},{4,6},{5,7},{6,4},{7,5},{8,10},{9,11},{10,... | collective-permute-start | bytes 196616 | tf_op jit(solution)/shard_map/ppermute | solution.py:422
  3.0 2.6 %collective-permute-start.1 = (bf16[256,128]{1,0:T(8,128)(2,1)}, bf16[256,128]{1,0:T(8,128)(2,1)S(1)}, u32[]{:S(2)}, u32[]{:S(2)}) collective-permute-start(bf16[256,128]{1,0:T(8,128)(2,1)} %own.1), channel_id=1, source_target_pairs={{0,8},{1,9},{2,10},{3,11},{4,12},{5,13},{6,14},{7,15},{8,0},{9,1},... | collective-permute-start | bytes 196616 | tf_op jit(solution)/shard_map/ppermute | solution.py:422
  5.6 1.6 %collective-permute-start = (bf16[256,128]{1,0:T(8,128)(2,1)}, bf16[256,128]{1,0:T(8,128)(2,1)S(1)}, u32[]{:S(2)}, u32[]{:S(2)}) collective-permute-start(bf16[256,128]{1,0:T(8,128)(2,1)} %own.1), channel_id=1, source_target_pairs={{0,4},{1,5},{2,6},{3,7},{4,0},{5,1},{6,2},{7,3},{8,12},{9,13},{10,... | collective-permute-start | bytes 196616 | tf_op jit(solution)/shard_map/ppermute | solution.py:422
  8.0 0.8 %select_reduce_fusion.6 = s32[64]{0:T(128)S(1)} fusion(s32[64]{0:T(128)} %param.9, s32[32]{0:T(128)} %param.8), kind=kLoop, calls=%fused_computation.15 | loop fusion | flops 6080 | bytes 640 | tf_op jit(solution)/shard_map/reduce_sum | solution.py:21
  8.8 0.7 %and_select_fusion.7 = (s32[64]{0:T(128)S(1)}, s32[64]{0:T(128)S(1)}, s32[64]{0:T(128)S(1)}, s32[64]{0:T(128)S(1)}) fusion(s32[]{:T(128)} %bitcast.1, s32[64]{0:T(128)} %param.10, s32[]{:T(128)S(6)} %axis_index.12, s32[64]{0:T(128)S(1)} %select_reduce_fusion.6), kind=kLoop, calls=%fused_computation.48 | loop fusion | flops 4416 | bytes 1544 | tf_op jit(solution)/shard_map/jit(remainder)/select_n | solution.py:36
  10.6 0.6 %collective-permute-start.5 = (bf16[256,128]{1,0:T(8,128)(2,1)S(1)}, bf16[256,128]{1,0:T(8,128)(2,1)S(1)}, u32[]{:S(2)}, u32[]{:S(2)}) collective-permute-start(bf16[256,128]{1,0:T(8,128)(2,1)S(1)} %collective-permute-done.4.refs_3_), channel_id=1, source_target_pairs={{0,1},{1,0},{2,3},{3,2},{4,5},{5,4},{6,7},{7,6},{8,9},{9,8},{10,11... | collective-permute-start | bytes 196616 | tf_op jit(solution)/shard_map/ppermute | solution.py:422
  11.6 1.8 %collective-permute-done.7.refs_1_ = bf16[256,128]{1,0:T(8,128)(2,1)S(1)} collective-permute-done((bf16[256,128]{1,0:T(8,128)(2,1)}, bf16[256,128]{1,0:T(8,128)(2,1)S(1)}, u32[]{:S(2)}, u32[]{:S(2)}) %collective-permute-start.7) | collective-permute-done | bytes 65568 | tf_op jit(solution)/shard_map/ppermute | solution.py:422
  13.4 0.5 %collective-permute-start.8 = (bf16[256,128]{1,0:T(8,128)(2,1)S(1)}, bf16[256,128]{1,0:T(8,128)(2,1)S(1)}, u32[]{:S(2)}, u32[]{:S(2)}) collective-permute-start(bf16[256,128]{1,0:T(8,128)(2,1)S(1)} %collective-permute-done.7.refs_1_), channel_id=1, source_target_pairs={{0,2},{1,3},{2,0},{3,1},{4,6},{5,7},{6,4},{7,5},{8,10},{9,11},{10,... | collective-permute-start | bytes 196616 | tf_op jit(solution)/shard_map/ppermute | solution.py:422
  14.0 0.5 %slice-done.2 = s8[2097152]{0:T(1024)(128)(4,1)S(1)} async-done(((s8[10485760]{0:T(1024)(128)(4,1)}), s8[2097152]{0:T(1024)(128)(4,1)S(1)}, s32[]{:S(2)}) %slice-start.2) | async-done | bytes 2097176
  14.4 1.8 %begin.1 = (f32[8,128,640]{2,1,0:T(8,128)S(1)}, s32[64]{0:T(128)S(1)}) custom-call(s32[96]{0:T(128)S(1)} %get-tuple-element.53.slot_ref.refs_0_, s32[96]{0:T(128)S(1)} %get-tuple-element.52.block_ref.refs_1_, s32[64]{0:T(128)S(1)} %pad_add_fusion.gid_ref.refs_2_, s32[16]{0:T(128)S(1)} %select_reduce_fusion.9.bit_ref.refs_6_, ...), custom_call_target="tpu_custom_call" | custom-call | flops 1342177280 | bytes 5242880 | tf_op jit(solution)/shard_map/begin/pallas_call | solution.py:154
  17.1 1.0 %collective-permute-done.8.refs_2_ = bf16[256,128]{1,0:T(8,128)(2,1)S(1)} collective-permute-done((bf16[256,128]{1,0:T(8,128)(2,1)S(1)}, bf16[256,128]{1,0:T(8,128)(2,1)S(1)}, u32[]{:S(2)}, u32[]{:S(2)}) %collective-permute-start.8) | collective-permute-done | bytes 65568 | tf_op jit(solution)/shard_map/ppermute | solution.py:422
  18.3 1.4 %collective-permute-done.9.refs_10_ = bf16[4,256,128]{2,1,0:T(8,128)(2,1)S(1)} collective-permute-done((bf16[4,256,128]{2,1,0:T(8,128)(2,1)S(1)}, bf16[4,256,128]{2,1,0:T(8,128)(2,1)S(1)}, u32[]{:S(2)}, u32[]{:S(2)}) %collective-permute-start.9) | collective-permute-done | bytes 262176 | tf_op jit(solution)/shard_map/ppermute | solution.py:422
  19.7 4.2 %first_part.1 = (bf16[3,144,128]{2,1,0:T(8,128)(2,1)S(1)}, bf16[3,144,128]{2,1,0:T(8,128)(2,1)S(1)}, bf16[3,144,128]{2,1,0:T(8,128)(2,1)S(1)}, bf16[3,144,128]{2...) custom-call(s32[96]{0:T(128)S(1)} %get-tuple-element.53.slot_ref.ref, ...), custom_call_target="tpu_custom_call", output_to_operand_aliasing={{5}: (8, {})} | custom-call | flops 2013265920 | bytes 5242880 | tf_op jit(solution)/shard_map/first_part/pallas_call | solution.py:216
  23.9 0.6 %collective-permute-start.10 = (bf16[3,144,128]{2,1,0:T(8,128)(2,1)S(1)}, bf16[3,144,128]{2,1,0:T(8,128)(2,1)S(1)}, u32[]{:S(2)}, u32[]{:S(2)}) collective-permute-start(bf16[3,144,128]{2,1,0:T(8,128)(2,1)S(1)} %get-tuple-element.22), channel_id=1, source_target_pairs={{0,1},{1,0},{2,3},{3,2},{4,5},{5,4},{6,7},{7,6},{8,9},{9,8},{10,11... | collective-permute-start | bytes 331784 | tf_op jit(solution)/shard_map/ppermute | solution.py:422
  24.6 1.8 %collective-permute-start.14 = (bf16[3,144,128]{2,1,0:T(8,128)(2,1)S(1)}, bf16[3,144,128]{2,1,0:T(8,128)(2,1)S(1)}, u32[]{:S(2)}, u32[]{:S(2)}) collective-permute-start(bf16[3,144,128]{2,1,0:T(8,128)(2,1)S(1)} %get-tuple-element.28), channel_id=1, source_target_pairs={{0,2},{1,3},{2,0},{3,1},{4,6},{5,7},{6,4},{7,5},{8,10},{9,11},{10,... | collective-permute-start | bytes 331784 | tf_op jit(solution)/shard_map/ppermute | solution.py:422
  26.5 1.6 %second_part.1 = (bf16[1,144,128]{2,1,0:T(8,128)(2,1)S(1)}, bf16[1,144,128]{2,1,0:T(8,128)(2,1)S(1)}, bf16[1,144,128]{2,1,0:T(8,128)(2,1)S(1)}, bf16[1,144,128]{2,1,0:T(8,128)(2,1)S(1)}) custom-call(s32[96]{0:T(128)S(1)} %get-tuple-element.51.refs_3_.slot_ref, s32[96]{0:T(128)S(1)} %get-tuple-element.50.refs_4_.block_ref, ...), custom_call_target="tpu_custom_call" | custom-call | flops 10000000000 | bytes 5242880 | tf_op jit(solution)/shard_map/second_part/pallas_call | solution.py:249
  28.0 0.4 collective-permute-start.11
  28.5 2.0 %collective-permute-start.12 = (bf16[1,144,128]{2,1,0:T(8,128)(2,1)S(1)}, bf16[1,144,128]{2,1,0:T(8,128)(2,1)S(1)}, u32[]{:S(2)}, u32[]{:S(2)}) collective-permute-start(bf16[1,144,128]{2,1,0:T(8,128)(2,1)S(1)} %get-tuple-element.25), channel_id=1, source_target_pairs={{0,2},{1,3},{2,0},{3,1},{4,6},{5,7},{6,4},{7,5},{8,10},{9,11},{10,... | collective-permute-start | bytes 110600 | tf_op jit(solution)/shard_map/ppermute | solution.py:422
  30.5 1.6 %collective-permute-done.15.refs_3_ = bf16[3,144,128]{2,1,0:T(8,128)(2,1)S(1)} collective-permute-done((bf16[3,144,128]{2,1,0:T(8,128)(2,1)S(1)}, bf16[3,144,128]{2,1,0:T(8,128)(2,1)S(1)}, u32[]{:S(2)}, u32[]{:S(2)}) %collective-permute-start.15) | collective-permute-done | bytes 110624 | tf_op jit(solution)/shard_map/ppermute | solution.py:422
  32.3 3.6 %collective-permute-start.16 = (bf16[256,128]{1,0:T(8,128)(2,1)S(1)}, bf16[256,128]{1,0:T(8,128)(2,1)S(1)}, u32[]{:S(2)}, u32[]{:S(2)}) collective-permute-start(bf16[256,128]{1,0:T(8,128)(2,1)S(1)} %get-tuple-element.30), channel_id=1, source_target_pairs={{0,12},{1,13},{2,14},{3,15},{4,8},{5,9},{6,10},{7,11},{8,4},{9,5},... | collective-permute-start | bytes 196616 | tf_op jit(solution)/shard_map/ppermute | solution.py:422
  35.9 0.7 %collective-permute-start.17 = (bf16[256,128]{1,0:T(8,128)(2,1)S(1)}, bf16[256,128]{1,0:T(8,128)(2,1)S(1)}, u32[]{:S(2)}, u32[]{:S(2)}) collective-permute-start(bf16[256,128]{1,0:T(8,128)(2,1)S(1)} %get-tuple-element.31), channel_id=1, source_target_pairs={{0,8},{1,9},{2,10},{3,11},{4,12},{5,13},{6,14},{7,15},{8,0},{9,1},... | collective-permute-start | bytes 196616 | tf_op jit(solution)/shard_map/ppermute | solution.py:422
  36.8 2.3 %collective-permute-done.16.refs_1_ = bf16[256,128]{1,0:T(8,128)(2,1)S(1)} collective-permute-done((bf16[256,128]{1,0:T(8,128)(2,1)S(1)}, bf16[256,128]{1,0:T(8,128)(2,1)S(1)}, u32[]{:S(2)}, u32[]{:S(2)}) %collective-permute-start.16) | collective-permute-done | bytes 65568 | tf_op jit(solution)/shard_map/ppermute | solution.py:422
  39.1 4.2 %collective-permute-done.17.refs_2_ = bf16[256,128]{1,0:T(8,128)(2,1)S(1)} collective-permute-done((bf16[256,128]{1,0:T(8,128)(2,1)S(1)}, bf16[256,128]{1,0:T(8,128)(2,1)S(1)}, u32[]{:S(2)}, u32[]{:S(2)}) %collective-permute-start.17) | collective-permute-done | bytes 65568 | tf_op jit(solution)/shard_map/ppermute | solution.py:422
  43.3 0.7 %total_of.1 = bf16[256,128]{1,0:T(8,128)(2,1)} custom-call(f32[256,128]{1,0:T(8,128)S(1)} %spread.2.refs_0_, bf16[256,128]{1,0:T(8,128)(2,1)S(1)} %collective-permute-done.16.refs_1_, bf16[256,128]{1,0:T(8,128)(2,1)S(1)} %collective-permute-done.17.refs_2_, bf16[256,128]{1,0:T(8,128)(2,1)S(1)} %collective-permute-done.18.refs_3_), custom_call_target="tpu_custom_call" | custom-call | tf_op jit(solution)/shard_map/total_of/pallas_call | solution.py:382
  (62 shorter events, 3.2 us)
Async XLA Ops:
  0.0 10.6 %collective-permute-start.4 = (bf16[256,128]{1,0:T(8,128)(2,1)}, bf16[256,128]{1,0:T(8,128)(2,1)S(1)}, u32[]{:S(2)}, u32[]{:S(2)}) collective-permute-start(bf16[256,128]{1,0:T(8,128)(2,1)} %own.1), channel_id=1, source_target_pairs={{0,2},{1,3},{2,0},{3,1},{4,6},{5,7},{6,4},{7,5},{8,10},{9,11},{10,... | collective-permute-start | bytes 196616 | tf_op jit(solution)/shard_map/ppermute | solution.py:422
  3.0 11.0 %collective-permute-start.3 = (bf16[256,128]{1,0:T(8,128)(2,1)}, bf16[256,128]{1,0:T(8,128)(2,1)S(1)}, u32[]{:S(2)}, u32[]{:S(2)}) collective-permute-start(bf16[256,128]{1,0:T(8,128)(2,1)} %own.1), channel_id=1, source_target_pairs={{0,1},{1,0},{2,3},{3,2},{4,5},{5,4},{6,7},{7,6},{8,9},{9,8},{10,11... | collective-permute-start | bytes 196616 | tf_op jit(solution)/shard_map/ppermute | solution.py:422
  3.0 7.4 %collective-permute-start.1 = (bf16[256,128]{1,0:T(8,128)(2,1)}, bf16[256,128]{1,0:T(8,128)(2,1)S(1)}, u32[]{:S(2)}, u32[]{:S(2)}) collective-permute-start(bf16[256,128]{1,0:T(8,128)(2,1)} %own.1), channel_id=1, source_target_pairs={{0,8},{1,9},{2,10},{3,11},{4,12},{5,13},{6,14},{7,15},{8,0},{9,1},... | collective-permute-start | bytes 196616 | tf_op jit(solution)/shard_map/ppermute | solution.py:422
  5.6 4.8 %collective-permute-start = (bf16[256,128]{1,0:T(8,128)(2,1)}, bf16[256,128]{1,0:T(8,128)(2,1)S(1)}, u32[]{:S(2)}, u32[]{:S(2)}) collective-permute-start(bf16[256,128]{1,0:T(8,128)(2,1)} %own.1), channel_id=1, source_target_pairs={{0,4},{1,5},{2,6},{3,7},{4,0},{5,1},{6,2},{7,3},{8,12},{9,13},{10,... | collective-permute-start | bytes 196616 | tf_op jit(solution)/shard_map/ppermute | solution.py:422
  7.1 6.3 %collective-permute-start.7 = (bf16[256,128]{1,0:T(8,128)(2,1)}, bf16[256,128]{1,0:T(8,128)(2,1)S(1)}, u32[]{:S(2)}, u32[]{:S(2)}) collective-permute-start(bf16[256,128]{1,0:T(8,128)(2,1)} %own.1), channel_id=1, source_target_pairs={{0,12},{1,13},{2,14},{3,15},{4,8},{5,9},{6,10},{7,11},{8,4},{9,5},... | collective-permute-start | bytes 196616 | tf_op jit(solution)/shard_map/ppermute | solution.py:422
  10.3 3.6 %slice-start = ((s8[10485760]{0:T(1024)(128)(4,1)}), s8[4194304]{0:T(1024)(128)(4,1)S(1)}, s32[]{:S(2)}) async-start(s8[10485760]{0:T(1024)(128)(4,1)} %bitcast.2), calls=%async_computation | async-start | bytes 8388608
  10.4 3.6 %slice-start.1 = ((s8[10485760]{0:T(1024)(128)(4,1)}), s8[4194304]{0:T(1024)(128)(4,1)S(1)}, s32[]{:S(2)}) async-start(s8[10485760]{0:T(1024)(128)(4,1)} %bitcast.2), calls=%async_computation.1 | async-start | bytes 8388608
  10.4 4.0 %slice-start.2 = ((s8[10485760]{0:T(1024)(128)(4,1)}), s8[2097152]{0:T(1024)(128)(4,1)S(1)}, s32[]{:S(2)}) async-start(s8[10485760]{0:T(1024)(128)(4,1)} %bitcast.2), calls=%async_computation.2 | async-start | bytes 4194304
  10.4 4.0 %copy-start = (bf16[256,128]{1,0:T(8,128)(2,1)S(1)}, bf16[256,128]{1,0:T(8,128)(2,1)}, u32[]{:S(2)}) copy-start(bf16[256,128]{1,0:T(8,128)(2,1)} %own.1) | copy-start | bytes 196612
  10.4 3.5 %collective-permute-start.2 = (bf16[2,256,128]{2,1,0:T(8,128)(2,1)S(1)}, bf16[2,256,128]{2,1,0:T(8,128)(2,1)S(1)}, u32[]{:S(2)}, u32[]{:S(2)}) collective-permute-start(bf16[2,256,128]{2,1,0:T(8,128)(2,1)S(1)} %merge.1.refs_0_), channel_id=1, source_target_pairs={{0,1},{1,0},{2,3},{3,2},{4,5},{5,4},{6,7},{7,6},{8,9},{9,8},{10,11... | collective-permute-start | bytes 393224 | tf_op jit(solution)/shard_map/ppermute | solution.py:422
  10.6 3.3 %collective-permute-start.5 = (bf16[256,128]{1,0:T(8,128)(2,1)S(1)}, bf16[256,128]{1,0:T(8,128)(2,1)S(1)}, u32[]{:S(2)}, u32[]{:S(2)}) collective-permute-start(bf16[256,128]{1,0:T(8,128)(2,1)S(1)} %collective-permute-done.4.refs_3_), channel_id=1, source_target_pairs={{0,1},{1,0},{2,3},{3,2},{4,5},{5,4},{6,7},{7,6},{8,9},{9,8},{10,11... | collective-permute-start | bytes 196616 | tf_op jit(solution)/shard_map/ppermute | solution.py:422
  11.3 6.8 %collective-permute-start.6 = (bf16[2,256,128]{2,1,0:T(8,128)(2,1)S(1)}, bf16[2,256,128]{2,1,0:T(8,128)(2,1)S(1)}, u32[]{:S(2)}, u32[]{:S(2)}) collective-permute-start(bf16[2,256,128]{2,1,0:T(8,128)(2,1)S(1)} %merge.1.refs_0_), channel_id=1, source_target_pairs={{0,2},{1,3},{2,0},{3,1},{4,6},{5,7},{6,4},{7,5},{8,10},{9,11},{10,... | collective-permute-start | bytes 393224 | tf_op jit(solution)/shard_map/ppermute | solution.py:422
  13.4 4.7 %collective-permute-start.8 = (bf16[256,128]{1,0:T(8,128)(2,1)S(1)}, bf16[256,128]{1,0:T(8,128)(2,1)S(1)}, u32[]{:S(2)}, u32[]{:S(2)}) collective-permute-start(bf16[256,128]{1,0:T(8,128)(2,1)S(1)} %collective-permute-done.7.refs_1_), channel_id=1, source_target_pairs={{0,2},{1,3},{2,0},{3,1},{4,6},{5,7},{6,4},{7,5},{8,10},{9,11},{10,... | collective-permute-start | bytes 196616 | tf_op jit(solution)/shard_map/ppermute | solution.py:422
  18.1 1.6 %collective-permute-start.9 = (bf16[4,256,128]{2,1,0:T(8,128)(2,1)S(1)}, bf16[4,256,128]{2,1,0:T(8,128)(2,1)S(1)}, u32[]{:S(2)}, u32[]{:S(2)}) collective-permute-start(bf16[4,256,128]{2,1,0:T(8,128)(2,1)S(1)} %gate.1.refs_9_), channel_id=1, source_target_pairs={{0,1},{1,0},{2,3},{3,2},{4,5},{5,4},{6,7},{7,6},{8,9},{9,8},{10,11... | collective-permute-start | bytes 786440 | tf_op jit(solution)/shard_map/ppermute | solution.py:422
  23.9 2.5 %collective-permute-start.10 = (bf16[3,144,128]{2,1,0:T(8,128)(2,1)S(1)}, bf16[3,144,128]{2,1,0:T(8,128)(2,1)S(1)}, u32[]{:S(2)}, u32[]{:S(2)}) collective-permute-start(bf16[3,144,128]{2,1,0:T(8,128)(2,1)S(1)} %get-tuple-element.22), channel_id=1, source_target_pairs={{0,1},{1,0},{2,3},{3,2},{4,5},{5,4},{6,7},{7,6},{8,9},{9,8},{10,11... | collective-permute-start | bytes 331784 | tf_op jit(solution)/shard_map/ppermute | solution.py:422
  24.6 5.9 %collective-permute-start.14 = (bf16[3,144,128]{2,1,0:T(8,128)(2,1)S(1)}, bf16[3,144,128]{2,1,0:T(8,128)(2,1)S(1)}, u32[]{:S(2)}, u32[]{:S(2)}) collective-permute-start(bf16[3,144,128]{2,1,0:T(8,128)(2,1)S(1)} %get-tuple-element.28), channel_id=1, source_target_pairs={{0,2},{1,3},{2,0},{3,1},{4,6},{5,7},{6,4},{7,5},{8,10},{9,11},{10,... | collective-permute-start | bytes 331784 | tf_op jit(solution)/shard_map/ppermute | solution.py:422
  26.4 5.7 %collective-permute-start.15 = (bf16[3,144,128]{2,1,0:T(8,128)(2,1)S(1)}, bf16[3,144,128]{2,1,0:T(8,128)(2,1)S(1)}, u32[]{:S(2)}, u32[]{:S(2)}) collective-permute-start(bf16[3,144,128]{2,1,0:T(8,128)(2,1)S(1)} %get-tuple-element.29), channel_id=1, source_target_pairs={{0,3},{1,2},{2,1},{3,0},{4,7},{5,6},{6,5},{7,4},{8,11},{9,10},{10,... | collective-permute-start | bytes 331784 | tf_op jit(solution)/shard_map/ppermute | solution.py:422
  28.0 8.6 %collective-permute-start.11 = (bf16[1,144,128]{2,1,0:T(8,128)(2,1)S(1)}, bf16[1,144,128]{2,1,0:T(8,128)(2,1)S(1)}, u32[]{:S(2)}, u32[]{:S(2)}) collective-permute-start(bf16[1,144,128]{2,1,0:T(8,128)(2,1)S(1)} %get-tuple-element.24), channel_id=1, source_target_pairs={{0,1},{1,0},{2,3},{3,2},{4,5},{5,4},{6,7},{7,6},{8,9},{9,8},{10,11... | collective-permute-start | bytes 110600 | tf_op jit(solution)/shard_map/ppermute | solution.py:422
  28.5 8.3 %collective-permute-start.12 = (bf16[1,144,128]{2,1,0:T(8,128)(2,1)S(1)}, bf16[1,144,128]{2,1,0:T(8,128)(2,1)S(1)}, u32[]{:S(2)}, u32[]{:S(2)}) collective-permute-start(bf16[1,144,128]{2,1,0:T(8,128)(2,1)S(1)} %get-tuple-element.25), channel_id=1, source_target_pairs={{0,2},{1,3},{2,0},{3,1},{4,6},{5,7},{6,4},{7,5},{8,10},{9,11},{10,... | collective-permute-start | bytes 110600 | tf_op jit(solution)/shard_map/ppermute | solution.py:422
  30.4 6.3 %collective-permute-start.13 = (bf16[1,144,128]{2,1,0:T(8,128)(2,1)S(1)}, bf16[1,144,128]{2,1,0:T(8,128)(2,1)S(1)}, u32[]{:S(2)}, u32[]{:S(2)}) collective-permute-start(bf16[1,144,128]{2,1,0:T(8,128)(2,1)S(1)} %get-tuple-element.26), channel_id=1, source_target_pairs={{0,3},{1,2},{2,1},{3,0},{4,7},{5,6},{6,5},{7,4},{8,11},{9,10},{10,... | collective-permute-start | bytes 110600 | tf_op jit(solution)/shard_map/ppermute | solution.py:422
  32.3 6.8 %collective-permute-start.16 = (bf16[256,128]{1,0:T(8,128)(2,1)S(1)}, bf16[256,128]{1,0:T(8,128)(2,1)S(1)}, u32[]{:S(2)}, u32[]{:S(2)}) collective-permute-start(bf16[256,128]{1,0:T(8,128)(2,1)S(1)} %get-tuple-element.30), channel_id=1, source_target_pairs={{0,12},{1,13},{2,14},{3,15},{4,8},{5,9},{6,10},{7,11},{8,4},{9,5},... | collective-permute-start | bytes 196616 | tf_op jit(solution)/shard_map/ppermute | solution.py:422
  35.9 7.4 %collective-permute-start.17 = (bf16[256,128]{1,0:T(8,128)(2,1)S(1)}, bf16[256,128]{1,0:T(8,128)(2,1)S(1)}, u32[]{:S(2)}, u32[]{:S(2)}) collective-permute-start(bf16[256,128]{1,0:T(8,128)(2,1)S(1)} %get-tuple-element.31), channel_id=1, source_target_pairs={{0,8},{1,9},{2,10},{3,11},{4,12},{5,13},{6,14},{7,15},{8,0},{9,1},... | collective-permute-start | bytes 196616 | tf_op jit(solution)/shard_map/ppermute | solution.py:422
  36.6 6.7 %collective-permute-start.18 = (bf16[256,128]{1,0:T(8,128)(2,1)S(1)}, bf16[256,128]{1,0:T(8,128)(2,1)S(1)}, u32[]{:S(2)}, u32[]{:S(2)}) collective-permute-start(bf16[256,128]{1,0:T(8,128)(2,1)S(1)} %get-tuple-element.32), channel_id=1, source_target_pairs={{0,4},{1,5},{2,6},{3,7},{4,0},{5,1},{6,2},{7,3},{8,12},{9,13},{10,... | collective-permute-start | bytes 196616 | tf_op jit(solution)/shard_map/ppermute | solution.py:422

commit v14 on v13

--- a/solution.py
+++ b/solution.py
@@ -17,16 +17,13 @@
 
 
 def pack_slots(tile_block, tile_aux, live, basis_order, base, bb_dev):
-    nbb = basis_order.shape[0]
-    position = jnp.sum(
-        jnp.where(
-            basis_order[None, :] == tile_block[:, None], lax.iota(jnp.int32, nbb)[None, :], 0
-        ),
-        axis=1,
-    )
-    owner = jnp.bitwise_xor(position // bb_dev, base)
-    alive = (lax.iota(jnp.int32, tile_block.shape[0]) < live[0]).astype(jnp.int32)
-    return ((owner * bb_dev + position % bb_dev) * AB_DEV + tile_aux) * 2 + alive
+    slots, nbb = tile_block.shape[0], basis_order.shape[0]
+    k = lax.iota(jnp.int32, nbb)
+    owner = jnp.bitwise_xor(k // bb_dev, base)
+    value = (owner * bb_dev + k % bb_dev)[None, :] * AB_DEV + tile_aux[:, None]
+    value = jnp.where(basis_order[None, :] == tile_block[:, None], value * 2, 0)
+    alive = jnp.pad(live, (0, nbb - 1))[None, :] > lax.iota(jnp.int32, slots)[:, None]
+    return jnp.sum(value + alive.astype(jnp.int32), axis=1)
 
 
 def unpack_slots(packed, bb_dev):

time: 44 us -> 44.3 us (level)
  Pallas kernels: 8.54 us -> 10 us
  other arithmetic: 3.39 us -> 2.75 us
  local copies, waits for them, and re-layouts: 0.48 us -> 0.03 us
    pallas_call x1, Pallas kernels: 4.2 us -> 5.2 us  [first_part(): pl.pallas_call(kernel, out_shape=out_shape, in_specs=[smem] * 7 + [vmem]...]
    select_n x1, other arithmetic: 0.69 us -> 0.03 us  [unpack_slots(): return (rest // bb_dev, rest % bb_dev, tile_aux, packed % 2 == 1)]
    pallas_call x1, Pallas kernels: 1.84 us -> 2.4 us  [begin(): pl.pallas_call(kernel, out_shape=[jax.ShapeDtypeStruct((AB_DEV, nocc, aux...]
    unnamed x8, local copies, waits for them, and re-layouts: 0.48 us -> 0.03 us
  transfers between devices with their start and end apart: 19 -> 19, of which waited for: 6 -> 9; matrix products, arithmetic and copies ran while one was open for 8% -> 6% of each run, Pallas kernels for 8% -> 9%
where the time goes in v14:
time: 44.3 us; the launch traced here: 43.9 us
  starting transfers between devices  18.1 us (41%)
  waiting for transfers between devices  12.1 us (27%)
  Pallas kernels  10 us (23%)
  other arithmetic  2.75 us (6%)
  between operations  0.91 us (2%)
    ppermute x19, starting transfers between devices, swap(): return lax.ppermute(array, 'aux', [(i, i ^ m) for i in range(n_aux)])  18.1 us
    ppermute x19, waiting for transfers between devices, swap(): return lax.ppermute(array, 'aux', [(i, i ^ m) for i in range(n_aux)])  12.1 us
    pallas_call x1, Pallas kernels, first_part(): pl.pallas_call(kernel, out_shape=out_shape, in_specs=[smem] * 7 + [vmem]...  5.2 us
    pallas_call x1, Pallas kernels, begin(): pl.pallas_call(kernel, out_shape=[jax.ShapeDtypeStruct((AB_DEV, nocc, aux...  2.4 us
    pallas_call x1, Pallas kernels, second_part(): pl.pallas_call(kernel, out_shape=[jax.ShapeDtypeStruct(shape, jnp.bfloat1...  1.53 us
  transfers between devices with their start and end apart: 19, of which 9 were waited for; matrix products, arithmetic and copies ran while one was open for 6% of the time, Pallas kernels for 9%

profile of v14, /device:TPU:0, one launch (start us, length us, event | category | flops | bytes accessed | tf_op | source)
XLA Modules:
  0.0 43.9 jit_solution(8588677973707060495)
XLA Ops:
  0.0 3.0 %collective-permute-start.4 = (bf16[256,128]{1,0:T(8,128)(2,1)}, bf16[256,128]{1,0:T(8,128)(2,1)S(1)}, u32[]{:S(2)}, u32[]{:S(2)}) collective-permute-start(bf16[256,128]{1,0:T(8,128)(2,1)} %own.1), channel_id=1, source_target_pairs={{0,2},{1,3},{2,0},{3,1},{4,6},{5,7},{6,4},{7,5},{8,10},{9,11},{10,... | collective-permute-start | bytes 196616 | tf_op jit(solution)/shard_map/ppermute | solution.py:419
  3.0 2.6 %collective-permute-start.1 = (bf16[256,128]{1,0:T(8,128)(2,1)}, bf16[256,128]{1,0:T(8,128)(2,1)S(1)}, u32[]{:S(2)}, u32[]{:S(2)}) collective-permute-start(bf16[256,128]{1,0:T(8,128)(2,1)} %own.1), channel_id=1, source_target_pairs={{0,8},{1,9},{2,10},{3,11},{4,12},{5,13},{6,14},{7,15},{8,0},{9,1},... | collective-permute-start | bytes 196616 | tf_op jit(solution)/shard_map/ppermute | solution.py:419
  5.6 1.6 %collective-permute-start = (bf16[256,128]{1,0:T(8,128)(2,1)}, bf16[256,128]{1,0:T(8,128)(2,1)S(1)}, u32[]{:S(2)}, u32[]{:S(2)}) collective-permute-start(bf16[256,128]{1,0:T(8,128)(2,1)} %own.1), channel_id=1, source_target_pairs={{0,4},{1,5},{2,6},{3,7},{4,0},{5,1},{6,2},{7,3},{8,12},{9,13},{10,... | collective-permute-start | bytes 196616 | tf_op jit(solution)/shard_map/ppermute | solution.py:419
  8.0 0.8 %add_reduce_fusion.packed_ref = s32[64]{0:T(128)S(1)} fusion(s32[32]{0:T(128)S(1)} %pad.4, s32[64]{0:T(128)} %param.10, s32[32]{0:T(128)S(1)} %fusion.9, s32[64]{0:T(128)} %param.9, s32[32]{0:T(128)} %param.8), kind=kLoop, calls=%fused_computation.15 | loop fusion | flops 16320 | bytes 1152 | tf_op jit(solution)/shard_map/reduce_sum | solution.py:26
  10.5 0.6 %collective-permute-start.5 = (bf16[256,128]{1,0:T(8,128)(2,1)S(1)}, bf16[256,128]{1,0:T(8,128)(2,1)S(1)}, u32[]{:S(2)}, u32[]{:S(2)}) collective-permute-start(bf16[256,128]{1,0:T(8,128)(2,1)S(1)} %collective-permute-done.4.refs_3_), channel_id=1, source_target_pairs={{0,1},{1,0},{2,3},{3,2},{4,5},{5,4},{6,7},{7,6},{8,9},{9,8},{10,11... | collective-permute-start | bytes 196616 | tf_op jit(solution)/shard_map/ppermute | solution.py:419
  11.2 0.5 %collective-permute-start.6 = (bf16[2,256,128]{2,1,0:T(8,128)(2,1)S(1)}, bf16[2,256,128]{2,1,0:T(8,128)(2,1)S(1)}, u32[]{:S(2)}, u32[]{:S(2)}) collective-permute-start(bf16[2,256,128]{2,1,0:T(8,128)(2,1)S(1)} %merge.1.refs_0_), channel_id=1, source_target_pairs={{0,2},{1,3},{2,0},{3,1},{4,6},{5,7},{6,4},{7,5},{8,10},{9,11},{10,... | collective-permute-start | bytes 393224 | tf_op jit(solution)/shard_map/ppermute | solution.py:419
  11.6 1.8 %collective-permute-done.7.refs_1_ = bf16[256,128]{1,0:T(8,128)(2,1)S(1)} collective-permute-done((bf16[256,128]{1,0:T(8,128)(2,1)}, bf16[256,128]{1,0:T(8,128)(2,1)S(1)}, u32[]{:S(2)}, u32[]{:S(2)}) %collective-permute-start.7) | collective-permute-done | bytes 65568 | tf_op jit(solution)/shard_map/ppermute | solution.py:419
  13.4 0.5 %collective-permute-start.8 = (bf16[256,128]{1,0:T(8,128)(2,1)S(1)}, bf16[256,128]{1,0:T(8,128)(2,1)S(1)}, u32[]{:S(2)}, u32[]{:S(2)}) collective-permute-start(bf16[256,128]{1,0:T(8,128)(2,1)S(1)} %collective-permute-done.7.refs_1_), channel_id=1, source_target_pairs={{0,2},{1,3},{2,0},{3,1},{4,6},{5,7},{6,4},{7,5},{8,10},{9,11},{10,... | collective-permute-start | bytes 196616 | tf_op jit(solution)/shard_map/ppermute | solution.py:419
  14.0 2.4 %begin.1 = (f32[8,128,640]{2,1,0:T(8,128)S(1)}, s32[64]{0:T(128)S(1)}) custom-call(s32[96]{0:T(128)S(1)} %get-tuple-element.52.slot_ref.refs_0_, s32[96]{0:T(128)S(1)} %get-tuple-element.51.block_ref.refs_1_, s32[64]{0:T(128)S(1)} %pad_add_fusion.gid_ref.refs_2_, s32[16]{0:T(128)S(1)} %select_reduce_fusion.8.bit_ref.refs_6_, ...), custom_call_target="tpu_custom_call" | custom-call | flops 1342177280 | bytes 5242880 | tf_op jit(solution)/shard_map/begin/pallas_call | solution.py:151
  17.3 0.7 %collective-permute-done.8.refs_2_ = bf16[256,128]{1,0:T(8,128)(2,1)S(1)} collective-permute-done((bf16[256,128]{1,0:T(8,128)(2,1)S(1)}, bf16[256,128]{1,0:T(8,128)(2,1)S(1)}, u32[]{:S(2)}, u32[]{:S(2)}) %collective-permute-start.8) | collective-permute-done | bytes 65568 | tf_op jit(solution)/shard_map/ppermute | solution.py:419
  18.2 1.4 %collective-permute-done.9.refs_10_ = bf16[4,256,128]{2,1,0:T(8,128)(2,1)S(1)} collective-permute-done((bf16[4,256,128]{2,1,0:T(8,128)(2,1)S(1)}, bf16[4,256,128]{2,1,0:T(8,128)(2,1)S(1)}, u32[]{:S(2)}, u32[]{:S(2)}) %collective-permute-start.9) | collective-permute-done | bytes 262176 | tf_op jit(solution)/shard_map/ppermute | solution.py:419
  19.6 5.2 %first_part.1 = (bf16[3,144,128]{2,1,0:T(8,128)(2,1)S(1)}, bf16[3,144,128]{2,1,0:T(8,128)(2,1)S(1)}, bf16[3,144,128]{2,1,0:T(8,128)(2,1)S(1)}, bf16[3,144,128]{2...) custom-call(s32[96]{0:T(128)S(1)} %get-tuple-element.52.slot_ref.ref, ...), custom_call_target="tpu_custom_call", output_to_operand_aliasing={{5}: (8, {})} | custom-call | flops 2013265920 | bytes 5242880 | tf_op jit(solution)/shard_map/first_part/pallas_call | solution.py:213
  24.8 0.7 %collective-permute-start.10 = (bf16[3,144,128]{2,1,0:T(8,128)(2,1)S(1)}, bf16[3,144,128]{2,1,0:T(8,128)(2,1)S(1)}, u32[]{:S(2)}, u32[]{:S(2)}) collective-permute-start(bf16[3,144,128]{2,1,0:T(8,128)(2,1)S(1)} %get-tuple-element.22), channel_id=1, source_target_pairs={{0,1},{1,0},{2,3},{3,2},{4,5},{5,4},{6,7},{7,6},{8,9},{9,8},{10,11... | collective-permute-start | bytes 331784 | tf_op jit(solution)/shard_map/ppermute | solution.py:419
  25.6 1.4 %collective-permute-start.15 = (bf16[3,144,128]{2,1,0:T(8,128)(2,1)S(1)}, bf16[3,144,128]{2,1,0:T(8,128)(2,1)S(1)}, u32[]{:S(2)}, u32[]{:S(2)}) collective-permute-start(bf16[3,144,128]{2,1,0:T(8,128)(2,1)S(1)} %get-tuple-element.29), channel_id=1, source_target_pairs={{0,3},{1,2},{2,1},{3,0},{4,7},{5,6},{6,5},{7,4},{8,11},{9,10},{10,... | collective-permute-start | bytes 331784 | tf_op jit(solution)/shard_map/ppermute | solution.py:419
  27.0 1.5 %second_part.1 = (bf16[1,144,128]{2,1,0:T(8,128)(2,1)S(1)}, bf16[1,144,128]{2,1,0:T(8,128)(2,1)S(1)}, bf16[1,144,128]{2,1,0:T(8,128)(2,1)S(1)}, bf16[1,144,128]{2,1,0:T(8,128)(2,1)S(1)}) custom-call(s32[96]{0:T(128)S(1)} %get-tuple-element.50.refs_3_.slot_ref, s32[96]{0:T(128)S(1)} %get-tuple-element.49.refs_4_.block_ref, ...), custom_call_target="tpu_custom_call" | custom-call | flops 10000000000 | bytes 5242880 | tf_op jit(solution)/shard_map/second_part/pallas_call | solution.py:246
  28.5 1.1 %collective-permute-start.11 = (bf16[1,144,128]{2,1,0:T(8,128)(2,1)S(1)}, bf16[1,144,128]{2,1,0:T(8,128)(2,1)S(1)}, u32[]{:S(2)}, u32[]{:S(2)}) collective-permute-start(bf16[1,144,128]{2,1,0:T(8,128)(2,1)S(1)} %get-tuple-element.24), channel_id=1, source_target_pairs={{0,1},{1,0},{2,3},{3,2},{4,5},{5,4},{6,7},{7,6},{8,9},{9,8},{10,11... | collective-permute-start | bytes 110600 | tf_op jit(solution)/shard_map/ppermute | solution.py:419
  29.7 1.3 %collective-permute-start.13 = (bf16[1,144,128]{2,1,0:T(8,128)(2,1)S(1)}, bf16[1,144,128]{2,1,0:T(8,128)(2,1)S(1)}, u32[]{:S(2)}, u32[]{:S(2)}) collective-permute-start(bf16[1,144,128]{2,1,0:T(8,128)(2,1)S(1)} %get-tuple-element.26), channel_id=1, source_target_pairs={{0,3},{1,2},{2,1},{3,0},{4,7},{5,6},{6,5},{7,4},{8,11},{9,10},{10,... | collective-permute-start | bytes 110600 | tf_op jit(solution)/shard_map/ppermute | solution.py:419
  31.0 0.4 collective-permute-done.14.refs_2_
  31.4 0.6 %collective-permute-done.15.refs_3_ = bf16[3,144,128]{2,1,0:T(8,128)(2,1)S(1)} collective-permute-done((bf16[3,144,128]{2,1,0:T(8,128)(2,1)S(1)}, bf16[3,144,128]{2,1,0:T(8,128)(2,1)S(1)}, u32[]{:S(2)}, u32[]{:S(2)}) %collective-permute-start.15) | collective-permute-done | bytes 110624 | tf_op jit(solution)/shard_map/ppermute | solution.py:419
  32.2 3.1 %collective-permute-start.16 = (bf16[256,128]{1,0:T(8,128)(2,1)S(1)}, bf16[256,128]{1,0:T(8,128)(2,1)S(1)}, u32[]{:S(2)}, u32[]{:S(2)}) collective-permute-start(bf16[256,128]{1,0:T(8,128)(2,1)S(1)} %get-tuple-element.30), channel_id=1, source_target_pairs={{0,12},{1,13},{2,14},{3,15},{4,8},{5,9},{6,10},{7,11},{8,4},{9,5},... | collective-permute-start | bytes 196616 | tf_op jit(solution)/shard_map/ppermute | solution.py:419
  35.3 0.9 %collective-permute-start.17 = (bf16[256,128]{1,0:T(8,128)(2,1)S(1)}, bf16[256,128]{1,0:T(8,128)(2,1)S(1)}, u32[]{:S(2)}, u32[]{:S(2)}) collective-permute-start(bf16[256,128]{1,0:T(8,128)(2,1)S(1)} %get-tuple-element.31), channel_id=1, source_target_pairs={{0,8},{1,9},{2,10},{3,11},{4,12},{5,13},{6,14},{7,15},{8,0},{9,1},... | collective-permute-start | bytes 196616 | tf_op jit(solution)/shard_map/ppermute | solution.py:419
  36.7 1.8 %collective-permute-done.16.refs_1_ = bf16[256,128]{1,0:T(8,128)(2,1)S(1)} collective-permute-done((bf16[256,128]{1,0:T(8,128)(2,1)S(1)}, bf16[256,128]{1,0:T(8,128)(2,1)S(1)}, u32[]{:S(2)}, u32[]{:S(2)}) %collective-permute-start.16) | collective-permute-done | bytes 65568 | tf_op jit(solution)/shard_map/ppermute | solution.py:419
  38.6 4.7 %collective-permute-done.17.refs_2_ = bf16[256,128]{1,0:T(8,128)(2,1)S(1)} collective-permute-done((bf16[256,128]{1,0:T(8,128)(2,1)S(1)}, bf16[256,128]{1,0:T(8,128)(2,1)S(1)}, u32[]{:S(2)}, u32[]{:S(2)}) %collective-permute-start.17) | collective-permute-done | bytes 65568 | tf_op jit(solution)/shard_map/ppermute | solution.py:419
  43.3 0.7 %total_of.1 = bf16[256,128]{1,0:T(8,128)(2,1)} custom-call(f32[256,128]{1,0:T(8,128)S(1)} %spread.2.refs_0_, bf16[256,128]{1,0:T(8,128)(2,1)S(1)} %collective-permute-done.16.refs_1_, bf16[256,128]{1,0:T(8,128)(2,1)S(1)} %collective-permute-done.17.refs_2_, bf16[256,128]{1,0:T(8,128)(2,1)S(1)} %collective-permute-done.18.refs_3_), custom_call_target="tpu_custom_call" | custom-call | tf_op jit(solution)/shard_map/total_of/pallas_call | solution.py:379
  (64 shorter events, 3.7 us)
Async XLA Ops:
  0.0 10.5 %collective-permute-start.4 = (bf16[256,128]{1,0:T(8,128)(2,1)}, bf16[256,128]{1,0:T(8,128)(2,1)S(1)}, u32[]{:S(2)}, u32[]{:S(2)}) collective-permute-start(bf16[256,128]{1,0:T(8,128)(2,1)} %own.1), channel_id=1, source_target_pairs={{0,2},{1,3},{2,0},{3,1},{4,6},{5,7},{6,4},{7,5},{8,10},{9,11},{10,... | collective-permute-start | bytes 196616 | tf_op jit(solution)/shard_map/ppermute | solution.py:419
  3.0 11.0 %collective-permute-start.3 = (bf16[256,128]{1,0:T(8,128)(2,1)}, bf16[256,128]{1,0:T(8,128)(2,1)S(1)}, u32[]{:S(2)}, u32[]{:S(2)}) collective-permute-start(bf16[256,128]{1,0:T(8,128)(2,1)} %own.1), channel_id=1, source_target_pairs={{0,1},{1,0},{2,3},{3,2},{4,5},{5,4},{6,7},{7,6},{8,9},{9,8},{10,11... | collective-permute-start | bytes 196616 | tf_op jit(solution)/shard_map/ppermute | solution.py:419
  3.0 7.0 %collective-permute-start.1 = (bf16[256,128]{1,0:T(8,128)(2,1)}, bf16[256,128]{1,0:T(8,128)(2,1)S(1)}, u32[]{:S(2)}, u32[]{:S(2)}) collective-permute-start(bf16[256,128]{1,0:T(8,128)(2,1)} %own.1), channel_id=1, source_target_pairs={{0,8},{1,9},{2,10},{3,11},{4,12},{5,13},{6,14},{7,15},{8,0},{9,1},... | collective-permute-start | bytes 196616 | tf_op jit(solution)/shard_map/ppermute | solution.py:419
  5.6 4.8 %collective-permute-start = (bf16[256,128]{1,0:T(8,128)(2,1)}, bf16[256,128]{1,0:T(8,128)(2,1)S(1)}, u32[]{:S(2)}, u32[]{:S(2)}) collective-permute-start(bf16[256,128]{1,0:T(8,128)(2,1)} %own.1), channel_id=1, source_target_pairs={{0,4},{1,5},{2,6},{3,7},{4,0},{5,1},{6,2},{7,3},{8,12},{9,13},{10,... | collective-permute-start | bytes 196616 | tf_op jit(solution)/shard_map/ppermute | solution.py:419
  7.1 6.3 %collective-permute-start.7 = (bf16[256,128]{1,0:T(8,128)(2,1)}, bf16[256,128]{1,0:T(8,128)(2,1)S(1)}, u32[]{:S(2)}, u32[]{:S(2)}) collective-permute-start(bf16[256,128]{1,0:T(8,128)(2,1)} %own.1), channel_id=1, source_target_pairs={{0,12},{1,13},{2,14},{3,15},{4,8},{5,9},{6,10},{7,11},{8,4},{9,5},... | collective-permute-start | bytes 196616 | tf_op jit(solution)/shard_map/ppermute | solution.py:419
  9.7 4.2 %slice-start = ((s8[10485760]{0:T(1024)(128)(4,1)}), s8[4194304]{0:T(1024)(128)(4,1)S(1)}, s32[]{:S(2)}) async-start(s8[10485760]{0:T(1024)(128)(4,1)} %bitcast), calls=%async_computation | async-start | bytes 8388608
  9.7 4.2 %slice-start.1 = ((s8[10485760]{0:T(1024)(128)(4,1)}), s8[4194304]{0:T(1024)(128)(4,1)S(1)}, s32[]{:S(2)}) async-start(s8[10485760]{0:T(1024)(128)(4,1)} %bitcast), calls=%async_computation.1 | async-start | bytes 8388608
  9.8 4.2 %slice-start.2 = ((s8[10485760]{0:T(1024)(128)(4,1)}), s8[2097152]{0:T(1024)(128)(4,1)S(1)}, s32[]{:S(2)}) async-start(s8[10485760]{0:T(1024)(128)(4,1)} %bitcast), calls=%async_computation.2 | async-start | bytes 4194304
  9.8 4.2 %copy-start = (bf16[256,128]{1,0:T(8,128)(2,1)S(1)}, bf16[256,128]{1,0:T(8,128)(2,1)}, u32[]{:S(2)}) copy-start(bf16[256,128]{1,0:T(8,128)(2,1)} %own.1) | copy-start | bytes 196612
  10.3 3.6 %collective-permute-start.2 = (bf16[2,256,128]{2,1,0:T(8,128)(2,1)S(1)}, bf16[2,256,128]{2,1,0:T(8,128)(2,1)S(1)}, u32[]{:S(2)}, u32[]{:S(2)}) collective-permute-start(bf16[2,256,128]{2,1,0:T(8,128)(2,1)S(1)} %merge.1.refs_0_), channel_id=1, source_target_pairs={{0,1},{1,0},{2,3},{3,2},{4,5},{5,4},{6,7},{7,6},{8,9},{9,8},{10,11... | collective-permute-start | bytes 393224 | tf_op jit(solution)/shard_map/ppermute | solution.py:419
  10.5 3.4 %collective-permute-start.5 = (bf16[256,128]{1,0:T(8,128)(2,1)S(1)}, bf16[256,128]{1,0:T(8,128)(2,1)S(1)}, u32[]{:S(2)}, u32[]{:S(2)}) collective-permute-start(bf16[256,128]{1,0:T(8,128)(2,1)S(1)} %collective-permute-done.4.refs_3_), channel_id=1, source_target_pairs={{0,1},{1,0},{2,3},{3,2},{4,5},{5,4},{6,7},{7,6},{8,9},{9,8},{10,11... | collective-permute-start | bytes 196616 | tf_op jit(solution)/shard_map/ppermute | solution.py:419
  11.2 6.8 %collective-permute-start.6 = (bf16[2,256,128]{2,1,0:T(8,128)(2,1)S(1)}, bf16[2,256,128]{2,1,0:T(8,128)(2,1)S(1)}, u32[]{:S(2)}, u32[]{:S(2)}) collective-permute-start(bf16[2,256,128]{2,1,0:T(8,128)(2,1)S(1)} %merge.1.refs_0_), channel_id=1, source_target_pairs={{0,2},{1,3},{2,0},{3,1},{4,6},{5,7},{6,4},{7,5},{8,10},{9,11},{10,... | collective-permute-start | bytes 393224 | tf_op jit(solution)/shard_map/ppermute | solution.py:419
  13.4 4.6 %collective-permute-start.8 = (bf16[256,128]{1,0:T(8,128)(2,1)S(1)}, bf16[256,128]{1,0:T(8,128)(2,1)S(1)}, u32[]{:S(2)}, u32[]{:S(2)}) collective-permute-start(bf16[256,128]{1,0:T(8,128)(2,1)S(1)} %collective-permute-done.7.refs_1_), channel_id=1, source_target_pairs={{0,2},{1,3},{2,0},{3,1},{4,6},{5,7},{6,4},{7,5},{8,10},{9,11},{10,... | collective-permute-start | bytes 196616 | tf_op jit(solution)/shard_map/ppermute | solution.py:419
  18.0 1.6 %collective-permute-start.9 = (bf16[4,256,128]{2,1,0:T(8,128)(2,1)S(1)}, bf16[4,256,128]{2,1,0:T(8,128)(2,1)S(1)}, u32[]{:S(2)}, u32[]{:S(2)}) collective-permute-start(bf16[4,256,128]{2,1,0:T(8,128)(2,1)S(1)} %gate.1.refs_9_), channel_id=1, source_target_pairs={{0,1},{1,0},{2,3},{3,2},{4,5},{5,4},{6,7},{7,6},{8,9},{9,8},{10,11... | collective-permute-start | bytes 786440 | tf_op jit(solution)/shard_map/ppermute | solution.py:419
  24.8 2.1 %collective-permute-start.10 = (bf16[3,144,128]{2,1,0:T(8,128)(2,1)S(1)}, bf16[3,144,128]{2,1,0:T(8,128)(2,1)S(1)}, u32[]{:S(2)}, u32[]{:S(2)}) collective-permute-start(bf16[3,144,128]{2,1,0:T(8,128)(2,1)S(1)} %get-tuple-element.22), channel_id=1, source_target_pairs={{0,1},{1,0},{2,3},{3,2},{4,5},{5,4},{6,7},{7,6},{8,9},{9,8},{10,11... | collective-permute-start | bytes 331784 | tf_op jit(solution)/shard_map/ppermute | solution.py:419
  25.5 5.9 %collective-permute-start.14 = (bf16[3,144,128]{2,1,0:T(8,128)(2,1)S(1)}, bf16[3,144,128]{2,1,0:T(8,128)(2,1)S(1)}, u32[]{:S(2)}, u32[]{:S(2)}) collective-permute-start(bf16[3,144,128]{2,1,0:T(8,128)(2,1)S(1)} %get-tuple-element.28), channel_id=1, source_target_pairs={{0,2},{1,3},{2,0},{3,1},{4,6},{5,7},{6,4},{7,5},{8,10},{9,11},{10,... | collective-permute-start | bytes 331784 | tf_op jit(solution)/shard_map/ppermute | solution.py:419
  25.6 6.5 %collective-permute-start.15 = (bf16[3,144,128]{2,1,0:T(8,128)(2,1)S(1)}, bf16[3,144,128]{2,1,0:T(8,128)(2,1)S(1)}, u32[]{:S(2)}, u32[]{:S(2)}) collective-permute-start(bf16[3,144,128]{2,1,0:T(8,128)(2,1)S(1)} %get-tuple-element.29), channel_id=1, source_target_pairs={{0,3},{1,2},{2,1},{3,0},{4,7},{5,6},{6,5},{7,4},{8,11},{9,10},{10,... | collective-permute-start | bytes 331784 | tf_op jit(solution)/shard_map/ppermute | solution.py:419
  28.5 7.8 %collective-permute-start.11 = (bf16[1,144,128]{2,1,0:T(8,128)(2,1)S(1)}, bf16[1,144,128]{2,1,0:T(8,128)(2,1)S(1)}, u32[]{:S(2)}, u32[]{:S(2)}) collective-permute-start(bf16[1,144,128]{2,1,0:T(8,128)(2,1)S(1)} %get-tuple-element.24), channel_id=1, source_target_pairs={{0,1},{1,0},{2,3},{3,2},{4,5},{5,4},{6,7},{7,6},{8,9},{9,8},{10,11... | collective-permute-start | bytes 110600 | tf_op jit(solution)/shard_map/ppermute | solution.py:419
  29.6 7.1 %collective-permute-start.12 = (bf16[1,144,128]{2,1,0:T(8,128)(2,1)S(1)}, bf16[1,144,128]{2,1,0:T(8,128)(2,1)S(1)}, u32[]{:S(2)}, u32[]{:S(2)}) collective-permute-start(bf16[1,144,128]{2,1,0:T(8,128)(2,1)S(1)} %get-tuple-element.25), channel_id=1, source_target_pairs={{0,2},{1,3},{2,0},{3,1},{4,6},{5,7},{6,4},{7,5},{8,10},{9,11},{10,... | collective-permute-start | bytes 110600 | tf_op jit(solution)/shard_map/ppermute | solution.py:419
  29.7 7.0 %collective-permute-start.13 = (bf16[1,144,128]{2,1,0:T(8,128)(2,1)S(1)}, bf16[1,144,128]{2,1,0:T(8,128)(2,1)S(1)}, u32[]{:S(2)}, u32[]{:S(2)}) collective-permute-start(bf16[1,144,128]{2,1,0:T(8,128)(2,1)S(1)} %get-tuple-element.26), channel_id=1, source_target_pairs={{0,3},{1,2},{2,1},{3,0},{4,7},{5,6},{6,5},{7,4},{8,11},{9,10},{10,... | collective-permute-start | bytes 110600 | tf_op jit(solution)/shard_map/ppermute | solution.py:419
  32.2 6.3 %collective-permute-start.16 = (bf16[256,128]{1,0:T(8,128)(2,1)S(1)}, bf16[256,128]{1,0:T(8,128)(2,1)S(1)}, u32[]{:S(2)}, u32[]{:S(2)}) collective-permute-start(bf16[256,128]{1,0:T(8,128)(2,1)S(1)} %get-tuple-element.30), channel_id=1, source_target_pairs={{0,12},{1,13},{2,14},{3,15},{4,8},{5,9},{6,10},{7,11},{8,4},{9,5},... | collective-permute-start | bytes 196616 | tf_op jit(solution)/shard_map/ppermute | solution.py:419
  35.3 7.9 %collective-permute-start.17 = (bf16[256,128]{1,0:T(8,128)(2,1)S(1)}, bf16[256,128]{1,0:T(8,128)(2,1)S(1)}, u32[]{:S(2)}, u32[]{:S(2)}) collective-permute-start(bf16[256,128]{1,0:T(8,128)(2,1)S(1)} %get-tuple-element.31), channel_id=1, source_target_pairs={{0,8},{1,9},{2,10},{3,11},{4,12},{5,13},{6,14},{7,15},{8,0},{9,1},... | collective-permute-start | bytes 196616 | tf_op jit(solution)/shard_map/ppermute | solution.py:419
  36.3 7.0 %collective-permute-start.18 = (bf16[256,128]{1,0:T(8,128)(2,1)S(1)}, bf16[256,128]{1,0:T(8,128)(2,1)S(1)}, u32[]{:S(2)}, u32[]{:S(2)}) collective-permute-start(bf16[256,128]{1,0:T(8,128)(2,1)S(1)} %get-tuple-element.32), channel_id=1, source_target_pairs={{0,4},{1,5},{2,6},{3,7},{4,0},{5,1},{6,2},{7,3},{8,12},{9,13},{10,... | collective-permute-start | bytes 196616 | tf_op jit(solution)/shard_map/ppermute | solution.py:419

commit v15 on v14

--- a/solution.py
+++ b/solution.py
@@ -432,7 +432,7 @@
 
     depth = n_aux // PLANE
     side = where_to % PLANE >= 2
-    last = (where_to >= 3 * PLANE) | ((where_to >= PLANE) & side)
+    last = (where_to >= 3 * PLANE) | ((where_to > 2) & side)
     fit_lists = chunk_lists(where_to, last, alive, group, n_aux)
     two = swap(c_orbitals, 2 * PLANE)
     one = swap(c_orbitals, PLANE)
@@ -442,9 +442,9 @@
     pair = merge([one, two], [], SPREAD_COST)
     pair_beside = swap(pair, 2)
     three_beside = swap(three, 2)
-    early = [pair, swap(pair, 1), across, beside, swap(beside, 1)]
-    early_from = [(1, (2, None)), (2, (3, None)), (3, (4, None))]
-    late_from = []
+    early = [pair, swap(pair, 1), across, beside]
+    early_from = [(1, (2, None)), (2, (3, None))]
+    late_from = [(3, (1, 4))]
     for core in range(2):
         early_from += [(PLANE + core, (core, 0)), (2 * PLANE + core, (core, 1))]
         late_from += [
@@ -456,7 +456,7 @@
     partial_fit, packed = begin(
         n_aux, fit_lists, bit, packed, tiles, c_orbitals, early, early_from
     )
-    late = gate([pair_beside, three, three_beside], partial_fit)
+    late = gate([pair_beside, three, three_beside, beside], partial_fit)
     where_to, _, group, alive = unpack_slots(packed, bb_dev)
     lists = chunk_lists(where_to, where_to < PLANE, alive, group, n_aux)
     *far, fitted, _ = first_part(

time: 44.3 us -> 44.2 us (level)
    ppermute x19 -> x18, starting transfers between devices: 18.1 us -> 18.4 us  [swap(): return lax.ppermute(array, 'aux', [(i, i ^ m) for i in range(n_aux)])]
    ppermute x19 -> x18, waiting for transfers between devices: 12.1 us -> 11.9 us  [swap(): return lax.ppermute(array, 'aux', [(i, i ^ m) for i in range(n_aux)])]
  transfers between devices with their start and end apart: 19 -> 18, of which waited for: 9 -> 10; matrix products, arithmetic and copies ran while one was open for 6% -> 6% of each run, Pallas kernels for 9% -> 10%
where the time goes in v15:
time: 44.2 us; the launch traced here: 43.9 us
  starting transfers between devices  18.4 us (42%)
  waiting for transfers between devices  11.9 us (27%)
  Pallas kernels  9.84 us (22%)
  other arithmetic  2.75 us (6%)
  between operations  0.91 us (2%)
    ppermute x18, starting transfers between devices, swap(): return lax.ppermute(array, 'aux', [(i, i ^ m) for i in range(n_aux)])  18.4 us
    ppermute x18, waiting for transfers between devices, swap(): return lax.ppermute(array, 'aux', [(i, i ^ m) for i in range(n_aux)])  11.9 us
    pallas_call x1, Pallas kernels, first_part(): pl.pallas_call(kernel, out_shape=out_shape, in_specs=[smem] * 7 + [vmem]...  4.88 us
    pallas_call x1, Pallas kernels, begin(): pl.pallas_call(kernel, out_shape=[jax.ShapeDtypeStruct((AB_DEV, nocc, aux...  2.13 us
    pallas_call x1, Pallas kernels, second_part(): pl.pallas_call(kernel, out_shape=[jax.ShapeDtypeStruct(shape, jnp.bfloat1...  1.93 us
  transfers between devices with their start and end apart: 18, of which 10 were waited for; matrix products, arithmetic and copies ran while one was open for 6% of the time, Pallas kernels for 10%

profile of v15, /device:TPU:0, one launch (start us, length us, event | category | flops | bytes accessed | tf_op | source)
XLA Modules:
  0.0 43.9 jit_solution(4644868137739340190)
XLA Ops:
  0.0 3.0 %collective-permute-start.4 = (bf16[256,128]{1,0:T(8,128)(2,1)}, bf16[256,128]{1,0:T(8,128)(2,1)S(1)}, u32[]{:S(2)}, u32[]{:S(2)}) collective-permute-start(bf16[256,128]{1,0:T(8,128)(2,1)} %own.1), channel_id=1, source_target_pairs={{0,2},{1,3},{2,0},{3,1},{4,6},{5,7},{6,4},{7,5},{8,10},{9,11},{10,... | collective-permute-start | bytes 196616 | tf_op jit(solution)/shard_map/ppermute | solution.py:419
  3.0 2.6 %collective-permute-start.1 = (bf16[256,128]{1,0:T(8,128)(2,1)}, bf16[256,128]{1,0:T(8,128)(2,1)S(1)}, u32[]{:S(2)}, u32[]{:S(2)}) collective-permute-start(bf16[256,128]{1,0:T(8,128)(2,1)} %own.1), channel_id=1, source_target_pairs={{0,8},{1,9},{2,10},{3,11},{4,12},{5,13},{6,14},{7,15},{8,0},{9,1},... | collective-permute-start | bytes 196616 | tf_op jit(solution)/shard_map/ppermute | solution.py:419
  5.6 1.6 %collective-permute-start = (bf16[256,128]{1,0:T(8,128)(2,1)}, bf16[256,128]{1,0:T(8,128)(2,1)S(1)}, u32[]{:S(2)}, u32[]{:S(2)}) collective-permute-start(bf16[256,128]{1,0:T(8,128)(2,1)} %own.1), channel_id=1, source_target_pairs={{0,4},{1,5},{2,6},{3,7},{4,0},{5,1},{6,2},{7,3},{8,12},{9,13},{10,... | collective-permute-start | bytes 196616 | tf_op jit(solution)/shard_map/ppermute | solution.py:419
  8.0 0.8 %add_reduce_fusion.packed_ref = s32[64]{0:T(128)S(1)} fusion(s32[32]{0:T(128)S(1)} %pad.4, s32[64]{0:T(128)} %param.10, s32[32]{0:T(128)S(1)} %fusion.9, s32[64]{0:T(128)} %param.9, s32[32]{0:T(128)} %param.8), kind=kLoop, calls=%fused_computation.15 | loop fusion | flops 16320 | bytes 1152 | tf_op jit(solution)/shard_map/reduce_sum | solution.py:26
  10.0 0.3 collective-permute-done.refs_0_
  10.6 0.5 %collective-permute-start.5 = (bf16[2,256,128]{2,1,0:T(8,128)(2,1)S(1)}, bf16[2,256,128]{2,1,0:T(8,128)(2,1)S(1)}, u32[]{:S(2)}, u32[]{:S(2)}) collective-permute-start(bf16[2,256,128]{2,1,0:T(8,128)(2,1)S(1)} %merge.1.refs_0_), channel_id=1, source_target_pairs={{0,2},{1,3},{2,0},{3,1},{4,6},{5,7},{6,4},{7,5},{8,10},{9,11},{10,... | collective-permute-start | bytes 393224 | tf_op jit(solution)/shard_map/ppermute | solution.py:419
  11.1 2.3 %collective-permute-done.6.refs_1_ = bf16[256,128]{1,0:T(8,128)(2,1)S(1)} collective-permute-done((bf16[256,128]{1,0:T(8,128)(2,1)}, bf16[256,128]{1,0:T(8,128)(2,1)S(1)}, u32[]{:S(2)}, u32[]{:S(2)}) %collective-permute-start.6) | collective-permute-done | bytes 65568 | tf_op jit(solution)/shard_map/ppermute | solution.py:419
  13.4 0.5 %collective-permute-start.7 = (bf16[256,128]{1,0:T(8,128)(2,1)S(1)}, bf16[256,128]{1,0:T(8,128)(2,1)S(1)}, u32[]{:S(2)}, u32[]{:S(2)}) collective-permute-start(bf16[256,128]{1,0:T(8,128)(2,1)S(1)} %collective-permute-done.6.refs_1_), channel_id=1, source_target_pairs={{0,2},{1,3},{2,0},{3,1},{4,6},{5,7},{6,4},{7,5},{8,10},{9,11},{10,... | collective-permute-start | bytes 196616 | tf_op jit(solution)/shard_map/ppermute | solution.py:419
  14.0 2.1 %begin.1 = (f32[8,128,640]{2,1,0:T(8,128)S(1)}, s32[64]{0:T(128)S(1)}) custom-call(s32[96]{0:T(128)S(1)} %get-tuple-element.52.slot_ref.refs_0_, s32[96]{0:T(128)S(1)} %get-tuple-element.51.block_ref.refs_1_, s32[64]{0:T(128)S(1)} %pad_add_fusion.gid_ref.refs_2_, s32[16]{0:T(128)S(1)} %select_reduce_fusion.8.bit_ref.refs_6_, ...), custom_call_target="tpu_custom_call" | custom-call | flops 1342177280 | bytes 5242880 | tf_op jit(solution)/shard_map/begin/pallas_call | solution.py:151
  17.0 0.9 %collective-permute-done.7.refs_2_ = bf16[256,128]{1,0:T(8,128)(2,1)S(1)} collective-permute-done((bf16[256,128]{1,0:T(8,128)(2,1)S(1)}, bf16[256,128]{1,0:T(8,128)(2,1)S(1)}, u32[]{:S(2)}, u32[]{:S(2)}) %collective-permute-start.7) | collective-permute-done | bytes 65568 | tf_op jit(solution)/shard_map/ppermute | solution.py:419
  18.1 1.5 %collective-permute-done.8.refs_10_ = bf16[5,256,128]{2,1,0:T(8,128)(2,1)S(1)} collective-permute-done((bf16[5,256,128]{2,1,0:T(8,128)(2,1)S(1)}, bf16[5,256,128]{2,1,0:T(8,128)(2,1)S(1)}, u32[]{:S(2)}, u32[]{:S(2)}) %collective-permute-start.8) | collective-permute-done | bytes 327712 | tf_op jit(solution)/shard_map/ppermute | solution.py:419
  19.6 4.9 %first_part.1 = (bf16[3,144,128]{2,1,0:T(8,128)(2,1)S(1)}, bf16[3,144,128]{2,1,0:T(8,128)(2,1)S(1)}, bf16[3,144,128]{2,1,0:T(8,128)(2,1)S(1)}, bf16[3,144,128]{2...) custom-call(s32[96]{0:T(128)S(1)} %get-tuple-element.52.slot_ref.ref, ...), custom_call_target="tpu_custom_call", output_to_operand_aliasing={{5}: (8, {})} | custom-call | flops 2013265920 | bytes 5242880 | tf_op jit(solution)/shard_map/first_part/pallas_call | solution.py:213
  24.5 1.1 %collective-permute-start.9 = (bf16[3,144,128]{2,1,0:T(8,128)(2,1)S(1)}, bf16[3,144,128]{2,1,0:T(8,128)(2,1)S(1)}, u32[]{:S(2)}, u32[]{:S(2)}) collective-permute-start(bf16[3,144,128]{2,1,0:T(8,128)(2,1)S(1)} %get-tuple-element.22), channel_id=1, source_target_pairs={{0,1},{1,0},{2,3},{3,2},{4,5},{5,4},{6,7},{7,6},{8,9},{9,8},{10,11... | collective-permute-start | bytes 331784 | tf_op jit(solution)/shard_map/ppermute | solution.py:419
  25.9 1.2 %collective-permute-start.14 = (bf16[3,144,128]{2,1,0:T(8,128)(2,1)S(1)}, bf16[3,144,128]{2,1,0:T(8,128)(2,1)S(1)}, u32[]{:S(2)}, u32[]{:S(2)}) collective-permute-start(bf16[3,144,128]{2,1,0:T(8,128)(2,1)S(1)} %get-tuple-element.29), channel_id=1, source_target_pairs={{0,3},{1,2},{2,1},{3,0},{4,7},{5,6},{6,5},{7,4},{8,11},{9,10},{10,... | collective-permute-start | bytes 331784 | tf_op jit(solution)/shard_map/ppermute | solution.py:419
  27.0 1.9 %second_part.1 = (bf16[1,144,128]{2,1,0:T(8,128)(2,1)S(1)}, bf16[1,144,128]{2,1,0:T(8,128)(2,1)S(1)}, bf16[1,144,128]{2,1,0:T(8,128)(2,1)S(1)}, bf16[1,144,128]{2,1,0:T(8,128)(2,1)S(1)}) custom-call(s32[96]{0:T(128)S(1)} %get-tuple-element.50.refs_3_.slot_ref, s32[96]{0:T(128)S(1)} %get-tuple-element.49.refs_4_.block_ref, ...), custom_call_target="tpu_custom_call" | custom-call | flops 10000000000 | bytes 5242880 | tf_op jit(solution)/shard_map/second_part/pallas_call | solution.py:246
  29.0 0.6 %collective-permute-start.10 = (bf16[1,144,128]{2,1,0:T(8,128)(2,1)S(1)}, bf16[1,144,128]{2,1,0:T(8,128)(2,1)S(1)}, u32[]{:S(2)}, u32[]{:S(2)}) collective-permute-start(bf16[1,144,128]{2,1,0:T(8,128)(2,1)S(1)} %get-tuple-element.24), channel_id=1, source_target_pairs={{0,1},{1,0},{2,3},{3,2},{4,5},{5,4},{6,7},{7,6},{8,9},{9,8},{10,11... | collective-permute-start | bytes 110600 | tf_op jit(solution)/shard_map/ppermute | solution.py:419
  29.7 1.3 %collective-permute-start.12 = (bf16[1,144,128]{2,1,0:T(8,128)(2,1)S(1)}, bf16[1,144,128]{2,1,0:T(8,128)(2,1)S(1)}, u32[]{:S(2)}, u32[]{:S(2)}) collective-permute-start(bf16[1,144,128]{2,1,0:T(8,128)(2,1)S(1)} %get-tuple-element.26), channel_id=1, source_target_pairs={{0,3},{1,2},{2,1},{3,0},{4,7},{5,6},{6,5},{7,4},{8,11},{9,10},{10,... | collective-permute-start | bytes 110600 | tf_op jit(solution)/shard_map/ppermute | solution.py:419
  31.0 0.5 %collective-permute-done.13.refs_2_ = bf16[3,144,128]{2,1,0:T(8,128)(2,1)S(1)} collective-permute-done((bf16[3,144,128]{2,1,0:T(8,128)(2,1)S(1)}, bf16[3,144,128]{2,1,0:T(8,128)(2,1)S(1)}, u32[]{:S(2)}, u32[]{:S(2)}) %collective-permute-start.13) | collective-permute-done | bytes 110624 | tf_op jit(solution)/shard_map/ppermute | solution.py:419
  31.5 0.6 %collective-permute-done.14.refs_3_ = bf16[3,144,128]{2,1,0:T(8,128)(2,1)S(1)} collective-permute-done((bf16[3,144,128]{2,1,0:T(8,128)(2,1)S(1)}, bf16[3,144,128]{2,1,0:T(8,128)(2,1)S(1)}, u32[]{:S(2)}, u32[]{:S(2)}) %collective-permute-start.14) | collective-permute-done | bytes 110624 | tf_op jit(solution)/shard_map/ppermute | solution.py:419
  32.3 4.8 %collective-permute-start.15 = (bf16[256,128]{1,0:T(8,128)(2,1)S(1)}, bf16[256,128]{1,0:T(8,128)(2,1)S(1)}, u32[]{:S(2)}, u32[]{:S(2)}) collective-permute-start(bf16[256,128]{1,0:T(8,128)(2,1)S(1)} %get-tuple-element.30), channel_id=1, source_target_pairs={{0,12},{1,13},{2,14},{3,15},{4,8},{5,9},{6,10},{7,11},{8,4},{9,5},... | collective-permute-start | bytes 196616 | tf_op jit(solution)/shard_map/ppermute | solution.py:419
  37.1 0.6 %collective-permute-start.17 = (bf16[256,128]{1,0:T(8,128)(2,1)S(1)}, bf16[256,128]{1,0:T(8,128)(2,1)S(1)}, u32[]{:S(2)}, u32[]{:S(2)}) collective-permute-start(bf16[256,128]{1,0:T(8,128)(2,1)S(1)} %get-tuple-element.32), channel_id=1, source_target_pairs={{0,4},{1,5},{2,6},{3,7},{4,0},{5,1},{6,2},{7,3},{8,12},{9,13},{10,... | collective-permute-start | bytes 196616 | tf_op jit(solution)/shard_map/ppermute | solution.py:419
  37.8 2.0 %collective-permute-done.15.refs_1_ = bf16[256,128]{1,0:T(8,128)(2,1)S(1)} collective-permute-done((bf16[256,128]{1,0:T(8,128)(2,1)S(1)}, bf16[256,128]{1,0:T(8,128)(2,1)S(1)}, u32[]{:S(2)}, u32[]{:S(2)}) %collective-permute-start.15) | collective-permute-done | bytes 65568 | tf_op jit(solution)/shard_map/ppermute | solution.py:419
  39.8 3.3 %collective-permute-done.16.refs_2_ = bf16[256,128]{1,0:T(8,128)(2,1)S(1)} collective-permute-done((bf16[256,128]{1,0:T(8,128)(2,1)S(1)}, bf16[256,128]{1,0:T(8,128)(2,1)S(1)}, u32[]{:S(2)}, u32[]{:S(2)}) %collective-permute-start.16) | collective-permute-done | bytes 65568 | tf_op jit(solution)/shard_map/ppermute | solution.py:419
  43.2 0.7 %total_of.1 = bf16[256,128]{1,0:T(8,128)(2,1)} custom-call(f32[256,128]{1,0:T(8,128)S(1)} %spread.2.refs_0_, bf16[256,128]{1,0:T(8,128)(2,1)S(1)} %collective-permute-done.15.refs_1_, bf16[256,128]{1,0:T(8,128)(2,1)S(1)} %collective-permute-done.16.refs_2_, bf16[256,128]{1,0:T(8,128)(2,1)S(1)} %collective-permute-done.17.refs_3_), custom_call_target="tpu_custom_call" | custom-call | tf_op jit(solution)/shard_map/total_of/pallas_call | solution.py:379
  (62 shorter events, 3.4 us)
Async XLA Ops:
  0.0 13.9 %collective-permute-start.4 = (bf16[256,128]{1,0:T(8,128)(2,1)}, bf16[256,128]{1,0:T(8,128)(2,1)S(1)}, u32[]{:S(2)}, u32[]{:S(2)}) collective-permute-start(bf16[256,128]{1,0:T(8,128)(2,1)} %own.1), channel_id=1, source_target_pairs={{0,2},{1,3},{2,0},{3,1},{4,6},{5,7},{6,4},{7,5},{8,10},{9,11},{10,... | collective-permute-start | bytes 196616 | tf_op jit(solution)/shard_map/ppermute | solution.py:419
  3.0 11.0 %collective-permute-start.3 = (bf16[256,128]{1,0:T(8,128)(2,1)}, bf16[256,128]{1,0:T(8,128)(2,1)S(1)}, u32[]{:S(2)}, u32[]{:S(2)}) collective-permute-start(bf16[256,128]{1,0:T(8,128)(2,1)} %own.1), channel_id=1, source_target_pairs={{0,1},{1,0},{2,3},{3,2},{4,5},{5,4},{6,7},{7,6},{8,9},{9,8},{10,11... | collective-permute-start | bytes 196616 | tf_op jit(solution)/shard_map/ppermute | solution.py:419
  3.0 7.0 %collective-permute-start.1 = (bf16[256,128]{1,0:T(8,128)(2,1)}, bf16[256,128]{1,0:T(8,128)(2,1)S(1)}, u32[]{:S(2)}, u32[]{:S(2)}) collective-permute-start(bf16[256,128]{1,0:T(8,128)(2,1)} %own.1), channel_id=1, source_target_pairs={{0,8},{1,9},{2,10},{3,11},{4,12},{5,13},{6,14},{7,15},{8,0},{9,1},... | collective-permute-start | bytes 196616 | tf_op jit(solution)/shard_map/ppermute | solution.py:419
  5.6 4.8 %collective-permute-start = (bf16[256,128]{1,0:T(8,128)(2,1)}, bf16[256,128]{1,0:T(8,128)(2,1)S(1)}, u32[]{:S(2)}, u32[]{:S(2)}) collective-permute-start(bf16[256,128]{1,0:T(8,128)(2,1)} %own.1), channel_id=1, source_target_pairs={{0,4},{1,5},{2,6},{3,7},{4,0},{5,1},{6,2},{7,3},{8,12},{9,13},{10,... | collective-permute-start | bytes 196616 | tf_op jit(solution)/shard_map/ppermute | solution.py:419
  7.1 6.3 %collective-permute-start.6 = (bf16[256,128]{1,0:T(8,128)(2,1)}, bf16[256,128]{1,0:T(8,128)(2,1)S(1)}, u32[]{:S(2)}, u32[]{:S(2)}) collective-permute-start(bf16[256,128]{1,0:T(8,128)(2,1)} %own.1), channel_id=1, source_target_pairs={{0,12},{1,13},{2,14},{3,15},{4,8},{5,9},{6,10},{7,11},{8,4},{9,5},... | collective-permute-start | bytes 196616 | tf_op jit(solution)/shard_map/ppermute | solution.py:419
  9.7 4.2 %slice-start = ((s8[10485760]{0:T(1024)(128)(4,1)}), s8[4194304]{0:T(1024)(128)(4,1)S(1)}, s32[]{:S(2)}) async-start(s8[10485760]{0:T(1024)(128)(4,1)} %bitcast), calls=%async_computation | async-start | bytes 8388608
  9.7 4.2 %slice-start.1 = ((s8[10485760]{0:T(1024)(128)(4,1)}), s8[4194304]{0:T(1024)(128)(4,1)S(1)}, s32[]{:S(2)}) async-start(s8[10485760]{0:T(1024)(128)(4,1)} %bitcast), calls=%async_computation.1 | async-start | bytes 8388608
  9.8 4.2 %slice-start.2 = ((s8[10485760]{0:T(1024)(128)(4,1)}), s8[2097152]{0:T(1024)(128)(4,1)S(1)}, s32[]{:S(2)}) async-start(s8[10485760]{0:T(1024)(128)(4,1)} %bitcast), calls=%async_computation.2 | async-start | bytes 4194304
  9.8 4.2 %copy-start = (bf16[256,128]{1,0:T(8,128)(2,1)S(1)}, bf16[256,128]{1,0:T(8,128)(2,1)}, u32[]{:S(2)}) copy-start(bf16[256,128]{1,0:T(8,128)(2,1)} %own.1) | copy-start | bytes 196612
  10.3 3.6 %collective-permute-start.2 = (bf16[2,256,128]{2,1,0:T(8,128)(2,1)S(1)}, bf16[2,256,128]{2,1,0:T(8,128)(2,1)S(1)}, u32[]{:S(2)}, u32[]{:S(2)}) collective-permute-start(bf16[2,256,128]{2,1,0:T(8,128)(2,1)S(1)} %merge.1.refs_0_), channel_id=1, source_target_pairs={{0,1},{1,0},{2,3},{3,2},{4,5},{5,4},{6,7},{7,6},{8,9},{9,8},{10,11... | collective-permute-start | bytes 393224 | tf_op jit(solution)/shard_map/ppermute | solution.py:419
  10.6 7.3 %collective-permute-start.5 = (bf16[2,256,128]{2,1,0:T(8,128)(2,1)S(1)}, bf16[2,256,128]{2,1,0:T(8,128)(2,1)S(1)}, u32[]{:S(2)}, u32[]{:S(2)}) collective-permute-start(bf16[2,256,128]{2,1,0:T(8,128)(2,1)S(1)} %merge.1.refs_0_), channel_id=1, source_target_pairs={{0,2},{1,3},{2,0},{3,1},{4,6},{5,7},{6,4},{7,5},{8,10},{9,11},{10,... | collective-permute-start | bytes 393224 | tf_op jit(solution)/shard_map/ppermute | solution.py:419
  13.4 4.5 %collective-permute-start.7 = (bf16[256,128]{1,0:T(8,128)(2,1)S(1)}, bf16[256,128]{1,0:T(8,128)(2,1)S(1)}, u32[]{:S(2)}, u32[]{:S(2)}) collective-permute-start(bf16[256,128]{1,0:T(8,128)(2,1)S(1)} %collective-permute-done.6.refs_1_), channel_id=1, source_target_pairs={{0,2},{1,3},{2,0},{3,1},{4,6},{5,7},{6,4},{7,5},{8,10},{9,11},{10,... | collective-permute-start | bytes 196616 | tf_op jit(solution)/shard_map/ppermute | solution.py:419
  18.0 1.7 %collective-permute-start.8 = (bf16[5,256,128]{2,1,0:T(8,128)(2,1)S(1)}, bf16[5,256,128]{2,1,0:T(8,128)(2,1)S(1)}, u32[]{:S(2)}, u32[]{:S(2)}) collective-permute-start(bf16[5,256,128]{2,1,0:T(8,128)(2,1)S(1)} %gate.1.refs_9_), channel_id=1, source_target_pairs={{0,1},{1,0},{2,3},{3,2},{4,5},{5,4},{6,7},{7,6},{8,9},{9,8},{10,11... | collective-permute-start | bytes 983048 | tf_op jit(solution)/shard_map/ppermute | solution.py:419
  24.5 2.5 %collective-permute-start.9 = (bf16[3,144,128]{2,1,0:T(8,128)(2,1)S(1)}, bf16[3,144,128]{2,1,0:T(8,128)(2,1)S(1)}, u32[]{:S(2)}, u32[]{:S(2)}) collective-permute-start(bf16[3,144,128]{2,1,0:T(8,128)(2,1)S(1)} %get-tuple-element.22), channel_id=1, source_target_pairs={{0,1},{1,0},{2,3},{3,2},{4,5},{5,4},{6,7},{7,6},{8,9},{9,8},{10,11... | collective-permute-start | bytes 331784 | tf_op jit(solution)/shard_map/ppermute | solution.py:419
  25.6 5.9 %collective-permute-start.13 = (bf16[3,144,128]{2,1,0:T(8,128)(2,1)S(1)}, bf16[3,144,128]{2,1,0:T(8,128)(2,1)S(1)}, u32[]{:S(2)}, u32[]{:S(2)}) collective-permute-start(bf16[3,144,128]{2,1,0:T(8,128)(2,1)S(1)} %get-tuple-element.28), channel_id=1, source_target_pairs={{0,2},{1,3},{2,0},{3,1},{4,6},{5,7},{6,4},{7,5},{8,10},{9,11},{10,... | collective-permute-start | bytes 331784 | tf_op jit(solution)/shard_map/ppermute | solution.py:419
  25.9 6.3 %collective-permute-start.14 = (bf16[3,144,128]{2,1,0:T(8,128)(2,1)S(1)}, bf16[3,144,128]{2,1,0:T(8,128)(2,1)S(1)}, u32[]{:S(2)}, u32[]{:S(2)}) collective-permute-start(bf16[3,144,128]{2,1,0:T(8,128)(2,1)S(1)} %get-tuple-element.29), channel_id=1, source_target_pairs={{0,3},{1,2},{2,1},{3,0},{4,7},{5,6},{6,5},{7,4},{8,11},{9,10},{10,... | collective-permute-start | bytes 331784 | tf_op jit(solution)/shard_map/ppermute | solution.py:419
  29.0 8.1 %collective-permute-start.10 = (bf16[1,144,128]{2,1,0:T(8,128)(2,1)S(1)}, bf16[1,144,128]{2,1,0:T(8,128)(2,1)S(1)}, u32[]{:S(2)}, u32[]{:S(2)}) collective-permute-start(bf16[1,144,128]{2,1,0:T(8,128)(2,1)S(1)} %get-tuple-element.24), channel_id=1, source_target_pairs={{0,1},{1,0},{2,3},{3,2},{4,5},{5,4},{6,7},{7,6},{8,9},{9,8},{10,11... | collective-permute-start | bytes 110600 | tf_op jit(solution)/shard_map/ppermute | solution.py:419
  29.6 8.1 %collective-permute-start.11 = (bf16[1,144,128]{2,1,0:T(8,128)(2,1)S(1)}, bf16[1,144,128]{2,1,0:T(8,128)(2,1)S(1)}, u32[]{:S(2)}, u32[]{:S(2)}) collective-permute-start(bf16[1,144,128]{2,1,0:T(8,128)(2,1)S(1)} %get-tuple-element.25), channel_id=1, source_target_pairs={{0,2},{1,3},{2,0},{3,1},{4,6},{5,7},{6,4},{7,5},{8,10},{9,11},{10,... | collective-permute-start | bytes 110600 | tf_op jit(solution)/shard_map/ppermute | solution.py:419
  29.7 8.0 %collective-permute-start.12 = (bf16[1,144,128]{2,1,0:T(8,128)(2,1)S(1)}, bf16[1,144,128]{2,1,0:T(8,128)(2,1)S(1)}, u32[]{:S(2)}, u32[]{:S(2)}) collective-permute-start(bf16[1,144,128]{2,1,0:T(8,128)(2,1)S(1)} %get-tuple-element.26), channel_id=1, source_target_pairs={{0,3},{1,2},{2,1},{3,0},{4,7},{5,6},{6,5},{7,4},{8,11},{9,10},{10,... | collective-permute-start | bytes 110600 | tf_op jit(solution)/shard_map/ppermute | solution.py:419
  32.3 7.5 %collective-permute-start.15 = (bf16[256,128]{1,0:T(8,128)(2,1)S(1)}, bf16[256,128]{1,0:T(8,128)(2,1)S(1)}, u32[]{:S(2)}, u32[]{:S(2)}) collective-permute-start(bf16[256,128]{1,0:T(8,128)(2,1)S(1)} %get-tuple-element.30), channel_id=1, source_target_pairs={{0,12},{1,13},{2,14},{3,15},{4,8},{5,9},{6,10},{7,11},{8,4},{9,5},... | collective-permute-start | bytes 196616 | tf_op jit(solution)/shard_map/ppermute | solution.py:419
  37.1 6.0 %collective-permute-start.16 = (bf16[256,128]{1,0:T(8,128)(2,1)S(1)}, bf16[256,128]{1,0:T(8,128)(2,1)S(1)}, u32[]{:S(2)}, u32[]{:S(2)}) collective-permute-start(bf16[256,128]{1,0:T(8,128)(2,1)S(1)} %get-tuple-element.31), channel_id=1, source_target_pairs={{0,8},{1,9},{2,10},{3,11},{4,12},{5,13},{6,14},{7,15},{8,0},{9,1},... | collective-permute-start | bytes 196616 | tf_op jit(solution)/shard_map/ppermute | solution.py:419
  37.1 6.2 %collective-permute-start.17 = (bf16[256,128]{1,0:T(8,128)(2,1)S(1)}, bf16[256,128]{1,0:T(8,128)(2,1)S(1)}, u32[]{:S(2)}, u32[]{:S(2)}) collective-permute-start(bf16[256,128]{1,0:T(8,128)(2,1)S(1)} %get-tuple-element.32), channel_id=1, source_target_pairs={{0,4},{1,5},{2,6},{3,7},{4,0},{5,1},{6,2},{7,3},{8,12},{9,13},{10,... | collective-permute-start | bytes 196616 | tf_op jit(solution)/shard_map/ppermute | solution.py:419

commit v16 on v14

--- a/solution.py
+++ b/solution.py
@@ -9,7 +9,7 @@
 
 AB_DEV = 8
 CHUNK = 2
-TURNS = (8, 2, 1)
+TURNS = (8, 4, 2, 1)
 TAIL = 16
 PLANE = 4
 SPREAD_COST = 10**10
@@ -466,7 +466,7 @@
     near = second_part(n_aux, lists, bit, tiles, fitted, far[1])
     near = [near[0]] + [swap(near[r], r) for r in range(1, PLANE)]
     far = spread(far, jnp.bfloat16, blk, bb_dev)
-    far = [swap(far[dz - 1], dz * PLANE) for dz in range(depth - 1, 0, -1)]
+    far = [swap(far[dz - 1], dz * PLANE) for dz in range(1, depth)]
     near = spread(near, jnp.float32, blk, bb_dev)
     return total_of(list(near) + far)
 

time: 44.3 us -> 44.8 us (1.011)
  starting transfers between devices: 18.1 us -> 18.6 us
    ppermute x19, starting transfers between devices: 18.1 us -> 18.6 us  [swap(): return lax.ppermute(array, 'aux', [(i, i ^ m) for i in range(n_aux)])]
  transfers between devices with their start and end apart: 19 -> 19, of which waited for: 9 -> 10; matrix products, arithmetic and copies ran while one was open for 6% -> 6% of each run, Pallas kernels for 9% -> 10%
where the time goes in v16:
time: 44.8 us; the launch traced here: 44.5 us
  starting transfers between devices  18.6 us (42%)
  waiting for transfers between devices  12.1 us (27%)
  Pallas kernels  10.1 us (23%)
  other arithmetic  2.75 us (6%)
  between operations  0.91 us (2%)
    ppermute x19, starting transfers between devices, swap(): return lax.ppermute(array, 'aux', [(i, i ^ m) for i in range(n_aux)])  18.6 us
    ppermute x19, waiting for transfers between devices, swap(): return lax.ppermute(array, 'aux', [(i, i ^ m) for i in range(n_aux)])  12.1 us
    pallas_call x1, Pallas kernels, first_part(): pl.pallas_call(kernel, out_shape=out_shape, in_specs=[smem] * 7 + [vmem]...  5.11 us
    pallas_call x1, Pallas kernels, begin(): pl.pallas_call(kernel, out_shape=[jax.ShapeDtypeStruct((AB_DEV, nocc, aux...  2.35 us
    pallas_call x1, Pallas kernels, second_part(): pl.pallas_call(kernel, out_shape=[jax.ShapeDtypeStruct(shape, jnp.bfloat1...  1.77 us
  transfers between devices with their start and end apart: 19, of which 10 were waited for; matrix products, arithmetic and copies ran while one was open for 6% of the time, Pallas kernels for 10%

profile of v16, /device:TPU:0, one launch (start us, length us, event | category | flops | bytes accessed | tf_op | source)
XLA Modules:
  0.0 44.5 jit_solution(1783527300113205358)
XLA Ops:
  0.0 3.0 %collective-permute-start.4 = (bf16[256,128]{1,0:T(8,128)(2,1)}, bf16[256,128]{1,0:T(8,128)(2,1)S(1)}, u32[]{:S(2)}, u32[]{:S(2)}) collective-permute-start(bf16[256,128]{1,0:T(8,128)(2,1)} %own.1), channel_id=1, source_target_pairs={{0,2},{1,3},{2,0},{3,1},{4,6},{5,7},{6,4},{7,5},{8,10},{9,11},{10,... | collective-permute-start | bytes 196616 | tf_op jit(solution)/shard_map/ppermute | solution.py:419
  3.0 2.6 %collective-permute-start.1 = (bf16[256,128]{1,0:T(8,128)(2,1)}, bf16[256,128]{1,0:T(8,128)(2,1)S(1)}, u32[]{:S(2)}, u32[]{:S(2)}) collective-permute-start(bf16[256,128]{1,0:T(8,128)(2,1)} %own.1), channel_id=1, source_target_pairs={{0,8},{1,9},{2,10},{3,11},{4,12},{5,13},{6,14},{7,15},{8,0},{9,1},... | collective-permute-start | bytes 196616 | tf_op jit(solution)/shard_map/ppermute | solution.py:419
  5.6 1.6 %collective-permute-start = (bf16[256,128]{1,0:T(8,128)(2,1)}, bf16[256,128]{1,0:T(8,128)(2,1)S(1)}, u32[]{:S(2)}, u32[]{:S(2)}) collective-permute-start(bf16[256,128]{1,0:T(8,128)(2,1)} %own.1), channel_id=1, source_target_pairs={{0,4},{1,5},{2,6},{3,7},{4,0},{5,1},{6,2},{7,3},{8,12},{9,13},{10,... | collective-permute-start | bytes 196616 | tf_op jit(solution)/shard_map/ppermute | solution.py:419
  8.0 0.8 %add_reduce_fusion.packed_ref = s32[64]{0:T(128)S(1)} fusion(s32[32]{0:T(128)S(1)} %pad.4, s32[64]{0:T(128)} %param.10, s32[32]{0:T(128)S(1)} %fusion.9, s32[64]{0:T(128)} %param.9, s32[32]{0:T(128)} %param.8), kind=kLoop, calls=%fused_computation.15 | loop fusion | flops 16320 | bytes 1152 | tf_op jit(solution)/shard_map/reduce_sum | solution.py:26
  10.5 0.6 %collective-permute-start.5 = (bf16[256,128]{1,0:T(8,128)(2,1)S(1)}, bf16[256,128]{1,0:T(8,128)(2,1)S(1)}, u32[]{:S(2)}, u32[]{:S(2)}) collective-permute-start(bf16[256,128]{1,0:T(8,128)(2,1)S(1)} %collective-permute-done.4.refs_3_), channel_id=1, source_target_pairs={{0,1},{1,0},{2,3},{3,2},{4,5},{5,4},{6,7},{7,6},{8,9},{9,8},{10,11... | collective-permute-start | bytes 196616 | tf_op jit(solution)/shard_map/ppermute | solution.py:419
  11.6 1.8 %collective-permute-done.7.refs_1_ = bf16[256,128]{1,0:T(8,128)(2,1)S(1)} collective-permute-done((bf16[256,128]{1,0:T(8,128)(2,1)}, bf16[256,128]{1,0:T(8,128)(2,1)S(1)}, u32[]{:S(2)}, u32[]{:S(2)}) %collective-permute-start.7) | collective-permute-done | bytes 65568 | tf_op jit(solution)/shard_map/ppermute | solution.py:419
  13.4 0.5 %collective-permute-start.8 = (bf16[256,128]{1,0:T(8,128)(2,1)S(1)}, bf16[256,128]{1,0:T(8,128)(2,1)S(1)}, u32[]{:S(2)}, u32[]{:S(2)}) collective-permute-start(bf16[256,128]{1,0:T(8,128)(2,1)S(1)} %collective-permute-done.7.refs_1_), channel_id=1, source_target_pairs={{0,2},{1,3},{2,0},{3,1},{4,6},{5,7},{6,4},{7,5},{8,10},{9,11},{10,... | collective-permute-start | bytes 196616 | tf_op jit(solution)/shard_map/ppermute | solution.py:419
  14.0 2.4 %begin.1 = (f32[8,128,640]{2,1,0:T(8,128)S(1)}, s32[64]{0:T(128)S(1)}) custom-call(s32[96]{0:T(128)S(1)} %get-tuple-element.52.slot_ref.refs_0_, s32[96]{0:T(128)S(1)} %get-tuple-element.51.block_ref.refs_1_, s32[64]{0:T(128)S(1)} %pad_add_fusion.gid_ref.refs_2_, s32[16]{0:T(128)S(1)} %select_reduce_fusion.8.bit_ref.refs_6_, ...), custom_call_target="tpu_custom_call" | custom-call | flops 1342177280 | bytes 5242880 | tf_op jit(solution)/shard_map/begin/pallas_call | solution.py:151
  17.2 0.8 %collective-permute-done.8.refs_2_ = bf16[256,128]{1,0:T(8,128)(2,1)S(1)} collective-permute-done((bf16[256,128]{1,0:T(8,128)(2,1)S(1)}, bf16[256,128]{1,0:T(8,128)(2,1)S(1)}, u32[]{:S(2)}, u32[]{:S(2)}) %collective-permute-start.8) | collective-permute-done | bytes 65568 | tf_op jit(solution)/shard_map/ppermute | solution.py:419
  18.2 1.4 %collective-permute-done.9.refs_10_ = bf16[4,256,128]{2,1,0:T(8,128)(2,1)S(1)} collective-permute-done((bf16[4,256,128]{2,1,0:T(8,128)(2,1)S(1)}, bf16[4,256,128]{2,1,0:T(8,128)(2,1)S(1)}, u32[]{:S(2)}, u32[]{:S(2)}) %collective-permute-start.9) | collective-permute-done | bytes 262176 | tf_op jit(solution)/shard_map/ppermute | solution.py:419
  19.6 5.1 %first_part.1 = (bf16[3,144,128]{2,1,0:T(8,128)(2,1)S(1)}, bf16[3,144,128]{2,1,0:T(8,128)(2,1)S(1)}, bf16[3,144,128]{2,1,0:T(8,128)(2,1)S(1)}, bf16[3,144,128]{2...) custom-call(s32[96]{0:T(128)S(1)} %get-tuple-element.52.slot_ref.ref, ...), custom_call_target="tpu_custom_call", output_to_operand_aliasing={{5}: (8, {})} | custom-call | flops 2013265920 | bytes 5242880 | tf_op jit(solution)/shard_map/first_part/pallas_call | solution.py:213
  24.8 0.7 %collective-permute-start.10 = (bf16[3,144,128]{2,1,0:T(8,128)(2,1)S(1)}, bf16[3,144,128]{2,1,0:T(8,128)(2,1)S(1)}, u32[]{:S(2)}, u32[]{:S(2)}) collective-permute-start(bf16[3,144,128]{2,1,0:T(8,128)(2,1)S(1)} %get-tuple-element.22), channel_id=1, source_target_pairs={{0,1},{1,0},{2,3},{3,2},{4,5},{5,4},{6,7},{7,6},{8,9},{9,8},{10,11... | collective-permute-start | bytes 331784 | tf_op jit(solution)/shard_map/ppermute | solution.py:419
  25.5 0.7 %collective-permute-start.14 = (bf16[3,144,128]{2,1,0:T(8,128)(2,1)S(1)}, bf16[3,144,128]{2,1,0:T(8,128)(2,1)S(1)}, u32[]{:S(2)}, u32[]{:S(2)}) collective-permute-start(bf16[3,144,128]{2,1,0:T(8,128)(2,1)S(1)} %get-tuple-element.28), channel_id=1, source_target_pairs={{0,2},{1,3},{2,0},{3,1},{4,6},{5,7},{6,4},{7,5},{8,10},{9,11},{10,... | collective-permute-start | bytes 331784 | tf_op jit(solution)/shard_map/ppermute | solution.py:419
  26.1 0.8 %collective-permute-start.15 = (bf16[3,144,128]{2,1,0:T(8,128)(2,1)S(1)}, bf16[3,144,128]{2,1,0:T(8,128)(2,1)S(1)}, u32[]{:S(2)}, u32[]{:S(2)}) collective-permute-start(bf16[3,144,128]{2,1,0:T(8,128)(2,1)S(1)} %get-tuple-element.29), channel_id=1, source_target_pairs={{0,3},{1,2},{2,1},{3,0},{4,7},{5,6},{6,5},{7,4},{8,11},{9,10},{10,... | collective-permute-start | bytes 331784 | tf_op jit(solution)/shard_map/ppermute | solution.py:419
  26.9 1.8 %second_part.1 = (bf16[1,144,128]{2,1,0:T(8,128)(2,1)S(1)}, bf16[1,144,128]{2,1,0:T(8,128)(2,1)S(1)}, bf16[1,144,128]{2,1,0:T(8,128)(2,1)S(1)}, bf16[1,144,128]{2,1,0:T(8,128)(2,1)S(1)}) custom-call(s32[96]{0:T(128)S(1)} %get-tuple-element.50.refs_3_.slot_ref, s32[96]{0:T(128)S(1)} %get-tuple-element.49.refs_4_.block_ref, ...), custom_call_target="tpu_custom_call" | custom-call | flops 10000000000 | bytes 5242880 | tf_op jit(solution)/shard_map/second_part/pallas_call | solution.py:246
  28.7 0.9 %collective-permute-start.11 = (bf16[1,144,128]{2,1,0:T(8,128)(2,1)S(1)}, bf16[1,144,128]{2,1,0:T(8,128)(2,1)S(1)}, u32[]{:S(2)}, u32[]{:S(2)}) collective-permute-start(bf16[1,144,128]{2,1,0:T(8,128)(2,1)S(1)} %get-tuple-element.24), channel_id=1, source_target_pairs={{0,1},{1,0},{2,3},{3,2},{4,5},{5,4},{6,7},{7,6},{8,9},{9,8},{10,11... | collective-permute-start | bytes 110600 | tf_op jit(solution)/shard_map/ppermute | solution.py:419
  29.6 0.7 %collective-permute-start.12 = (bf16[1,144,128]{2,1,0:T(8,128)(2,1)S(1)}, bf16[1,144,128]{2,1,0:T(8,128)(2,1)S(1)}, u32[]{:S(2)}, u32[]{:S(2)}) collective-permute-start(bf16[1,144,128]{2,1,0:T(8,128)(2,1)S(1)} %get-tuple-element.25), channel_id=1, source_target_pairs={{0,2},{1,3},{2,0},{3,1},{4,6},{5,7},{6,4},{7,5},{8,10},{9,11},{10,... | collective-permute-start | bytes 110600 | tf_op jit(solution)/shard_map/ppermute | solution.py:419
  30.2 0.8 %collective-permute-start.13 = (bf16[1,144,128]{2,1,0:T(8,128)(2,1)S(1)}, bf16[1,144,128]{2,1,0:T(8,128)(2,1)S(1)}, u32[]{:S(2)}, u32[]{:S(2)}) collective-permute-start(bf16[1,144,128]{2,1,0:T(8,128)(2,1)S(1)} %get-tuple-element.26), channel_id=1, source_target_pairs={{0,3},{1,2},{2,1},{3,0},{4,7},{5,6},{6,5},{7,4},{8,11},{9,10},{10,... | collective-permute-start | bytes 110600 | tf_op jit(solution)/shard_map/ppermute | solution.py:419
  31.4 0.6 %collective-permute-done.15.refs_3_ = bf16[3,144,128]{2,1,0:T(8,128)(2,1)S(1)} collective-permute-done((bf16[3,144,128]{2,1,0:T(8,128)(2,1)S(1)}, bf16[3,144,128]{2,1,0:T(8,128)(2,1)S(1)}, u32[]{:S(2)}, u32[]{:S(2)}) %collective-permute-start.15) | collective-permute-done | bytes 110624 | tf_op jit(solution)/shard_map/ppermute | solution.py:419
  32.2 2.7 %collective-permute-start.16 = (bf16[256,128]{1,0:T(8,128)(2,1)S(1)}, bf16[256,128]{1,0:T(8,128)(2,1)S(1)}, u32[]{:S(2)}, u32[]{:S(2)}) collective-permute-start(bf16[256,128]{1,0:T(8,128)(2,1)S(1)} %get-tuple-element.30), channel_id=1, source_target_pairs={{0,4},{1,5},{2,6},{3,7},{4,0},{5,1},{6,2},{7,3},{8,12},{9,13},{10,... | collective-permute-start | bytes 196616 | tf_op jit(solution)/shard_map/ppermute | solution.py:419
  34.9 2.4 %collective-permute-start.17 = (bf16[256,128]{1,0:T(8,128)(2,1)S(1)}, bf16[256,128]{1,0:T(8,128)(2,1)S(1)}, u32[]{:S(2)}, u32[]{:S(2)}) collective-permute-start(bf16[256,128]{1,0:T(8,128)(2,1)S(1)} %get-tuple-element.31), channel_id=1, source_target_pairs={{0,8},{1,9},{2,10},{3,11},{4,12},{5,13},{6,14},{7,15},{8,0},{9,1},... | collective-permute-start | bytes 196616 | tf_op jit(solution)/shard_map/ppermute | solution.py:419
  37.5 4.5 %collective-permute-done.17.refs_2_ = bf16[256,128]{1,0:T(8,128)(2,1)S(1)} collective-permute-done((bf16[256,128]{1,0:T(8,128)(2,1)S(1)}, bf16[256,128]{1,0:T(8,128)(2,1)S(1)}, u32[]{:S(2)}, u32[]{:S(2)}) %collective-permute-start.17) | collective-permute-done | bytes 65568 | tf_op jit(solution)/shard_map/ppermute | solution.py:419
  42.1 1.8 %collective-permute-done.18.refs_3_ = bf16[256,128]{1,0:T(8,128)(2,1)S(1)} collective-permute-done((bf16[256,128]{1,0:T(8,128)(2,1)S(1)}, bf16[256,128]{1,0:T(8,128)(2,1)S(1)}, u32[]{:S(2)}, u32[]{:S(2)}) %collective-permute-start.18) | collective-permute-done | bytes 65568 | tf_op jit(solution)/shard_map/ppermute | solution.py:419
  43.9 0.7 %total_of.1 = bf16[256,128]{1,0:T(8,128)(2,1)} custom-call(f32[256,128]{1,0:T(8,128)S(1)} %spread.2.refs_0_, bf16[256,128]{1,0:T(8,128)(2,1)S(1)} %collective-permute-done.16.refs_1_, bf16[256,128]{1,0:T(8,128)(2,1)S(1)} %collective-permute-done.17.refs_2_, bf16[256,128]{1,0:T(8,128)(2,1)S(1)} %collective-permute-done.18.refs_3_), custom_call_target="tpu_custom_call" | custom-call | tf_op jit(solution)/shard_map/total_of/pallas_call | solution.py:379
  (64 shorter events, 4.2 us)
Async XLA Ops:
  0.0 10.5 %collective-permute-start.4 = (bf16[256,128]{1,0:T(8,128)(2,1)}, bf16[256,128]{1,0:T(8,128)(2,1)S(1)}, u32[]{:S(2)}, u32[]{:S(2)}) collective-permute-start(bf16[256,128]{1,0:T(8,128)(2,1)} %own.1), channel_id=1, source_target_pairs={{0,2},{1,3},{2,0},{3,1},{4,6},{5,7},{6,4},{7,5},{8,10},{9,11},{10,... | collective-permute-start | bytes 196616 | tf_op jit(solution)/shard_map/ppermute | solution.py:419
  3.0 11.0 %collective-permute-start.3 = (bf16[256,128]{1,0:T(8,128)(2,1)}, bf16[256,128]{1,0:T(8,128)(2,1)S(1)}, u32[]{:S(2)}, u32[]{:S(2)}) collective-permute-start(bf16[256,128]{1,0:T(8,128)(2,1)} %own.1), channel_id=1, source_target_pairs={{0,1},{1,0},{2,3},{3,2},{4,5},{5,4},{6,7},{7,6},{8,9},{9,8},{10,11... | collective-permute-start | bytes 196616 | tf_op jit(solution)/shard_map/ppermute | solution.py:419
  3.0 7.0 %collective-permute-start.1 = (bf16[256,128]{1,0:T(8,128)(2,1)}, bf16[256,128]{1,0:T(8,128)(2,1)S(1)}, u32[]{:S(2)}, u32[]{:S(2)}) collective-permute-start(bf16[256,128]{1,0:T(8,128)(2,1)} %own.1), channel_id=1, source_target_pairs={{0,8},{1,9},{2,10},{3,11},{4,12},{5,13},{6,14},{7,15},{8,0},{9,1},... | collective-permute-start | bytes 196616 | tf_op jit(solution)/shard_map/ppermute | solution.py:419
  5.6 4.8 %collective-permute-start = (bf16[256,128]{1,0:T(8,128)(2,1)}, bf16[256,128]{1,0:T(8,128)(2,1)S(1)}, u32[]{:S(2)}, u32[]{:S(2)}) collective-permute-start(bf16[256,128]{1,0:T(8,128)(2,1)} %own.1), channel_id=1, source_target_pairs={{0,4},{1,5},{2,6},{3,7},{4,0},{5,1},{6,2},{7,3},{8,12},{9,13},{10,... | collective-permute-start | bytes 196616 | tf_op jit(solution)/shard_map/ppermute | solution.py:419
  7.1 6.3 %collective-permute-start.7 = (bf16[256,128]{1,0:T(8,128)(2,1)}, bf16[256,128]{1,0:T(8,128)(2,1)S(1)}, u32[]{:S(2)}, u32[]{:S(2)}) collective-permute-start(bf16[256,128]{1,0:T(8,128)(2,1)} %own.1), channel_id=1, source_target_pairs={{0,12},{1,13},{2,14},{3,15},{4,8},{5,9},{6,10},{7,11},{8,4},{9,5},... | collective-permute-start | bytes 196616 | tf_op jit(solution)/shard_map/ppermute | solution.py:419
  9.7 4.2 %slice-start = ((s8[10485760]{0:T(1024)(128)(4,1)}), s8[4194304]{0:T(1024)(128)(4,1)S(1)}, s32[]{:S(2)}) async-start(s8[10485760]{0:T(1024)(128)(4,1)} %bitcast), calls=%async_computation | async-start | bytes 8388608
  9.7 4.2 %slice-start.1 = ((s8[10485760]{0:T(1024)(128)(4,1)}), s8[4194304]{0:T(1024)(128)(4,1)S(1)}, s32[]{:S(2)}) async-start(s8[10485760]{0:T(1024)(128)(4,1)} %bitcast), calls=%async_computation.1 | async-start | bytes 8388608
  9.8 4.2 %slice-start.2 = ((s8[10485760]{0:T(1024)(128)(4,1)}), s8[2097152]{0:T(1024)(128)(4,1)S(1)}, s32[]{:S(2)}) async-start(s8[10485760]{0:T(1024)(128)(4,1)} %bitcast), calls=%async_computation.2 | async-start | bytes 4194304
  9.8 4.2 %copy-start = (bf16[256,128]{1,0:T(8,128)(2,1)S(1)}, bf16[256,128]{1,0:T(8,128)(2,1)}, u32[]{:S(2)}) copy-start(bf16[256,128]{1,0:T(8,128)(2,1)} %own.1) | copy-start | bytes 196612
  10.3 3.6 %collective-permute-start.2 = (bf16[2,256,128]{2,1,0:T(8,128)(2,1)S(1)}, bf16[2,256,128]{2,1,0:T(8,128)(2,1)S(1)}, u32[]{:S(2)}, u32[]{:S(2)}) collective-permute-start(bf16[2,256,128]{2,1,0:T(8,128)(2,1)S(1)} %merge.1.refs_0_), channel_id=1, source_target_pairs={{0,1},{1,0},{2,3},{3,2},{4,5},{5,4},{6,7},{7,6},{8,9},{9,8},{10,11... | collective-permute-start | bytes 393224 | tf_op jit(solution)/shard_map/ppermute | solution.py:419
  10.5 3.4 %collective-permute-start.5 = (bf16[256,128]{1,0:T(8,128)(2,1)S(1)}, bf16[256,128]{1,0:T(8,128)(2,1)S(1)}, u32[]{:S(2)}, u32[]{:S(2)}) collective-permute-start(bf16[256,128]{1,0:T(8,128)(2,1)S(1)} %collective-permute-done.4.refs_3_), channel_id=1, source_target_pairs={{0,1},{1,0},{2,3},{3,2},{4,5},{5,4},{6,7},{7,6},{8,9},{9,8},{10,11... | collective-permute-start | bytes 196616 | tf_op jit(solution)/shard_map/ppermute | solution.py:419
  11.2 6.8 %collective-permute-start.6 = (bf16[2,256,128]{2,1,0:T(8,128)(2,1)S(1)}, bf16[2,256,128]{2,1,0:T(8,128)(2,1)S(1)}, u32[]{:S(2)}, u32[]{:S(2)}) collective-permute-start(bf16[2,256,128]{2,1,0:T(8,128)(2,1)S(1)} %merge.1.refs_0_), channel_id=1, source_target_pairs={{0,2},{1,3},{2,0},{3,1},{4,6},{5,7},{6,4},{7,5},{8,10},{9,11},{10,... | collective-permute-start | bytes 393224 | tf_op jit(solution)/shard_map/ppermute | solution.py:419
  13.4 4.6 %collective-permute-start.8 = (bf16[256,128]{1,0:T(8,128)(2,1)S(1)}, bf16[256,128]{1,0:T(8,128)(2,1)S(1)}, u32[]{:S(2)}, u32[]{:S(2)}) collective-permute-start(bf16[256,128]{1,0:T(8,128)(2,1)S(1)} %collective-permute-done.7.refs_1_), channel_id=1, source_target_pairs={{0,2},{1,3},{2,0},{3,1},{4,6},{5,7},{6,4},{7,5},{8,10},{9,11},{10,... | collective-permute-start | bytes 196616 | tf_op jit(solution)/shard_map/ppermute | solution.py:419
  18.0 1.6 %collective-permute-start.9 = (bf16[4,256,128]{2,1,0:T(8,128)(2,1)S(1)}, bf16[4,256,128]{2,1,0:T(8,128)(2,1)S(1)}, u32[]{:S(2)}, u32[]{:S(2)}) collective-permute-start(bf16[4,256,128]{2,1,0:T(8,128)(2,1)S(1)} %gate.1.refs_9_), channel_id=1, source_target_pairs={{0,1},{1,0},{2,3},{3,2},{4,5},{5,4},{6,7},{7,6},{8,9},{9,8},{10,11... | collective-permute-start | bytes 786440 | tf_op jit(solution)/shard_map/ppermute | solution.py:419
  24.8 2.2 %collective-permute-start.10 = (bf16[3,144,128]{2,1,0:T(8,128)(2,1)S(1)}, bf16[3,144,128]{2,1,0:T(8,128)(2,1)S(1)}, u32[]{:S(2)}, u32[]{:S(2)}) collective-permute-start(bf16[3,144,128]{2,1,0:T(8,128)(2,1)S(1)} %get-tuple-element.22), channel_id=1, source_target_pairs={{0,1},{1,0},{2,3},{3,2},{4,5},{5,4},{6,7},{7,6},{8,9},{9,8},{10,11... | collective-permute-start | bytes 331784 | tf_op jit(solution)/shard_map/ppermute | solution.py:419
  25.5 5.9 %collective-permute-start.14 = (bf16[3,144,128]{2,1,0:T(8,128)(2,1)S(1)}, bf16[3,144,128]{2,1,0:T(8,128)(2,1)S(1)}, u32[]{:S(2)}, u32[]{:S(2)}) collective-permute-start(bf16[3,144,128]{2,1,0:T(8,128)(2,1)S(1)} %get-tuple-element.28), channel_id=1, source_target_pairs={{0,2},{1,3},{2,0},{3,1},{4,6},{5,7},{6,4},{7,5},{8,10},{9,11},{10,... | collective-permute-start | bytes 331784 | tf_op jit(solution)/shard_map/ppermute | solution.py:419
  26.1 5.9 %collective-permute-start.15 = (bf16[3,144,128]{2,1,0:T(8,128)(2,1)S(1)}, bf16[3,144,128]{2,1,0:T(8,128)(2,1)S(1)}, u32[]{:S(2)}, u32[]{:S(2)}) collective-permute-start(bf16[3,144,128]{2,1,0:T(8,128)(2,1)S(1)} %get-tuple-element.29), channel_id=1, source_target_pairs={{0,3},{1,2},{2,1},{3,0},{4,7},{5,6},{6,5},{7,4},{8,11},{9,10},{10,... | collective-permute-start | bytes 331784 | tf_op jit(solution)/shard_map/ppermute | solution.py:419
  28.7 8.6 %collective-permute-start.11 = (bf16[1,144,128]{2,1,0:T(8,128)(2,1)S(1)}, bf16[1,144,128]{2,1,0:T(8,128)(2,1)S(1)}, u32[]{:S(2)}, u32[]{:S(2)}) collective-permute-start(bf16[1,144,128]{2,1,0:T(8,128)(2,1)S(1)} %get-tuple-element.24), channel_id=1, source_target_pairs={{0,1},{1,0},{2,3},{3,2},{4,5},{5,4},{6,7},{7,6},{8,9},{9,8},{10,11... | collective-permute-start | bytes 110600 | tf_op jit(solution)/shard_map/ppermute | solution.py:419
  29.6 7.8 %collective-permute-start.12 = (bf16[1,144,128]{2,1,0:T(8,128)(2,1)S(1)}, bf16[1,144,128]{2,1,0:T(8,128)(2,1)S(1)}, u32[]{:S(2)}, u32[]{:S(2)}) collective-permute-start(bf16[1,144,128]{2,1,0:T(8,128)(2,1)S(1)} %get-tuple-element.25), channel_id=1, source_target_pairs={{0,2},{1,3},{2,0},{3,1},{4,6},{5,7},{6,4},{7,5},{8,10},{9,11},{10,... | collective-permute-start | bytes 110600 | tf_op jit(solution)/shard_map/ppermute | solution.py:419
  30.2 7.1 %collective-permute-start.13 = (bf16[1,144,128]{2,1,0:T(8,128)(2,1)S(1)}, bf16[1,144,128]{2,1,0:T(8,128)(2,1)S(1)}, u32[]{:S(2)}, u32[]{:S(2)}) collective-permute-start(bf16[1,144,128]{2,1,0:T(8,128)(2,1)S(1)} %get-tuple-element.26), channel_id=1, source_target_pairs={{0,3},{1,2},{2,1},{3,0},{4,7},{5,6},{6,5},{7,4},{8,11},{9,10},{10,... | collective-permute-start | bytes 110600 | tf_op jit(solution)/shard_map/ppermute | solution.py:419
  32.2 5.3 %collective-permute-start.16 = (bf16[256,128]{1,0:T(8,128)(2,1)S(1)}, bf16[256,128]{1,0:T(8,128)(2,1)S(1)}, u32[]{:S(2)}, u32[]{:S(2)}) collective-permute-start(bf16[256,128]{1,0:T(8,128)(2,1)S(1)} %get-tuple-element.30), channel_id=1, source_target_pairs={{0,4},{1,5},{2,6},{3,7},{4,0},{5,1},{6,2},{7,3},{8,12},{9,13},{10,... | collective-permute-start | bytes 196616 | tf_op jit(solution)/shard_map/ppermute | solution.py:419
  34.9 7.2 %collective-permute-start.17 = (bf16[256,128]{1,0:T(8,128)(2,1)S(1)}, bf16[256,128]{1,0:T(8,128)(2,1)S(1)}, u32[]{:S(2)}, u32[]{:S(2)}) collective-permute-start(bf16[256,128]{1,0:T(8,128)(2,1)S(1)} %get-tuple-element.31), channel_id=1, source_target_pairs={{0,8},{1,9},{2,10},{3,11},{4,12},{5,13},{6,14},{7,15},{8,0},{9,1},... | collective-permute-start | bytes 196616 | tf_op jit(solution)/shard_map/ppermute | solution.py:419
  37.3 6.6 %collective-permute-start.18 = (bf16[256,128]{1,0:T(8,128)(2,1)S(1)}, bf16[256,128]{1,0:T(8,128)(2,1)S(1)}, u32[]{:S(2)}, u32[]{:S(2)}) collective-permute-start(bf16[256,128]{1,0:T(8,128)(2,1)S(1)} %get-tuple-element.32), channel_id=1, source_target_pairs={{0,12},{1,13},{2,14},{3,15},{4,8},{5,9},{6,10},{7,11},{8,4},{9,5},... | collective-permute-start | bytes 196616 | tf_op jit(solution)/shard_map/ppermute | solution.py:419

commit v17 on v14

--- a/solution.py
+++ b/solution.py
@@ -466,7 +466,7 @@
     near = second_part(n_aux, lists, bit, tiles, fitted, far[1])
     near = [near[0]] + [swap(near[r], r) for r in range(1, PLANE)]
     far = spread(far, jnp.bfloat16, blk, bb_dev)
-    far = [swap(far[dz - 1], dz * PLANE) for dz in range(depth - 1, 0, -1)]
+    far = [swap(far[dz - 1], dz * PLANE) for dz in [*range(2, depth), 1]]
     near = spread(near, jnp.float32, blk, bb_dev)
     return total_of(list(near) + far)
 

time: 44.3 us -> 43.5 us (0.982)
  Pallas kernels: 10 us -> 9.43 us
    pallas_call x1, Pallas kernels: 5.2 us -> 4.53 us  [first_part(): pl.pallas_call(kernel, out_shape=out_shape, in_specs=[smem] * 7 + [vmem]...]
  transfers between devices with their start and end apart: 19 -> 19, of which waited for: 9 -> 10; matrix products, arithmetic and copies ran while one was open for 6% -> 6% of each run, Pallas kernels for 9% -> 10%
where the time goes in v17:
time: 43.5 us; the launch traced here: 43.4 us
  starting transfers between devices  18.4 us (42%)
  waiting for transfers between devices  11.9 us (27%)
  Pallas kernels  9.43 us (22%)
  other arithmetic  2.75 us (6%)
  between operations  0.92 us (2%)
    ppermute x19, starting transfers between devices, swap(): return lax.ppermute(array, 'aux', [(i, i ^ m) for i in range(n_aux)])  18.4 us
    ppermute x19, waiting for transfers between devices, swap(): return lax.ppermute(array, 'aux', [(i, i ^ m) for i in range(n_aux)])  11.9 us
    pallas_call x1, Pallas kernels, first_part(): pl.pallas_call(kernel, out_shape=out_shape, in_specs=[smem] * 7 + [vmem]...  4.53 us
    pallas_call x1, Pallas kernels, begin(): pl.pallas_call(kernel, out_shape=[jax.ShapeDtypeStruct((AB_DEV, nocc, aux...  2.07 us
    pallas_call x1, Pallas kernels, second_part(): pl.pallas_call(kernel, out_shape=[jax.ShapeDtypeStruct(shape, jnp.bfloat1...  1.92 us
  transfers between devices with their start and end apart: 19, of which 10 were waited for; matrix products, arithmetic and copies ran while one was open for 6% of the time, Pallas kernels for 10%

profile of v17, /device:TPU:0, one launch (start us, length us, event | category | flops | bytes accessed | tf_op | source)
XLA Modules:
  0.0 43.4 jit_solution(7220077024198110225)
XLA Ops:
  0.0 3.0 %collective-permute-start.4 = (bf16[256,128]{1,0:T(8,128)(2,1)}, bf16[256,128]{1,0:T(8,128)(2,1)S(1)}, u32[]{:S(2)}, u32[]{:S(2)}) collective-permute-start(bf16[256,128]{1,0:T(8,128)(2,1)} %own.1), channel_id=1, source_target_pairs={{0,2},{1,3},{2,0},{3,1},{4,6},{5,7},{6,4},{7,5},{8,10},{9,11},{10,... | collective-permute-start | bytes 196616 | tf_op jit(solution)/shard_map/ppermute | solution.py:419
  3.0 2.6 %collective-permute-start.1 = (bf16[256,128]{1,0:T(8,128)(2,1)}, bf16[256,128]{1,0:T(8,128)(2,1)S(1)}, u32[]{:S(2)}, u32[]{:S(2)}) collective-permute-start(bf16[256,128]{1,0:T(8,128)(2,1)} %own.1), channel_id=1, source_target_pairs={{0,8},{1,9},{2,10},{3,11},{4,12},{5,13},{6,14},{7,15},{8,0},{9,1},... | collective-permute-start | bytes 196616 | tf_op jit(solution)/shard_map/ppermute | solution.py:419
  5.6 1.6 %collective-permute-start = (bf16[256,128]{1,0:T(8,128)(2,1)}, bf16[256,128]{1,0:T(8,128)(2,1)S(1)}, u32[]{:S(2)}, u32[]{:S(2)}) collective-permute-start(bf16[256,128]{1,0:T(8,128)(2,1)} %own.1), channel_id=1, source_target_pairs={{0,4},{1,5},{2,6},{3,7},{4,0},{5,1},{6,2},{7,3},{8,12},{9,13},{10,... | collective-permute-start | bytes 196616 | tf_op jit(solution)/shard_map/ppermute | solution.py:419
  8.0 0.8 %add_reduce_fusion.packed_ref = s32[64]{0:T(128)S(1)} fusion(s32[32]{0:T(128)S(1)} %pad.4, s32[64]{0:T(128)} %param.10, s32[32]{0:T(128)S(1)} %fusion.9, s32[64]{0:T(128)} %param.9, s32[32]{0:T(128)} %param.8), kind=kLoop, calls=%fused_computation.15 | loop fusion | flops 16320 | bytes 1152 | tf_op jit(solution)/shard_map/reduce_sum | solution.py:26
  10.5 0.6 %collective-permute-start.5 = (bf16[256,128]{1,0:T(8,128)(2,1)S(1)}, bf16[256,128]{1,0:T(8,128)(2,1)S(1)}, u32[]{:S(2)}, u32[]{:S(2)}) collective-permute-start(bf16[256,128]{1,0:T(8,128)(2,1)S(1)} %collective-permute-done.4.refs_3_), channel_id=1, source_target_pairs={{0,1},{1,0},{2,3},{3,2},{4,5},{5,4},{6,7},{7,6},{8,9},{9,8},{10,11... | collective-permute-start | bytes 196616 | tf_op jit(solution)/shard_map/ppermute | solution.py:419
  11.6 1.8 %collective-permute-done.7.refs_1_ = bf16[256,128]{1,0:T(8,128)(2,1)S(1)} collective-permute-done((bf16[256,128]{1,0:T(8,128)(2,1)}, bf16[256,128]{1,0:T(8,128)(2,1)S(1)}, u32[]{:S(2)}, u32[]{:S(2)}) %collective-permute-start.7) | collective-permute-done | bytes 65568 | tf_op jit(solution)/shard_map/ppermute | solution.py:419
  13.4 0.5 %collective-permute-start.8 = (bf16[256,128]{1,0:T(8,128)(2,1)S(1)}, bf16[256,128]{1,0:T(8,128)(2,1)S(1)}, u32[]{:S(2)}, u32[]{:S(2)}) collective-permute-start(bf16[256,128]{1,0:T(8,128)(2,1)S(1)} %collective-permute-done.7.refs_1_), channel_id=1, source_target_pairs={{0,2},{1,3},{2,0},{3,1},{4,6},{5,7},{6,4},{7,5},{8,10},{9,11},{10,... | collective-permute-start | bytes 196616 | tf_op jit(solution)/shard_map/ppermute | solution.py:419
  14.0 2.1 %begin.1 = (f32[8,128,640]{2,1,0:T(8,128)S(1)}, s32[64]{0:T(128)S(1)}) custom-call(s32[96]{0:T(128)S(1)} %get-tuple-element.52.slot_ref.refs_0_, s32[96]{0:T(128)S(1)} %get-tuple-element.51.block_ref.refs_1_, s32[64]{0:T(128)S(1)} %pad_add_fusion.gid_ref.refs_2_, s32[16]{0:T(128)S(1)} %select_reduce_fusion.8.bit_ref.refs_6_, ...), custom_call_target="tpu_custom_call" | custom-call | flops 1342177280 | bytes 5242880 | tf_op jit(solution)/shard_map/begin/pallas_call | solution.py:151
  16.9 1.1 %collective-permute-done.8.refs_2_ = bf16[256,128]{1,0:T(8,128)(2,1)S(1)} collective-permute-done((bf16[256,128]{1,0:T(8,128)(2,1)S(1)}, bf16[256,128]{1,0:T(8,128)(2,1)S(1)}, u32[]{:S(2)}, u32[]{:S(2)}) %collective-permute-start.8) | collective-permute-done | bytes 65568 | tf_op jit(solution)/shard_map/ppermute | solution.py:419
  18.2 1.4 %collective-permute-done.9.refs_10_ = bf16[4,256,128]{2,1,0:T(8,128)(2,1)S(1)} collective-permute-done((bf16[4,256,128]{2,1,0:T(8,128)(2,1)S(1)}, bf16[4,256,128]{2,1,0:T(8,128)(2,1)S(1)}, u32[]{:S(2)}, u32[]{:S(2)}) %collective-permute-start.9) | collective-permute-done | bytes 262176 | tf_op jit(solution)/shard_map/ppermute | solution.py:419
  19.6 4.5 %first_part.1 = (bf16[3,144,128]{2,1,0:T(8,128)(2,1)S(1)}, bf16[3,144,128]{2,1,0:T(8,128)(2,1)S(1)}, bf16[3,144,128]{2,1,0:T(8,128)(2,1)S(1)}, bf16[3,144,128]{2...) custom-call(s32[96]{0:T(128)S(1)} %get-tuple-element.52.slot_ref.ref, ...), custom_call_target="tpu_custom_call", output_to_operand_aliasing={{5}: (8, {})} | custom-call | flops 2013265920 | bytes 5242880 | tf_op jit(solution)/shard_map/first_part/pallas_call | solution.py:213
  24.2 1.1 %collective-permute-start.10 = (bf16[3,144,128]{2,1,0:T(8,128)(2,1)S(1)}, bf16[3,144,128]{2,1,0:T(8,128)(2,1)S(1)}, u32[]{:S(2)}, u32[]{:S(2)}) collective-permute-start(bf16[3,144,128]{2,1,0:T(8,128)(2,1)S(1)} %get-tuple-element.22), channel_id=1, source_target_pairs={{0,1},{1,0},{2,3},{3,2},{4,5},{5,4},{6,7},{7,6},{8,9},{9,8},{10,11... | collective-permute-start | bytes 331784 | tf_op jit(solution)/shard_map/ppermute | solution.py:419
  25.3 1.0 %collective-permute-start.14 = (bf16[3,144,128]{2,1,0:T(8,128)(2,1)S(1)}, bf16[3,144,128]{2,1,0:T(8,128)(2,1)S(1)}, u32[]{:S(2)}, u32[]{:S(2)}) collective-permute-start(bf16[3,144,128]{2,1,0:T(8,128)(2,1)S(1)} %get-tuple-element.28), channel_id=1, source_target_pairs={{0,2},{1,3},{2,0},{3,1},{4,6},{5,7},{6,4},{7,5},{8,10},{9,11},{10,... | collective-permute-start | bytes 331784 | tf_op jit(solution)/shard_map/ppermute | solution.py:419
  26.7 1.9 %second_part.1 = (bf16[1,144,128]{2,1,0:T(8,128)(2,1)S(1)}, bf16[1,144,128]{2,1,0:T(8,128)(2,1)S(1)}, bf16[1,144,128]{2,1,0:T(8,128)(2,1)S(1)}, bf16[1,144,128]{2,1,0:T(8,128)(2,1)S(1)}) custom-call(s32[96]{0:T(128)S(1)} %get-tuple-element.50.refs_3_.slot_ref, s32[96]{0:T(128)S(1)} %get-tuple-element.49.refs_4_.block_ref, ...), custom_call_target="tpu_custom_call" | custom-call | flops 10000000000 | bytes 5242880 | tf_op jit(solution)/shard_map/second_part/pallas_call | solution.py:246
  28.7 0.7 %collective-permute-start.11 = (bf16[1,144,128]{2,1,0:T(8,128)(2,1)S(1)}, bf16[1,144,128]{2,1,0:T(8,128)(2,1)S(1)}, u32[]{:S(2)}, u32[]{:S(2)}) collective-permute-start(bf16[1,144,128]{2,1,0:T(8,128)(2,1)S(1)} %get-tuple-element.24), channel_id=1, source_target_pairs={{0,1},{1,0},{2,3},{3,2},{4,5},{5,4},{6,7},{7,6},{8,9},{9,8},{10,11... | collective-permute-start | bytes 110600 | tf_op jit(solution)/shard_map/ppermute | solution.py:419
  29.4 0.9 %collective-permute-start.12 = (bf16[1,144,128]{2,1,0:T(8,128)(2,1)S(1)}, bf16[1,144,128]{2,1,0:T(8,128)(2,1)S(1)}, u32[]{:S(2)}, u32[]{:S(2)}) collective-permute-start(bf16[1,144,128]{2,1,0:T(8,128)(2,1)S(1)} %get-tuple-element.25), channel_id=1, source_target_pairs={{0,2},{1,3},{2,0},{3,1},{4,6},{5,7},{6,4},{7,5},{8,10},{9,11},{10,... | collective-permute-start | bytes 110600 | tf_op jit(solution)/shard_map/ppermute | solution.py:419
  30.3 0.5 %collective-permute-start.13 = (bf16[1,144,128]{2,1,0:T(8,128)(2,1)S(1)}, bf16[1,144,128]{2,1,0:T(8,128)(2,1)S(1)}, u32[]{:S(2)}, u32[]{:S(2)}) collective-permute-start(bf16[1,144,128]{2,1,0:T(8,128)(2,1)S(1)} %get-tuple-element.26), channel_id=1, source_target_pairs={{0,3},{1,2},{2,1},{3,0},{4,7},{5,6},{6,5},{7,4},{8,11},{9,10},{10,... | collective-permute-start | bytes 110600 | tf_op jit(solution)/shard_map/ppermute | solution.py:419
  31.2 0.8 %collective-permute-done.15.refs_3_ = bf16[3,144,128]{2,1,0:T(8,128)(2,1)S(1)} collective-permute-done((bf16[3,144,128]{2,1,0:T(8,128)(2,1)S(1)}, bf16[3,144,128]{2,1,0:T(8,128)(2,1)S(1)}, u32[]{:S(2)}, u32[]{:S(2)}) %collective-permute-start.15) | collective-permute-done | bytes 110624 | tf_op jit(solution)/shard_map/ppermute | solution.py:419
  32.2 2.2 %collective-permute-start.16 = (bf16[256,128]{1,0:T(8,128)(2,1)S(1)}, bf16[256,128]{1,0:T(8,128)(2,1)S(1)}, u32[]{:S(2)}, u32[]{:S(2)}) collective-permute-start(bf16[256,128]{1,0:T(8,128)(2,1)S(1)} %get-tuple-element.30), channel_id=1, source_target_pairs={{0,8},{1,9},{2,10},{3,11},{4,12},{5,13},{6,14},{7,15},{8,0},{9,1},... | collective-permute-start | bytes 196616 | tf_op jit(solution)/shard_map/ppermute | solution.py:419
  34.4 2.5 %collective-permute-start.17 = (bf16[256,128]{1,0:T(8,128)(2,1)S(1)}, bf16[256,128]{1,0:T(8,128)(2,1)S(1)}, u32[]{:S(2)}, u32[]{:S(2)}) collective-permute-start(bf16[256,128]{1,0:T(8,128)(2,1)S(1)} %get-tuple-element.31), channel_id=1, source_target_pairs={{0,12},{1,13},{2,14},{3,15},{4,8},{5,9},{6,10},{7,11},{8,4},{9,5},... | collective-permute-start | bytes 196616 | tf_op jit(solution)/shard_map/ppermute | solution.py:419
  37.0 1.1 %collective-permute-done.16.refs_1_ = bf16[256,128]{1,0:T(8,128)(2,1)S(1)} collective-permute-done((bf16[256,128]{1,0:T(8,128)(2,1)S(1)}, bf16[256,128]{1,0:T(8,128)(2,1)S(1)}, u32[]{:S(2)}, u32[]{:S(2)}) %collective-permute-start.16) | collective-permute-done | bytes 65568 | tf_op jit(solution)/shard_map/ppermute | solution.py:419
  38.0 3.3 %collective-permute-done.17.refs_2_ = bf16[256,128]{1,0:T(8,128)(2,1)S(1)} collective-permute-done((bf16[256,128]{1,0:T(8,128)(2,1)S(1)}, bf16[256,128]{1,0:T(8,128)(2,1)S(1)}, u32[]{:S(2)}, u32[]{:S(2)}) %collective-permute-start.17) | collective-permute-done | bytes 65568 | tf_op jit(solution)/shard_map/ppermute | solution.py:419
  41.3 1.4 %collective-permute-done.18.refs_3_ = bf16[256,128]{1,0:T(8,128)(2,1)S(1)} collective-permute-done((bf16[256,128]{1,0:T(8,128)(2,1)S(1)}, bf16[256,128]{1,0:T(8,128)(2,1)S(1)}, u32[]{:S(2)}, u32[]{:S(2)}) %collective-permute-start.18) | collective-permute-done | bytes 65568 | tf_op jit(solution)/shard_map/ppermute | solution.py:419
  42.8 0.7 %total_of.1 = bf16[256,128]{1,0:T(8,128)(2,1)} custom-call(f32[256,128]{1,0:T(8,128)S(1)} %spread.2.refs_0_, bf16[256,128]{1,0:T(8,128)(2,1)S(1)} %collective-permute-done.16.refs_1_, bf16[256,128]{1,0:T(8,128)(2,1)S(1)} %collective-permute-done.17.refs_2_, bf16[256,128]{1,0:T(8,128)(2,1)S(1)} %collective-permute-done.18.refs_3_), custom_call_target="tpu_custom_call" | custom-call | tf_op jit(solution)/shard_map/total_of/pallas_call | solution.py:379
  (64 shorter events, 4.5 us)
Async XLA Ops:
  0.0 10.5 %collective-permute-start.4 = (bf16[256,128]{1,0:T(8,128)(2,1)}, bf16[256,128]{1,0:T(8,128)(2,1)S(1)}, u32[]{:S(2)}, u32[]{:S(2)}) collective-permute-start(bf16[256,128]{1,0:T(8,128)(2,1)} %own.1), channel_id=1, source_target_pairs={{0,2},{1,3},{2,0},{3,1},{4,6},{5,7},{6,4},{7,5},{8,10},{9,11},{10,... | collective-permute-start | bytes 196616 | tf_op jit(solution)/shard_map/ppermute | solution.py:419
  3.0 11.0 %collective-permute-start.3 = (bf16[256,128]{1,0:T(8,128)(2,1)}, bf16[256,128]{1,0:T(8,128)(2,1)S(1)}, u32[]{:S(2)}, u32[]{:S(2)}) collective-permute-start(bf16[256,128]{1,0:T(8,128)(2,1)} %own.1), channel_id=1, source_target_pairs={{0,1},{1,0},{2,3},{3,2},{4,5},{5,4},{6,7},{7,6},{8,9},{9,8},{10,11... | collective-permute-start | bytes 196616 | tf_op jit(solution)/shard_map/ppermute | solution.py:419
  3.0 7.0 %collective-permute-start.1 = (bf16[256,128]{1,0:T(8,128)(2,1)}, bf16[256,128]{1,0:T(8,128)(2,1)S(1)}, u32[]{:S(2)}, u32[]{:S(2)}) collective-permute-start(bf16[256,128]{1,0:T(8,128)(2,1)} %own.1), channel_id=1, source_target_pairs={{0,8},{1,9},{2,10},{3,11},{4,12},{5,13},{6,14},{7,15},{8,0},{9,1},... | collective-permute-start | bytes 196616 | tf_op jit(solution)/shard_map/ppermute | solution.py:419
  5.6 4.8 %collective-permute-start = (bf16[256,128]{1,0:T(8,128)(2,1)}, bf16[256,128]{1,0:T(8,128)(2,1)S(1)}, u32[]{:S(2)}, u32[]{:S(2)}) collective-permute-start(bf16[256,128]{1,0:T(8,128)(2,1)} %own.1), channel_id=1, source_target_pairs={{0,4},{1,5},{2,6},{3,7},{4,0},{5,1},{6,2},{7,3},{8,12},{9,13},{10,... | collective-permute-start | bytes 196616 | tf_op jit(solution)/shard_map/ppermute | solution.py:419
  7.1 6.3 %collective-permute-start.7 = (bf16[256,128]{1,0:T(8,128)(2,1)}, bf16[256,128]{1,0:T(8,128)(2,1)S(1)}, u32[]{:S(2)}, u32[]{:S(2)}) collective-permute-start(bf16[256,128]{1,0:T(8,128)(2,1)} %own.1), channel_id=1, source_target_pairs={{0,12},{1,13},{2,14},{3,15},{4,8},{5,9},{6,10},{7,11},{8,4},{9,5},... | collective-permute-start | bytes 196616 | tf_op jit(solution)/shard_map/ppermute | solution.py:419
  9.7 4.2 %slice-start = ((s8[10485760]{0:T(1024)(128)(4,1)}), s8[4194304]{0:T(1024)(128)(4,1)S(1)}, s32[]{:S(2)}) async-start(s8[10485760]{0:T(1024)(128)(4,1)} %bitcast), calls=%async_computation | async-start | bytes 8388608
  9.7 4.2 %slice-start.1 = ((s8[10485760]{0:T(1024)(128)(4,1)}), s8[4194304]{0:T(1024)(128)(4,1)S(1)}, s32[]{:S(2)}) async-start(s8[10485760]{0:T(1024)(128)(4,1)} %bitcast), calls=%async_computation.1 | async-start | bytes 8388608
  9.8 4.2 %slice-start.2 = ((s8[10485760]{0:T(1024)(128)(4,1)}), s8[2097152]{0:T(1024)(128)(4,1)S(1)}, s32[]{:S(2)}) async-start(s8[10485760]{0:T(1024)(128)(4,1)} %bitcast), calls=%async_computation.2 | async-start | bytes 4194304
  9.8 4.2 %copy-start = (bf16[256,128]{1,0:T(8,128)(2,1)S(1)}, bf16[256,128]{1,0:T(8,128)(2,1)}, u32[]{:S(2)}) copy-start(bf16[256,128]{1,0:T(8,128)(2,1)} %own.1) | copy-start | bytes 196612
  10.3 3.6 %collective-permute-start.2 = (bf16[2,256,128]{2,1,0:T(8,128)(2,1)S(1)}, bf16[2,256,128]{2,1,0:T(8,128)(2,1)S(1)}, u32[]{:S(2)}, u32[]{:S(2)}) collective-permute-start(bf16[2,256,128]{2,1,0:T(8,128)(2,1)S(1)} %merge.1.refs_0_), channel_id=1, source_target_pairs={{0,1},{1,0},{2,3},{3,2},{4,5},{5,4},{6,7},{7,6},{8,9},{9,8},{10,11... | collective-permute-start | bytes 393224 | tf_op jit(solution)/shard_map/ppermute | solution.py:419
  10.5 3.4 %collective-permute-start.5 = (bf16[256,128]{1,0:T(8,128)(2,1)S(1)}, bf16[256,128]{1,0:T(8,128)(2,1)S(1)}, u32[]{:S(2)}, u32[]{:S(2)}) collective-permute-start(bf16[256,128]{1,0:T(8,128)(2,1)S(1)} %collective-permute-done.4.refs_3_), channel_id=1, source_target_pairs={{0,1},{1,0},{2,3},{3,2},{4,5},{5,4},{6,7},{7,6},{8,9},{9,8},{10,11... | collective-permute-start | bytes 196616 | tf_op jit(solution)/shard_map/ppermute | solution.py:419
  11.2 6.8 %collective-permute-start.6 = (bf16[2,256,128]{2,1,0:T(8,128)(2,1)S(1)}, bf16[2,256,128]{2,1,0:T(8,128)(2,1)S(1)}, u32[]{:S(2)}, u32[]{:S(2)}) collective-permute-start(bf16[2,256,128]{2,1,0:T(8,128)(2,1)S(1)} %merge.1.refs_0_), channel_id=1, source_target_pairs={{0,2},{1,3},{2,0},{3,1},{4,6},{5,7},{6,4},{7,5},{8,10},{9,11},{10,... | collective-permute-start | bytes 393224 | tf_op jit(solution)/shard_map/ppermute | solution.py:419
  13.4 4.6 %collective-permute-start.8 = (bf16[256,128]{1,0:T(8,128)(2,1)S(1)}, bf16[256,128]{1,0:T(8,128)(2,1)S(1)}, u32[]{:S(2)}, u32[]{:S(2)}) collective-permute-start(bf16[256,128]{1,0:T(8,128)(2,1)S(1)} %collective-permute-done.7.refs_1_), channel_id=1, source_target_pairs={{0,2},{1,3},{2,0},{3,1},{4,6},{5,7},{6,4},{7,5},{8,10},{9,11},{10,... | collective-permute-start | bytes 196616 | tf_op jit(solution)/shard_map/ppermute | solution.py:419
  18.0 1.6 %collective-permute-start.9 = (bf16[4,256,128]{2,1,0:T(8,128)(2,1)S(1)}, bf16[4,256,128]{2,1,0:T(8,128)(2,1)S(1)}, u32[]{:S(2)}, u32[]{:S(2)}) collective-permute-start(bf16[4,256,128]{2,1,0:T(8,128)(2,1)S(1)} %gate.1.refs_9_), channel_id=1, source_target_pairs={{0,1},{1,0},{2,3},{3,2},{4,5},{5,4},{6,7},{7,6},{8,9},{9,8},{10,11... | collective-permute-start | bytes 786440 | tf_op jit(solution)/shard_map/ppermute | solution.py:419
  24.2 2.5 %collective-permute-start.10 = (bf16[3,144,128]{2,1,0:T(8,128)(2,1)S(1)}, bf16[3,144,128]{2,1,0:T(8,128)(2,1)S(1)}, u32[]{:S(2)}, u32[]{:S(2)}) collective-permute-start(bf16[3,144,128]{2,1,0:T(8,128)(2,1)S(1)} %get-tuple-element.22), channel_id=1, source_target_pairs={{0,1},{1,0},{2,3},{3,2},{4,5},{5,4},{6,7},{7,6},{8,9},{9,8},{10,11... | collective-permute-start | bytes 331784 | tf_op jit(solution)/shard_map/ppermute | solution.py:419
  25.3 5.9 %collective-permute-start.14 = (bf16[3,144,128]{2,1,0:T(8,128)(2,1)S(1)}, bf16[3,144,128]{2,1,0:T(8,128)(2,1)S(1)}, u32[]{:S(2)}, u32[]{:S(2)}) collective-permute-start(bf16[3,144,128]{2,1,0:T(8,128)(2,1)S(1)} %get-tuple-element.28), channel_id=1, source_target_pairs={{0,2},{1,3},{2,0},{3,1},{4,6},{5,7},{6,4},{7,5},{8,10},{9,11},{10,... | collective-permute-start | bytes 331784 | tf_op jit(solution)/shard_map/ppermute | solution.py:419
  26.3 5.7 %collective-permute-start.15 = (bf16[3,144,128]{2,1,0:T(8,128)(2,1)S(1)}, bf16[3,144,128]{2,1,0:T(8,128)(2,1)S(1)}, u32[]{:S(2)}, u32[]{:S(2)}) collective-permute-start(bf16[3,144,128]{2,1,0:T(8,128)(2,1)S(1)} %get-tuple-element.29), channel_id=1, source_target_pairs={{0,3},{1,2},{2,1},{3,0},{4,7},{5,6},{6,5},{7,4},{8,11},{9,10},{10,... | collective-permute-start | bytes 331784 | tf_op jit(solution)/shard_map/ppermute | solution.py:419
  28.7 8.2 %collective-permute-start.11 = (bf16[1,144,128]{2,1,0:T(8,128)(2,1)S(1)}, bf16[1,144,128]{2,1,0:T(8,128)(2,1)S(1)}, u32[]{:S(2)}, u32[]{:S(2)}) collective-permute-start(bf16[1,144,128]{2,1,0:T(8,128)(2,1)S(1)} %get-tuple-element.24), channel_id=1, source_target_pairs={{0,1},{1,0},{2,3},{3,2},{4,5},{5,4},{6,7},{7,6},{8,9},{9,8},{10,11... | collective-permute-start | bytes 110600 | tf_op jit(solution)/shard_map/ppermute | solution.py:419
  29.4 7.5 %collective-permute-start.12 = (bf16[1,144,128]{2,1,0:T(8,128)(2,1)S(1)}, bf16[1,144,128]{2,1,0:T(8,128)(2,1)S(1)}, u32[]{:S(2)}, u32[]{:S(2)}) collective-permute-start(bf16[1,144,128]{2,1,0:T(8,128)(2,1)S(1)} %get-tuple-element.25), channel_id=1, source_target_pairs={{0,2},{1,3},{2,0},{3,1},{4,6},{5,7},{6,4},{7,5},{8,10},{9,11},{10,... | collective-permute-start | bytes 110600 | tf_op jit(solution)/shard_map/ppermute | solution.py:419
  30.3 6.6 %collective-permute-start.13 = (bf16[1,144,128]{2,1,0:T(8,128)(2,1)S(1)}, bf16[1,144,128]{2,1,0:T(8,128)(2,1)S(1)}, u32[]{:S(2)}, u32[]{:S(2)}) collective-permute-start(bf16[1,144,128]{2,1,0:T(8,128)(2,1)S(1)} %get-tuple-element.26), channel_id=1, source_target_pairs={{0,3},{1,2},{2,1},{3,0},{4,7},{5,6},{6,5},{7,4},{8,11},{9,10},{10,... | collective-permute-start | bytes 110600 | tf_op jit(solution)/shard_map/ppermute | solution.py:419
  32.2 5.9 %collective-permute-start.16 = (bf16[256,128]{1,0:T(8,128)(2,1)S(1)}, bf16[256,128]{1,0:T(8,128)(2,1)S(1)}, u32[]{:S(2)}, u32[]{:S(2)}) collective-permute-start(bf16[256,128]{1,0:T(8,128)(2,1)S(1)} %get-tuple-element.30), channel_id=1, source_target_pairs={{0,8},{1,9},{2,10},{3,11},{4,12},{5,13},{6,14},{7,15},{8,0},{9,1},... | collective-permute-start | bytes 196616 | tf_op jit(solution)/shard_map/ppermute | solution.py:419
  34.4 6.9 %collective-permute-start.17 = (bf16[256,128]{1,0:T(8,128)(2,1)S(1)}, bf16[256,128]{1,0:T(8,128)(2,1)S(1)}, u32[]{:S(2)}, u32[]{:S(2)}) collective-permute-start(bf16[256,128]{1,0:T(8,128)(2,1)S(1)} %get-tuple-element.31), channel_id=1, source_target_pairs={{0,12},{1,13},{2,14},{3,15},{4,8},{5,9},{6,10},{7,11},{8,4},{9,5},... | collective-permute-start | bytes 196616 | tf_op jit(solution)/shard_map/ppermute | solution.py:419
  36.9 5.8 %collective-permute-start.18 = (bf16[256,128]{1,0:T(8,128)(2,1)S(1)}, bf16[256,128]{1,0:T(8,128)(2,1)S(1)}, u32[]{:S(2)}, u32[]{:S(2)}) collective-permute-start(bf16[256,128]{1,0:T(8,128)(2,1)S(1)} %get-tuple-element.32), channel_id=1, source_target_pairs={{0,4},{1,5},{2,6},{3,7},{4,0},{5,1},{6,2},{7,3},{8,12},{9,13},{10,... | collective-permute-start | bytes 196616 | tf_op jit(solution)/shard_map/ppermute | solution.py:419

commit v18 on v14

--- a/solution.py
+++ b/solution.py
@@ -9,7 +9,7 @@
 
 AB_DEV = 8
 CHUNK = 2
-TURNS = (8, 2, 1)
+TURNS = (4, 1)
 TAIL = 16
 PLANE = 4
 SPREAD_COST = 10**10

time: 44.3 us -> 44.4 us (level); the launches traced: 43.9 us -> 44.7 us
  Pallas kernels: 10 us -> 10.7 us
  starting transfers between devices: 18.1 us -> 18.8 us
  waiting for transfers between devices: 12.1 us -> 11.5 us
    ppermute x19, starting transfers between devices: 18.1 us -> 18.8 us  [swap(): return lax.ppermute(array, 'aux', [(i, i ^ m) for i in range(n_aux)])]
    ppermute x19, waiting for transfers between devices: 12.1 us -> 11.5 us  [swap(): return lax.ppermute(array, 'aux', [(i, i ^ m) for i in range(n_aux)])]
  transfers between devices with their start and end apart: 19 -> 19, of which waited for: 9 -> 8; matrix products, arithmetic and copies ran while one was open for 6% -> 6% of each run, Pallas kernels for 9% -> 11%
where the time goes in v18:
time: 44.4 us; the launch traced here: 44.7 us
  starting transfers between devices  18.8 us (42%)
  waiting for transfers between devices  11.5 us (26%)
  Pallas kernels  10.7 us (24%)
  other arithmetic  2.75 us (6%)
  between operations  0.91 us (2%)
    ppermute x19, starting transfers between devices, swap(): return lax.ppermute(array, 'aux', [(i, i ^ m) for i in range(n_aux)])  18.8 us
    ppermute x19, waiting for transfers between devices, swap(): return lax.ppermute(array, 'aux', [(i, i ^ m) for i in range(n_aux)])  11.5 us
    pallas_call x1, Pallas kernels, first_part(): pl.pallas_call(kernel, out_shape=out_shape, in_specs=[smem] * 7 + [vmem]...  5.15 us
    pallas_call x1, Pallas kernels, begin(): pl.pallas_call(kernel, out_shape=[jax.ShapeDtypeStruct((AB_DEV, nocc, aux...  2.68 us
    pallas_call x1, Pallas kernels, second_part(): pl.pallas_call(kernel, out_shape=[jax.ShapeDtypeStruct(shape, jnp.bfloat1...  1.92 us
  transfers between devices with their start and end apart: 19, of which 8 were waited for; matrix products, arithmetic and copies ran while one was open for 6% of the time, Pallas kernels for 11%

profile of v18, /device:TPU:0, one launch (start us, length us, event | category | flops | bytes accessed | tf_op | source)
XLA Modules:
  0.0 44.7 jit_solution(16871990309352576000)
XLA Ops:
  0.0 3.0 %collective-permute-start.4 = (bf16[256,128]{1,0:T(8,128)(2,1)}, bf16[256,128]{1,0:T(8,128)(2,1)S(1)}, u32[]{:S(2)}, u32[]{:S(2)}) collective-permute-start(bf16[256,128]{1,0:T(8,128)(2,1)} %own.1), channel_id=1, source_target_pairs={{0,2},{1,3},{2,0},{3,1},{4,6},{5,7},{6,4},{7,5},{8,10},{9,11},{10,... | collective-permute-start | bytes 196616 | tf_op jit(solution)/shard_map/ppermute | solution.py:419
  3.0 2.6 %collective-permute-start.1 = (bf16[256,128]{1,0:T(8,128)(2,1)}, bf16[256,128]{1,0:T(8,128)(2,1)S(1)}, u32[]{:S(2)}, u32[]{:S(2)}) collective-permute-start(bf16[256,128]{1,0:T(8,128)(2,1)} %own.1), channel_id=1, source_target_pairs={{0,8},{1,9},{2,10},{3,11},{4,12},{5,13},{6,14},{7,15},{8,0},{9,1},... | collective-permute-start | bytes 196616 | tf_op jit(solution)/shard_map/ppermute | solution.py:419
  5.6 1.6 %collective-permute-start = (bf16[256,128]{1,0:T(8,128)(2,1)}, bf16[256,128]{1,0:T(8,128)(2,1)S(1)}, u32[]{:S(2)}, u32[]{:S(2)}) collective-permute-start(bf16[256,128]{1,0:T(8,128)(2,1)} %own.1), channel_id=1, source_target_pairs={{0,4},{1,5},{2,6},{3,7},{4,0},{5,1},{6,2},{7,3},{8,12},{9,13},{10,... | collective-permute-start | bytes 196616 | tf_op jit(solution)/shard_map/ppermute | solution.py:419
  8.0 0.8 %add_reduce_fusion.packed_ref = s32[64]{0:T(128)S(1)} fusion(s32[32]{0:T(128)S(1)} %pad.4, s32[64]{0:T(128)} %param.10, s32[32]{0:T(128)S(1)} %fusion.9, s32[64]{0:T(128)} %param.9, s32[32]{0:T(128)} %param.8), kind=kLoop, calls=%fused_computation.15 | loop fusion | flops 16320 | bytes 1152 | tf_op jit(solution)/shard_map/reduce_sum | solution.py:26
  10.0 0.3 collective-permute-done.refs_0_
  10.5 0.6 %collective-permute-start.5 = (bf16[256,128]{1,0:T(8,128)(2,1)S(1)}, bf16[256,128]{1,0:T(8,128)(2,1)S(1)}, u32[]{:S(2)}, u32[]{:S(2)}) collective-permute-start(bf16[256,128]{1,0:T(8,128)(2,1)S(1)} %collective-permute-done.4.refs_3_), channel_id=1, source_target_pairs={{0,1},{1,0},{2,3},{3,2},{4,5},{5,4},{6,7},{7,6},{8,9},{9,8},{10,11... | collective-permute-start | bytes 196616 | tf_op jit(solution)/shard_map/ppermute | solution.py:419
  11.2 0.5 %collective-permute-start.6 = (bf16[2,256,128]{2,1,0:T(8,128)(2,1)S(1)}, bf16[2,256,128]{2,1,0:T(8,128)(2,1)S(1)}, u32[]{:S(2)}, u32[]{:S(2)}) collective-permute-start(bf16[2,256,128]{2,1,0:T(8,128)(2,1)S(1)} %merge.1.refs_0_), channel_id=1, source_target_pairs={{0,2},{1,3},{2,0},{3,1},{4,6},{5,7},{6,4},{7,5},{8,10},{9,11},{10,... | collective-permute-start | bytes 393224 | tf_op jit(solution)/shard_map/ppermute | solution.py:419
  11.6 1.8 %collective-permute-done.7.refs_1_ = bf16[256,128]{1,0:T(8,128)(2,1)S(1)} collective-permute-done((bf16[256,128]{1,0:T(8,128)(2,1)}, bf16[256,128]{1,0:T(8,128)(2,1)S(1)}, u32[]{:S(2)}, u32[]{:S(2)}) %collective-permute-start.7) | collective-permute-done | bytes 65568 | tf_op jit(solution)/shard_map/ppermute | solution.py:419
  13.4 0.5 %collective-permute-start.8 = (bf16[256,128]{1,0:T(8,128)(2,1)S(1)}, bf16[256,128]{1,0:T(8,128)(2,1)S(1)}, u32[]{:S(2)}, u32[]{:S(2)}) collective-permute-start(bf16[256,128]{1,0:T(8,128)(2,1)S(1)} %collective-permute-done.7.refs_1_), channel_id=1, source_target_pairs={{0,2},{1,3},{2,0},{3,1},{4,6},{5,7},{6,4},{7,5},{8,10},{9,11},{10,... | collective-permute-start | bytes 196616 | tf_op jit(solution)/shard_map/ppermute | solution.py:419
  14.0 2.7 %begin.1 = (f32[8,128,640]{2,1,0:T(8,128)S(1)}, s32[64]{0:T(128)S(1)}) custom-call(s32[96]{0:T(128)S(1)} %get-tuple-element.52.slot_ref.refs_0_, s32[96]{0:T(128)S(1)} %get-tuple-element.51.block_ref.refs_1_, s32[64]{0:T(128)S(1)} %pad_add_fusion.gid_ref.refs_2_, s32[16]{0:T(128)S(1)} %select_reduce_fusion.8.bit_ref.refs_6_, ...), custom_call_target="tpu_custom_call" | custom-call | flops 1342177280 | bytes 5242880 | tf_op jit(solution)/shard_map/begin/pallas_call | solution.py:151
  17.5 0.5 %collective-permute-done.8.refs_2_ = bf16[256,128]{1,0:T(8,128)(2,1)S(1)} collective-permute-done((bf16[256,128]{1,0:T(8,128)(2,1)S(1)}, bf16[256,128]{1,0:T(8,128)(2,1)S(1)}, u32[]{:S(2)}, u32[]{:S(2)}) %collective-permute-start.8) | collective-permute-done | bytes 65568 | tf_op jit(solution)/shard_map/ppermute | solution.py:419
  18.2 1.4 %collective-permute-done.9.refs_10_ = bf16[4,256,128]{2,1,0:T(8,128)(2,1)S(1)} collective-permute-done((bf16[4,256,128]{2,1,0:T(8,128)(2,1)S(1)}, bf16[4,256,128]{2,1,0:T(8,128)(2,1)S(1)}, u32[]{:S(2)}, u32[]{:S(2)}) %collective-permute-start.9) | collective-permute-done | bytes 262176 | tf_op jit(solution)/shard_map/ppermute | solution.py:419
  19.6 5.1 %first_part.1 = (bf16[3,144,128]{2,1,0:T(8,128)(2,1)S(1)}, bf16[3,144,128]{2,1,0:T(8,128)(2,1)S(1)}, bf16[3,144,128]{2,1,0:T(8,128)(2,1)S(1)}, bf16[3,144,128]{2...) custom-call(s32[96]{0:T(128)S(1)} %get-tuple-element.52.slot_ref.ref, ...), custom_call_target="tpu_custom_call", output_to_operand_aliasing={{5}: (8, {})} | custom-call | flops 2013265920 | bytes 5242880 | tf_op jit(solution)/shard_map/first_part/pallas_call | solution.py:213
  24.8 0.9 %collective-permute-start.10 = (bf16[3,144,128]{2,1,0:T(8,128)(2,1)S(1)}, bf16[3,144,128]{2,1,0:T(8,128)(2,1)S(1)}, u32[]{:S(2)}, u32[]{:S(2)}) collective-permute-start(bf16[3,144,128]{2,1,0:T(8,128)(2,1)S(1)} %get-tuple-element.22), channel_id=1, source_target_pairs={{0,1},{1,0},{2,3},{3,2},{4,5},{5,4},{6,7},{7,6},{8,9},{9,8},{10,11... | collective-permute-start | bytes 331784 | tf_op jit(solution)/shard_map/ppermute | solution.py:419
  25.7 1.7 %collective-permute-start.14 = (bf16[3,144,128]{2,1,0:T(8,128)(2,1)S(1)}, bf16[3,144,128]{2,1,0:T(8,128)(2,1)S(1)}, u32[]{:S(2)}, u32[]{:S(2)}) collective-permute-start(bf16[3,144,128]{2,1,0:T(8,128)(2,1)S(1)} %get-tuple-element.28), channel_id=1, source_target_pairs={{0,2},{1,3},{2,0},{3,1},{4,6},{5,7},{6,4},{7,5},{8,10},{9,11},{10,... | collective-permute-start | bytes 331784 | tf_op jit(solution)/shard_map/ppermute | solution.py:419
  27.5 1.9 %second_part.1 = (bf16[1,144,128]{2,1,0:T(8,128)(2,1)S(1)}, bf16[1,144,128]{2,1,0:T(8,128)(2,1)S(1)}, bf16[1,144,128]{2,1,0:T(8,128)(2,1)S(1)}, bf16[1,144,128]{2,1,0:T(8,128)(2,1)S(1)}) custom-call(s32[96]{0:T(128)S(1)} %get-tuple-element.50.refs_3_.slot_ref, s32[96]{0:T(128)S(1)} %get-tuple-element.49.refs_4_.block_ref, ...), custom_call_target="tpu_custom_call" | custom-call | flops 10000000000 | bytes 5242880 | tf_op jit(solution)/shard_map/second_part/pallas_call | solution.py:246
  29.4 0.9 %collective-permute-start.11 = (bf16[1,144,128]{2,1,0:T(8,128)(2,1)S(1)}, bf16[1,144,128]{2,1,0:T(8,128)(2,1)S(1)}, u32[]{:S(2)}, u32[]{:S(2)}) collective-permute-start(bf16[1,144,128]{2,1,0:T(8,128)(2,1)S(1)} %get-tuple-element.24), channel_id=1, source_target_pairs={{0,1},{1,0},{2,3},{3,2},{4,5},{5,4},{6,7},{7,6},{8,9},{9,8},{10,11... | collective-permute-start | bytes 110600 | tf_op jit(solution)/shard_map/ppermute | solution.py:419
  30.3 1.2 %collective-permute-start.12 = (bf16[1,144,128]{2,1,0:T(8,128)(2,1)S(1)}, bf16[1,144,128]{2,1,0:T(8,128)(2,1)S(1)}, u32[]{:S(2)}, u32[]{:S(2)}) collective-permute-start(bf16[1,144,128]{2,1,0:T(8,128)(2,1)S(1)} %get-tuple-element.25), channel_id=1, source_target_pairs={{0,2},{1,3},{2,0},{3,1},{4,6},{5,7},{6,4},{7,5},{8,10},{9,11},{10,... | collective-permute-start | bytes 110600 | tf_op jit(solution)/shard_map/ppermute | solution.py:419
  31.8 1.4 %collective-permute-done.15.refs_3_ = bf16[3,144,128]{2,1,0:T(8,128)(2,1)S(1)} collective-permute-done((bf16[3,144,128]{2,1,0:T(8,128)(2,1)S(1)}, bf16[3,144,128]{2,1,0:T(8,128)(2,1)S(1)}, u32[]{:S(2)}, u32[]{:S(2)}) %collective-permute-start.15) | collective-permute-done | bytes 110624 | tf_op jit(solution)/shard_map/ppermute | solution.py:419
  33.3 4.2 %collective-permute-start.16 = (bf16[256,128]{1,0:T(8,128)(2,1)S(1)}, bf16[256,128]{1,0:T(8,128)(2,1)S(1)}, u32[]{:S(2)}, u32[]{:S(2)}) collective-permute-start(bf16[256,128]{1,0:T(8,128)(2,1)S(1)} %get-tuple-element.30), channel_id=1, source_target_pairs={{0,12},{1,13},{2,14},{3,15},{4,8},{5,9},{6,10},{7,11},{8,4},{9,5},... | collective-permute-start | bytes 196616 | tf_op jit(solution)/shard_map/ppermute | solution.py:419
  37.5 0.6 %collective-permute-start.18 = (bf16[256,128]{1,0:T(8,128)(2,1)S(1)}, bf16[256,128]{1,0:T(8,128)(2,1)S(1)}, u32[]{:S(2)}, u32[]{:S(2)}) collective-permute-start(bf16[256,128]{1,0:T(8,128)(2,1)S(1)} %get-tuple-element.32), channel_id=1, source_target_pairs={{0,4},{1,5},{2,6},{3,7},{4,0},{5,1},{6,2},{7,3},{8,12},{9,13},{10,... | collective-permute-start | bytes 196616 | tf_op jit(solution)/shard_map/ppermute | solution.py:419
  38.2 2.3 %collective-permute-done.16.refs_1_ = bf16[256,128]{1,0:T(8,128)(2,1)S(1)} collective-permute-done((bf16[256,128]{1,0:T(8,128)(2,1)S(1)}, bf16[256,128]{1,0:T(8,128)(2,1)S(1)}, u32[]{:S(2)}, u32[]{:S(2)}) %collective-permute-start.16) | collective-permute-done | bytes 65568 | tf_op jit(solution)/shard_map/ppermute | solution.py:419
  40.5 3.5 %collective-permute-done.17.refs_2_ = bf16[256,128]{1,0:T(8,128)(2,1)S(1)} collective-permute-done((bf16[256,128]{1,0:T(8,128)(2,1)S(1)}, bf16[256,128]{1,0:T(8,128)(2,1)S(1)}, u32[]{:S(2)}, u32[]{:S(2)}) %collective-permute-start.17) | collective-permute-done | bytes 65568 | tf_op jit(solution)/shard_map/ppermute | solution.py:419
  44.0 0.7 %total_of.1 = bf16[256,128]{1,0:T(8,128)(2,1)} custom-call(f32[256,128]{1,0:T(8,128)S(1)} %spread.2.refs_0_, bf16[256,128]{1,0:T(8,128)(2,1)S(1)} %collective-permute-done.16.refs_1_, bf16[256,128]{1,0:T(8,128)(2,1)S(1)} %collective-permute-done.17.refs_2_, bf16[256,128]{1,0:T(8,128)(2,1)S(1)} %collective-permute-done.18.refs_3_), custom_call_target="tpu_custom_call" | custom-call | tf_op jit(solution)/shard_map/total_of/pallas_call | solution.py:379
  (64 shorter events, 3.2 us)
Async XLA Ops:
  0.0 10.5 %collective-permute-start.4 = (bf16[256,128]{1,0:T(8,128)(2,1)}, bf16[256,128]{1,0:T(8,128)(2,1)S(1)}, u32[]{:S(2)}, u32[]{:S(2)}) collective-permute-start(bf16[256,128]{1,0:T(8,128)(2,1)} %own.1), channel_id=1, source_target_pairs={{0,2},{1,3},{2,0},{3,1},{4,6},{5,7},{6,4},{7,5},{8,10},{9,11},{10,... | collective-permute-start | bytes 196616 | tf_op jit(solution)/shard_map/ppermute | solution.py:419
  3.0 11.0 %collective-permute-start.3 = (bf16[256,128]{1,0:T(8,128)(2,1)}, bf16[256,128]{1,0:T(8,128)(2,1)S(1)}, u32[]{:S(2)}, u32[]{:S(2)}) collective-permute-start(bf16[256,128]{1,0:T(8,128)(2,1)} %own.1), channel_id=1, source_target_pairs={{0,1},{1,0},{2,3},{3,2},{4,5},{5,4},{6,7},{7,6},{8,9},{9,8},{10,11... | collective-permute-start | bytes 196616 | tf_op jit(solution)/shard_map/ppermute | solution.py:419
  3.0 7.0 %collective-permute-start.1 = (bf16[256,128]{1,0:T(8,128)(2,1)}, bf16[256,128]{1,0:T(8,128)(2,1)S(1)}, u32[]{:S(2)}, u32[]{:S(2)}) collective-permute-start(bf16[256,128]{1,0:T(8,128)(2,1)} %own.1), channel_id=1, source_target_pairs={{0,8},{1,9},{2,10},{3,11},{4,12},{5,13},{6,14},{7,15},{8,0},{9,1},... | collective-permute-start | bytes 196616 | tf_op jit(solution)/shard_map/ppermute | solution.py:419
  5.6 4.8 %collective-permute-start = (bf16[256,128]{1,0:T(8,128)(2,1)}, bf16[256,128]{1,0:T(8,128)(2,1)S(1)}, u32[]{:S(2)}, u32[]{:S(2)}) collective-permute-start(bf16[256,128]{1,0:T(8,128)(2,1)} %own.1), channel_id=1, source_target_pairs={{0,4},{1,5},{2,6},{3,7},{4,0},{5,1},{6,2},{7,3},{8,12},{9,13},{10,... | collective-permute-start | bytes 196616 | tf_op jit(solution)/shard_map/ppermute | solution.py:419
  7.1 6.3 %collective-permute-start.7 = (bf16[256,128]{1,0:T(8,128)(2,1)}, bf16[256,128]{1,0:T(8,128)(2,1)S(1)}, u32[]{:S(2)}, u32[]{:S(2)}) collective-permute-start(bf16[256,128]{1,0:T(8,128)(2,1)} %own.1), channel_id=1, source_target_pairs={{0,12},{1,13},{2,14},{3,15},{4,8},{5,9},{6,10},{7,11},{8,4},{9,5},... | collective-permute-start | bytes 196616 | tf_op jit(solution)/shard_map/ppermute | solution.py:419
  9.7 4.2 %slice-start = ((s8[10485760]{0:T(1024)(128)(4,1)}), s8[4194304]{0:T(1024)(128)(4,1)S(1)}, s32[]{:S(2)}) async-start(s8[10485760]{0:T(1024)(128)(4,1)} %bitcast), calls=%async_computation | async-start | bytes 8388608
  9.7 4.2 %slice-start.1 = ((s8[10485760]{0:T(1024)(128)(4,1)}), s8[4194304]{0:T(1024)(128)(4,1)S(1)}, s32[]{:S(2)}) async-start(s8[10485760]{0:T(1024)(128)(4,1)} %bitcast), calls=%async_computation.1 | async-start | bytes 8388608
  9.8 4.2 %slice-start.2 = ((s8[10485760]{0:T(1024)(128)(4,1)}), s8[2097152]{0:T(1024)(128)(4,1)S(1)}, s32[]{:S(2)}) async-start(s8[10485760]{0:T(1024)(128)(4,1)} %bitcast), calls=%async_computation.2 | async-start | bytes 4194304
  9.8 4.2 %copy-start = (bf16[256,128]{1,0:T(8,128)(2,1)S(1)}, bf16[256,128]{1,0:T(8,128)(2,1)}, u32[]{:S(2)}) copy-start(bf16[256,128]{1,0:T(8,128)(2,1)} %own.1) | copy-start | bytes 196612
  10.3 3.6 %collective-permute-start.2 = (bf16[2,256,128]{2,1,0:T(8,128)(2,1)S(1)}, bf16[2,256,128]{2,1,0:T(8,128)(2,1)S(1)}, u32[]{:S(2)}, u32[]{:S(2)}) collective-permute-start(bf16[2,256,128]{2,1,0:T(8,128)(2,1)S(1)} %merge.1.refs_0_), channel_id=1, source_target_pairs={{0,1},{1,0},{2,3},{3,2},{4,5},{5,4},{6,7},{7,6},{8,9},{9,8},{10,11... | collective-permute-start | bytes 393224 | tf_op jit(solution)/shard_map/ppermute | solution.py:419
  10.5 3.4 %collective-permute-start.5 = (bf16[256,128]{1,0:T(8,128)(2,1)S(1)}, bf16[256,128]{1,0:T(8,128)(2,1)S(1)}, u32[]{:S(2)}, u32[]{:S(2)}) collective-permute-start(bf16[256,128]{1,0:T(8,128)(2,1)S(1)} %collective-permute-done.4.refs_3_), channel_id=1, source_target_pairs={{0,1},{1,0},{2,3},{3,2},{4,5},{5,4},{6,7},{7,6},{8,9},{9,8},{10,11... | collective-permute-start | bytes 196616 | tf_op jit(solution)/shard_map/ppermute | solution.py:419
  11.2 6.8 %collective-permute-start.6 = (bf16[2,256,128]{2,1,0:T(8,128)(2,1)S(1)}, bf16[2,256,128]{2,1,0:T(8,128)(2,1)S(1)}, u32[]{:S(2)}, u32[]{:S(2)}) collective-permute-start(bf16[2,256,128]{2,1,0:T(8,128)(2,1)S(1)} %merge.1.refs_0_), channel_id=1, source_target_pairs={{0,2},{1,3},{2,0},{3,1},{4,6},{5,7},{6,4},{7,5},{8,10},{9,11},{10,... | collective-permute-start | bytes 393224 | tf_op jit(solution)/shard_map/ppermute | solution.py:419
  13.4 4.6 %collective-permute-start.8 = (bf16[256,128]{1,0:T(8,128)(2,1)S(1)}, bf16[256,128]{1,0:T(8,128)(2,1)S(1)}, u32[]{:S(2)}, u32[]{:S(2)}) collective-permute-start(bf16[256,128]{1,0:T(8,128)(2,1)S(1)} %collective-permute-done.7.refs_1_), channel_id=1, source_target_pairs={{0,2},{1,3},{2,0},{3,1},{4,6},{5,7},{6,4},{7,5},{8,10},{9,11},{10,... | collective-permute-start | bytes 196616 | tf_op jit(solution)/shard_map/ppermute | solution.py:419
  18.0 1.6 %collective-permute-start.9 = (bf16[4,256,128]{2,1,0:T(8,128)(2,1)S(1)}, bf16[4,256,128]{2,1,0:T(8,128)(2,1)S(1)}, u32[]{:S(2)}, u32[]{:S(2)}) collective-permute-start(bf16[4,256,128]{2,1,0:T(8,128)(2,1)S(1)} %gate.1.refs_9_), channel_id=1, source_target_pairs={{0,1},{1,0},{2,3},{3,2},{4,5},{5,4},{6,7},{7,6},{8,9},{9,8},{10,11... | collective-permute-start | bytes 786440 | tf_op jit(solution)/shard_map/ppermute | solution.py:419
  24.8 2.7 %collective-permute-start.10 = (bf16[3,144,128]{2,1,0:T(8,128)(2,1)S(1)}, bf16[3,144,128]{2,1,0:T(8,128)(2,1)S(1)}, u32[]{:S(2)}, u32[]{:S(2)}) collective-permute-start(bf16[3,144,128]{2,1,0:T(8,128)(2,1)S(1)} %get-tuple-element.22), channel_id=1, source_target_pairs={{0,1},{1,0},{2,3},{3,2},{4,5},{5,4},{6,7},{7,6},{8,9},{9,8},{10,11... | collective-permute-start | bytes 331784 | tf_op jit(solution)/shard_map/ppermute | solution.py:419
  25.7 6.1 %collective-permute-start.14 = (bf16[3,144,128]{2,1,0:T(8,128)(2,1)S(1)}, bf16[3,144,128]{2,1,0:T(8,128)(2,1)S(1)}, u32[]{:S(2)}, u32[]{:S(2)}) collective-permute-start(bf16[3,144,128]{2,1,0:T(8,128)(2,1)S(1)} %get-tuple-element.28), channel_id=1, source_target_pairs={{0,2},{1,3},{2,0},{3,1},{4,6},{5,7},{6,4},{7,5},{8,10},{9,11},{10,... | collective-permute-start | bytes 331784 | tf_op jit(solution)/shard_map/ppermute | solution.py:419
  27.4 5.7 %collective-permute-start.15 = (bf16[3,144,128]{2,1,0:T(8,128)(2,1)S(1)}, bf16[3,144,128]{2,1,0:T(8,128)(2,1)S(1)}, u32[]{:S(2)}, u32[]{:S(2)}) collective-permute-start(bf16[3,144,128]{2,1,0:T(8,128)(2,1)S(1)} %get-tuple-element.29), channel_id=1, source_target_pairs={{0,3},{1,2},{2,1},{3,0},{4,7},{5,6},{6,5},{7,4},{8,11},{9,10},{10,... | collective-permute-start | bytes 331784 | tf_op jit(solution)/shard_map/ppermute | solution.py:419
  29.4 8.1 %collective-permute-start.11 = (bf16[1,144,128]{2,1,0:T(8,128)(2,1)S(1)}, bf16[1,144,128]{2,1,0:T(8,128)(2,1)S(1)}, u32[]{:S(2)}, u32[]{:S(2)}) collective-permute-start(bf16[1,144,128]{2,1,0:T(8,128)(2,1)S(1)} %get-tuple-element.24), channel_id=1, source_target_pairs={{0,1},{1,0},{2,3},{3,2},{4,5},{5,4},{6,7},{7,6},{8,9},{9,8},{10,11... | collective-permute-start | bytes 110600 | tf_op jit(solution)/shard_map/ppermute | solution.py:419
  30.3 7.8 %collective-permute-start.12 = (bf16[1,144,128]{2,1,0:T(8,128)(2,1)S(1)}, bf16[1,144,128]{2,1,0:T(8,128)(2,1)S(1)}, u32[]{:S(2)}, u32[]{:S(2)}) collective-permute-start(bf16[1,144,128]{2,1,0:T(8,128)(2,1)S(1)} %get-tuple-element.25), channel_id=1, source_target_pairs={{0,2},{1,3},{2,0},{3,1},{4,6},{5,7},{6,4},{7,5},{8,10},{9,11},{10,... | collective-permute-start | bytes 110600 | tf_op jit(solution)/shard_map/ppermute | solution.py:419
  31.5 6.6 %collective-permute-start.13 = (bf16[1,144,128]{2,1,0:T(8,128)(2,1)S(1)}, bf16[1,144,128]{2,1,0:T(8,128)(2,1)S(1)}, u32[]{:S(2)}, u32[]{:S(2)}) collective-permute-start(bf16[1,144,128]{2,1,0:T(8,128)(2,1)S(1)} %get-tuple-element.26), channel_id=1, source_target_pairs={{0,3},{1,2},{2,1},{3,0},{4,7},{5,6},{6,5},{7,4},{8,11},{9,10},{10,... | collective-permute-start | bytes 110600 | tf_op jit(solution)/shard_map/ppermute | solution.py:419
  33.3 7.2 %collective-permute-start.16 = (bf16[256,128]{1,0:T(8,128)(2,1)S(1)}, bf16[256,128]{1,0:T(8,128)(2,1)S(1)}, u32[]{:S(2)}, u32[]{:S(2)}) collective-permute-start(bf16[256,128]{1,0:T(8,128)(2,1)S(1)} %get-tuple-element.30), channel_id=1, source_target_pairs={{0,12},{1,13},{2,14},{3,15},{4,8},{5,9},{6,10},{7,11},{8,4},{9,5},... | collective-permute-start | bytes 196616 | tf_op jit(solution)/shard_map/ppermute | solution.py:419
  37.5 6.6 %collective-permute-start.17 = (bf16[256,128]{1,0:T(8,128)(2,1)S(1)}, bf16[256,128]{1,0:T(8,128)(2,1)S(1)}, u32[]{:S(2)}, u32[]{:S(2)}) collective-permute-start(bf16[256,128]{1,0:T(8,128)(2,1)S(1)} %get-tuple-element.31), channel_id=1, source_target_pairs={{0,8},{1,9},{2,10},{3,11},{4,12},{5,13},{6,14},{7,15},{8,0},{9,1},... | collective-permute-start | bytes 196616 | tf_op jit(solution)/shard_map/ppermute | solution.py:419
  37.5 6.6 %collective-permute-start.18 = (bf16[256,128]{1,0:T(8,128)(2,1)S(1)}, bf16[256,128]{1,0:T(8,128)(2,1)S(1)}, u32[]{:S(2)}, u32[]{:S(2)}) collective-permute-start(bf16[256,128]{1,0:T(8,128)(2,1)S(1)} %get-tuple-element.32), channel_id=1, source_target_pairs={{0,4},{1,5},{2,6},{3,7},{4,0},{5,1},{6,2},{7,3},{8,12},{9,13},{10,... | collective-permute-start | bytes 196616 | tf_op jit(solution)/shard_map/ppermute | solution.py:419
